TPU v7x, 32 devices: a whole 2x2x4 slice. The times are simulated.
32 devices in a mesh: groups: 2 (over x), expert: 16 (over z, y, core).
Axes of the slice: x: 2, y: 2, z: 4, core: 2. Of those that a mesh axis runs over, the one named last changes fastest.
Arguments:
- tokens: bfloat16 [4096, 2048], P(('groups', 'expert')), parts along dimension 0, may hold values from -6 to 6
- cotangent: bfloat16 [4096, 2048], P(('groups', 'expert')), parts along dimension 0, may hold values from -4 to 4
- expert_ids: int32 [4096, 4], P(('groups', 'expert')), parts along dimension 0, may hold values from 0 to 15, all different within a row; in each aligned block of 128 rows (0 to 127, 128 to 255, ...) at most 48 rows name the same one
- gate_levels: int32 [4096, 4], P(('groups', 'expert')), parts along dimension 0, may hold values from 1 to 256
- w_gate: bfloat16 [16, 2048, 384], P('expert'), may hold values from -0.125 to 0.125
- w_up: bfloat16 [16, 2048, 384], P('expert'), may hold values from -0.125 to 0.125
- w_down: bfloat16 [16, 384, 2048], P('expert'), may hold values from -0.3125 to 0.3125
Outputs:
- input_grad: bfloat16 [4096, 2048], P(('groups', 'expert')), parts along dimension 0
- router_grad: bfloat16 [4096, 4], P(('groups', 'expert')), parts along dimension 0
- gate_delta: bfloat16 [32, 2048, 384], P(('groups', 'expert')), parts along dimension 0
- up_delta: bfloat16 [32, 2048, 384], P(('groups', 'expert')), parts along dimension 0
- down_delta: bfloat16 [32, 384, 2048], P(('groups', 'expert')), parts along dimension 0
There are 2 independent parts, one for each index of `groups`. A program takes and returns all parts, laid end to end along the dimension named above; an argument that names none is the same for every part. Nothing has to cross between parts.
Inputs may be any that keep to these rules, and one draw needn't show every extreme that they name: `expert_ids`: each token names 4 different experts. Among the tokens of one device no expert is named more than 48 times, and in every draw some expert is named exactly 48 times by some device.
All inputs are finite; a program needn't handle non-finite values.
Results may differ from a plain program's by a relative error of at most 0.014.
Values may be sent and summed in bfloat16 or wider, within the bound.
No kernel may reach another device: no remote copies, remote signals or barrier semaphores. Data moves between devices by JAX's collectives and lax.ppermute only.
A program may use at most 128 MiB of HBM per device.

v0:
```python
import jax
import jax.numpy as jnp
from jax import lax
from jax.sharding import PartitionSpec as P


def project(inputs, gate_mat, up_mat):
    gate_pre = jnp.dot(inputs, gate_mat, preferred_element_type=jnp.float32)
    up_pre = jnp.dot(inputs, up_mat, preferred_element_type=jnp.float32)
    return (gate_pre, up_pre)


def backward(inputs, prepared, cotangent, gating, gate_mat, up_mat, down_mat):
    gate_pre, up_pre = prepared
    sigmoid_gate = jax.nn.sigmoid(gate_pre)
    hidden = (gate_pre * sigmoid_gate * up_pre).astype(jnp.bfloat16)
    back_grad = lax.dot_general(
        cotangent, down_mat, (((1,), (1,)), ((), ())), preferred_element_type=jnp.float32
    )
    router_term = jnp.sum(hidden.astype(jnp.float32) * back_grad, axis=1).astype(jnp.bfloat16)
    hidden_grad = gating[:, None] * back_grad
    gate_grad = (
        hidden_grad * up_pre * sigmoid_gate * (1.0 + gate_pre * (1.0 - sigmoid_gate))
    ).astype(jnp.bfloat16)
    up_grad = (hidden_grad * gate_pre * sigmoid_gate).astype(jnp.bfloat16)
    input_term = lax.dot_general(
        gate_grad, gate_mat, (((1,), (1,)), ((), ())), preferred_element_type=jnp.float32
    )
    input_term = input_term + lax.dot_general(
        up_grad, up_mat, (((1,), (1,)), ((), ())), preferred_element_type=jnp.float32
    )
    input_term = input_term.astype(jnp.bfloat16)
    scaled = (gating[:, None] * cotangent.astype(jnp.float32)).astype(jnp.bfloat16)
    down_delta = lax.dot_general(
        hidden, scaled, (((0,), (0,)), ((), ())), preferred_element_type=jnp.float32
    )
    gate_delta = lax.dot_general(
        inputs, gate_grad, (((0,), (0,)), ((), ())), preferred_element_type=jnp.float32
    )
    up_delta = lax.dot_general(
        inputs, up_grad, (((0,), (0,)), ((), ())), preferred_element_type=jnp.float32
    )
    return (input_term, router_term, gate_delta, up_delta, down_delta)


def on_device(tokens, cotangent, expert_ids, gate_levels, w_gate, w_up, w_down):
    devices = lax.axis_size("expert")
    tok_rows, fanout = expert_ids.shape
    features = tokens.shape[1]
    capacity = 3 * tok_rows * fanout // (2 * devices)
    slot_rows = devices * capacity
    gate_mat = w_gate[0]
    up_mat = w_up[0]
    down_mat = w_down[0]
    chosen = expert_ids.reshape(-1)
    indicator = (chosen[:, None] == jnp.arange(devices, dtype=jnp.int32)[None, :]).astype(jnp.int32)
    earlier = jnp.cumsum(indicator, axis=0) - indicator
    position = jnp.sum(earlier * indicator, axis=1)
    target = chosen * capacity + position
    gating_local = (gate_levels.reshape(-1).astype(jnp.float32) / 256.0).astype(jnp.bfloat16)
    outbox_x = (
        jnp.zeros((slot_rows, features), jnp.bfloat16)
        .at[target]
        .set(jnp.repeat(tokens, fanout, axis=0))
    )
    outbox_dy = (
        jnp.zeros((slot_rows, features), jnp.bfloat16)
        .at[target]
        .set(jnp.repeat(cotangent, fanout, axis=0))
    )
    outbox_g = jnp.zeros((slot_rows,), jnp.bfloat16).at[target].set(gating_local)
    outbox_x = outbox_x.reshape(devices, capacity, features)
    outbox_dy = outbox_dy.reshape(devices, capacity, features)
    outbox_g = outbox_g.reshape(devices, capacity)
    prepared = None
    arrived_x, arrived_dy, arrived_g = (
        lax.all_to_all(outbox_x, "expert", split_axis=0, concat_axis=0, tiled=True),
        lax.all_to_all(outbox_dy, "expert", split_axis=0, concat_axis=0, tiled=True),
        lax.all_to_all(outbox_g, "expert", split_axis=0, concat_axis=0, tiled=True),
    )
    rows_x = arrived_x.reshape(slot_rows, features)
    rows_dy = arrived_dy.reshape(slot_rows, features)
    rows_g = arrived_g.reshape(-1).astype(jnp.float32)
    prepared = project(rows_x, gate_mat, up_mat)
    input_term, router_term, gate_delta, up_delta, down_delta = backward(
        rows_x, prepared, rows_dy, rows_g, gate_mat, up_mat, down_mat
    )
    back_term, back_router = (
        lax.all_to_all(
            input_term.reshape(devices, capacity, features),
            "expert",
            split_axis=0,
            concat_axis=0,
            tiled=True,
        ),
        lax.all_to_all(
            router_term.reshape(devices, capacity),
            "expert",
            split_axis=0,
            concat_axis=0,
            tiled=True,
        ),
    )
    gathered_term = back_term.reshape(slot_rows, features)[target].astype(jnp.float32)
    input_grad = jnp.sum(gathered_term.reshape(tok_rows, fanout, features), axis=1).astype(
        jnp.bfloat16
    )
    router_grad = back_router.reshape(-1)[target].reshape(tok_rows, fanout)
    return (
        input_grad,
        router_grad,
        gate_delta.astype(jnp.bfloat16)[None],
        up_delta.astype(jnp.bfloat16)[None],
        down_delta.astype(jnp.bfloat16)[None],
    )


def solution(mesh):
    in_specs = (
        P(("groups", "expert"), None),
        P(("groups", "expert"), None),
        P(("groups", "expert"), None),
        P(("groups", "expert"), None),
        P("expert", None, None),
        P("expert", None, None),
        P("expert", None, None),
    )
    out_specs = (
        P(("groups", "expert"), None),
        P(("groups", "expert"), None),
        P(("groups", "expert"), None, None),
        P(("groups", "expert"), None, None),
        P(("groups", "expert"), None, None),
    )
    return jax.shard_map(
        on_device, mesh=mesh, in_specs=in_specs, out_specs=out_specs, check_vma=False
    )
```

profile of v0, /device:TPU:15, one launch (start us, length us, event | category | flops | bytes accessed | tf_op | source)
XLA Modules:
  0.0 292.4 jit_solution(17450733246968188835)
XLA Ops:
  0.6 0.0 copy-start
  0.6 0.8 broadcast_multiply_fusion
  1.4 0.8 copy.19
  2.2 0.1 eq.29
  2.3 0.1 eq.25
  2.5 0.7 multiply_convert_fusion.9
  3.1 0.1 copy.22
  3.3 0.1 reshape.154
  3.4 0.1 copy.18
  3.5 0.1 mul.64
  3.6 1.2 reduce-window.6
  4.8 0.2 slice_reduce_fusion
  5.1 0.1 fusion.21
  5.2 3.8 %scatter_custom_fusion = bf16[768]{0:T(1024)(128)(2,1)S(1)} fusion(s32[512]{0:T(512)S(1)} %bitcast.64, bf16[512]{0:T(512)(128)(2,1)S(1)} %reshape.154, bf16[]{:T(256)} %constant.7.clone.1), kind=kCustom, calls=%fused_computation.47 | custom fusion | bytes 1538 | tf_op jit(solution)/shard_map/scatter | solution.py:71
  8.9 0.7 all_to_all.25
  9.6 6.6 %all-to-all-start = ((bf16[16,1,48]{2,1,0:T(2,128)(2,1)}), bf16[16,1,48]{2,1,0:T(2,128)(2,1)S(1)}, u32[]{:S(2)}, u32[]{:S(2)}) async-start(bf16[16,1,48]{2,1,0:T(2,128)(2,1)} %all_to_all.25), calls=%async_computation | async-start | bytes 16384 | tf_op jit(solution)/shard_map/all_to_all | solution.py:79
  16.2 3.4 %broadcast_in_dim.28 = bf16[128,4,2048]{2,1,0:T(4,128)(2,1)} broadcast(bf16[128,2048]{1,0:T(8,128)(2,1)} %param.7), dimensions={0,2} | broadcast | bytes 2621440 | tf_op jit(solution)/shard_map/broadcast_in_dim | solution.py:64
  19.6 4.0 %reshape.170 = bf16[512,2048]{1,0:T(8,128)(2,1)} reshape(bf16[128,4,2048]{2,1,0:T(4,128)(2,1)} %broadcast_in_dim.28) | data formatting | bytes 4194304 | tf_op jit(solution)/shard_map/reshape | solution.py:64
  23.5 6.7 %scatter_custom_fusion.2 = bf16[768,2048]{1,0:T(8,128)(2,1)} fusion(s32[512]{0:T(512)S(1)} %bitcast.65, bf16[512,2048]{1,0:T(8,128)(2,1)} %reshape.170, bf16[]{:T(256)} %constant.7.clone.1), kind=kCustom, calls=%fused_computation.24 | custom fusion | bytes 3146240 | tf_op jit(solution)/shard_map/scatter | solution.py:64
  30.3 0.0 all-to-all-done
  30.3 6.2 %all-to-all-start.2 = ((bf16[16,48,2048]{2,1,0:T(8,128)(2,1)}), bf16[16,48,2048]{2,1,0:T(8,128)(2,1)}, u32[]{:S(2)}, u32[]{:S(2)}) async-start(bf16[16,48,2048]{2,1,0:T(8,128)(2,1)} %bitcast.62), calls=%async_computation.2 | async-start | bytes 6291456 | tf_op jit(solution)/shard_map/all_to_all | solution.py:77
  36.4 2.4 broadcast_in_dim.13
  38.8 4.0 %reshape.162 = bf16[512,2048]{1,0:T(8,128)(2,1)} reshape(bf16[128,4,2048]{2,1,0:T(4,128)(2,1)} %broadcast_in_dim.13) | data formatting | bytes 4194304 | tf_op jit(solution)/shard_map/reshape | solution.py:69
  42.8 6.7 %scatter_custom_fusion.1 = bf16[768,2048]{1,0:T(8,128)(2,1)} fusion(s32[512]{0:T(512)S(1)} %bitcast.66, bf16[512,2048]{1,0:T(8,128)(2,1)} %reshape.162, bf16[]{:T(256)} %constant.7.clone.1), kind=kCustom, calls=%fused_computation.26 | custom fusion | bytes 3146240 | tf_op jit(solution)/shard_map/scatter | solution.py:69
  49.5 56.9 %all-to-all-done.2 = bf16[16,48,2048]{2,1,0:T(8,128)(2,1)} async-done(((bf16[16,48,2048]{2,1,0:T(8,128)(2,1)}), bf16[16,48,2048]{2,1,0:T(8,128)(2,1)}, u32[]{:S(2)}, u32[]{:S(2)}) %all-to-all-start.2) | async-done | bytes 3145760 | tf_op jit(solution)/shard_map/all_to_all | solution.py:77
  106.4 4.9 %all-to-all-start.1 = ((bf16[16,48,2048]{2,1,0:T(8,128)(2,1)}), bf16[16,48,2048]{2,1,0:T(8,128)(2,1)}, u32[]{:S(2)}, u32[]{:S(2)}) async-start(bf16[16,48,2048]{2,1,0:T(8,128)(2,1)} %bitcast.61), calls=%async_computation.1 | async-start | bytes 6291456 | tf_op jit(solution)/shard_map/all_to_all | solution.py:78
  111.4 0.1 reshape.133
  111.4 4.4 %fusion.8 = f32[768,384]{0,1:T(8,128)} fusion(bf16[768,2048]{1,0:T(8,128)(2,1)} %bitcast.7, bf16[1,2048,384]{2,1,0:T(8,128)(2,1)S(1)} %copy-done), kind=kOutput, calls=%fused_computation.17 | convolution fusion | flops 1207959552 | bytes 5898240 | tf_op jit(solution)/shard_map/dot_general | solution.py:8
  115.9 4.3 %fusion.11 = f32[768,384]{0,1:T(8,128)} fusion(bf16[768,2048]{1,0:T(8,128)(2,1)} %bitcast.7, bf16[1,2048,384]{2,1,0:T(8,128)(2,1)S(1)} %copy-done.1), kind=kOutput, calls=%fused_computation.20 | convolution fusion | flops 1207959552 | bytes 5898240 | tf_op jit(solution)/shard_map/dot_general | solution.py:9
  120.2 61.1 %all-to-all-done.1 = bf16[16,48,2048]{2,1,0:T(8,128)(2,1)} async-done(((bf16[16,48,2048]{2,1,0:T(8,128)(2,1)}), bf16[16,48,2048]{2,1,0:T(8,128)(2,1)}, u32[]{:S(2)}, u32[]{:S(2)}) %all-to-all-start.1) | async-done | bytes 3145760 | tf_op jit(solution)/shard_map/all_to_all | solution.py:78
  181.3 6.2 %multiply_reduce_fusion = (bf16[768]{0:T(1024)(128)(2,1)S(1)}, bf16[768,384]{0,1:T(8,128)(2,1)}, bf16[768,384]{0,1:T(8,128)(2,1)}, bf16[768,384]{0,1:T(8,128)(2,1)}) fusion(f32[768,384]{0,1:T(8,128)} %fusion.11, f32[768,384]{0,1:T(8,128)} %fusion.8, f32[768]{0:T(1024)S(1)} %reshape.133, bf16[768,2048]{1,0:T(8,128)(2,1)} %bitcast.4, ...), kind=kOutput, calls=%fused_computation.28 | convolution fusion | flops 1213857024 | bytes 8851968 | tf_op jit(solution)/shard_map/dot_general | solution.py:17
  187.5 0.7 convert_element_type.94
  188.2 4.9 %all-to-all-start.4 = ((bf16[16,1,48]{2,1,0:T(2,128)(2,1)}), bf16[16,1,48]{2,1,0:T(2,128)(2,1)S(1)}, u32[]{:S(2)}, u32[]{:S(2)}) async-start(bf16[16,1,48]{2,1,0:T(2,128)(2,1)} %convert_element_type.94), calls=%async_computation.4 | async-start | bytes 16384 | tf_op jit(solution)/shard_map/all_to_all | solution.py:96
  193.1 3.0 %fusion.6 = f32[768,2048]{1,0:T(8,128)S(1)} fusion(bf16[768,384]{0,1:T(8,128)(2,1)} %get-tuple-element.17, bf16[1,2048,384]{2,1,0:T(8,128)(2,1)S(1)} %copy-done), kind=kOutput, calls=%fused_computation.15 | convolution fusion | flops 1207959552 | bytes 8454144 | tf_op jit(solution)/shard_map/dot_general | solution.py:26
  196.1 3.5 %add_convert_fusion = bf16[768,2048]{1,0:T(8,128)(2,1)} fusion(f32[768,2048]{1,0:T(8,128)S(1)} %fusion.6, bf16[768,384]{0,1:T(8,128)(2,1)S(1)} %copy-done.3, bf16[1,2048,384]{2,1,0:T(8,128)(2,1)S(1)} %copy-done.1), kind=kOutput, calls=%fused_computation.6 | convolution fusion | flops 1211105280 | bytes 11599872 | tf_op jit(solution)/shard_map/dot_general | solution.py:29
  199.6 0.0 all-to-all-done.4
  199.6 6.2 %all-to-all-start.3 = ((bf16[16,48,2048]{2,1,0:T(8,128)(2,1)}), bf16[16,48,2048]{2,1,0:T(8,128)(2,1)}, u32[]{:S(2)}, u32[]{:S(2)}) async-start(bf16[16,48,2048]{2,1,0:T(8,128)(2,1)} %bitcast.63), calls=%async_computation.3 | async-start | bytes 6291456 | tf_op jit(solution)/shard_map/all_to_all | solution.py:89
  205.8 4.9 %fusion.3 = bf16[1,2048,384]{2,1,0:T(8,128)(2,1)} fusion(bf16[768,2048]{1,0:T(8,128)(2,1)} %bitcast.7, bf16[768,384]{0,1:T(8,128)(2,1)S(1)} %copy-done.2), kind=kOutput, calls=%fused_computation.12 | convolution fusion | flops 1208745984 | bytes 5308416 | tf_op jit(solution)/shard_map/dot_general | solution.py:37
  210.7 5.0 %fusion.4 = bf16[1,2048,384]{2,1,0:T(8,128)(2,1)} fusion(bf16[768,2048]{1,0:T(8,128)(2,1)} %bitcast.7, bf16[768,384]{0,1:T(8,128)(2,1)S(1)} %copy-done.4), kind=kOutput, calls=%fused_computation.13 | convolution fusion | flops 1208745984 | bytes 5308416 | tf_op jit(solution)/shard_map/dot_general | solution.py:40
  215.7 4.5 %fusion.5 = bf16[1,384,2048]{2,1,0:T(8,128)(2,1)} fusion(bf16[768,384]{0,1:T(8,128)(2,1)S(1)} %copy-done.6, bf16[768,2048]{1,0:T(8,128)(2,1)} %bitcast.4, f32[768]{0:T(1024)S(1)} %reshape.133), kind=kOutput, calls=%fused_computation.14 | convolution fusion | flops 1213464576 | bytes 5311488 | tf_op jit(solution)/shard_map/dot_general | solution.py:34
  220.3 0.1 reshape.131
  220.4 3.5 %gather_fusion.1 = bf16[512]{0:T(512)(128)(2,1)S(1)} fusion(bf16[768]{0:T(1024)(128)(2,1)S(1)} %reshape.131, s32[1024]{0:T(1024)S(1)} %pad_clamp_fusion), kind=kCustom, calls=%fused_computation.1 | custom fusion | bytes 4096 | tf_op jit(solution)/shard_map/gather | solution.py:108
  223.9 0.1 reshape.132
  224.0 0.7 copy.25
  224.7 51.1 %all-to-all-done.3 = bf16[16,48,2048]{2,1,0:T(8,128)(2,1)} async-done(((bf16[16,48,2048]{2,1,0:T(8,128)(2,1)}), bf16[16,48,2048]{2,1,0:T(8,128)(2,1)}, u32[]{:S(2)}, u32[]{:S(2)}) %all-to-all-start.3) | async-done | bytes 3145760 | tf_op jit(solution)/shard_map/all_to_all | solution.py:89
  275.7 7.6 %gather_fusion = bf16[512,2048]{1,0:T(8,128)(2,1)} fusion(bf16[768,2048]{1,0:T(8,128)(2,1)} %bitcast.11, s32[1024]{0:T(1024)S(1)} %pad_clamp_fusion), kind=kCustom, calls=%fused_computation | custom fusion | bytes 4196352 | tf_op jit(solution)/shard_map/gather | solution.py:104
  283.3 4.1 %gather.9 = bf16[128,4,2048]{2,1,0:T(4,128)(2,1)} reshape(bf16[512,2048]{1,0:T(8,128)(2,1)} %gather_fusion) | data formatting | bytes 4194304 | tf_op jit(solution)/shard_map/gather | solution.py:104
  287.4 5.0 %reduce_sum.34 = bf16[128,2048]{1,0:T(8,128)(2,1)} reduce(bf16[128,4,2048]{2,1,0:T(4,128)(2,1)} %gather.9, bf16[]{:T(256)} %constant.7.clone.1), dimensions={1}, to_apply=%region_6.7 | reduce | flops 786432 | bytes 2621442 | tf_op jit(solution)/shard_map/reduce_sum | solution.py:105
  (20 shorter events, 0.1 us)
Async XLA Ops:
  0.6 110.8 %copy-start = (bf16[1,2048,384]{2,1,0:T(8,128)(2,1)S(1)}, bf16[1,2048,384]{2,1,0:T(8,128)(2,1)}, u32[]{:S(2)}) copy-start(bf16[1,2048,384]{2,1,0:T(8,128)(2,1)} %param.11) | copy-start | bytes 4718596
  9.6 20.6 %all-to-all-start = ((bf16[16,1,48]{2,1,0:T(2,128)(2,1)}), bf16[16,1,48]{2,1,0:T(2,128)(2,1)S(1)}, u32[]{:S(2)}, u32[]{:S(2)}) async-start(bf16[16,1,48]{2,1,0:T(2,128)(2,1)} %all_to_all.25), calls=%async_computation | async-start | bytes 16384 | tf_op jit(solution)/shard_map/all_to_all | solution.py:79
  30.3 6.2 %copy-start.5 = (bf16[128,2048]{1,0:T(8,128)(2,1)S(1)}, bf16[128,2048]{1,0:T(8,128)(2,1)}, u32[]{:S(2)}) copy-start(bf16[128,2048]{1,0:T(8,128)(2,1)} %param.8) | copy-start | bytes 1572868
  30.3 76.1 %all-to-all-start.2 = ((bf16[16,48,2048]{2,1,0:T(8,128)(2,1)}), bf16[16,48,2048]{2,1,0:T(8,128)(2,1)}, u32[]{:S(2)}, u32[]{:S(2)}) async-start(bf16[16,48,2048]{2,1,0:T(8,128)(2,1)} %bitcast.62), calls=%async_computation.2 | async-start | bytes 6291456 | tf_op jit(solution)/shard_map/all_to_all | solution.py:77
  106.4 74.9 %all-to-all-start.1 = ((bf16[16,48,2048]{2,1,0:T(8,128)(2,1)}), bf16[16,48,2048]{2,1,0:T(8,128)(2,1)}, u32[]{:S(2)}, u32[]{:S(2)}) async-start(bf16[16,48,2048]{2,1,0:T(8,128)(2,1)} %bitcast.61), calls=%async_computation.1 | async-start | bytes 6291456 | tf_op jit(solution)/shard_map/all_to_all | solution.py:78
  111.4 4.5 %copy-start.1 = (bf16[1,2048,384]{2,1,0:T(8,128)(2,1)S(1)}, bf16[1,2048,384]{2,1,0:T(8,128)(2,1)}, u32[]{:S(2)}) copy-start(bf16[1,2048,384]{2,1,0:T(8,128)(2,1)} %param.12) | copy-start | bytes 4718596
  188.2 11.4 %all-to-all-start.4 = ((bf16[16,1,48]{2,1,0:T(2,128)(2,1)}), bf16[16,1,48]{2,1,0:T(2,128)(2,1)S(1)}, u32[]{:S(2)}, u32[]{:S(2)}) async-start(bf16[16,1,48]{2,1,0:T(2,128)(2,1)} %convert_element_type.94), calls=%async_computation.4 | async-start | bytes 16384 | tf_op jit(solution)/shard_map/all_to_all | solution.py:96
  193.1 3.0 %copy-start.3 = (bf16[768,384]{0,1:T(8,128)(2,1)S(1)}, bf16[768,384]{0,1:T(8,128)(2,1)}, u32[]{:S(2)}) copy-start(bf16[768,384]{0,1:T(8,128)(2,1)} %get-tuple-element.18) | copy-start | bytes 1769476
  199.6 6.2 %copy-start.2 = (bf16[768,384]{0,1:T(8,128)(2,1)S(1)}, bf16[768,384]{0,1:T(8,128)(2,1)}, u32[]{:S(2)}) copy-start(bf16[768,384]{0,1:T(8,128)(2,1)} %get-tuple-element.17) | copy-start | bytes 1769476
  199.6 76.1 %all-to-all-start.3 = ((bf16[16,48,2048]{2,1,0:T(8,128)(2,1)}), bf16[16,48,2048]{2,1,0:T(8,128)(2,1)}, u32[]{:S(2)}, u32[]{:S(2)}) async-start(bf16[16,48,2048]{2,1,0:T(8,128)(2,1)} %bitcast.63), calls=%async_computation.3 | async-start | bytes 6291456 | tf_op jit(solution)/shard_map/all_to_all | solution.py:89
  205.8 5.0 %copy-start.4 = (bf16[768,384]{0,1:T(8,128)(2,1)S(1)}, bf16[768,384]{0,1:T(8,128)(2,1)}, u32[]{:S(2)}) copy-start(bf16[768,384]{0,1:T(8,128)(2,1)} %get-tuple-element.18) | copy-start | bytes 1769476
  210.7 5.0 %copy-start.6 = (bf16[768,384]{0,1:T(8,128)(2,1)S(1)}, bf16[768,384]{0,1:T(8,128)(2,1)}, u32[]{:S(2)}) copy-start(bf16[768,384]{0,1:T(8,128)(2,1)} %get-tuple-element.16) | copy-start | bytes 1769476
where the time goes:
time: 293 us; the launch traced here: 292 us
  waiting for transfers between devices  169 us (58%)
  local copies, waits for them, and re-layouts  50.2 us (17%)
  matrix products  35.9 us (12%)
  starting transfers between devices  28.7 us (10%)
  other arithmetic  7.83 us (3%)
    all_to_all x1, waiting for transfers between devices, on_device(): lax.all_to_all(outbox_dy, 'expert', split_axis=0, concat_axis=0, tiled=True)  61.1 us
    all_to_all x1, waiting for transfers between devices, on_device(): lax.all_to_all(outbox_x, 'expert', split_axis=0, concat_axis=0, tiled=True)  56.9 us
    all_to_all x1, waiting for transfers between devices, on_device(): lax.all_to_all(input_term.reshape(devices, capacity, features), 'expert',...  51.1 us
    gather x2, local copies, waits for them, and re-layouts, on_device(): back_term.reshape(slot_rows, features)[target].astype(jnp.float32)  11.7 us
    scatter x1, local copies, waits for them, and re-layouts, on_device(): outbox_x = jnp.zeros((slot_rows, features), jnp.bfloat16).at[target].set(...  6.75 us
    scatter x1, local copies, waits for them, and re-layouts, on_device(): outbox_dy = jnp.zeros((slot_rows, features), jnp.bfloat16).at[target].set...  6.74 us
    all_to_all x1, starting transfers between devices, on_device(): lax.all_to_all(outbox_g, 'expert', split_axis=0, concat_axis=0, tiled=True)  6.55 us
    dot_general x1, matrix products, backward(): lax.dot_general(cotangent, down_mat, (((1,), (1,)), ((), ())), preferred_...  6.17 us
  transfers between devices with their start and end apart: 5, of which 3 were waited for; matrix products, arithmetic and copies ran while one was open for 21% of the time, Pallas kernels for 0%

commit v1 on v0

--- a/solution.py
+++ b/solution.py
@@ -1,7 +1,16 @@
+import functools
+
 import jax
 import jax.numpy as jnp
 from jax import lax
+from jax.experimental import pallas as pl
+from jax.experimental.pallas import tpu as pltpu
 from jax.sharding import PartitionSpec as P
+
+BF16 = jnp.bfloat16
+F32 = jnp.float32
+LANES = 128
+PLANE = 4
 
 
 def project(inputs, gate_mat, up_mat):
@@ -43,7 +52,7 @@
     return (input_term, router_term, gate_delta, up_delta, down_delta)
 
 
-def on_device(tokens, cotangent, expert_ids, gate_levels, w_gate, w_up, w_down):
+def direct(tokens, cotangent, expert_ids, gate_levels, w_gate, w_up, w_down):
     devices = lax.axis_size("expert")
     tok_rows, fanout = expert_ids.shape
     features = tokens.shape[1]
@@ -72,35 +81,18 @@
     outbox_x = outbox_x.reshape(devices, capacity, features)
     outbox_dy = outbox_dy.reshape(devices, capacity, features)
     outbox_g = outbox_g.reshape(devices, capacity)
-    prepared = None
-    arrived_x, arrived_dy, arrived_g = (
-        lax.all_to_all(outbox_x, "expert", split_axis=0, concat_axis=0, tiled=True),
-        lax.all_to_all(outbox_dy, "expert", split_axis=0, concat_axis=0, tiled=True),
-        lax.all_to_all(outbox_g, "expert", split_axis=0, concat_axis=0, tiled=True),
-    )
-    rows_x = arrived_x.reshape(slot_rows, features)
-    rows_dy = arrived_dy.reshape(slot_rows, features)
-    rows_g = arrived_g.reshape(-1).astype(jnp.float32)
+    exchange = functools.partial(
+        lax.all_to_all, axis_name="expert", split_axis=0, concat_axis=0, tiled=True
+    )
+    rows_x = exchange(outbox_x).reshape(slot_rows, features)
+    rows_dy = exchange(outbox_dy).reshape(slot_rows, features)
+    rows_g = exchange(outbox_g).reshape(-1).astype(jnp.float32)
     prepared = project(rows_x, gate_mat, up_mat)
     input_term, router_term, gate_delta, up_delta, down_delta = backward(
         rows_x, prepared, rows_dy, rows_g, gate_mat, up_mat, down_mat
     )
-    back_term, back_router = (
-        lax.all_to_all(
-            input_term.reshape(devices, capacity, features),
-            "expert",
-            split_axis=0,
-            concat_axis=0,
-            tiled=True,
-        ),
-        lax.all_to_all(
-            router_term.reshape(devices, capacity),
-            "expert",
-            split_axis=0,
-            concat_axis=0,
-            tiled=True,
-        ),
-    )
+    back_term = exchange(input_term.reshape(devices, capacity, features))
+    back_router = exchange(router_term.reshape(devices, capacity))
     gathered_term = back_term.reshape(slot_rows, features)[target].astype(jnp.float32)
     input_grad = jnp.sum(gathered_term.reshape(tok_rows, fanout, features), axis=1).astype(
         jnp.bfloat16
@@ -115,23 +107,250 @@
     )
 
 
+def dot(a, b, contract=((1,), (0,))):
+    return lax.dot_general(a, b, (contract, ((), ())), preferred_element_type=F32)
+
+
+def call(kernel, outs, name, *operands, scratch=(), smem=0, limit=60):
+    vmem = pl.BlockSpec(memory_space=pltpu.VMEM)
+    scalar = pl.BlockSpec(memory_space=pltpu.SMEM)
+    return pl.pallas_call(
+        kernel,
+        out_shape=[jax.ShapeDtypeStruct(shape, kind) for shape, kind in outs],
+        in_specs=[scalar] * smem + [vmem] * (len(operands) - smem),
+        out_specs=[vmem] * len(outs),
+        scratch_shapes=list(scratch),
+        name=name,
+        compiler_params=pltpu.CompilerParams(vmem_limit_bytes=limit << 20),
+        cost_estimate=pl.CostEstimate(flops=1000, bytes_accessed=1000, transcendentals=0),
+    )(*operands)
+
+
+def pack_kernel(ids_ref, levels_ref, x_ref, out_ref):
+    fanout, rows = ids_ref.shape
+    features = x_ref.shape[1]
+    expert = lax.broadcasted_iota(jnp.int32, (LANES, rows), 0)
+    gates = jnp.zeros((LANES, rows), F32)
+    for k in range(fanout):
+        value = levels_ref[k : k + 1, :].astype(F32) * (1.0 / 256.0)
+        gates = gates + jnp.where(ids_ref[k : k + 1, :] == expert, value, 0.0)
+    out_ref[:, :features] = x_ref[...]
+    out_ref[:, features:] = gates.T.astype(BF16)
+
+
+def slot_kernel(capacity, me_ref, x_ref, pick_ref, *slot_refs):
+    rows = x_ref.shape[0]
+    features = x_ref.shape[1] - LANES
+    me = me_ref[0]
+    expert = lax.broadcasted_iota(jnp.int32, (8, LANES), 1)
+    wanted = jnp.bitwise_xor(lax.broadcasted_iota(jnp.int32, (8, LANES), 0), me)
+    chooser = jnp.where(expert == wanted, 1.0, 0.0).astype(BF16)
+    gates = dot(chooser, x_ref[:, features:], ((1,), (1,)))
+    routed = jnp.where(gates > 0.0, 1.0, 0.0)
+    before = lax.broadcasted_iota(jnp.int32, (rows, rows), 0)
+    after = lax.broadcasted_iota(jnp.int32, (rows, rows), 1)
+    earlier = jnp.where(before < after, 1.0, 0.0).astype(BF16)
+    place = dot(routed.astype(BF16), earlier)
+    place = jnp.where(routed > 0.0, place, -1.0)
+    slot = lax.broadcasted_iota(jnp.int32, (capacity, rows), 0).astype(F32)
+    pick = jnp.concatenate(
+        [jnp.where(place[j : j + 1, :] == slot, 1.0, 0.0) for j in range(PLANE)], axis=0
+    ).astype(BF16)
+    pick_ref[...] = pick
+    picked = dot(pick, x_ref[...]).astype(BF16)
+    for j in range(PLANE):
+        slot_refs[j][...] = picked[j * capacity : (j + 1) * capacity, :]
+
+
+def gather_kernel(capacity, pick_ref, d_ref, *slot_refs):
+    picked = dot(pick_ref[...], d_ref[...]).astype(BF16)
+    for j in range(PLANE):
+        slot_refs[j][...] = picked[j * capacity : (j + 1) * capacity, :]
+
+
+def expert_kernel(capacity, me_ref, *refs):
+    x_refs, d_refs = refs[:PLANE], refs[PLANE : 2 * PLANE]
+    gate_ref, up_ref, down_ref = refs[2 * PLANE : 2 * PLANE + 3]
+    term_refs = refs[2 * PLANE + 3 : 3 * PLANE + 3]
+    grads_ref, hidden_ref = refs[3 * PLANE + 3 :]
+    features = d_refs[0].shape[1]
+    units = gate_ref.shape[1]
+    rows = PLANE * capacity
+    x = jnp.concatenate([ref[:, :features] for ref in x_refs], axis=0)
+    gates = jnp.concatenate([ref[:, features:] for ref in x_refs], axis=0).astype(F32)
+    mine = lax.broadcasted_iota(jnp.int32, (rows, LANES), 1) == me_ref[0]
+    gating = jnp.sum(jnp.where(mine, gates, 0.0), axis=1, keepdims=True)
+    d = jnp.concatenate([ref[...] for ref in d_refs], axis=0)
+    gate_pre = dot(x, gate_ref[...])
+    up_pre = dot(x, up_ref[...])
+    back_grad = dot(d, down_ref[...], ((1,), (1,)))
+    sigmoid_gate = jax.nn.sigmoid(gate_pre)
+    silu = gate_pre * sigmoid_gate
+    hidden = (silu * up_pre).astype(BF16).astype(F32)
+    router = jnp.sum(hidden * back_grad, axis=1, keepdims=True)
+    hidden_grad = gating * back_grad
+    gate_grad = (hidden_grad * up_pre * sigmoid_gate * (1.0 + gate_pre * (1.0 - sigmoid_gate))).astype(BF16)
+    up_grad = (hidden_grad * silu).astype(BF16)
+    grads_ref[:, :units] = gate_grad
+    grads_ref[:, units:] = up_grad
+    hidden_ref[...] = (gating * hidden).astype(BF16)
+    term = dot(gate_grad, gate_ref[...], ((1,), (1,))) + dot(up_grad, up_ref[...], ((1,), (1,)))
+    term = term.astype(BF16)
+    router = jnp.where(mine, router, 0.0).astype(BF16)
+    for j in range(PLANE):
+        part = slice(j * capacity, (j + 1) * capacity)
+        term_refs[j][:, :features] = term[part, :]
+        term_refs[j][:, features:] = router[part, :]
+
+
+def combine_kernel(pick_ref, *refs):
+    terms = jnp.concatenate([ref[...] for ref in refs[:PLANE]], axis=0)
+    refs[PLANE][...] = dot(pick_ref[...], terms, ((0,), (0,))).astype(BF16)
+
+
+def total_kernel(ids_ref, *refs):
+    parts, (grad_ref, router_ref) = refs[:-2], refs[-2:]
+    fanout, rows = ids_ref.shape
+    features = grad_ref.shape[1]
+    total = parts[0][...].astype(F32)
+    for part in parts[1:]:
+        total = total + part[...].astype(F32)
+    grad_ref[...] = total[:, :features].astype(BF16)
+    router = total[:, features:].T
+    expert = lax.broadcasted_iota(jnp.int32, (LANES, rows), 0)
+    for k in range(fanout):
+        own = jnp.where(ids_ref[k : k + 1, :] == expert, router, 0.0)
+        router_ref[k : k + 1, :] = jnp.sum(own, axis=0, keepdims=True).astype(BF16)
+
+
+def delta_kernel(chunks, *refs):
+    x_refs, d_refs = refs[: chunks * PLANE], refs[chunks * PLANE : 2 * chunks * PLANE]
+    grads_refs = refs[2 * chunks * PLANE : 2 * chunks * PLANE + chunks]
+    hidden_refs = refs[2 * chunks * PLANE + chunks : 2 * chunks * PLANE + 2 * chunks]
+    gate_ref, up_ref, down_ref, x_all, d_all = refs[-5:]
+    units = gate_ref.shape[1]
+    features = gate_ref.shape[0]
+    capacity = x_refs[0].shape[0]
+    for i in range(chunks * PLANE):
+        part = slice(i * capacity, (i + 1) * capacity)
+        x_all[part, :] = x_refs[i][:, :features]
+        d_all[part, :] = d_refs[i][...]
+    grads = jnp.concatenate([ref[...] for ref in grads_refs], axis=0)
+    hidden = jnp.concatenate([ref[...] for ref in hidden_refs], axis=0)
+    step = 512
+
+    @pl.loop(0, features // step)
+    def _(i):
+        cols = pl.ds(pl.multiple_of(i * step, step), step)
+        both = dot(x_all[:, cols], grads, ((0,), (0,))).astype(BF16)
+        gate_ref[cols, :] = both[:, :units]
+        up_ref[cols, :] = both[:, units:]
+        down_ref[:, cols] = dot(hidden, d_all[:, cols], ((0,), (0,))).astype(BF16)
+
+
+def staged(tokens, cotangent, expert_ids, gate_levels, w_gate, w_up, w_down):
+    devices = lax.axis_size("expert")
+    planes = devices // PLANE
+    tok_rows, fanout = expert_ids.shape
+    features = tokens.shape[1]
+    units = w_gate.shape[2]
+    capacity = 3 * tok_rows * fanout // (2 * devices)
+    wide = features + LANES
+    me = lax.axis_index("expert").reshape(1)
+    ids = expert_ids.T
+    gate_mat, up_mat, down_mat = w_gate[0], w_up[0], w_down[0]
+
+    def along(array, distance):
+        pairs = [(i, (i + distance * PLANE) % devices) for i in range(devices)]
+        return lax.ppermute(array, "expert", pairs)
+
+    def within(arrays):
+        moved = [
+            lax.ppermute(arrays[j], "expert", [(i, i ^ j) for i in range(devices)])
+            for j in range(1, PLANE)
+        ]
+        return [arrays[0]] + moved
+
+    (packed,) = call(pack_kernel, [((tok_rows, wide), BF16)], "pack", ids, gate_levels.T, tokens)
+    xs, ds = [packed], [cotangent]
+    for _ in range(planes - 1):
+        xs.append(along(xs[-1], 1))
+        ds.append(along(ds[-1], 1))
+
+    all_x, all_d, all_grads, all_hidden, parts = [], [], [], [], []
+    rows = PLANE * capacity
+    for s in range(planes):
+        pick, *slots = call(
+            functools.partial(slot_kernel, capacity),
+            [((rows, tok_rows), BF16)] + [((capacity, wide), BF16)] * PLANE,
+            "slots_x",
+            me,
+            xs[s],
+            smem=1,
+        )
+        rows_x = within(slots)
+        slots = call(
+            functools.partial(gather_kernel, capacity),
+            [((capacity, features), BF16)] * PLANE,
+            "slots_d",
+            pick,
+            ds[s],
+        )
+        rows_d = within(slots)
+        *terms, grads, hidden = call(
+            functools.partial(expert_kernel, capacity),
+            [((capacity, wide), BF16)] * PLANE + [((rows, 2 * units), BF16), ((rows, units), BF16)],
+            "expert",
+            me,
+            *rows_x,
+            *rows_d,
+            gate_mat,
+            up_mat,
+            down_mat,
+            smem=1,
+        )
+        (part,) = call(combine_kernel, [((tok_rows, wide), BF16)], "combine", pick, *within(terms))
+        parts.append(along(part, -s) if s else part)
+        all_x += rows_x
+        all_d += rows_d
+        all_grads.append(grads)
+        all_hidden.append(hidden)
+
+    gate_delta, up_delta, down_delta = call(
+        functools.partial(delta_kernel, planes),
+        [((features, units), BF16), ((features, units), BF16), ((units, features), BF16)],
+        "deltas",
+        *all_x,
+        *all_d,
+        *all_grads,
+        *all_hidden,
+        scratch=[pltpu.VMEM((planes * rows, features), BF16)] * 2,
+    )
+    input_grad, router_grad = call(
+        total_kernel,
+        [((tok_rows, features), BF16), ((fanout, tok_rows), BF16)],
+        "total",
+        ids,
+        *parts,
+    )
+    return input_grad, router_grad.T, gate_delta[None], up_delta[None], down_delta[None]
+
+
 def solution(mesh):
-    in_specs = (
-        P(("groups", "expert"), None),
-        P(("groups", "expert"), None),
-        P(("groups", "expert"), None),
-        P(("groups", "expert"), None),
-        P("expert", None, None),
-        P("expert", None, None),
-        P("expert", None, None),
-    )
-    out_specs = (
-        P(("groups", "expert"), None),
-        P(("groups", "expert"), None),
-        P(("groups", "expert"), None, None),
-        P(("groups", "expert"), None, None),
-        P(("groups", "expert"), None, None),
-    )
+    devices = mesh.shape["expert"]
+    tokens, experts = P(("groups", "expert"), None), P("expert", None, None)
+    deltas = P(("groups", "expert"), None, None)
+
+    def on_device(*arrays):
+        tok_rows, fanout = arrays[2].shape
+        capacity = 3 * tok_rows * fanout // (2 * devices)
+        plan = staged if PLANE * capacity > tok_rows and devices % PLANE == 0 else direct
+        return plan(*arrays)
+
     return jax.shard_map(
-        on_device, mesh=mesh, in_specs=in_specs, out_specs=out_specs, check_vma=False
-    )
+        on_device,
+        mesh=mesh,
+        in_specs=(tokens, tokens, tokens, tokens, experts, experts, experts),
+        out_specs=(tokens, tokens, deltas, deltas, deltas),
+        check_vma=False,
+    )

time: 293 us -> 205 us (0.70)
  the two profiles are of different devices: /device:TPU:15 before, /device:TPU:0 now
where the time goes in v1:
time: 205 us; the launch traced here: 204 us
  waiting for transfers between devices  90.2 us (44%)
  Pallas kernels  70.6 us (34%)
  starting transfers between devices  38.4 us (19%)
  local copies, waits for them, and re-layouts  3.91 us (2%)
    pallas_call x19, Pallas kernels, call(): pl.pallas_call(kernel, out_shape=[jax.ShapeDtypeStruct(shape, kind) for s...  70.6 us
    ppermute x9, waiting for transfers between devices, along(): return lax.ppermute(array, 'expert', pairs)  51.2 us
    ppermute x36, waiting for transfers between devices, within(): lax.ppermute(arrays[j], 'expert', [(i, i ^ j) for i in range(devices)])  39 us
    ppermute x36, starting transfers between devices, within(): lax.ppermute(arrays[j], 'expert', [(i, i ^ j) for i in range(devices)])  28.5 us
    ppermute x9, starting transfers between devices, along(): return lax.ppermute(array, 'expert', pairs)  9.93 us
  transfers between devices with their start and end apart: 45, of which 20 were waited for; matrix products, arithmetic and copies ran while one was open for 0% of the time, Pallas kernels for 32%

profile of v1, /device:TPU:0, one launch (start us, length us, event | category | flops | bytes accessed | tf_op | source)
XLA Modules:
  0.0 204.2 jit_solution(7007078225376684597)
XLA Ops:
  0.6 2.0 pack.1.x_ref
  2.6 3.0 %collective-permute-start.9 = (bf16[128,2176]{1,0:T(8,128)(2,1)}, bf16[128,2176]{1,0:T(8,128)(2,1)S(1)}, u32[]{:S(2)}, u32[]{:S(2)}) collective-permute-start(bf16[128,2176]{1,0:T(8,128)(2,1)} %pack.1.x_ref), channel_id=1, source_target_pairs={{0,4},{1,5},{2,6},{3,7},{4,8},{5,9},{6,10},{7,11},{8,12},{9,13},{1... | collective-permute-start | bytes 1671176 | tf_op jit(solution)/shard_map/ppermute | solution.py:265
  5.6 1.6 collective-permute-start.13
  7.2 14.1 %collective-permute-done.9.x_ref = bf16[128,2176]{1,0:T(8,128)(2,1)S(1)} collective-permute-done((bf16[128,2176]{1,0:T(8,128)(2,1)}, bf16[128,2176]{1,0:T(8,128)(2,1)S(1)}, u32[]{:S(2)}, u32[]{:S(2)}) %collective-permute-start.9) | collective-permute-done | bytes 557088 | tf_op jit(solution)/shard_map/ppermute | solution.py:265
  21.4 11.3 %collective-permute-done.13.d_ref = bf16[128,2048]{1,0:T(8,128)(2,1)} collective-permute-done((bf16[128,2048]{1,0:T(8,128)(2,1)}, bf16[128,2048]{1,0:T(8,128)(2,1)}, u32[]{:S(2)}, u32[]{:S(2)}) %collective-permute-start.13) | collective-permute-done | bytes 524320 | tf_op jit(solution)/shard_map/ppermute | solution.py:265
  32.7 2.5 %slots_x.4 = (bf16[192,128]{1,0:T(8,128)(2,1)}, bf16[48,2176]{1,0:T(8,128)(2,1)}, bf16[48,2176]{1,0:T(8,128)(2,1)}, bf16[48,2176]{1,0:T(8,128)(2,1)}, bf16[48,2176]{1,0:T(8,128)(2,1)}) custom-call(s32[1]{0:T(128)} %bitcast.1.me_ref, bf16[128,2176]{1,0:T(8,128)(2,1)} %pack.1.x_ref), custom_call_target="tpu_custom_call" | custom-call | flops 1000 | bytes 1000 | tf_op jit(solution)/shard_map/slots_x/pallas_call | solution.py:117
  35.2 2.3 %slots_d.4 = (bf16[48,2048]{1,0:T(8,128)(2,1)}, bf16[48,2048]{1,0:T(8,128)(2,1)}, bf16[48,2048]{1,0:T(8,128)(2,1)}, bf16[48,2048]{1,0:T(8,128)(2,1)}) custom-call(bf16[192,128]{1,0:T(8,128)(2,1)} %get-tuple-element.70.pick_ref, bf16[128,2048]{1,0:T(8,128)(2,1)} %d_ref.1), custom_call_target="tpu_custom_call" | custom-call | flops 1000 | bytes 1000 | tf_op jit(solution)/shard_map/slots_d/pallas_call | solution.py:117
  37.5 2.6 %slots_x.5 = (bf16[192,128]{1,0:T(8,128)(2,1)}, bf16[48,2176]{1,0:T(8,128)(2,1)}, bf16[48,2176]{1,0:T(8,128)(2,1)}, bf16[48,2176]{1,0:T(8,128)(2,1)}, bf16[48,2176]{1,0:T(8,128)(2,1)}) custom-call(s32[1]{0:T(128)} %bitcast.1.me_ref, bf16[128,2176]{1,0:T(8,128)(2,1)} %copy-done.30), custom_call_target="tpu_custom_call" | custom-call | flops 1000 | bytes 1000 | tf_op jit(solution)/shard_map/slots_x/pallas_call | solution.py:117
  40.1 2.2 %slots_d.5 = (bf16[48,2048]{1,0:T(8,128)(2,1)}, bf16[48,2048]{1,0:T(8,128)(2,1)}, bf16[48,2048]{1,0:T(8,128)(2,1)}, bf16[48,2048]{1,0:T(8,128)(2,1)}) custom-call(bf16[192,128]{1,0:T(8,128)(2,1)} %get-tuple-element.83.pick_ref, bf16[128,2048]{1,0:T(8,128)(2,1)} %collective-permute-done.13.d_ref), custom_call_target="tpu_custom_call" | custom-call | flops 1000 | bytes 1000 | tf_op jit(solution)/shard_map/slots_d/pallas_call | solution.py:117
  42.9 1.6 collective-permute-done.21.x_ref
  44.5 11.3 %collective-permute-done.25.d_ref = bf16[128,2048]{1,0:T(8,128)(2,1)} collective-permute-done((bf16[128,2048]{1,0:T(8,128)(2,1)}, bf16[128,2048]{1,0:T(8,128)(2,1)}, u32[]{:S(2)}, u32[]{:S(2)}) %collective-permute-start.25) | collective-permute-done | bytes 524320 | tf_op jit(solution)/shard_map/ppermute | solution.py:265
  55.9 1.7 collective-permute-start.15
  58.0 5.2 %collective-permute-done.15.refs_6_.refs_22_ = bf16[48,2048]{1,0:T(8,128)(2,1)S(1)} collective-permute-done((bf16[48,2048]{1,0:T(8,128)(2,1)}, bf16[48,2048]{1,0:T(8,128)(2,1)S(1)}, u32[]{:S(2)}, u32[]{:S(2)}) %collective-permute-start.15) | collective-permute-done | bytes 196640 | tf_op jit(solution)/shard_map/ppermute | solution.py:269
  63.2 2.4 %collective-permute-start.11 = (bf16[48,2176]{1,0:T(8,128)(2,1)}, bf16[48,2176]{1,0:T(8,128)(2,1)S(1)}, u32[]{:S(2)}, u32[]{:S(2)}) collective-permute-start(bf16[48,2176]{1,0:T(8,128)(2,1)} %get-tuple-element.86), channel_id=1, source_target_pairs={{0,2},{1,3},{2,0},{3,1},{4,6},{5,7},{6,4},{7,5},{8,10},{9,11},{10,... | collective-permute-start | bytes 626696 | tf_op jit(solution)/shard_map/ppermute | solution.py:269
  65.6 1.7 collective-permute-done.16.refs_7_.refs_23_
  67.3 2.2 %collective-permute-start.12 = (bf16[48,2176]{1,0:T(8,128)(2,1)}, bf16[48,2176]{1,0:T(8,128)(2,1)S(1)}, u32[]{:S(2)}, u32[]{:S(2)}) collective-permute-start(bf16[48,2176]{1,0:T(8,128)(2,1)} %get-tuple-element.87), channel_id=1, source_target_pairs={{0,3},{1,2},{2,1},{3,0},{4,7},{5,6},{6,5},{7,4},{8,11},{9,10},{10,... | collective-permute-start | bytes 626696 | tf_op jit(solution)/shard_map/ppermute | solution.py:269
  69.5 2.6 %slots_x.6 = (bf16[192,128]{1,0:T(8,128)(2,1)}, bf16[48,2176]{1,0:T(8,128)(2,1)}, bf16[48,2176]{1,0:T(8,128)(2,1)}, bf16[48,2176]{1,0:T(8,128)(2,1)}, bf16[48,2176]{1,0:T(8,128)(2,1)}) custom-call(s32[1]{0:T(128)} %bitcast.1.me_ref, bf16[128,2176]{1,0:T(8,128)(2,1)} %copy-done.24), custom_call_target="tpu_custom_call" | custom-call | flops 1000 | bytes 1000 | tf_op jit(solution)/shard_map/slots_x/pallas_call | solution.py:117
  72.1 2.3 %slots_d.6 = (bf16[48,2048]{1,0:T(8,128)(2,1)}, bf16[48,2048]{1,0:T(8,128)(2,1)}, bf16[48,2048]{1,0:T(8,128)(2,1)}, bf16[48,2048]{1,0:T(8,128)(2,1)}) custom-call(bf16[192,128]{1,0:T(8,128)(2,1)} %get-tuple-element.96.pick_ref, bf16[128,2048]{1,0:T(8,128)(2,1)} %collective-permute-done.25.d_ref), custom_call_target="tpu_custom_call" | custom-call | flops 1000 | bytes 1000 | tf_op jit(solution)/shard_map/slots_d/pallas_call | solution.py:117
  76.4 1.8 collective-permute-done.37.d_ref
  78.2 1.5 collective-permute-start.23
  80.5 2.6 %slots_x.7 = (bf16[192,128]{1,0:T(8,128)(2,1)}, bf16[48,2176]{1,0:T(8,128)(2,1)}, bf16[48,2176]{1,0:T(8,128)(2,1)}, bf16[48,2176]{1,0:T(8,128)(2,1)}, bf16[48,2176]{1,0:T(8,128)(2,1)}) custom-call(s32[1]{0:T(128)} %bitcast.1.me_ref, bf16[128,2176]{1,0:T(8,128)(2,1)} %copy-done.29), custom_call_target="tpu_custom_call" | custom-call | flops 1000 | bytes 1000 | tf_op jit(solution)/shard_map/slots_x/pallas_call | solution.py:117
  83.1 2.3 %slots_d.7 = (bf16[48,2048]{1,0:T(8,128)(2,1)}, bf16[48,2048]{1,0:T(8,128)(2,1)}, bf16[48,2048]{1,0:T(8,128)(2,1)}, bf16[48,2048]{1,0:T(8,128)(2,1)}) custom-call(bf16[192,128]{1,0:T(8,128)(2,1)} %get-tuple-element.109.pick_ref, bf16[128,2048]{1,0:T(8,128)(2,1)} %collective-permute-done.37.d_ref), custom_call_target="tpu_custom_call" | custom-call | flops 1000 | bytes 1000 | tf_op jit(solution)/shard_map/slots_d/pallas_call | solution.py:117
  85.4 2.4 %collective-permute-start.39 = (bf16[48,2048]{1,0:T(8,128)(2,1)}, bf16[48,2048]{1,0:T(8,128)(2,1)S(1)}, u32[]{:S(2)}, u32[]{:S(2)}) collective-permute-start(bf16[48,2048]{1,0:T(8,128)(2,1)} %get-tuple-element.116), channel_id=1, source_target_pairs={{0,2},{1,3},{2,0},{3,1},{4,6},{5,7},{6,4},{7,5},{8,10},{9,11},{10,... | collective-permute-start | bytes 589832 | tf_op jit(solution)/shard_map/ppermute | solution.py:269
  88.3 3.3 %collective-permute-done.23.refs_2_.refs_10_ = bf16[48,2176]{1,0:T(8,128)(2,1)S(1)} collective-permute-done((bf16[48,2176]{1,0:T(8,128)(2,1)}, bf16[48,2176]{1,0:T(8,128)(2,1)S(1)}, u32[]{:S(2)}, u32[]{:S(2)}) %collective-permute-start.23) | collective-permute-done | bytes 208928 | tf_op jit(solution)/shard_map/ppermute | solution.py:269
  91.6 2.7 %collective-permute-done.24.refs_3_.refs_11_ = bf16[48,2176]{1,0:T(8,128)(2,1)S(1)} collective-permute-done((bf16[48,2176]{1,0:T(8,128)(2,1)}, bf16[48,2176]{1,0:T(8,128)(2,1)S(1)}, u32[]{:S(2)}, u32[]{:S(2)}) %collective-permute-start.24) | collective-permute-done | bytes 208928 | tf_op jit(solution)/shard_map/ppermute | solution.py:269
  94.3 2.4 %collective-permute-start.35 = (bf16[48,2176]{1,0:T(8,128)(2,1)}, bf16[48,2176]{1,0:T(8,128)(2,1)S(1)}, u32[]{:S(2)}, u32[]{:S(2)}) collective-permute-start(bf16[48,2176]{1,0:T(8,128)(2,1)} %get-tuple-element.112), channel_id=1, source_target_pairs={{0,2},{1,3},{2,0},{3,1},{4,6},{5,7},{6,4},{7,5},{8,10},{9,11},{10,... | collective-permute-start | bytes 626696 | tf_op jit(solution)/shard_map/ppermute | solution.py:269
  97.3 6.5 %expert.5 = (bf16[48,2176]{1,0:T(8,128)(2,1)}, bf16[48,2176]{1,0:T(8,128)(2,1)}, bf16[48,2176]{1,0:T(8,128)(2,1)}, bf16[48,2176]{1,0:T(8,128)(2,1)}, bf16[192,768]{1,0:T(8,128)(2,1)}, /*index=5*/bf16[192,384]{1,0:T(8,128)(2,1)}) custom-call(s32[1]{0:T(128)} %bitcast.1.me_ref, bf16[48,2176]{1,0:T(8,128)(2,1)} %get-tuple-element.84.refs_0_.refs_4_, ...), custom_call_target="tpu_custom_call" | custom-call | flops 1000 | bytes 1000 | tf_op jit(solution)/shard_map/expert/pallas_call | solution.py:117
  104.0 1.6 collective-permute-start.18
  105.6 6.6 %expert.6 = (bf16[48,2176]{1,0:T(8,128)(2,1)}, bf16[48,2176]{1,0:T(8,128)(2,1)}, bf16[48,2176]{1,0:T(8,128)(2,1)}, bf16[48,2176]{1,0:T(8,128)(2,1)}, bf16[192,768]{1,0:T(8,128)(2,1)}, /*index=5*/bf16[192,384]{1,0:T(8,128)(2,1)}) custom-call(s32[1]{0:T(128)} %bitcast.1.me_ref, bf16[48,2176]{1,0:T(8,128)(2,1)} %get-tuple-element.97.refs_0_.refs_8_, ...), custom_call_target="tpu_custom_call" | custom-call | flops 1000 | bytes 1000 | tf_op jit(solution)/shard_map/expert/pallas_call | solution.py:117
  113.0 1.6 collective-permute-start.30
  114.6 6.6 %expert.7 = (bf16[48,2176]{1,0:T(8,128)(2,1)}, bf16[48,2176]{1,0:T(8,128)(2,1)}, bf16[48,2176]{1,0:T(8,128)(2,1)}, bf16[48,2176]{1,0:T(8,128)(2,1)}, bf16[192,768]{1,0:T(8,128)(2,1)}, /*index=5*/bf16[192,384]{1,0:T(8,128)(2,1)}) custom-call(s32[1]{0:T(128)} %bitcast.1.me_ref, bf16[48,2176]{1,0:T(8,128)(2,1)} %get-tuple-element.110.refs_0_.refs_12_, ...), custom_call_target="tpu_custom_call" | custom-call | flops 1000 | bytes 1000 | tf_op jit(solution)/shard_map/expert/pallas_call | solution.py:117
  123.6 3.3 %collective-permute-done.30.refs_2_ = bf16[48,2176]{1,0:T(8,128)(2,1)S(1)} collective-permute-done((bf16[48,2176]{1,0:T(8,128)(2,1)}, bf16[48,2176]{1,0:T(8,128)(2,1)S(1)}, u32[]{:S(2)}, u32[]{:S(2)}) %collective-permute-start.30) | collective-permute-done | bytes 208928 | tf_op jit(solution)/shard_map/ppermute | solution.py:269
  126.9 2.7 %collective-permute-done.31.refs_3_ = bf16[48,2176]{1,0:T(8,128)(2,1)S(1)} collective-permute-done((bf16[48,2176]{1,0:T(8,128)(2,1)S(1)}, bf16[48,2176]{1,0:T(8,128)(2,1)S(1)}, u32[]{:S(2)}, u32[]{:S(2)}) %collective-permute-start.31) | collective-permute-done | bytes 208928 | tf_op jit(solution)/shard_map/ppermute | solution.py:269
  129.6 2.4 %collective-permute-start.4 = (bf16[48,2048]{1,0:T(8,128)(2,1)}, bf16[48,2048]{1,0:T(8,128)(2,1)S(1)}, u32[]{:S(2)}, u32[]{:S(2)}) collective-permute-start(bf16[48,2048]{1,0:T(8,128)(2,1)} %get-tuple-element.77), channel_id=1, source_target_pairs={{0,2},{1,3},{2,0},{3,1},{4,6},{5,7},{6,4},{7,5},{8,10},{9,11},{10,... | collective-permute-start | bytes 589832 | tf_op jit(solution)/shard_map/ppermute | solution.py:269
  132.5 3.3 %collective-permute-done.42.refs_2_ = bf16[48,2176]{1,0:T(8,128)(2,1)S(1)} collective-permute-done((bf16[48,2176]{1,0:T(8,128)(2,1)}, bf16[48,2176]{1,0:T(8,128)(2,1)S(1)}, u32[]{:S(2)}, u32[]{:S(2)}) %collective-permute-start.42) | collective-permute-done | bytes 208928 | tf_op jit(solution)/shard_map/ppermute | solution.py:269
  135.8 2.7 %collective-permute-done.43.refs_3_ = bf16[48,2176]{1,0:T(8,128)(2,1)S(1)} collective-permute-done((bf16[48,2176]{1,0:T(8,128)(2,1)}, bf16[48,2176]{1,0:T(8,128)(2,1)S(1)}, u32[]{:S(2)}, u32[]{:S(2)}) %collective-permute-start.43) | collective-permute-done | bytes 208928 | tf_op jit(solution)/shard_map/ppermute | solution.py:269
  139.5 2.4 %combine.5 = bf16[128,2176]{1,0:T(8,128)(2,1)} custom-call(bf16[192,128]{1,0:T(8,128)(2,1)} %get-tuple-element.83.pick_ref, bf16[48,2176]{1,0:T(8,128)(2,1)} %get-tuple-element.92.refs_0_, bf16[48,2176]{1,0:T(8,128)(2,1)} %copy-done.31, bf16[48,2176]{1,0:T(8,128)(2,1)} %copy-done.32, bf16[48,2176]{1,0:T(8,128)(2,1)} %copy-done.33), custom_call_target="tpu_custom_call" | custom-call | flops 1000 | bytes 1000 | tf_op jit(solution)/shard_map/combine/pallas_call | solution.py:117
  141.9 2.5 %combine.6 = bf16[128,2176]{1,0:T(8,128)(2,1)} custom-call(bf16[192,128]{1,0:T(8,128)(2,1)} %get-tuple-element.96.pick_ref, bf16[48,2176]{1,0:T(8,128)(2,1)} %get-tuple-element.105.refs_0_, bf16[48,2176]{1,0:T(8,128)(2,1)} %copy-done.34, bf16[48,2176]{1,0:T(8,128)(2,1)} %copy-done.35, bf16[48,2176]{1,0:T(8,128)(2,1)} %copy-done.36), custom_call_target="tpu_custom_call" | custom-call | flops 1000 | bytes 1000 | tf_op jit(solution)/shard_map/combine/pallas_call | solution.py:117
  144.4 2.4 %combine.7 = bf16[128,2176]{1,0:T(8,128)(2,1)} custom-call(bf16[192,128]{1,0:T(8,128)(2,1)} %get-tuple-element.109.pick_ref, bf16[48,2176]{1,0:T(8,128)(2,1)} %get-tuple-element.118.refs_0_, bf16[48,2176]{1,0:T(8,128)(2,1)} %copy-done.37, bf16[48,2176]{1,0:T(8,128)(2,1)} %copy-done.38, bf16[48,2176]{1,0:T(8,128)(2,1)} %copy-done.39), custom_call_target="tpu_custom_call" | custom-call | flops 1000 | bytes 1000 | tf_op jit(solution)/shard_map/combine/pallas_call | solution.py:117
  146.8 3.8 %collective-permute-start.20 = (bf16[128,2176]{1,0:T(8,128)(2,1)S(1)}, bf16[128,2176]{1,0:T(8,128)(2,1)S(1)}, u32[]{:S(2)}, u32[]{:S(2)}) collective-permute-start(bf16[128,2176]{1,0:T(8,128)(2,1)S(1)} %copy-done.25), channel_id=1, source_target_pairs={{0,12},{1,13},{2,14},{3,15},{4,0},{5,1},{6,2},{7,3},{8,4},{9,5},{1... | collective-permute-start | bytes 1671176 | tf_op jit(solution)/shard_map/ppermute | solution.py:265
  153.2 2.7 %collective-permute-done.2.refs_3_ = bf16[48,2176]{1,0:T(8,128)(2,1)S(1)} collective-permute-done((bf16[48,2176]{1,0:T(8,128)(2,1)S(1)}, bf16[48,2176]{1,0:T(8,128)(2,1)S(1)}, u32[]{:S(2)}, u32[]{:S(2)}) %collective-permute-start.2) | collective-permute-done | bytes 208928 | tf_op jit(solution)/shard_map/ppermute | solution.py:269
  156.6 6.5 %expert.4 = (bf16[48,2176]{1,0:T(8,128)(2,1)}, bf16[48,2176]{1,0:T(8,128)(2,1)}, bf16[48,2176]{1,0:T(8,128)(2,1)}, bf16[48,2176]{1,0:T(8,128)(2,1)}, bf16[192,768]{1,0:T(8,128)(2,1)}, /*index=5*/bf16[192,384]{1,0:T(8,128)(2,1)}) custom-call(s32[1]{0:T(128)} %bitcast.1.me_ref, bf16[48,2176]{1,0:T(8,128)(2,1)} %get-tuple-element.71.refs_0_, ...), custom_call_target="tpu_custom_call" | custom-call | flops 1000 | bytes 1000 | tf_op jit(solution)/shard_map/expert/pallas_call | solution.py:117
  166.4 6.0 %collective-permute-done.7.refs_2_ = bf16[48,2176]{1,0:T(8,128)(2,1)S(1)} collective-permute-done((bf16[48,2176]{1,0:T(8,128)(2,1)}, bf16[48,2176]{1,0:T(8,128)(2,1)S(1)}, u32[]{:S(2)}, u32[]{:S(2)}) %collective-permute-start.7) | collective-permute-done | bytes 208928 | tf_op jit(solution)/shard_map/ppermute | solution.py:269
  172.4 2.7 %collective-permute-done.8.refs_3_ = bf16[48,2176]{1,0:T(8,128)(2,1)S(1)} collective-permute-done((bf16[48,2176]{1,0:T(8,128)(2,1)}, bf16[48,2176]{1,0:T(8,128)(2,1)S(1)}, u32[]{:S(2)}, u32[]{:S(2)}) %collective-permute-start.8) | collective-permute-done | bytes 208928 | tf_op jit(solution)/shard_map/ppermute | solution.py:269
  175.8 2.4 %combine.4.refs_0_ = bf16[128,2176]{1,0:T(8,128)(2,1)} custom-call(bf16[192,128]{1,0:T(8,128)(2,1)} %get-tuple-element.70.pick_ref, bf16[48,2176]{1,0:T(8,128)(2,1)} %get-tuple-element.79.refs_0_, bf16[48,2176]{1,0:T(8,128)(2,1)} %copy-done.40, bf16[48,2176]{1,0:T(8,128)(2,1)} %copy-done.41, bf16[48,2176]{1,0:T(8,128)(2,1)} %copy-done.42), custom_call_target="tpu_custom_call" | custom-call | flops 1000 | bytes 1000 | tf_op jit(solution)/shard_map/combine/pallas_call | solution.py:117
  178.2 10.4 %deltas.1 = (bf16[2048,384]{1,0:T(8,128)(2,1)}, bf16[2048,384]{1,0:T(8,128)(2,1)}, bf16[384,2048]{1,0:T(8,128)(2,1)}) custom-call(bf16[48,2176]{1,0:T(8,128)(2,1)} %get-tuple-element.71.refs_0_, bf16[48,2176]{1,0:T(8,128)(2,1)} %copy-done.9, bf16[48,2176]{1,0:T(8,128)(2,1)} %copy-done.10, bf16[48,2176]{1,0:T(8,128)(2,1)} %copy-done.11, ...), custom_call_target="tpu_custom_call" | custom-call | flops 1000 | bytes 1000 | tf_op jit(solution)/shard_map/deltas/pallas_call | solution.py:117
  188.7 11.0 %collective-permute-done.32.refs_2_ = bf16[128,2176]{1,0:T(8,128)(2,1)S(1)} collective-permute-done((bf16[128,2176]{1,0:T(8,128)(2,1)}, bf16[128,2176]{1,0:T(8,128)(2,1)S(1)}, u32[]{:S(2)}, u32[]{:S(2)}) %collective-permute-start.32) | collective-permute-done | bytes 557088 | tf_op jit(solution)/shard_map/ppermute | solution.py:265
  201.3 2.9 %total.1 = (bf16[128,2048]{1,0:T(8,128)(2,1)}, bf16[4,128]{1,0:T(4,128)(2,1)}) custom-call(s32[4,128]{1,0:T(4,128)} %bitcast.23, bf16[128,2176]{1,0:T(8,128)(2,1)} %combine.4.refs_0_, bf16[128,2176]{1,0:T(8,128)(2,1)} %copy-done.26, bf16[128,2176]{1,0:T(8,128)(2,1)} %copy-done.27, bf16[128,2176]{1,0:T(8,128)(2,1)} %copy-done.28), custom_call_target="tpu_custom_call" | custom-call | flops 1000 | bytes 1000 | tf_op jit(solution)/shard_map/total/pallas_call | solution.py:117
  (157 shorter events, 18.4 us)
Async XLA Ops:
  2.6 18.7 %collective-permute-start.9 = (bf16[128,2176]{1,0:T(8,128)(2,1)}, bf16[128,2176]{1,0:T(8,128)(2,1)S(1)}, u32[]{:S(2)}, u32[]{:S(2)}) collective-permute-start(bf16[128,2176]{1,0:T(8,128)(2,1)} %pack.1.x_ref), channel_id=1, source_target_pairs={{0,4},{1,5},{2,6},{3,7},{4,8},{5,9},{6,10},{7,11},{8,12},{9,13},{1... | collective-permute-start | bytes 1671176 | tf_op jit(solution)/shard_map/ppermute | solution.py:265
  5.6 27.0 %collective-permute-start.13 = (bf16[128,2048]{1,0:T(8,128)(2,1)}, bf16[128,2048]{1,0:T(8,128)(2,1)}, u32[]{:S(2)}, u32[]{:S(2)}) collective-permute-start(bf16[128,2048]{1,0:T(8,128)(2,1)} %d_ref.1), channel_id=1, source_target_pairs={{0,4},{1,5},{2,6},{3,7},{4,8},{5,9},{6,10},{7,11},{8,12},{9,13},{1... | collective-permute-start | bytes 1572872 | tf_op jit(solution)/shard_map/ppermute | solution.py:265
  21.3 23.2 %collective-permute-start.21 = (bf16[128,2176]{1,0:T(8,128)(2,1)S(1)}, bf16[128,2176]{1,0:T(8,128)(2,1)S(1)}, u32[]{:S(2)}, u32[]{:S(2)}) collective-permute-start(bf16[128,2176]{1,0:T(8,128)(2,1)S(1)} %collective-permute-done.9.x_ref), channel_id=1, source_target_pairs={{0,4},{1,5},{2,6},{3,7},{4,8},{5,9},{6,10},{7,11},{8,12},{9,13},{1... | collective-permute-start | bytes 1671176 | tf_op jit(solution)/shard_map/ppermute | solution.py:265
  32.7 23.2 %collective-permute-start.25 = (bf16[128,2048]{1,0:T(8,128)(2,1)}, bf16[128,2048]{1,0:T(8,128)(2,1)}, u32[]{:S(2)}, u32[]{:S(2)}) collective-permute-start(bf16[128,2048]{1,0:T(8,128)(2,1)} %collective-permute-done.13.d_ref), channel_id=1, source_target_pairs={{0,4},{1,5},{2,6},{3,7},{4,8},{5,9},{6,10},{7,11},{8,12},{9,13},{1... | collective-permute-start | bytes 1572872 | tf_op jit(solution)/shard_map/ppermute | solution.py:265
  37.5 20.1 %collective-permute-start.3 = (bf16[48,2048]{1,0:T(8,128)(2,1)}, bf16[48,2048]{1,0:T(8,128)(2,1)S(1)}, u32[]{:S(2)}, u32[]{:S(2)}) collective-permute-start(bf16[48,2048]{1,0:T(8,128)(2,1)} %get-tuple-element.76), channel_id=1, source_target_pairs={{0,1},{1,0},{2,3},{3,2},{4,5},{5,4},{6,7},{7,6},{8,9},{9,8},{10,11... | collective-permute-start | bytes 589832 | tf_op jit(solution)/shard_map/ppermute | solution.py:269
  42.4 15.3 %collective-permute-start.14 = (bf16[48,2048]{1,0:T(8,128)(2,1)}, bf16[48,2048]{1,0:T(8,128)(2,1)S(1)}, u32[]{:S(2)}, u32[]{:S(2)}) collective-permute-start(bf16[48,2048]{1,0:T(8,128)(2,1)} %get-tuple-element.89), channel_id=1, source_target_pairs={{0,1},{1,0},{2,3},{3,2},{4,5},{5,4},{6,7},{7,6},{8,9},{9,8},{10,11... | collective-permute-start | bytes 589832 | tf_op jit(solution)/shard_map/ppermute | solution.py:269
  44.5 35.2 %collective-permute-start.33 = (bf16[128,2176]{1,0:T(8,128)(2,1)S(1)}, bf16[128,2176]{1,0:T(8,128)(2,1)S(1)}, u32[]{:S(2)}, u32[]{:S(2)}) collective-permute-start(bf16[128,2176]{1,0:T(8,128)(2,1)S(1)} %collective-permute-done.21.x_ref), channel_id=1, source_target_pairs={{0,4},{1,5},{2,6},{3,7},{4,8},{5,9},{6,10},{7,11},{8,12},{9,13},{1... | collective-permute-start | bytes 1671176 | tf_op jit(solution)/shard_map/ppermute | solution.py:265
  55.8 22.3 %collective-permute-start.37 = (bf16[128,2048]{1,0:T(8,128)(2,1)}, bf16[128,2048]{1,0:T(8,128)(2,1)}, u32[]{:S(2)}, u32[]{:S(2)}) collective-permute-start(bf16[128,2048]{1,0:T(8,128)(2,1)} %collective-permute-done.25.d_ref), channel_id=1, source_target_pairs={{0,4},{1,5},{2,6},{3,7},{4,8},{5,9},{6,10},{7,11},{8,12},{9,13},{1... | collective-permute-start | bytes 1572872 | tf_op jit(solution)/shard_map/ppermute | solution.py:265
  55.9 7.3 %collective-permute-start.15 = (bf16[48,2048]{1,0:T(8,128)(2,1)}, bf16[48,2048]{1,0:T(8,128)(2,1)S(1)}, u32[]{:S(2)}, u32[]{:S(2)}) collective-permute-start(bf16[48,2048]{1,0:T(8,128)(2,1)} %get-tuple-element.90), channel_id=1, source_target_pairs={{0,2},{1,3},{2,0},{3,1},{4,6},{5,7},{6,4},{7,5},{8,10},{9,11},{10,... | collective-permute-start | bytes 589832 | tf_op jit(solution)/shard_map/ppermute | solution.py:269
  57.6 46.2 %copy-start.12 = (bf16[48,2048]{1,0:T(8,128)(2,1)}, bf16[48,2048]{1,0:T(8,128)(2,1)S(1)}, u32[]{:S(2)}) copy-start(bf16[48,2048]{1,0:T(8,128)(2,1)S(1)} %collective-permute-done.3.refs_5_.refs_17_) | copy-start | bytes 589828
  57.6 9.7 %collective-permute-start.16 = (bf16[48,2048]{1,0:T(8,128)(2,1)}, bf16[48,2048]{1,0:T(8,128)(2,1)S(1)}, u32[]{:S(2)}, u32[]{:S(2)}) collective-permute-start(bf16[48,2048]{1,0:T(8,128)(2,1)} %get-tuple-element.91), channel_id=1, source_target_pairs={{0,3},{1,2},{2,1},{3,0},{4,7},{5,6},{6,5},{7,4},{8,11},{9,10},{10,... | collective-permute-start | bytes 589832 | tf_op jit(solution)/shard_map/ppermute | solution.py:269
  57.6 39.6 %copy-start.13 = (bf16[48,2048]{1,0:T(8,128)(2,1)}, bf16[48,2048]{1,0:T(8,128)(2,1)S(1)}, u32[]{:S(2)}) copy-start(bf16[48,2048]{1,0:T(8,128)(2,1)S(1)} %collective-permute-done.14.refs_5_.refs_21_) | copy-start | bytes 589828
  57.6 16.7 %collective-permute-start.10 = (bf16[48,2176]{1,0:T(8,128)(2,1)}, bf16[48,2176]{1,0:T(8,128)(2,1)S(1)}, u32[]{:S(2)}, u32[]{:S(2)}) collective-permute-start(bf16[48,2176]{1,0:T(8,128)(2,1)} %get-tuple-element.85), channel_id=1, source_target_pairs={{0,1},{1,0},{2,3},{3,2},{4,5},{5,4},{6,7},{7,6},{8,9},{9,8},{10,11... | collective-permute-start | bytes 626696 | tf_op jit(solution)/shard_map/ppermute | solution.py:269
  63.2 34.0 %copy-start.14 = (bf16[48,2048]{1,0:T(8,128)(2,1)}, bf16[48,2048]{1,0:T(8,128)(2,1)S(1)}, u32[]{:S(2)}) copy-start(bf16[48,2048]{1,0:T(8,128)(2,1)S(1)} %collective-permute-done.15.refs_6_.refs_22_) | copy-start | bytes 589828
  63.2 11.2 %collective-permute-start.11 = (bf16[48,2176]{1,0:T(8,128)(2,1)}, bf16[48,2176]{1,0:T(8,128)(2,1)S(1)}, u32[]{:S(2)}, u32[]{:S(2)}) collective-permute-start(bf16[48,2176]{1,0:T(8,128)(2,1)} %get-tuple-element.86), channel_id=1, source_target_pairs={{0,2},{1,3},{2,0},{3,1},{4,6},{5,7},{6,4},{7,5},{8,10},{9,11},{10,... | collective-permute-start | bytes 626696 | tf_op jit(solution)/shard_map/ppermute | solution.py:269
  67.3 7.6 %collective-permute-start.12 = (bf16[48,2176]{1,0:T(8,128)(2,1)}, bf16[48,2176]{1,0:T(8,128)(2,1)S(1)}, u32[]{:S(2)}, u32[]{:S(2)}) collective-permute-start(bf16[48,2176]{1,0:T(8,128)(2,1)} %get-tuple-element.87), channel_id=1, source_target_pairs={{0,3},{1,2},{2,1},{3,0},{4,7},{5,6},{6,5},{7,4},{8,11},{9,10},{10,... | collective-permute-start | bytes 626696 | tf_op jit(solution)/shard_map/ppermute | solution.py:269
  74.3 1.7 collective-permute-start.26
  74.4 13.4 %collective-permute-start.22 = (bf16[48,2176]{1,0:T(8,128)(2,1)}, bf16[48,2176]{1,0:T(8,128)(2,1)S(1)}, u32[]{:S(2)}, u32[]{:S(2)}) collective-permute-start(bf16[48,2176]{1,0:T(8,128)(2,1)} %get-tuple-element.98), channel_id=1, source_target_pairs={{0,1},{1,0},{2,3},{3,2},{4,5},{5,4},{6,7},{7,6},{8,9},{9,8},{10,11... | collective-permute-start | bytes 626696 | tf_op jit(solution)/shard_map/ppermute | solution.py:269
  74.9 10.4 %collective-permute-start.27 = (bf16[48,2048]{1,0:T(8,128)(2,1)}, bf16[48,2048]{1,0:T(8,128)(2,1)S(1)}, u32[]{:S(2)}, u32[]{:S(2)}) collective-permute-start(bf16[48,2048]{1,0:T(8,128)(2,1)} %get-tuple-element.103), channel_id=1, source_target_pairs={{0,2},{1,3},{2,0},{3,1},{4,6},{5,7},{6,4},{7,5},{8,10},{9,11},{10,... | collective-permute-start | bytes 589832 | tf_op jit(solution)/shard_map/ppermute | solution.py:269
  76.0 9.4 %collective-permute-start.28 = (bf16[48,2048]{1,0:T(8,128)(2,1)}, bf16[48,2048]{1,0:T(8,128)(2,1)S(1)}, u32[]{:S(2)}, u32[]{:S(2)}) collective-permute-start(bf16[48,2048]{1,0:T(8,128)(2,1)} %get-tuple-element.104), channel_id=1, source_target_pairs={{0,3},{1,2},{2,1},{3,0},{4,7},{5,6},{6,5},{7,4},{8,11},{9,10},{10,... | collective-permute-start | bytes 589832 | tf_op jit(solution)/shard_map/ppermute | solution.py:269
  78.2 13.4 %collective-permute-start.23 = (bf16[48,2176]{1,0:T(8,128)(2,1)}, bf16[48,2176]{1,0:T(8,128)(2,1)S(1)}, u32[]{:S(2)}, u32[]{:S(2)}) collective-permute-start(bf16[48,2176]{1,0:T(8,128)(2,1)} %get-tuple-element.99), channel_id=1, source_target_pairs={{0,2},{1,3},{2,0},{3,1},{4,6},{5,7},{6,4},{7,5},{8,10},{9,11},{10,... | collective-permute-start | bytes 626696 | tf_op jit(solution)/shard_map/ppermute | solution.py:269
  79.7 14.6 %collective-permute-start.24 = (bf16[48,2176]{1,0:T(8,128)(2,1)}, bf16[48,2176]{1,0:T(8,128)(2,1)S(1)}, u32[]{:S(2)}, u32[]{:S(2)}) collective-permute-start(bf16[48,2176]{1,0:T(8,128)(2,1)} %get-tuple-element.100), channel_id=1, source_target_pairs={{0,3},{1,2},{2,1},{3,0},{4,7},{5,6},{6,5},{7,4},{8,11},{9,10},{10,... | collective-permute-start | bytes 626696 | tf_op jit(solution)/shard_map/ppermute | solution.py:269
  85.3 11.4 %collective-permute-start.38 = (bf16[48,2048]{1,0:T(8,128)(2,1)}, bf16[48,2048]{1,0:T(8,128)(2,1)S(1)}, u32[]{:S(2)}, u32[]{:S(2)}) collective-permute-start(bf16[48,2048]{1,0:T(8,128)(2,1)} %get-tuple-element.115), channel_id=1, source_target_pairs={{0,1},{1,0},{2,3},{3,2},{4,5},{5,4},{6,7},{7,6},{8,9},{9,8},{10,11... | collective-permute-start | bytes 589832 | tf_op jit(solution)/shard_map/ppermute | solution.py:269
  85.4 18.5 %collective-permute-start.39 = (bf16[48,2048]{1,0:T(8,128)(2,1)}, bf16[48,2048]{1,0:T(8,128)(2,1)S(1)}, u32[]{:S(2)}, u32[]{:S(2)}) collective-permute-start(bf16[48,2048]{1,0:T(8,128)(2,1)} %get-tuple-element.116), channel_id=1, source_target_pairs={{0,2},{1,3},{2,0},{3,1},{4,6},{5,7},{6,4},{7,5},{8,10},{9,11},{10,... | collective-permute-start | bytes 589832 | tf_op jit(solution)/shard_map/ppermute | solution.py:269
  87.8 16.2 %collective-permute-start.40 = (bf16[48,2048]{1,0:T(8,128)(2,1)}, bf16[48,2048]{1,0:T(8,128)(2,1)S(1)}, u32[]{:S(2)}, u32[]{:S(2)}) collective-permute-start(bf16[48,2048]{1,0:T(8,128)(2,1)} %get-tuple-element.117), channel_id=1, source_target_pairs={{0,3},{1,2},{2,1},{3,0},{4,7},{5,6},{6,5},{7,4},{8,11},{9,10},{10,... | collective-permute-start | bytes 589832 | tf_op jit(solution)/shard_map/ppermute | solution.py:269
  91.6 20.7 %collective-permute-start.34 = (bf16[48,2176]{1,0:T(8,128)(2,1)}, bf16[48,2176]{1,0:T(8,128)(2,1)S(1)}, u32[]{:S(2)}, u32[]{:S(2)}) collective-permute-start(bf16[48,2176]{1,0:T(8,128)(2,1)} %get-tuple-element.111), channel_id=1, source_target_pairs={{0,1},{1,0},{2,3},{3,2},{4,5},{5,4},{6,7},{7,6},{8,9},{9,8},{10,11... | collective-permute-start | bytes 626696 | tf_op jit(solution)/shard_map/ppermute | solution.py:269
  94.3 18.3 %collective-permute-start.35 = (bf16[48,2176]{1,0:T(8,128)(2,1)}, bf16[48,2176]{1,0:T(8,128)(2,1)S(1)}, u32[]{:S(2)}, u32[]{:S(2)}) collective-permute-start(bf16[48,2176]{1,0:T(8,128)(2,1)} %get-tuple-element.112), channel_id=1, source_target_pairs={{0,2},{1,3},{2,0},{3,1},{4,6},{5,7},{6,4},{7,5},{8,10},{9,11},{10,... | collective-permute-start | bytes 626696 | tf_op jit(solution)/shard_map/ppermute | solution.py:269
  96.7 16.2 %collective-permute-start.36 = (bf16[48,2176]{1,0:T(8,128)(2,1)}, bf16[48,2176]{1,0:T(8,128)(2,1)S(1)}, u32[]{:S(2)}, u32[]{:S(2)}) collective-permute-start(bf16[48,2176]{1,0:T(8,128)(2,1)} %get-tuple-element.113), channel_id=1, source_target_pairs={{0,3},{1,2},{2,1},{3,0},{4,7},{5,6},{6,5},{7,4},{8,11},{9,10},{10,... | collective-permute-start | bytes 626696 | tf_op jit(solution)/shard_map/ppermute | solution.py:269
  103.9 17.3 %collective-permute-start.17 = (bf16[48,2176]{1,0:T(8,128)(2,1)}, bf16[48,2176]{1,0:T(8,128)(2,1)S(1)}, u32[]{:S(2)}, u32[]{:S(2)}) collective-permute-start(bf16[48,2176]{1,0:T(8,128)(2,1)} %get-tuple-element.93), channel_id=1, source_target_pairs={{0,1},{1,0},{2,3},{3,2},{4,5},{5,4},{6,7},{7,6},{8,9},{9,8},{10,11... | collective-permute-start | bytes 626696 | tf_op jit(solution)/shard_map/ppermute | solution.py:269
  104.0 17.6 %collective-permute-start.18 = (bf16[48,2176]{1,0:T(8,128)(2,1)}, bf16[48,2176]{1,0:T(8,128)(2,1)S(1)}, u32[]{:S(2)}, u32[]{:S(2)}) collective-permute-start(bf16[48,2176]{1,0:T(8,128)(2,1)} %get-tuple-element.94), channel_id=1, source_target_pairs={{0,2},{1,3},{2,0},{3,1},{4,6},{5,7},{6,4},{7,5},{8,10},{9,11},{10,... | collective-permute-start | bytes 626696 | tf_op jit(solution)/shard_map/ppermute | solution.py:269
  112.3 9.8 %collective-permute-start.19 = (bf16[48,2176]{1,0:T(8,128)(2,1)S(1)}, bf16[48,2176]{1,0:T(8,128)(2,1)S(1)}, u32[]{:S(2)}, u32[]{:S(2)}) collective-permute-start(bf16[48,2176]{1,0:T(8,128)(2,1)S(1)} %copy-done.46), channel_id=1, source_target_pairs={{0,3},{1,2},{2,1},{3,0},{4,7},{5,6},{6,5},{7,4},{8,11},{9,10},{10,... | collective-permute-start | bytes 626696 | tf_op jit(solution)/shard_map/ppermute | solution.py:269
  112.6 10.8 %collective-permute-start.29 = (bf16[48,2176]{1,0:T(8,128)(2,1)}, bf16[48,2176]{1,0:T(8,128)(2,1)S(1)}, u32[]{:S(2)}, u32[]{:S(2)}) collective-permute-start(bf16[48,2176]{1,0:T(8,128)(2,1)} %get-tuple-element.106), channel_id=1, source_target_pairs={{0,1},{1,0},{2,3},{3,2},{4,5},{5,4},{6,7},{7,6},{8,9},{9,8},{10,11... | collective-permute-start | bytes 626696 | tf_op jit(solution)/shard_map/ppermute | solution.py:269
  113.0 13.9 %collective-permute-start.30 = (bf16[48,2176]{1,0:T(8,128)(2,1)}, bf16[48,2176]{1,0:T(8,128)(2,1)S(1)}, u32[]{:S(2)}, u32[]{:S(2)}) collective-permute-start(bf16[48,2176]{1,0:T(8,128)(2,1)} %get-tuple-element.107), channel_id=1, source_target_pairs={{0,2},{1,3},{2,0},{3,1},{4,6},{5,7},{6,4},{7,5},{8,10},{9,11},{10,... | collective-permute-start | bytes 626696 | tf_op jit(solution)/shard_map/ppermute | solution.py:269
  121.2 8.4 %collective-permute-start.31 = (bf16[48,2176]{1,0:T(8,128)(2,1)S(1)}, bf16[48,2176]{1,0:T(8,128)(2,1)S(1)}, u32[]{:S(2)}, u32[]{:S(2)}) collective-permute-start(bf16[48,2176]{1,0:T(8,128)(2,1)S(1)} %copy-done.47), channel_id=1, source_target_pairs={{0,3},{1,2},{2,1},{3,0},{4,7},{5,6},{6,5},{7,4},{8,11},{9,10},{10,... | collective-permute-start | bytes 626696 | tf_op jit(solution)/shard_map/ppermute | solution.py:269
  121.6 10.4 %collective-permute-start.41 = (bf16[48,2176]{1,0:T(8,128)(2,1)}, bf16[48,2176]{1,0:T(8,128)(2,1)S(1)}, u32[]{:S(2)}, u32[]{:S(2)}) collective-permute-start(bf16[48,2176]{1,0:T(8,128)(2,1)} %get-tuple-element.119), channel_id=1, source_target_pairs={{0,1},{1,0},{2,3},{3,2},{4,5},{5,4},{6,7},{7,6},{8,9},{9,8},{10,11... | collective-permute-start | bytes 626696 | tf_op jit(solution)/shard_map/ppermute | solution.py:269
  122.1 13.8 %collective-permute-start.42 = (bf16[48,2176]{1,0:T(8,128)(2,1)}, bf16[48,2176]{1,0:T(8,128)(2,1)S(1)}, u32[]{:S(2)}, u32[]{:S(2)}) collective-permute-start(bf16[48,2176]{1,0:T(8,128)(2,1)} %get-tuple-element.120), channel_id=1, source_target_pairs={{0,2},{1,3},{2,0},{3,1},{4,6},{5,7},{6,4},{7,5},{8,10},{9,11},{10,... | collective-permute-start | bytes 626696 | tf_op jit(solution)/shard_map/ppermute | solution.py:269
  123.4 15.1 %collective-permute-start.43 = (bf16[48,2176]{1,0:T(8,128)(2,1)}, bf16[48,2176]{1,0:T(8,128)(2,1)S(1)}, u32[]{:S(2)}, u32[]{:S(2)}) collective-permute-start(bf16[48,2176]{1,0:T(8,128)(2,1)} %get-tuple-element.121), channel_id=1, source_target_pairs={{0,3},{1,2},{2,1},{3,0},{4,7},{5,6},{6,5},{7,4},{8,11},{9,10},{10,... | collective-permute-start | bytes 626696 | tf_op jit(solution)/shard_map/ppermute | solution.py:269
  126.9 23.8 %collective-permute-start = (bf16[48,2176]{1,0:T(8,128)(2,1)S(1)}, bf16[48,2176]{1,0:T(8,128)(2,1)S(1)}, u32[]{:S(2)}, u32[]{:S(2)}) collective-permute-start(bf16[48,2176]{1,0:T(8,128)(2,1)S(1)} %copy-done.45), channel_id=1, source_target_pairs={{0,1},{1,0},{2,3},{3,2},{4,5},{5,4},{6,7},{7,6},{8,9},{9,8},{10,11... | collective-permute-start | bytes 626696 | tf_op jit(solution)/shard_map/ppermute | solution.py:269
  129.6 17.2 %collective-permute-start.4 = (bf16[48,2048]{1,0:T(8,128)(2,1)}, bf16[48,2048]{1,0:T(8,128)(2,1)S(1)}, u32[]{:S(2)}, u32[]{:S(2)}) collective-permute-start(bf16[48,2048]{1,0:T(8,128)(2,1)} %get-tuple-element.77), channel_id=1, source_target_pairs={{0,2},{1,3},{2,0},{3,1},{4,6},{5,7},{6,4},{7,5},{8,10},{9,11},{10,... | collective-permute-start | bytes 589832 | tf_op jit(solution)/shard_map/ppermute | solution.py:269
  132.0 18.6 %collective-permute-start.5 = (bf16[48,2048]{1,0:T(8,128)(2,1)}, bf16[48,2048]{1,0:T(8,128)(2,1)S(1)}, u32[]{:S(2)}, u32[]{:S(2)}) collective-permute-start(bf16[48,2048]{1,0:T(8,128)(2,1)} %get-tuple-element.78), channel_id=1, source_target_pairs={{0,3},{1,2},{2,1},{3,0},{4,7},{5,6},{6,5},{7,4},{8,11},{9,10},{10,... | collective-permute-start | bytes 589832 | tf_op jit(solution)/shard_map/ppermute | solution.py:269
  135.8 17.4 %collective-permute-start.1 = (bf16[48,2176]{1,0:T(8,128)(2,1)S(1)}, bf16[48,2176]{1,0:T(8,128)(2,1)S(1)}, u32[]{:S(2)}, u32[]{:S(2)}) collective-permute-start(bf16[48,2176]{1,0:T(8,128)(2,1)S(1)} %copy-done.44), channel_id=1, source_target_pairs={{0,2},{1,3},{2,0},{3,1},{4,6},{5,7},{6,4},{7,5},{8,10},{9,11},{10,... | collective-permute-start | bytes 626696 | tf_op jit(solution)/shard_map/ppermute | solution.py:269
  138.5 17.4 %collective-permute-start.2 = (bf16[48,2176]{1,0:T(8,128)(2,1)S(1)}, bf16[48,2176]{1,0:T(8,128)(2,1)S(1)}, u32[]{:S(2)}, u32[]{:S(2)}) collective-permute-start(bf16[48,2176]{1,0:T(8,128)(2,1)S(1)} %copy-done.43), channel_id=1, source_target_pairs={{0,3},{1,2},{2,1},{3,0},{4,7},{5,6},{6,5},{7,4},{8,11},{9,10},{10,... | collective-permute-start | bytes 626696 | tf_op jit(solution)/shard_map/ppermute | solution.py:269
  146.8 41.8 %collective-permute-start.20 = (bf16[128,2176]{1,0:T(8,128)(2,1)S(1)}, bf16[128,2176]{1,0:T(8,128)(2,1)S(1)}, u32[]{:S(2)}, u32[]{:S(2)}) collective-permute-start(bf16[128,2176]{1,0:T(8,128)(2,1)S(1)} %copy-done.25), channel_id=1, source_target_pairs={{0,12},{1,13},{2,14},{3,15},{4,0},{5,1},{6,2},{7,3},{8,4},{9,5},{1... | collective-permute-start | bytes 1671176 | tf_op jit(solution)/shard_map/ppermute | solution.py:265
  150.6 49.0 %collective-permute-start.32 = (bf16[128,2176]{1,0:T(8,128)(2,1)}, bf16[128,2176]{1,0:T(8,128)(2,1)S(1)}, u32[]{:S(2)}, u32[]{:S(2)}) collective-permute-start(bf16[128,2176]{1,0:T(8,128)(2,1)} %combine.6), channel_id=1, source_target_pairs={{0,8},{1,9},{2,10},{3,11},{4,12},{5,13},{6,14},{7,15},{8,0},{9,1},... | collective-permute-start | bytes 1671176 | tf_op jit(solution)/shard_map/ppermute | solution.py:265
  150.7 49.0 %collective-permute-start.44 = (bf16[128,2176]{1,0:T(8,128)(2,1)}, bf16[128,2176]{1,0:T(8,128)(2,1)S(1)}, u32[]{:S(2)}, u32[]{:S(2)}) collective-permute-start(bf16[128,2176]{1,0:T(8,128)(2,1)} %combine.7), channel_id=1, source_target_pairs={{0,4},{1,5},{2,6},{3,7},{4,8},{5,9},{6,10},{7,11},{8,12},{9,13},{1... | collective-permute-start | bytes 1671176 | tf_op jit(solution)/shard_map/ppermute | solution.py:265
  163.1 2.4 %collective-permute-start.6 = (bf16[48,2176]{1,0:T(8,128)(2,1)}, bf16[48,2176]{1,0:T(8,128)(2,1)S(1)}, u32[]{:S(2)}, u32[]{:S(2)}) collective-permute-start(bf16[48,2176]{1,0:T(8,128)(2,1)} %get-tuple-element.80), channel_id=1, source_target_pairs={{0,1},{1,0},{2,3},{3,2},{4,5},{5,4},{6,7},{7,6},{8,9},{9,8},{10,11... | collective-permute-start | bytes 626696 | tf_op jit(solution)/shard_map/ppermute | solution.py:269
  164.2 8.2 %collective-permute-start.7 = (bf16[48,2176]{1,0:T(8,128)(2,1)}, bf16[48,2176]{1,0:T(8,128)(2,1)S(1)}, u32[]{:S(2)}, u32[]{:S(2)}) collective-permute-start(bf16[48,2176]{1,0:T(8,128)(2,1)} %get-tuple-element.81), channel_id=1, source_target_pairs={{0,2},{1,3},{2,0},{3,1},{4,6},{5,7},{6,4},{7,5},{8,10},{9,11},{10,... | collective-permute-start | bytes 626696 | tf_op jit(solution)/shard_map/ppermute | solution.py:269
  165.5 9.7 %collective-permute-start.8 = (bf16[48,2176]{1,0:T(8,128)(2,1)}, bf16[48,2176]{1,0:T(8,128)(2,1)S(1)}, u32[]{:S(2)}, u32[]{:S(2)}) collective-permute-start(bf16[48,2176]{1,0:T(8,128)(2,1)} %get-tuple-element.82), channel_id=1, source_target_pairs={{0,3},{1,2},{2,1},{3,0},{4,7},{5,6},{6,5},{7,4},{8,11},{9,10},{10,... | collective-permute-start | bytes 626696 | tf_op jit(solution)/shard_map/ppermute | solution.py:269
  (45 other events, 522.8 us)

commit v2 on v1

--- a/solution.py
+++ b/solution.py
@@ -111,22 +111,67 @@
     return lax.dot_general(a, b, (contract, ((), ())), preferred_element_type=F32)
 
 
-def call(kernel, outs, name, *operands, scratch=(), smem=0, limit=60):
-    vmem = pl.BlockSpec(memory_space=pltpu.VMEM)
-    scalar = pl.BlockSpec(memory_space=pltpu.SMEM)
-    return pl.pallas_call(
-        kernel,
-        out_shape=[jax.ShapeDtypeStruct(shape, kind) for shape, kind in outs],
-        in_specs=[scalar] * smem + [vmem] * (len(operands) - smem),
-        out_specs=[vmem] * len(outs),
-        scratch_shapes=list(scratch),
-        name=name,
-        compiler_params=pltpu.CompilerParams(vmem_limit_bytes=limit << 20),
-        cost_estimate=pl.CostEstimate(flops=1000, bytes_accessed=1000, transcendentals=0),
-    )(*operands)
-
-
-def pack_kernel(ids_ref, levels_ref, x_ref, out_ref):
+class Chain:
+    def __init__(self):
+        self.last = []
+
+    def __call__(self, kernel, outs, name, *operands, after=(), scratch=(), smem=0, limit=16):
+        vmem = pl.BlockSpec(memory_space=pltpu.VMEM)
+        scalar = pl.BlockSpec(memory_space=pltpu.SMEM)
+        unused = [*self.last, *after]
+        fixed = len(operands)
+
+        def body(*refs):
+            kernel(*refs[:fixed], *refs[fixed + len(unused) :])
+
+        made = pl.pallas_call(
+            body,
+            out_shape=[jax.ShapeDtypeStruct(shape, kind) for shape, kind in outs],
+            in_specs=[scalar] * smem
+            + [vmem] * (fixed - smem)
+            + [pl.BlockSpec(memory_space=pl.ANY)] * len(unused),
+            out_specs=[vmem] * len(outs),
+            scratch_shapes=list(scratch),
+            name=name,
+            compiler_params=pltpu.CompilerParams(vmem_limit_bytes=limit << 20),
+            cost_estimate=pl.CostEstimate(flops=1000, bytes_accessed=1000, transcendentals=0),
+        )(*operands, *unused)
+        self.last = made[:1]
+        return made
+
+    def hold(self, array, after=()):
+        unused = [*self.last, *after]
+        rows, width = array.shape
+        half = jax.ShapeDtypeStruct((rows // 2, width), array.dtype)
+
+        def body(*refs):
+            whole, halves, sems = refs[0], refs[-3:-1], refs[-1]
+            copies = [
+                pltpu.make_async_copy(whole.at[pl.ds(rows // 2 * i, rows // 2)], halves[i], sems.at[i])
+                for i in range(2)
+            ]
+            for copy in copies:
+                copy.start()
+            for copy in copies:
+                copy.wait()
+
+        vmem, anywhere = pl.BlockSpec(memory_space=pltpu.VMEM), pl.BlockSpec(memory_space=pl.ANY)
+        made = pl.pallas_call(
+            body,
+            out_shape=[jax.ShapeDtypeStruct(array.shape, array.dtype), half, half],
+            in_specs=[anywhere] * (1 + len(unused)),
+            out_specs=[anywhere, vmem, vmem],
+            input_output_aliases={0: 0},
+            scratch_shapes=[pltpu.SemaphoreType.DMA((2,))],
+            name="hold",
+            compiler_params=pltpu.CompilerParams(vmem_limit_bytes=4 << 20),
+            cost_estimate=pl.CostEstimate(flops=1000, bytes_accessed=1000, transcendentals=0),
+        )(array, *unused)
+        self.last = made[1:2]
+        return made[0], made[1:]
+
+
+def pack_kernel(ids_ref, levels_ref, x_ref, d_ref, out_ref, *half_refs):
     fanout, rows = ids_ref.shape
     features = x_ref.shape[1]
     expert = lax.broadcasted_iota(jnp.int32, (LANES, rows), 0)
@@ -134,53 +179,75 @@
     for k in range(fanout):
         value = levels_ref[k : k + 1, :].astype(F32) * (1.0 / 256.0)
         gates = gates + jnp.where(ids_ref[k : k + 1, :] == expert, value, 0.0)
+    gates = gates.T.astype(BF16)
     out_ref[:, :features] = x_ref[...]
-    out_ref[:, features:] = gates.T.astype(BF16)
-
-
-def slot_kernel(capacity, me_ref, x_ref, pick_ref, *slot_refs):
-    rows = x_ref.shape[0]
-    features = x_ref.shape[1] - LANES
+    out_ref[:, features:] = gates
+    for i in range(2):
+        part = slice(rows // 2 * i, rows // 2 * (i + 1))
+        half_refs[i][:, :features] = x_ref[part, :]
+        half_refs[i][:, features:] = gates[part, :]
+        half_refs[2 + i][...] = d_ref[part, :]
+
+
+def joined(upper_ref, lower_ref):
+    return jnp.concatenate([upper_ref[...], lower_ref[...]], axis=0)
+
+
+def slot_kernel(capacity, me_ref, mine_ref, upper_ref, lower_ref, pick_ref, own_ref, sent_ref):
+    rows = mine_ref.shape[0]
+    features = mine_ref.shape[1] - LANES
     me = me_ref[0]
     expert = lax.broadcasted_iota(jnp.int32, (8, LANES), 1)
-    wanted = jnp.bitwise_xor(lax.broadcasted_iota(jnp.int32, (8, LANES), 0), me)
+    wanted = jnp.bitwise_xor(2 * lax.broadcasted_iota(jnp.int32, (8, LANES), 0), me)
     chooser = jnp.where(expert == wanted, 1.0, 0.0).astype(BF16)
-    gates = dot(chooser, x_ref[:, features:], ((1,), (1,)))
-    routed = jnp.where(gates > 0.0, 1.0, 0.0)
     before = lax.broadcasted_iota(jnp.int32, (rows, rows), 0)
     after = lax.broadcasted_iota(jnp.int32, (rows, rows), 1)
     earlier = jnp.where(before < after, 1.0, 0.0).astype(BF16)
-    place = dot(routed.astype(BF16), earlier)
-    place = jnp.where(routed > 0.0, place, -1.0)
     slot = lax.broadcasted_iota(jnp.int32, (capacity, rows), 0).astype(F32)
-    pick = jnp.concatenate(
-        [jnp.where(place[j : j + 1, :] == slot, 1.0, 0.0) for j in range(PLANE)], axis=0
-    ).astype(BF16)
-    pick_ref[...] = pick
-    picked = dot(pick, x_ref[...]).astype(BF16)
-    for j in range(PLANE):
-        slot_refs[j][...] = picked[j * capacity : (j + 1) * capacity, :]
-
-
-def gather_kernel(capacity, pick_ref, d_ref, *slot_refs):
-    picked = dot(pick_ref[...], d_ref[...]).astype(BF16)
-    for j in range(PLANE):
-        slot_refs[j][...] = picked[j * capacity : (j + 1) * capacity, :]
-
-
-def expert_kernel(capacity, me_ref, *refs):
-    x_refs, d_refs = refs[:PLANE], refs[PLANE : 2 * PLANE]
-    gate_ref, up_ref, down_ref = refs[2 * PLANE : 2 * PLANE + 3]
-    term_refs = refs[2 * PLANE + 3 : 3 * PLANE + 3]
-    grads_ref, hidden_ref = refs[3 * PLANE + 3 :]
-    features = d_refs[0].shape[1]
+    for j, x in enumerate((mine_ref[...], joined(upper_ref, lower_ref))):
+        gates = dot(chooser, x[:, features:], ((1,), (1,)))
+        routed = jnp.where(gates > 0.0, 1.0, 0.0)
+        place = dot(routed.astype(BF16), earlier)
+        place = jnp.where(routed > 0.0, place, -1.0)
+        pick = jnp.concatenate(
+            [jnp.where(place[i : i + 1, :] == slot, 1.0, 0.0) for i in range(2)], axis=0
+        ).astype(BF16)
+        pick_ref[2 * capacity * j : 2 * capacity * (j + 1), :] = pick
+        picked = dot(pick, x).astype(BF16)
+        own_ref[capacity * j : capacity * (j + 1), :] = picked[:capacity, :]
+        sent_ref[capacity * j : capacity * (j + 1), :] = picked[capacity:, :]
+
+
+def gather_kernel(capacity, pick_ref, mine_ref, upper_ref, lower_ref, own_ref, sent_ref):
+    for j, d in enumerate((mine_ref[...], joined(upper_ref, lower_ref))):
+        picked = dot(pick_ref[2 * capacity * j : 2 * capacity * (j + 1), :], d).astype(BF16)
+        own_ref[capacity * j : capacity * (j + 1), :] = picked[:capacity, :]
+        sent_ref[capacity * j : capacity * (j + 1), :] = picked[capacity:, :]
+
+
+def expert_kernel(
+    me_ref,
+    x_own_ref,
+    x_far_ref,
+    d_own_ref,
+    d_far_ref,
+    gate_ref,
+    up_ref,
+    down_ref,
+    far_ref,
+    own_ref,
+    grads_ref,
+    hidden_ref,
+):
+    features = d_own_ref.shape[1]
     units = gate_ref.shape[1]
-    rows = PLANE * capacity
-    x = jnp.concatenate([ref[:, :features] for ref in x_refs], axis=0)
-    gates = jnp.concatenate([ref[:, features:] for ref in x_refs], axis=0).astype(F32)
+    half = d_own_ref.shape[0]
+    rows = 2 * half
+    x = jnp.concatenate([x_own_ref[:, :features], x_far_ref[:, :features]], axis=0)
+    gates = jnp.concatenate([x_own_ref[:, features:], x_far_ref[:, features:]], axis=0).astype(F32)
     mine = lax.broadcasted_iota(jnp.int32, (rows, LANES), 1) == me_ref[0]
     gating = jnp.sum(jnp.where(mine, gates, 0.0), axis=1, keepdims=True)
-    d = jnp.concatenate([ref[...] for ref in d_refs], axis=0)
+    d = jnp.concatenate([d_own_ref[...], d_far_ref[...]], axis=0)
     gate_pre = dot(x, gate_ref[...])
     up_pre = dot(x, up_ref[...])
     back_grad = dot(d, down_ref[...], ((1,), (1,)))
@@ -189,7 +256,8 @@
     hidden = (silu * up_pre).astype(BF16).astype(F32)
     router = jnp.sum(hidden * back_grad, axis=1, keepdims=True)
     hidden_grad = gating * back_grad
-    gate_grad = (hidden_grad * up_pre * sigmoid_gate * (1.0 + gate_pre * (1.0 - sigmoid_gate))).astype(BF16)
+    gate_grad = hidden_grad * up_pre * sigmoid_gate * (1.0 + gate_pre * (1.0 - sigmoid_gate))
+    gate_grad = gate_grad.astype(BF16)
     up_grad = (hidden_grad * silu).astype(BF16)
     grads_ref[:, :units] = gate_grad
     grads_ref[:, units:] = up_grad
@@ -197,24 +265,41 @@
     term = dot(gate_grad, gate_ref[...], ((1,), (1,))) + dot(up_grad, up_ref[...], ((1,), (1,)))
     term = term.astype(BF16)
     router = jnp.where(mine, router, 0.0).astype(BF16)
-    for j in range(PLANE):
-        part = slice(j * capacity, (j + 1) * capacity)
-        term_refs[j][:, :features] = term[part, :]
-        term_refs[j][:, features:] = router[part, :]
-
-
-def combine_kernel(pick_ref, *refs):
-    terms = jnp.concatenate([ref[...] for ref in refs[:PLANE]], axis=0)
-    refs[PLANE][...] = dot(pick_ref[...], terms, ((0,), (0,))).astype(BF16)
+    own_ref[:, :features] = term[:half, :]
+    own_ref[:, features:] = router[:half, :]
+    far_ref[:, :features] = term[half:, :]
+    far_ref[:, features:] = router[half:, :]
+
+
+def combine_kernel(capacity, pick_ref, own_ref, back_ref, upper_ref, lower_ref, mine_ref):
+    rows = mine_ref.shape[0]
+    for j in range(2):
+        part = slice(capacity * j, capacity * (j + 1))
+        terms = jnp.concatenate([own_ref[part, :], back_ref[part, :]], axis=0)
+        total = dot(pick_ref[2 * capacity * j : 2 * capacity * (j + 1), :], terms, ((0,), (0,)))
+        if j == 0:
+            mine_ref[...] = total
+        else:
+            upper_ref[...] = total[: rows // 2, :].astype(BF16)
+            lower_ref[...] = total[rows // 2 :, :].astype(BF16)
+
+
+def summed(mine_ref, upper_ref, lower_ref, *refs):
+    total = mine_ref[...] + joined(upper_ref, lower_ref).astype(F32)
+    for ref in refs:
+        total = total + ref[...].astype(F32)
+    return total
+
+
+def add_kernel(*refs):
+    refs[-1][...] = summed(*refs[:-1]).astype(BF16)
 
 
 def total_kernel(ids_ref, *refs):
     parts, (grad_ref, router_ref) = refs[:-2], refs[-2:]
     fanout, rows = ids_ref.shape
     features = grad_ref.shape[1]
-    total = parts[0][...].astype(F32)
-    for part in parts[1:]:
-        total = total + part[...].astype(F32)
+    total = summed(*parts)
     grad_ref[...] = total[:, :features].astype(BF16)
     router = total[:, features:].T
     expert = lax.broadcasted_iota(jnp.int32, (LANES, rows), 0)
@@ -223,16 +308,15 @@
         router_ref[k : k + 1, :] = jnp.sum(own, axis=0, keepdims=True).astype(BF16)
 
 
-def delta_kernel(chunks, *refs):
-    x_refs, d_refs = refs[: chunks * PLANE], refs[chunks * PLANE : 2 * chunks * PLANE]
-    grads_refs = refs[2 * chunks * PLANE : 2 * chunks * PLANE + chunks]
-    hidden_refs = refs[2 * chunks * PLANE + chunks : 2 * chunks * PLANE + 2 * chunks]
+def delta_kernel(blocks, *refs):
+    x_refs, d_refs = refs[:blocks], refs[blocks : 2 * blocks]
+    grads_refs = refs[2 * blocks : 5 * blocks // 2]
+    hidden_refs = refs[5 * blocks // 2 : 3 * blocks]
     gate_ref, up_ref, down_ref, x_all, d_all = refs[-5:]
-    units = gate_ref.shape[1]
-    features = gate_ref.shape[0]
-    capacity = x_refs[0].shape[0]
-    for i in range(chunks * PLANE):
-        part = slice(i * capacity, (i + 1) * capacity)
+    features, units = gate_ref.shape
+    rows = d_refs[0].shape[0]
+    for i in range(blocks):
+        part = slice(i * rows, (i + 1) * rows)
         x_all[part, :] = x_refs[i][:, :features]
         d_all[part, :] = d_refs[i][...]
     grads = jnp.concatenate([ref[...] for ref in grads_refs], axis=0)
@@ -256,82 +340,131 @@
     units = w_gate.shape[2]
     capacity = 3 * tok_rows * fanout // (2 * devices)
     wide = features + LANES
+    half = 2 * capacity
     me = lax.axis_index("expert").reshape(1)
     ids = expert_ids.T
     gate_mat, up_mat, down_mat = w_gate[0], w_up[0], w_down[0]
-
-    def along(array, distance):
-        pairs = [(i, (i + distance * PLANE) % devices) for i in range(devices)]
-        return lax.ppermute(array, "expert", pairs)
-
-    def within(arrays):
-        moved = [
-            lax.ppermute(arrays[j], "expert", [(i, i ^ j) for i in range(devices)])
-            for j in range(1, PLANE)
-        ]
-        return [arrays[0]] + moved
-
-    (packed,) = call(pack_kernel, [((tok_rows, wide), BF16)], "pack", ids, gate_levels.T, tokens)
-    xs, ds = [packed], [cotangent]
-    for _ in range(planes - 1):
-        xs.append(along(xs[-1], 1))
-        ds.append(along(ds[-1], 1))
-
-    all_x, all_d, all_grads, all_hidden, parts = [], [], [], [], []
-    rows = PLANE * capacity
-    for s in range(planes):
-        pick, *slots = call(
+    run = Chain()
+
+    def along(array):
+        return lax.ppermute(array, "expert", [(i, (i + PLANE) % devices) for i in range(devices)])
+
+    def across(array):
+        return lax.ppermute(array, "expert", [(i, i ^ 2) for i in range(devices)])
+
+    def cores(halves):
+        pairs = [(i, i ^ 1) for i in range(devices)]
+        return [lax.ppermute(half, "expert", pairs) for half in halves]
+
+    pick, own_x, far_x, own_d, far_d = ({} for _ in range(5))
+    own_t, far_t, grads, hidden = ({} for _ in range(4))
+
+    def slots_x(s, x, halves):
+        pick[s], own_x[s], sent = run(
             functools.partial(slot_kernel, capacity),
-            [((rows, tok_rows), BF16)] + [((capacity, wide), BF16)] * PLANE,
+            [((2 * half, tok_rows), BF16), ((half, wide), BF16), ((half, wide), BF16)],
             "slots_x",
             me,
-            xs[s],
+            x,
+            *cores(halves),
             smem=1,
         )
-        rows_x = within(slots)
-        slots = call(
+        far_x[s] = across(sent)
+
+    def slots_d(s, d, halves):
+        own_d[s], sent = run(
             functools.partial(gather_kernel, capacity),
-            [((capacity, features), BF16)] * PLANE,
+            [((half, features), BF16)] * 2,
             "slots_d",
-            pick,
-            ds[s],
+            pick[s],
+            d,
+            *cores(halves),
         )
-        rows_d = within(slots)
-        *terms, grads, hidden = call(
-            functools.partial(expert_kernel, capacity),
-            [((capacity, wide), BF16)] * PLANE + [((rows, 2 * units), BF16), ((rows, units), BF16)],
+        far_d[s] = across(sent)
+
+    def expert(s):
+        far, own_t[s], grads[s], hidden[s] = run(
+            expert_kernel,
+            [((half, wide), BF16)] * 2
+            + [((2 * half, 2 * units), BF16), ((2 * half, units), BF16)],
             "expert",
             me,
-            *rows_x,
-            *rows_d,
+            own_x[s],
+            far_x[s],
+            own_d[s],
+            far_d[s],
             gate_mat,
             up_mat,
             down_mat,
             smem=1,
+            limit=30,
         )
-        (part,) = call(combine_kernel, [((tok_rows, wide), BF16)], "combine", pick, *within(terms))
-        parts.append(along(part, -s) if s else part)
-        all_x += rows_x
-        all_d += rows_d
-        all_grads.append(grads)
-        all_hidden.append(hidden)
-
-    gate_delta, up_delta, down_delta = call(
-        functools.partial(delta_kernel, planes),
+        far_t[s] = across(far)
+
+    def combine(s):
+        *halves, mine = run(
+            functools.partial(combine_kernel, capacity),
+            [((tok_rows // 2, wide), BF16)] * 2 + [((tok_rows, wide), F32)],
+            "combine",
+            pick[s],
+            own_t[s],
+            far_t[s],
+        )
+        return [mine, *cores(halves)]
+
+    def add(*parts):
+        return along(run(add_kernel, [((tok_rows, wide), BF16)], "add", *parts)[0])
+
+    packed, *halves = run(
+        pack_kernel,
+        [((tok_rows, wide), BF16)]
+        + [((tok_rows // 2, wide), BF16)] * 2
+        + [((tok_rows // 2, features), BF16)] * 2,
+        "pack",
+        ids,
+        gate_levels.T,
+        tokens,
+        cotangent,
+    )
+    x, d = along(packed), along(cotangent)
+    slots_x(0, packed, halves[:2])
+    slots_d(0, cotangent, halves[2:])
+    last = planes - 1
+    for s in range(1, planes):
+        here, halves = run.hold(x, after=[far_x[s - 1]])
+        if s < last:
+            x = along(here)
+        slots_x(s, here, halves)
+        here, halves = run.hold(d, after=[far_d[s - 1]])
+        if s < last:
+            d = along(here)
+        slots_d(s, here, halves)
+        if 1 < s:
+            expert(s - 1)
+    passed = add(*combine(1))
+    expert(last)
+    expert(0)
+    passed = add(*combine(2), passed)
+    passed = add(*combine(3), passed)
+    order = range(planes)
+    gate_delta, up_delta, down_delta = run(
+        functools.partial(delta_kernel, 2 * planes),
         [((features, units), BF16), ((features, units), BF16), ((units, features), BF16)],
         "deltas",
-        *all_x,
-        *all_d,
-        *all_grads,
-        *all_hidden,
-        scratch=[pltpu.VMEM((planes * rows, features), BF16)] * 2,
-    )
-    input_grad, router_grad = call(
+        *[block for s in order for block in (own_x[s], far_x[s])],
+        *[block for s in order for block in (own_d[s], far_d[s])],
+        *[grads[s] for s in order],
+        *[hidden[s] for s in order],
+        scratch=[pltpu.VMEM((2 * planes * half, features), BF16)] * 2,
+        limit=40,
+    )
+    input_grad, router_grad = run(
         total_kernel,
         [((tok_rows, features), BF16), ((fanout, tok_rows), BF16)],
         "total",
         ids,
-        *parts,
+        *combine(0),
+        passed,
     )
     return input_grad, router_grad.T, gate_delta[None], up_delta[None], down_delta[None]
 

time: 205 us -> 157 us (0.77)
  Pallas kernels: 70.6 us -> 26.7 us
  starting transfers between devices: 38.4 us -> 29.7 us
  waiting for transfers between devices: 90.2 us -> 94.7 us
    pallas_call x19 -> x28, Pallas kernels: 70.6 us -> 26.7 us  [the longest x22 26.2 us: __call__(): pl.pallas_call(body, out_shape=[jax.ShapeDtypeStruct(shape, kind) for sha...]
    ppermute x45, starting transfers between devices: 38.4 us -> 29.7 us  [the longest x12 17.9 us: across(): return lax.ppermute(array, 'expert', [(i, i ^ 2) for i in range(devices)])]
    ppermute x45, waiting for transfers between devices: 90.2 us -> 94.7 us  [the longest x9 51.3 us: along(): lax.ppermute(array, 'expert', [(i, (i + PLANE) % devices) for i in range(...]
    unnamed x96 -> x20, local copies, waits for them, and re-layouts: 3.91 us -> 4.87 us
  transfers between devices with their start and end apart: 45 -> 45, of which waited for: 20 -> 23; matrix products, arithmetic and copies ran while one was open for 0% -> 0% of each run, Pallas kernels for 32% -> 16%
where the time goes in v2:
time: 157 us
  waiting for transfers between devices  94.7 us (60%)
  starting transfers between devices  29.7 us (19%)
  Pallas kernels  26.7 us (17%)
  local copies, waits for them, and re-layouts  4.87 us (3%)
    ppermute x9, waiting for transfers between devices, along(): lax.ppermute(array, 'expert', [(i, (i + PLANE) % devices) for i in range(...  51.3 us
    ppermute x12, waiting for transfers between devices, across(): return lax.ppermute(array, 'expert', [(i, i ^ 2) for i in range(devices)])  35 us
    pallas_call x22, Pallas kernels, __call__(): pl.pallas_call(body, out_shape=[jax.ShapeDtypeStruct(shape, kind) for sha...  26.2 us
    ppermute x12, starting transfers between devices, across(): return lax.ppermute(array, 'expert', [(i, i ^ 2) for i in range(devices)])  17.9 us
    ppermute x24, waiting for transfers between devices, cores(): return [lax.ppermute(half, 'expert', pairs) for half in halves]  8.42 us
    ppermute x24, starting transfers between devices, cores(): return [lax.ppermute(half, 'expert', pairs) for half in halves]  6.79 us
    ppermute x9, starting transfers between devices, along(): lax.ppermute(array, 'expert', [(i, (i + PLANE) % devices) for i in range(...  5.08 us
    unnamed x20, local copies, waits for them, and re-layouts  4.87 us
  transfers between devices with their start and end apart: 45, of which 23 were waited for; matrix products, arithmetic and copies ran while one was open for 0% of the time, Pallas kernels for 16%

profile of v2, /device:TPU:0, one launch (start us, length us, event | category | flops | bytes accessed | tf_op | source)
XLA Modules:
  0.0 157.0 jit_solution(9353728775901834909)
XLA Ops:
  0.6 1.0 copy-done.3
  1.7 1.0 copy-done.6
  2.7 0.7 copy-done.7
  3.4 0.7 copy-done.9
  4.2 0.5 collective-permute-start
  4.8 3.0 %collective-permute-start.6 = (bf16[128,2176]{1,0:T(8,128)(2,1)S(1)}, bf16[128,2176]{1,0:T(8,128)(2,1)S(1)}, u32[]{:S(2)}, u32[]{:S(2)}) collective-permute-start(bf16[128,2176]{1,0:T(8,128)(2,1)S(1)} %get-tuple-element.81.refs_1_.refs_4_), channel_id=1, source_target_pairs={{0,4},{1,5},{2,6},{3,7},{4,8},{5,9},{6,10},{7,11},{8,12},{9,13},{1... | collective-permute-start | bytes 1671176 | tf_op jit(solution)/shard_map/ppermute | solution.py:350
  7.8 0.9 slots_x.4
  8.7 1.6 %collective-permute-start.2 = (bf16[96,2176]{1,0:T(8,128)(2,1)S(1)}, bf16[96,2176]{1,0:T(8,128)(2,1)S(1)}, u32[]{:S(2)}, u32[]{:S(2)}) collective-permute-start(bf16[96,2176]{1,0:T(8,128)(2,1)S(1)} %get-tuple-element.86), channel_id=1, source_target_pairs={{0,2},{1,3},{2,0},{3,1},{4,6},{5,7},{6,4},{7,5},{8,10},{9,11},{10,... | collective-permute-start | bytes 1253384 | tf_op jit(solution)/shard_map/ppermute | solution.py:353
  10.3 0.5 collective-permute-start.4
  10.8 1.6 %collective-permute-start.10 = (bf16[128,2048]{1,0:T(8,128)(2,1)S(1)}, bf16[128,2048]{1,0:T(8,128)(2,1)S(1)}, u32[]{:S(2)}, u32[]{:S(2)}) collective-permute-start(bf16[128,2048]{1,0:T(8,128)(2,1)S(1)} %copy-done.4), channel_id=1, source_target_pairs={{0,4},{1,5},{2,6},{3,7},{4,8},{5,9},{6,10},{7,11},{8,12},{9,13},{1... | collective-permute-start | bytes 1572872 | tf_op jit(solution)/shard_map/ppermute | solution.py:350
  12.8 0.6 collective-permute-start.5
  13.3 9.9 %collective-permute-done.6.refs_0_ = bf16[128,2176]{1,0:T(8,128)(2,1)S(1)} collective-permute-done((bf16[128,2176]{1,0:T(8,128)(2,1)S(1)}, bf16[128,2176]{1,0:T(8,128)(2,1)S(1)}, u32[]{:S(2)}, u32[]{:S(2)}) %collective-permute-start.6) | collective-permute-done | bytes 557088 | tf_op jit(solution)/shard_map/ppermute | solution.py:350
  23.5 0.5 collective-permute-start.8
  24.0 1.0 collective-permute-done.9.refs_3_
  25.4 0.9 slots_x.5
  26.3 1.8 %collective-permute-start.13 = (bf16[96,2176]{1,0:T(8,128)(2,1)S(1)}, bf16[96,2176]{1,0:T(8,128)(2,1)S(1)}, u32[]{:S(2)}, u32[]{:S(2)}) collective-permute-start(bf16[96,2176]{1,0:T(8,128)(2,1)S(1)} %get-tuple-element.99), channel_id=1, source_target_pairs={{0,2},{1,3},{2,0},{3,1},{4,6},{5,7},{6,4},{7,5},{8,10},{9,11},{10,... | collective-permute-start | bytes 1253384 | tf_op jit(solution)/shard_map/ppermute | solution.py:353
  28.1 6.4 %collective-permute-done.10.refs_0_ = bf16[128,2048]{1,0:T(8,128)(2,1)S(1)} collective-permute-done((bf16[128,2048]{1,0:T(8,128)(2,1)S(1)}, bf16[128,2048]{1,0:T(8,128)(2,1)S(1)}, u32[]{:S(2)}, u32[]{:S(2)}) %collective-permute-start.10) | collective-permute-done | bytes 524320 | tf_op jit(solution)/shard_map/ppermute | solution.py:350
  35.2 1.0 collective-permute-done.12.refs_3_
  36.9 1.8 %collective-permute-start.15 = (bf16[96,2048]{1,0:T(8,128)(2,1)S(1)}, bf16[96,2048]{1,0:T(8,128)(2,1)S(1)}, u32[]{:S(2)}, u32[]{:S(2)}) collective-permute-start(bf16[96,2048]{1,0:T(8,128)(2,1)S(1)} %get-tuple-element.102), channel_id=1, source_target_pairs={{0,2},{1,3},{2,0},{3,1},{4,6},{5,7},{6,4},{7,5},{8,10},{9,11},{10,... | collective-permute-start | bytes 1179656 | tf_op jit(solution)/shard_map/ppermute | solution.py:353
  38.8 7.7 %collective-permute-done.7.refs_0_ = bf16[128,2176]{1,0:T(8,128)(2,1)S(1)} collective-permute-done((bf16[128,2176]{1,0:T(8,128)(2,1)S(1)}, bf16[128,2176]{1,0:T(8,128)(2,1)S(1)}, u32[]{:S(2)}, u32[]{:S(2)}) %collective-permute-start.7) | collective-permute-done | bytes 557088 | tf_op jit(solution)/shard_map/ppermute | solution.py:350
  47.2 1.0 collective-permute-done.17.refs_3_
  48.6 0.9 slots_x.6
  49.5 1.8 %collective-permute-start.21 = (bf16[96,2176]{1,0:T(8,128)(2,1)S(1)}, bf16[96,2176]{1,0:T(8,128)(2,1)S(1)}, u32[]{:S(2)}, u32[]{:S(2)}) collective-permute-start(bf16[96,2176]{1,0:T(8,128)(2,1)S(1)} %get-tuple-element.111), channel_id=1, source_target_pairs={{0,2},{1,3},{2,0},{3,1},{4,6},{5,7},{6,4},{7,5},{8,10},{9,11},{10,... | collective-permute-start | bytes 1253384 | tf_op jit(solution)/shard_map/ppermute | solution.py:353
  51.3 6.4 %collective-permute-done.18.refs_0_ = bf16[128,2048]{1,0:T(8,128)(2,1)S(1)} collective-permute-done((bf16[128,2048]{1,0:T(8,128)(2,1)S(1)}, bf16[128,2048]{1,0:T(8,128)(2,1)S(1)}, u32[]{:S(2)}, u32[]{:S(2)}) %collective-permute-start.18) | collective-permute-done | bytes 524320 | tf_op jit(solution)/shard_map/ppermute | solution.py:350
  58.4 1.0 collective-permute-done.20.refs_3_
  60.1 1.8 %collective-permute-start.26 = (bf16[96,2048]{1,0:T(8,128)(2,1)S(1)}, bf16[96,2048]{1,0:T(8,128)(2,1)S(1)}, u32[]{:S(2)}, u32[]{:S(2)}) collective-permute-start(bf16[96,2048]{1,0:T(8,128)(2,1)S(1)} %get-tuple-element.118), channel_id=1, source_target_pairs={{0,2},{1,3},{2,0},{3,1},{4,6},{5,7},{6,4},{7,5},{8,10},{9,11},{10,... | collective-permute-start | bytes 1179656 | tf_op jit(solution)/shard_map/ppermute | solution.py:353
  61.9 2.6 %expert.4 = (bf16[96,2176]{1,0:T(8,128)(2,1)S(1)}, bf16[96,2176]{1,0:T(8,128)(2,1)S(1)}, bf16[192,768]{1,0:T(8,128)(2,1)S(1)}, bf16[192,384]{1,0:T(8,128)(2,1)S(1)}) custom-call(s32[1]{0:T(128)} %bitcast.1.refs_0_, bf16[96,2176]{1,0:T(8,128)(2,1)S(1)} %get-tuple-element.101.refs_1_.refs_2_, bf16[96,2176]{1,0:T(8,128)(2,1)S(1)} %collective-permute-done.13.refs_2_.refs_3_, ...), custom_call_target="tpu_custom_call" | custom-call | flops 1000 | bytes 1000 | tf_op jit(solution)/shard_map/expert/pallas_call | solution.py:127
  64.6 5.0 %collective-permute-done.14.refs_0_ = bf16[128,2176]{1,0:T(8,128)(2,1)S(1)} collective-permute-done((bf16[128,2176]{1,0:T(8,128)(2,1)S(1)}, bf16[128,2176]{1,0:T(8,128)(2,1)S(1)}, u32[]{:S(2)}, u32[]{:S(2)}) %collective-permute-start.14) | collective-permute-done | bytes 557088 | tf_op jit(solution)/shard_map/ppermute | solution.py:350
  70.3 1.8 %collective-permute-start.30 = (bf16[96,2176]{1,0:T(8,128)(2,1)S(1)}, bf16[96,2176]{1,0:T(8,128)(2,1)S(1)}, u32[]{:S(2)}, u32[]{:S(2)}) collective-permute-start(bf16[96,2176]{1,0:T(8,128)(2,1)S(1)} %get-tuple-element.110.refs_1_), channel_id=1, source_target_pairs={{0,2},{1,3},{2,0},{3,1},{4,6},{5,7},{6,4},{7,5},{8,10},{9,11},{10,... | collective-permute-start | bytes 1253384 | tf_op jit(solution)/shard_map/ppermute | solution.py:353
  72.1 0.9 slots_x.7
  73.0 7.3 %collective-permute-done.25.refs_0_ = bf16[128,2048]{1,0:T(8,128)(2,1)S(1)} collective-permute-done((bf16[128,2048]{1,0:T(8,128)(2,1)S(1)}, bf16[128,2048]{1,0:T(8,128)(2,1)S(1)}, u32[]{:S(2)}, u32[]{:S(2)}) %collective-permute-start.25) | collective-permute-done | bytes 524320 | tf_op jit(solution)/shard_map/ppermute | solution.py:350
  80.9 1.0 collective-permute-done.28.refs_3_
  82.7 2.7 %expert.5 = (bf16[96,2176]{1,0:T(8,128)(2,1)S(1)}, bf16[96,2176]{1,0:T(8,128)(2,1)S(1)}, bf16[192,768]{1,0:T(8,128)(2,1)S(1)}, bf16[192,384]{1,0:T(8,128)(2,1)S(1)}) custom-call(s32[1]{0:T(128)} %bitcast.1.refs_0_, bf16[96,2176]{1,0:T(8,128)(2,1)S(1)} %get-tuple-element.125.refs_1_.refs_4_, bf16[96,2176]{1,0:T(8,128)(2,1)S(1)} %collective-permute-done.21.refs_2_.refs_5_, ...), custom_call_target="tpu_custom_call" | custom-call | flops 1000 | bytes 1000 | tf_op jit(solution)/shard_map/expert/pallas_call | solution.py:127
  86.5 1.5 collective-permute-start.24
  88.5 1.5 collective-permute-start.29
  90.4 8.5 %collective-permute-done.24.refs_2_.refs_7_ = bf16[96,2176]{1,0:T(8,128)(2,1)S(1)} collective-permute-done((bf16[96,2176]{1,0:T(8,128)(2,1)S(1)}, bf16[96,2176]{1,0:T(8,128)(2,1)S(1)}, u32[]{:S(2)}, u32[]{:S(2)}) %collective-permute-start.24) | collective-permute-done | bytes 417824 | tf_op jit(solution)/shard_map/ppermute | solution.py:353
  98.9 16.6 %collective-permute-done.29.refs_4_.refs_15_ = bf16[96,2048]{1,0:T(8,128)(2,1)S(1)} collective-permute-done((bf16[96,2048]{1,0:T(8,128)(2,1)S(1)}, bf16[96,2048]{1,0:T(8,128)(2,1)S(1)}, u32[]{:S(2)}, u32[]{:S(2)}) %collective-permute-start.29) | collective-permute-done | bytes 393248 | tf_op jit(solution)/shard_map/ppermute | solution.py:353
  115.5 2.7 %expert.6 = (bf16[96,2176]{1,0:T(8,128)(2,1)S(1)}, bf16[96,2176]{1,0:T(8,128)(2,1)S(1)}, bf16[192,768]{1,0:T(8,128)(2,1)S(1)}, bf16[192,384]{1,0:T(8,128)(2,1)S(1)}) custom-call(s32[1]{0:T(128)} %bitcast.1.refs_0_, bf16[96,2176]{1,0:T(8,128)(2,1)S(1)} %get-tuple-element.115.refs_1_.refs_6_, bf16[96,2176]{1,0:T(8,128)(2,1)S(1)} %collective-permute-done.24.refs_2_.refs_7_, ...), custom_call_target="tpu_custom_call" | custom-call | flops 1000 | bytes 1000 | tf_op jit(solution)/shard_map/expert/pallas_call | solution.py:127
  118.2 2.7 %expert.7 = (bf16[96,2176]{1,0:T(8,128)(2,1)S(1)}, bf16[96,2176]{1,0:T(8,128)(2,1)S(1)}, bf16[192,768]{1,0:T(8,128)(2,1)S(1)}, bf16[192,384]{1,0:T(8,128)(2,1)S(1)}) custom-call(s32[1]{0:T(128)} %bitcast.1.refs_0_, bf16[96,2176]{1,0:T(8,128)(2,1)S(1)} %get-tuple-element.85.refs_1_.refs_0_, bf16[96,2176]{1,0:T(8,128)(2,1)S(1)} %collective-permute-done.2.refs_2_.refs_1_, ...), custom_call_target="tpu_custom_call" | custom-call | flops 1000 | bytes 1000 | tf_op jit(solution)/shard_map/expert/pallas_call | solution.py:127
  121.9 1.5 collective-permute-start.34
  123.7 9.8 %collective-permute-done.34.refs_2_ = bf16[96,2176]{1,0:T(8,128)(2,1)S(1)} collective-permute-done((bf16[96,2176]{1,0:T(8,128)(2,1)S(1)}, bf16[96,2176]{1,0:T(8,128)(2,1)S(1)}, u32[]{:S(2)}, u32[]{:S(2)}) %collective-permute-start.34) | collective-permute-done | bytes 417824 | tf_op jit(solution)/shard_map/ppermute | solution.py:353
  134.6 1.5 collective-permute-start.33
  136.1 4.0 %collective-permute-done.41.refs_3_ = bf16[128,2176]{1,0:T(8,128)(2,1)S(1)} collective-permute-done((bf16[128,2176]{1,0:T(8,128)(2,1)S(1)}, bf16[128,2176]{1,0:T(8,128)(2,1)S(1)}, u32[]{:S(2)}, u32[]{:S(2)}) %collective-permute-start.41) | collective-permute-done | bytes 557088 | tf_op jit(solution)/shard_map/ppermute | solution.py:350
  140.3 7.0 %deltas.1 = (bf16[2048,384]{1,0:T(8,128)(2,1)}, bf16[2048,384]{1,0:T(8,128)(2,1)}, bf16[384,2048]{1,0:T(8,128)(2,1)}) custom-call(bf16[96,2176]{1,0:T(8,128)(2,1)S(1)} %get-tuple-element.85.refs_1_.refs_0_, bf16[96,2176]{1,0:T(8,128)(2,1)S(1)} %collective-permute-done.2.refs_2_.refs_1_, bf16[96,2176]{1,0:T(8,128)(2,1)S(1)} %get-tuple-element.101.refs_1_.refs_2_, ...), custom_call_target="tpu_custom_call" | custom-call | flops 1000 | bytes 1000 | tf_op jit(solution)/shard_map/deltas/pallas_call | solution.py:127
  147.3 1.4 copy-done.5
  149.8 1.0 collective-permute-done.43.refs_3_
  151.2 4.6 %collective-permute-done.44.refs_4_ = bf16[128,2176]{1,0:T(8,128)(2,1)S(1)} collective-permute-done((bf16[128,2176]{1,0:T(8,128)(2,1)S(1)}, bf16[128,2176]{1,0:T(8,128)(2,1)S(1)}, u32[]{:S(2)}, u32[]{:S(2)}) %collective-permute-start.44) | collective-permute-done | bytes 557088 | tf_op jit(solution)/shard_map/ppermute | solution.py:350
  155.8 1.1 total.1
  (90 shorter events, 13.1 us)
Async XLA Ops:
  4.2 3.6 %collective-permute-start = (bf16[64,2176]{1,0:T(8,128)(2,1)S(1)}, bf16[64,2176]{1,0:T(8,128)(2,1)S(1)}, u32[]{:S(2)}, u32[]{:S(2)}) collective-permute-start(bf16[64,2176]{1,0:T(8,128)(2,1)S(1)} %get-tuple-element.82), channel_id=1, source_target_pairs={{0,1},{1,0},{2,3},{3,2},{4,5},{5,4},{6,7},{7,6},{8,9},{9,8},{10,11... | collective-permute-start | bytes 835592 | tf_op jit(solution)/shard_map/ppermute | solution.py:357
  4.7 3.1 %collective-permute-start.1 = (bf16[64,2176]{1,0:T(8,128)(2,1)S(1)}, bf16[64,2176]{1,0:T(8,128)(2,1)S(1)}, u32[]{:S(2)}, u32[]{:S(2)}) collective-permute-start(bf16[64,2176]{1,0:T(8,128)(2,1)S(1)} %get-tuple-element.83), channel_id=1, source_target_pairs={{0,1},{1,0},{2,3},{3,2},{4,5},{5,4},{6,7},{7,6},{8,9},{9,8},{10,11... | collective-permute-start | bytes 835592 | tf_op jit(solution)/shard_map/ppermute | solution.py:357
  4.8 18.4 %collective-permute-start.6 = (bf16[128,2176]{1,0:T(8,128)(2,1)S(1)}, bf16[128,2176]{1,0:T(8,128)(2,1)S(1)}, u32[]{:S(2)}, u32[]{:S(2)}) collective-permute-start(bf16[128,2176]{1,0:T(8,128)(2,1)S(1)} %get-tuple-element.81.refs_1_.refs_4_), channel_id=1, source_target_pairs={{0,4},{1,5},{2,6},{3,7},{4,8},{5,9},{6,10},{7,11},{8,12},{9,13},{1... | collective-permute-start | bytes 1671176 | tf_op jit(solution)/shard_map/ppermute | solution.py:350
  8.7 14.6 %collective-permute-start.2 = (bf16[96,2176]{1,0:T(8,128)(2,1)S(1)}, bf16[96,2176]{1,0:T(8,128)(2,1)S(1)}, u32[]{:S(2)}, u32[]{:S(2)}) collective-permute-start(bf16[96,2176]{1,0:T(8,128)(2,1)S(1)} %get-tuple-element.86), channel_id=1, source_target_pairs={{0,2},{1,3},{2,0},{3,1},{4,6},{5,7},{6,4},{7,5},{8,10},{9,11},{10,... | collective-permute-start | bytes 1253384 | tf_op jit(solution)/shard_map/ppermute | solution.py:353
  10.3 2.1 %collective-permute-start.3 = (bf16[64,2048]{1,0:T(8,128)(2,1)S(1)}, bf16[64,2048]{1,0:T(8,128)(2,1)S(1)}, u32[]{:S(2)}, u32[]{:S(2)}) collective-permute-start(bf16[64,2048]{1,0:T(8,128)(2,1)S(1)} %get-tuple-element.87), channel_id=1, source_target_pairs={{0,1},{1,0},{2,3},{3,2},{4,5},{5,4},{6,7},{7,6},{8,9},{9,8},{10,11... | collective-permute-start | bytes 786440 | tf_op jit(solution)/shard_map/ppermute | solution.py:357
  10.3 2.1 %collective-permute-start.4 = (bf16[64,2048]{1,0:T(8,128)(2,1)S(1)}, bf16[64,2048]{1,0:T(8,128)(2,1)S(1)}, u32[]{:S(2)}, u32[]{:S(2)}) collective-permute-start(bf16[64,2048]{1,0:T(8,128)(2,1)S(1)} %get-tuple-element.88), channel_id=1, source_target_pairs={{0,1},{1,0},{2,3},{3,2},{4,5},{5,4},{6,7},{7,6},{8,9},{9,8},{10,11... | collective-permute-start | bytes 786440 | tf_op jit(solution)/shard_map/ppermute | solution.py:357
  10.8 23.7 %collective-permute-start.10 = (bf16[128,2048]{1,0:T(8,128)(2,1)S(1)}, bf16[128,2048]{1,0:T(8,128)(2,1)S(1)}, u32[]{:S(2)}, u32[]{:S(2)}) collective-permute-start(bf16[128,2048]{1,0:T(8,128)(2,1)S(1)} %copy-done.4), channel_id=1, source_target_pairs={{0,4},{1,5},{2,6},{3,7},{4,8},{5,9},{6,10},{7,11},{8,12},{9,13},{1... | collective-permute-start | bytes 1572872 | tf_op jit(solution)/shard_map/ppermute | solution.py:350
  12.8 21.7 %collective-permute-start.5 = (bf16[96,2048]{1,0:T(8,128)(2,1)S(1)}, bf16[96,2048]{1,0:T(8,128)(2,1)S(1)}, u32[]{:S(2)}, u32[]{:S(2)}) collective-permute-start(bf16[96,2048]{1,0:T(8,128)(2,1)S(1)} %get-tuple-element.90), channel_id=1, source_target_pairs={{0,2},{1,3},{2,0},{3,1},{4,6},{5,7},{6,4},{7,5},{8,10},{9,11},{10,... | collective-permute-start | bytes 1179656 | tf_op jit(solution)/shard_map/ppermute | solution.py:353
  23.4 1.6 %collective-permute-start.9 = (bf16[64,2176]{1,0:T(8,128)(2,1)S(1)}, bf16[64,2176]{1,0:T(8,128)(2,1)S(1)}, u32[]{:S(2)}, u32[]{:S(2)}) collective-permute-start(bf16[64,2176]{1,0:T(8,128)(2,1)S(1)} %get-tuple-element.93), channel_id=1, source_target_pairs={{0,1},{1,0},{2,3},{3,2},{4,5},{5,4},{6,7},{7,6},{8,9},{9,8},{10,11... | collective-permute-start | bytes 835592 | tf_op jit(solution)/shard_map/ppermute | solution.py:357
  23.5 1.9 %collective-permute-start.8 = (bf16[64,2176]{1,0:T(8,128)(2,1)S(1)}, bf16[64,2176]{1,0:T(8,128)(2,1)S(1)}, u32[]{:S(2)}, u32[]{:S(2)}) collective-permute-start(bf16[64,2176]{1,0:T(8,128)(2,1)S(1)} %get-tuple-element.92.refs_4_), channel_id=1, source_target_pairs={{0,1},{1,0},{2,3},{3,2},{4,5},{5,4},{6,7},{7,6},{8,9},{9,8},{10,11... | collective-permute-start | bytes 835592 | tf_op jit(solution)/shard_map/ppermute | solution.py:357
  23.9 22.5 %collective-permute-start.7 = (bf16[128,2176]{1,0:T(8,128)(2,1)S(1)}, bf16[128,2176]{1,0:T(8,128)(2,1)S(1)}, u32[]{:S(2)}, u32[]{:S(2)}) collective-permute-start(bf16[128,2176]{1,0:T(8,128)(2,1)S(1)} %get-tuple-element.91.refs_1_), channel_id=1, source_target_pairs={{0,4},{1,5},{2,6},{3,7},{4,8},{5,9},{6,10},{7,11},{8,12},{9,13},{1... | collective-permute-start | bytes 1671176 | tf_op jit(solution)/shard_map/ppermute | solution.py:350
  26.3 20.2 %collective-permute-start.13 = (bf16[96,2176]{1,0:T(8,128)(2,1)S(1)}, bf16[96,2176]{1,0:T(8,128)(2,1)S(1)}, u32[]{:S(2)}, u32[]{:S(2)}) collective-permute-start(bf16[96,2176]{1,0:T(8,128)(2,1)S(1)} %get-tuple-element.99), channel_id=1, source_target_pairs={{0,2},{1,3},{2,0},{3,1},{4,6},{5,7},{6,4},{7,5},{8,10},{9,11},{10,... | collective-permute-start | bytes 1253384 | tf_op jit(solution)/shard_map/ppermute | solution.py:353
  34.6 1.6 %collective-permute-start.12 = (bf16[64,2048]{1,0:T(8,128)(2,1)S(1)}, bf16[64,2048]{1,0:T(8,128)(2,1)S(1)}, u32[]{:S(2)}, u32[]{:S(2)}) collective-permute-start(bf16[64,2048]{1,0:T(8,128)(2,1)S(1)} %get-tuple-element.97), channel_id=1, source_target_pairs={{0,1},{1,0},{2,3},{3,2},{4,5},{5,4},{6,7},{7,6},{8,9},{9,8},{10,11... | collective-permute-start | bytes 786440 | tf_op jit(solution)/shard_map/ppermute | solution.py:357
  34.6 1.9 %collective-permute-start.11 = (bf16[64,2048]{1,0:T(8,128)(2,1)S(1)}, bf16[64,2048]{1,0:T(8,128)(2,1)S(1)}, u32[]{:S(2)}, u32[]{:S(2)}) collective-permute-start(bf16[64,2048]{1,0:T(8,128)(2,1)S(1)} %get-tuple-element.96.refs_4_), channel_id=1, source_target_pairs={{0,1},{1,0},{2,3},{3,2},{4,5},{5,4},{6,7},{7,6},{8,9},{9,8},{10,11... | collective-permute-start | bytes 786440 | tf_op jit(solution)/shard_map/ppermute | solution.py:357
  35.1 22.5 %collective-permute-start.18 = (bf16[128,2048]{1,0:T(8,128)(2,1)S(1)}, bf16[128,2048]{1,0:T(8,128)(2,1)S(1)}, u32[]{:S(2)}, u32[]{:S(2)}) collective-permute-start(bf16[128,2048]{1,0:T(8,128)(2,1)S(1)} %get-tuple-element.95.refs_1_), channel_id=1, source_target_pairs={{0,4},{1,5},{2,6},{3,7},{4,8},{5,9},{6,10},{7,11},{8,12},{9,13},{1... | collective-permute-start | bytes 1572872 | tf_op jit(solution)/shard_map/ppermute | solution.py:350
  36.9 20.8 %collective-permute-start.15 = (bf16[96,2048]{1,0:T(8,128)(2,1)S(1)}, bf16[96,2048]{1,0:T(8,128)(2,1)S(1)}, u32[]{:S(2)}, u32[]{:S(2)}) collective-permute-start(bf16[96,2048]{1,0:T(8,128)(2,1)S(1)} %get-tuple-element.102), channel_id=1, source_target_pairs={{0,2},{1,3},{2,0},{3,1},{4,6},{5,7},{6,4},{7,5},{8,10},{9,11},{10,... | collective-permute-start | bytes 1179656 | tf_op jit(solution)/shard_map/ppermute | solution.py:353
  46.4 15.5 %copy-start.2 = (bf16[1,384,2048]{2,1,0:T(8,128)(2,1)S(1)}, bf16[1,384,2048]{2,1,0:T(8,128)(2,1)}, u32[]{:S(2)}) copy-start(bf16[1,384,2048]{2,1,0:T(8,128)(2,1)} %param.13) | copy-start | bytes 4718596
  46.5 1.6 %collective-permute-start.17 = (bf16[64,2176]{1,0:T(8,128)(2,1)S(1)}, bf16[64,2176]{1,0:T(8,128)(2,1)S(1)}, u32[]{:S(2)}, u32[]{:S(2)}) collective-permute-start(bf16[64,2176]{1,0:T(8,128)(2,1)S(1)} %get-tuple-element.104), channel_id=1, source_target_pairs={{0,1},{1,0},{2,3},{3,2},{4,5},{5,4},{6,7},{7,6},{8,9},{9,8},{10,11... | collective-permute-start | bytes 835592 | tf_op jit(solution)/shard_map/ppermute | solution.py:357
  46.6 1.9 %collective-permute-start.16 = (bf16[64,2176]{1,0:T(8,128)(2,1)S(1)}, bf16[64,2176]{1,0:T(8,128)(2,1)S(1)}, u32[]{:S(2)}, u32[]{:S(2)}) collective-permute-start(bf16[64,2176]{1,0:T(8,128)(2,1)S(1)} %get-tuple-element.103.refs_4_), channel_id=1, source_target_pairs={{0,1},{1,0},{2,3},{3,2},{4,5},{5,4},{6,7},{7,6},{8,9},{9,8},{10,11... | collective-permute-start | bytes 835592 | tf_op jit(solution)/shard_map/ppermute | solution.py:357
  47.1 14.8 %copy-start = (bf16[1,2048,384]{2,1,0:T(8,128)(2,1)S(1)}, bf16[1,2048,384]{2,1,0:T(8,128)(2,1)}, u32[]{:S(2)}) copy-start(bf16[1,2048,384]{2,1,0:T(8,128)(2,1)} %param.11) | copy-start | bytes 4718596
  47.1 14.8 %copy-start.1 = (bf16[1,2048,384]{2,1,0:T(8,128)(2,1)S(1)}, bf16[1,2048,384]{2,1,0:T(8,128)(2,1)}, u32[]{:S(2)}) copy-start(bf16[1,2048,384]{2,1,0:T(8,128)(2,1)} %param.12) | copy-start | bytes 4718596
  47.1 22.5 %collective-permute-start.14 = (bf16[128,2176]{1,0:T(8,128)(2,1)S(1)}, bf16[128,2176]{1,0:T(8,128)(2,1)S(1)}, u32[]{:S(2)}, u32[]{:S(2)}) collective-permute-start(bf16[128,2176]{1,0:T(8,128)(2,1)S(1)} %get-tuple-element.100.refs_1_), channel_id=1, source_target_pairs={{0,4},{1,5},{2,6},{3,7},{4,8},{5,9},{6,10},{7,11},{8,12},{9,13},{1... | collective-permute-start | bytes 1671176 | tf_op jit(solution)/shard_map/ppermute | solution.py:350
  49.5 20.2 %collective-permute-start.21 = (bf16[96,2176]{1,0:T(8,128)(2,1)S(1)}, bf16[96,2176]{1,0:T(8,128)(2,1)S(1)}, u32[]{:S(2)}, u32[]{:S(2)}) collective-permute-start(bf16[96,2176]{1,0:T(8,128)(2,1)S(1)} %get-tuple-element.111), channel_id=1, source_target_pairs={{0,2},{1,3},{2,0},{3,1},{4,6},{5,7},{6,4},{7,5},{8,10},{9,11},{10,... | collective-permute-start | bytes 1253384 | tf_op jit(solution)/shard_map/ppermute | solution.py:353
  57.7 1.6 %collective-permute-start.20 = (bf16[64,2048]{1,0:T(8,128)(2,1)S(1)}, bf16[64,2048]{1,0:T(8,128)(2,1)S(1)}, u32[]{:S(2)}, u32[]{:S(2)}) collective-permute-start(bf16[64,2048]{1,0:T(8,128)(2,1)S(1)} %get-tuple-element.108), channel_id=1, source_target_pairs={{0,1},{1,0},{2,3},{3,2},{4,5},{5,4},{6,7},{7,6},{8,9},{9,8},{10,11... | collective-permute-start | bytes 786440 | tf_op jit(solution)/shard_map/ppermute | solution.py:357
  57.8 1.9 %collective-permute-start.19 = (bf16[64,2048]{1,0:T(8,128)(2,1)S(1)}, bf16[64,2048]{1,0:T(8,128)(2,1)S(1)}, u32[]{:S(2)}, u32[]{:S(2)}) collective-permute-start(bf16[64,2048]{1,0:T(8,128)(2,1)S(1)} %get-tuple-element.107.refs_4_), channel_id=1, source_target_pairs={{0,1},{1,0},{2,3},{3,2},{4,5},{5,4},{6,7},{7,6},{8,9},{9,8},{10,11... | collective-permute-start | bytes 786440 | tf_op jit(solution)/shard_map/ppermute | solution.py:357
  58.3 22.0 %collective-permute-start.25 = (bf16[128,2048]{1,0:T(8,128)(2,1)S(1)}, bf16[128,2048]{1,0:T(8,128)(2,1)S(1)}, u32[]{:S(2)}, u32[]{:S(2)}) collective-permute-start(bf16[128,2048]{1,0:T(8,128)(2,1)S(1)} %get-tuple-element.106.refs_1_), channel_id=1, source_target_pairs={{0,4},{1,5},{2,6},{3,7},{4,8},{5,9},{6,10},{7,11},{8,12},{9,13},{1... | collective-permute-start | bytes 1572872 | tf_op jit(solution)/shard_map/ppermute | solution.py:350
  60.1 20.2 %collective-permute-start.26 = (bf16[96,2048]{1,0:T(8,128)(2,1)S(1)}, bf16[96,2048]{1,0:T(8,128)(2,1)S(1)}, u32[]{:S(2)}, u32[]{:S(2)}) collective-permute-start(bf16[96,2048]{1,0:T(8,128)(2,1)S(1)} %get-tuple-element.118), channel_id=1, source_target_pairs={{0,2},{1,3},{2,0},{3,1},{4,6},{5,7},{6,4},{7,5},{8,10},{9,11},{10,... | collective-permute-start | bytes 1179656 | tf_op jit(solution)/shard_map/ppermute | solution.py:353
  69.7 2.3 %collective-permute-start.23 = (bf16[64,2176]{1,0:T(8,128)(2,1)S(1)}, bf16[64,2176]{1,0:T(8,128)(2,1)S(1)}, u32[]{:S(2)}, u32[]{:S(2)}) collective-permute-start(bf16[64,2176]{1,0:T(8,128)(2,1)S(1)} %get-tuple-element.114), channel_id=1, source_target_pairs={{0,1},{1,0},{2,3},{3,2},{4,5},{5,4},{6,7},{7,6},{8,9},{9,8},{10,11... | collective-permute-start | bytes 835592 | tf_op jit(solution)/shard_map/ppermute | solution.py:357
  69.8 2.3 %collective-permute-start.22 = (bf16[64,2176]{1,0:T(8,128)(2,1)S(1)}, bf16[64,2176]{1,0:T(8,128)(2,1)S(1)}, u32[]{:S(2)}, u32[]{:S(2)}) collective-permute-start(bf16[64,2176]{1,0:T(8,128)(2,1)S(1)} %get-tuple-element.113.refs_4_), channel_id=1, source_target_pairs={{0,1},{1,0},{2,3},{3,2},{4,5},{5,4},{6,7},{7,6},{8,9},{9,8},{10,11... | collective-permute-start | bytes 835592 | tf_op jit(solution)/shard_map/ppermute | solution.py:357
  70.3 15.1 %collective-permute-start.30 = (bf16[96,2176]{1,0:T(8,128)(2,1)S(1)}, bf16[96,2176]{1,0:T(8,128)(2,1)S(1)}, u32[]{:S(2)}, u32[]{:S(2)}) collective-permute-start(bf16[96,2176]{1,0:T(8,128)(2,1)S(1)} %get-tuple-element.110.refs_1_), channel_id=1, source_target_pairs={{0,2},{1,3},{2,0},{3,1},{4,6},{5,7},{6,4},{7,5},{8,10},{9,11},{10,... | collective-permute-start | bytes 1253384 | tf_op jit(solution)/shard_map/ppermute | solution.py:353
  80.4 1.6 %collective-permute-start.28 = (bf16[64,2048]{1,0:T(8,128)(2,1)S(1)}, bf16[64,2048]{1,0:T(8,128)(2,1)S(1)}, u32[]{:S(2)}, u32[]{:S(2)}) collective-permute-start(bf16[64,2048]{1,0:T(8,128)(2,1)S(1)} %get-tuple-element.121), channel_id=1, source_target_pairs={{0,1},{1,0},{2,3},{3,2},{4,5},{5,4},{6,7},{7,6},{8,9},{9,8},{10,11... | collective-permute-start | bytes 786440 | tf_op jit(solution)/shard_map/ppermute | solution.py:357
  80.4 1.9 %collective-permute-start.27 = (bf16[64,2048]{1,0:T(8,128)(2,1)S(1)}, bf16[64,2048]{1,0:T(8,128)(2,1)S(1)}, u32[]{:S(2)}, u32[]{:S(2)}) collective-permute-start(bf16[64,2048]{1,0:T(8,128)(2,1)S(1)} %get-tuple-element.120.refs_4_), channel_id=1, source_target_pairs={{0,1},{1,0},{2,3},{3,2},{4,5},{5,4},{6,7},{7,6},{8,9},{9,8},{10,11... | collective-permute-start | bytes 786440 | tf_op jit(solution)/shard_map/ppermute | solution.py:357
  85.9 4.1 %collective-permute-start.32 = (bf16[64,2176]{1,0:T(8,128)(2,1)S(1)}, bf16[64,2176]{1,0:T(8,128)(2,1)S(1)}, u32[]{:S(2)}, u32[]{:S(2)}) collective-permute-start(bf16[64,2176]{1,0:T(8,128)(2,1)S(1)} %get-tuple-element.129), channel_id=1, source_target_pairs={{0,1},{1,0},{2,3},{3,2},{4,5},{5,4},{6,7},{7,6},{8,9},{9,8},{10,11... | collective-permute-start | bytes 835592 | tf_op jit(solution)/shard_map/ppermute | solution.py:357
  86.1 3.9 %collective-permute-start.31 = (bf16[64,2176]{1,0:T(8,128)(2,1)S(1)}, bf16[64,2176]{1,0:T(8,128)(2,1)S(1)}, u32[]{:S(2)}, u32[]{:S(2)}) collective-permute-start(bf16[64,2176]{1,0:T(8,128)(2,1)S(1)} %get-tuple-element.128.refs_3_), channel_id=1, source_target_pairs={{0,1},{1,0},{2,3},{3,2},{4,5},{5,4},{6,7},{7,6},{8,9},{9,8},{10,11... | collective-permute-start | bytes 835592 | tf_op jit(solution)/shard_map/ppermute | solution.py:357
  86.5 12.5 %collective-permute-start.24 = (bf16[96,2176]{1,0:T(8,128)(2,1)S(1)}, bf16[96,2176]{1,0:T(8,128)(2,1)S(1)}, u32[]{:S(2)}, u32[]{:S(2)}) collective-permute-start(bf16[96,2176]{1,0:T(8,128)(2,1)S(1)} %get-tuple-element.116), channel_id=1, source_target_pairs={{0,2},{1,3},{2,0},{3,1},{4,6},{5,7},{6,4},{7,5},{8,10},{9,11},{10,... | collective-permute-start | bytes 1253384 | tf_op jit(solution)/shard_map/ppermute | solution.py:353
  88.0 32.9 %collective-permute-start.35 = (bf16[96,2176]{1,0:T(8,128)(2,1)S(1)}, bf16[96,2176]{1,0:T(8,128)(2,1)S(1)}, u32[]{:S(2)}, u32[]{:S(2)}) collective-permute-start(bf16[96,2176]{1,0:T(8,128)(2,1)S(1)} %get-tuple-element.126.refs_3_), channel_id=1, source_target_pairs={{0,2},{1,3},{2,0},{3,1},{4,6},{5,7},{6,4},{7,5},{8,10},{9,11},{10,... | collective-permute-start | bytes 1253384 | tf_op jit(solution)/shard_map/ppermute | solution.py:353
  88.5 27.0 %collective-permute-start.29 = (bf16[96,2048]{1,0:T(8,128)(2,1)S(1)}, bf16[96,2048]{1,0:T(8,128)(2,1)S(1)}, u32[]{:S(2)}, u32[]{:S(2)}) collective-permute-start(bf16[96,2048]{1,0:T(8,128)(2,1)S(1)} %get-tuple-element.123), channel_id=1, source_target_pairs={{0,2},{1,3},{2,0},{3,1},{4,6},{5,7},{6,4},{7,5},{8,10},{9,11},{10,... | collective-permute-start | bytes 1179656 | tf_op jit(solution)/shard_map/ppermute | solution.py:353
  90.1 33.3 %collective-permute-start.38 = (bf16[128,2176]{1,0:T(8,128)(2,1)S(1)}, bf16[128,2176]{1,0:T(8,128)(2,1)S(1)}, u32[]{:S(2)}, u32[]{:S(2)}) collective-permute-start(bf16[128,2176]{1,0:T(8,128)(2,1)S(1)} %add.3.refs_8_), channel_id=1, source_target_pairs={{0,4},{1,5},{2,6},{3,7},{4,8},{5,9},{6,10},{7,11},{8,12},{9,13},{1... | collective-permute-start | bytes 1671176 | tf_op jit(solution)/shard_map/ppermute | solution.py:350
  121.3 2.1 %collective-permute-start.37 = (bf16[64,2176]{1,0:T(8,128)(2,1)S(1)}, bf16[64,2176]{1,0:T(8,128)(2,1)S(1)}, u32[]{:S(2)}, u32[]{:S(2)}) collective-permute-start(bf16[64,2176]{1,0:T(8,128)(2,1)S(1)} %get-tuple-element.145), channel_id=1, source_target_pairs={{0,1},{1,0},{2,3},{3,2},{4,5},{5,4},{6,7},{7,6},{8,9},{9,8},{10,11... | collective-permute-start | bytes 835592 | tf_op jit(solution)/shard_map/ppermute | solution.py:357
  121.4 2.0 %collective-permute-start.36 = (bf16[64,2176]{1,0:T(8,128)(2,1)S(1)}, bf16[64,2176]{1,0:T(8,128)(2,1)S(1)}, u32[]{:S(2)}, u32[]{:S(2)}) collective-permute-start(bf16[64,2176]{1,0:T(8,128)(2,1)S(1)} %get-tuple-element.144.refs_4_), channel_id=1, source_target_pairs={{0,1},{1,0},{2,3},{3,2},{4,5},{5,4},{6,7},{7,6},{8,9},{9,8},{10,11... | collective-permute-start | bytes 835592 | tf_op jit(solution)/shard_map/ppermute | solution.py:357
  121.9 11.6 %collective-permute-start.34 = (bf16[96,2176]{1,0:T(8,128)(2,1)S(1)}, bf16[96,2176]{1,0:T(8,128)(2,1)S(1)}, u32[]{:S(2)}, u32[]{:S(2)}) collective-permute-start(bf16[96,2176]{1,0:T(8,128)(2,1)S(1)} %get-tuple-element.130.refs_8_), channel_id=1, source_target_pairs={{0,2},{1,3},{2,0},{3,1},{4,6},{5,7},{6,4},{7,5},{8,10},{9,11},{10,... | collective-permute-start | bytes 1253384 | tf_op jit(solution)/shard_map/ppermute | solution.py:353
  123.6 16.4 %collective-permute-start.41 = (bf16[128,2176]{1,0:T(8,128)(2,1)S(1)}, bf16[128,2176]{1,0:T(8,128)(2,1)S(1)}, u32[]{:S(2)}, u32[]{:S(2)}) collective-permute-start(bf16[128,2176]{1,0:T(8,128)(2,1)S(1)} %add.4.refs_3_), channel_id=1, source_target_pairs={{0,4},{1,5},{2,6},{3,7},{4,8},{5,9},{6,10},{7,11},{8,12},{9,13},{1... | collective-permute-start | bytes 1671176 | tf_op jit(solution)/shard_map/ppermute | solution.py:350
  134.0 2.1 %collective-permute-start.40 = (bf16[64,2176]{1,0:T(8,128)(2,1)S(1)}, bf16[64,2176]{1,0:T(8,128)(2,1)S(1)}, u32[]{:S(2)}, u32[]{:S(2)}) collective-permute-start(bf16[64,2176]{1,0:T(8,128)(2,1)S(1)} %get-tuple-element.148), channel_id=1, source_target_pairs={{0,1},{1,0},{2,3},{3,2},{4,5},{5,4},{6,7},{7,6},{8,9},{9,8},{10,11... | collective-permute-start | bytes 835592 | tf_op jit(solution)/shard_map/ppermute | solution.py:357
  134.1 2.0 %collective-permute-start.39 = (bf16[64,2176]{1,0:T(8,128)(2,1)S(1)}, bf16[64,2176]{1,0:T(8,128)(2,1)S(1)}, u32[]{:S(2)}, u32[]{:S(2)}) collective-permute-start(bf16[64,2176]{1,0:T(8,128)(2,1)S(1)} %get-tuple-element.147.refs_4_), channel_id=1, source_target_pairs={{0,1},{1,0},{2,3},{3,2},{4,5},{5,4},{6,7},{7,6},{8,9},{9,8},{10,11... | collective-permute-start | bytes 835592 | tf_op jit(solution)/shard_map/ppermute | solution.py:357
  134.6 12.7 %collective-permute-start.33 = (bf16[96,2176]{1,0:T(8,128)(2,1)S(1)}, bf16[96,2176]{1,0:T(8,128)(2,1)S(1)}, u32[]{:S(2)}, u32[]{:S(2)}) collective-permute-start(bf16[96,2176]{1,0:T(8,128)(2,1)S(1)} %get-tuple-element.132.refs_3_), channel_id=1, source_target_pairs={{0,2},{1,3},{2,0},{3,1},{4,6},{5,7},{6,4},{7,5},{8,10},{9,11},{10,... | collective-permute-start | bytes 1253384 | tf_op jit(solution)/shard_map/ppermute | solution.py:353
  140.2 15.6 %collective-permute-start.44 = (bf16[128,2176]{1,0:T(8,128)(2,1)S(1)}, bf16[128,2176]{1,0:T(8,128)(2,1)S(1)}, u32[]{:S(2)}, u32[]{:S(2)}) collective-permute-start(bf16[128,2176]{1,0:T(8,128)(2,1)S(1)} %add.5.refs_24_), channel_id=1, source_target_pairs={{0,4},{1,5},{2,6},{3,7},{4,8},{5,9},{6,10},{7,11},{8,12},{9,13},{1... | collective-permute-start | bytes 1671176 | tf_op jit(solution)/shard_map/ppermute | solution.py:350
  149.2 1.6 %collective-permute-start.43 = (bf16[64,2176]{1,0:T(8,128)(2,1)S(1)}, bf16[64,2176]{1,0:T(8,128)(2,1)S(1)}, u32[]{:S(2)}, u32[]{:S(2)}) collective-permute-start(bf16[64,2176]{1,0:T(8,128)(2,1)S(1)} %get-tuple-element.152), channel_id=1, source_target_pairs={{0,1},{1,0},{2,3},{3,2},{4,5},{5,4},{6,7},{7,6},{8,9},{9,8},{10,11... | collective-permute-start | bytes 835592 | tf_op jit(solution)/shard_map/ppermute | solution.py:357
  149.3 1.9 %collective-permute-start.42 = (bf16[64,2176]{1,0:T(8,128)(2,1)S(1)}, bf16[64,2176]{1,0:T(8,128)(2,1)S(1)}, u32[]{:S(2)}, u32[]{:S(2)}) collective-permute-start(bf16[64,2176]{1,0:T(8,128)(2,1)S(1)} %get-tuple-element.151.refs_5_), channel_id=1, source_target_pairs={{0,1},{1,0},{2,3},{3,2},{4,5},{5,4},{6,7},{7,6},{8,9},{9,8},{10,11... | collective-permute-start | bytes 835592 | tf_op jit(solution)/shard_map/ppermute | solution.py:357
  (7 other events, 20.2 us)

commit v3 on v1

v3 whole, which is shorter than its diff:
```python
import functools

import jax
import jax.numpy as jnp
from jax import lax
from jax.experimental import pallas as pl
from jax.experimental.pallas import tpu as pltpu
from jax.sharding import PartitionSpec as P

BF16 = jnp.bfloat16
F32 = jnp.float32
LANES = 128
PLANE = 4


def project(inputs, gate_mat, up_mat):
    gate_pre = jnp.dot(inputs, gate_mat, preferred_element_type=jnp.float32)
    up_pre = jnp.dot(inputs, up_mat, preferred_element_type=jnp.float32)
    return (gate_pre, up_pre)


def backward(inputs, prepared, cotangent, gating, gate_mat, up_mat, down_mat):
    gate_pre, up_pre = prepared
    sigmoid_gate = jax.nn.sigmoid(gate_pre)
    hidden = (gate_pre * sigmoid_gate * up_pre).astype(jnp.bfloat16)
    back_grad = lax.dot_general(
        cotangent, down_mat, (((1,), (1,)), ((), ())), preferred_element_type=jnp.float32
    )
    router_term = jnp.sum(hidden.astype(jnp.float32) * back_grad, axis=1).astype(jnp.bfloat16)
    hidden_grad = gating[:, None] * back_grad
    gate_grad = (
        hidden_grad * up_pre * sigmoid_gate * (1.0 + gate_pre * (1.0 - sigmoid_gate))
    ).astype(jnp.bfloat16)
    up_grad = (hidden_grad * gate_pre * sigmoid_gate).astype(jnp.bfloat16)
    input_term = lax.dot_general(
        gate_grad, gate_mat, (((1,), (1,)), ((), ())), preferred_element_type=jnp.float32
    )
    input_term = input_term + lax.dot_general(
        up_grad, up_mat, (((1,), (1,)), ((), ())), preferred_element_type=jnp.float32
    )
    input_term = input_term.astype(jnp.bfloat16)
    scaled = (gating[:, None] * cotangent.astype(jnp.float32)).astype(jnp.bfloat16)
    down_delta = lax.dot_general(
        hidden, scaled, (((0,), (0,)), ((), ())), preferred_element_type=jnp.float32
    )
    gate_delta = lax.dot_general(
        inputs, gate_grad, (((0,), (0,)), ((), ())), preferred_element_type=jnp.float32
    )
    up_delta = lax.dot_general(
        inputs, up_grad, (((0,), (0,)), ((), ())), preferred_element_type=jnp.float32
    )
    return (input_term, router_term, gate_delta, up_delta, down_delta)


def direct(tokens, cotangent, expert_ids, gate_levels, w_gate, w_up, w_down):
    devices = lax.axis_size("expert")
    tok_rows, fanout = expert_ids.shape
    features = tokens.shape[1]
    capacity = 3 * tok_rows * fanout // (2 * devices)
    slot_rows = devices * capacity
    gate_mat = w_gate[0]
    up_mat = w_up[0]
    down_mat = w_down[0]
    chosen = expert_ids.reshape(-1)
    indicator = (chosen[:, None] == jnp.arange(devices, dtype=jnp.int32)[None, :]).astype(jnp.int32)
    earlier = jnp.cumsum(indicator, axis=0) - indicator
    position = jnp.sum(earlier * indicator, axis=1)
    target = chosen * capacity + position
    gating_local = (gate_levels.reshape(-1).astype(jnp.float32) / 256.0).astype(jnp.bfloat16)
    outbox_x = (
        jnp.zeros((slot_rows, features), jnp.bfloat16)
        .at[target]
        .set(jnp.repeat(tokens, fanout, axis=0))
    )
    outbox_dy = (
        jnp.zeros((slot_rows, features), jnp.bfloat16)
        .at[target]
        .set(jnp.repeat(cotangent, fanout, axis=0))
    )
    outbox_g = jnp.zeros((slot_rows,), jnp.bfloat16).at[target].set(gating_local)
    outbox_x = outbox_x.reshape(devices, capacity, features)
    outbox_dy = outbox_dy.reshape(devices, capacity, features)
    outbox_g = outbox_g.reshape(devices, capacity)
    exchange = functools.partial(
        lax.all_to_all, axis_name="expert", split_axis=0, concat_axis=0, tiled=True
    )
    rows_x = exchange(outbox_x).reshape(slot_rows, features)
    rows_dy = exchange(outbox_dy).reshape(slot_rows, features)
    rows_g = exchange(outbox_g).reshape(-1).astype(jnp.float32)
    prepared = project(rows_x, gate_mat, up_mat)
    input_term, router_term, gate_delta, up_delta, down_delta = backward(
        rows_x, prepared, rows_dy, rows_g, gate_mat, up_mat, down_mat
    )
    back_term = exchange(input_term.reshape(devices, capacity, features))
    back_router = exchange(router_term.reshape(devices, capacity))
    gathered_term = back_term.reshape(slot_rows, features)[target].astype(jnp.float32)
    input_grad = jnp.sum(gathered_term.reshape(tok_rows, fanout, features), axis=1).astype(
        jnp.bfloat16
    )
    router_grad = back_router.reshape(-1)[target].reshape(tok_rows, fanout)
    return (
        input_grad,
        router_grad,
        gate_delta.astype(jnp.bfloat16)[None],
        up_delta.astype(jnp.bfloat16)[None],
        down_delta.astype(jnp.bfloat16)[None],
    )


def dot(a, b, contract=((1,), (0,))):
    return lax.dot_general(a, b, (contract, ((), ())), preferred_element_type=F32)


class Chain:
    def __init__(self):
        self.last = []
        self.pending = []

    def __call__(self, kernel, outs, name, *operands, after=(), scratch=(), smem=0, hbm=0, limit=16):
        vmem = pl.BlockSpec(memory_space=pltpu.VMEM)
        scalar = pl.BlockSpec(memory_space=pltpu.SMEM)
        anywhere = pl.BlockSpec(memory_space=pl.ANY)
        outside = pl.BlockSpec(memory_space=pltpu.HBM)
        unused = [*self.last, *after]
        fixed = len(operands)

        def body(*refs):
            kernel(*refs[:fixed], *refs[fixed + len(unused) :])

        made = pl.pallas_call(
            body,
            out_shape=[jax.ShapeDtypeStruct(shape, kind) for shape, kind in outs],
            in_specs=[scalar] * smem
            + [outside] * hbm
            + [vmem] * (fixed - smem - hbm)
            + [anywhere] * len(unused),
            out_specs=[vmem] * len(outs),
            scratch_shapes=list(scratch),
            name=name,
            compiler_params=pltpu.CompilerParams(vmem_limit_bytes=limit << 20),
            cost_estimate=pl.CostEstimate(flops=1000, bytes_accessed=1000, transcendentals=0),
        )(*operands, *unused)
        self.last = [min(made, key=lambda array: array.size)]
        return made

    def hold(self, *arrays, after=()):
        unused = [*self.last, *self.pending, *after]
        self.pending = []
        anywhere = pl.BlockSpec(memory_space=pl.ANY)
        held = pl.pallas_call(
            lambda *refs: None,
            out_shape=[jax.ShapeDtypeStruct(array.shape, array.dtype) for array in arrays],
            in_specs=[anywhere] * (len(arrays) + len(unused)),
            out_specs=[anywhere] * len(arrays),
            input_output_aliases={i: i for i in range(len(arrays))},
            name="hold",
            compiler_params=pltpu.CompilerParams(vmem_limit_bytes=1 << 20),
            cost_estimate=pl.CostEstimate(flops=1000, bytes_accessed=1000, transcendentals=0),
        )(*arrays, *unused)
        self.last = held[:1]
        return held


def pack_kernel(ids_ref, levels_ref, x_ref, out_ref, ids_here, levels_here, sems):
    fanout, rows = ids_ref.shape
    features = x_ref.shape[1]
    moves = [(ids_ref, ids_here), (levels_ref, levels_here), (x_ref, out_ref.at[:, :features])]
    copies = [
        pltpu.make_async_copy(source, target, sems.at[i])
        for i, (source, target) in enumerate(moves)
    ]
    for copy in copies:
        copy.start()
    for copy in copies[:2]:
        copy.wait()
    expert = lax.broadcasted_iota(jnp.int32, (LANES, rows), 0)
    gates = jnp.zeros((LANES, rows), F32)
    for k in range(fanout):
        value = levels_here[k : k + 1, :].astype(F32) * (1.0 / 256.0)
        gates = gates + jnp.where(ids_here[k : k + 1, :] == expert, value, 0.0)
    out_ref[:, features:] = gates.T.astype(BF16)
    copies[2].wait()


def joined(refs):
    return jnp.concatenate([ref[...] for ref in refs], axis=0)


def slot_kernel(capacity, me_ref, x_ref, pick_ref, scaled_ref, *block_refs):
    rows = x_ref.shape[0]
    features = x_ref.shape[1] - LANES
    expert = lax.broadcasted_iota(jnp.int32, (8, LANES), 1)
    wanted = jnp.bitwise_xor(lax.broadcasted_iota(jnp.int32, (8, LANES), 0), me_ref[0])
    chooser = jnp.where(expert == wanted, 1.0, 0.0).astype(BF16)
    gates = dot(chooser, x_ref[:, features:], ((1,), (1,)))
    routed = jnp.where(gates > 0.0, 1.0, 0.0)
    before = lax.broadcasted_iota(jnp.int32, (rows, rows), 0)
    after = lax.broadcasted_iota(jnp.int32, (rows, rows), 1)
    earlier = jnp.where(before < after, 1.0, 0.0).astype(BF16)
    place = dot(routed.astype(BF16), earlier)
    place = jnp.where(routed > 0.0, place, -1.0)
    slot = lax.broadcasted_iota(jnp.int32, (capacity, rows), 0).astype(F32)
    chosen = [place[i : i + 1, :] == slot for i in range(PLANE)]
    pick = jnp.concatenate([jnp.where(here, 1.0, 0.0) for here in chosen], axis=0).astype(BF16)
    pick_ref[...] = pick
    scaled_ref[...] = jnp.concatenate(
        [jnp.where(here, gates[i : i + 1, :], 0.0) for i, here in enumerate(chosen)], axis=0
    ).astype(BF16)
    picked = dot(pick, x_ref[:, :features]).astype(BF16)
    for i, block_ref in enumerate(block_refs):
        block_ref[...] = picked[capacity * i : capacity * (i + 1), :]


def gather_kernel(capacity, scaled_ref, d_ref, *block_refs):
    picked = dot(scaled_ref[...], d_ref[...]).astype(BF16)
    for i, block_ref in enumerate(block_refs):
        block_ref[...] = picked[capacity * i : capacity * (i + 1), :]


def join_kernel(*refs):
    refs[-1][...] = joined(refs[:-1])


def expert_kernel(me_ref, *refs):
    x_refs, d_refs, (gate_ref, up_ref, down_ref) = refs[:3], refs[3:6], refs[6:9]
    grads_ref, hidden_ref, *term_refs = refs[9:]
    features, units = gate_ref.shape
    x, d = joined(x_refs), joined(d_refs)
    rows = x.shape[0]
    gate_pre = dot(x, gate_ref[...])
    up_pre = dot(x, up_ref[...])
    hidden_grad = dot(d, down_ref[...], ((1,), (1,)))
    sigmoid_gate = jax.nn.sigmoid(gate_pre)
    silu = gate_pre * sigmoid_gate
    hidden = (silu * up_pre).astype(BF16)
    router = jnp.sum(hidden.astype(F32) * hidden_grad, axis=1, keepdims=True)
    gate_grad = hidden_grad * up_pre * sigmoid_gate * (1.0 + gate_pre * (1.0 - sigmoid_gate))
    gate_grad = gate_grad.astype(BF16)
    up_grad = (hidden_grad * silu).astype(BF16)
    grads_ref[:, :units] = gate_grad
    grads_ref[:, units:] = up_grad
    hidden_ref[...] = hidden
    term = dot(gate_grad, gate_ref[...], ((1,), (1,))) + dot(up_grad, up_ref[...], ((1,), (1,)))
    term = term.astype(BF16)
    mine = lax.broadcasted_iota(jnp.int32, (rows, LANES), 1) == me_ref[0]
    router = jnp.where(mine, router, 0.0).astype(BF16)
    count = rows // len(term_refs)
    for i, term_ref in enumerate(term_refs):
        part = slice(count * i, count * (i + 1))
        term_ref[:, :features] = term[part, :]
        term_ref[:, features:] = router[part, :]


def home_kernel(columns, pick_ref, *refs):
    terms = jnp.concatenate([ref[:, columns] for ref in refs[:3]], axis=0)
    total = dot(pick_ref[...], terms, ((0,), (0,)))
    for passed_ref in refs[3:-1]:
        passed = passed_ref[...]
        if passed.shape[1] > terms.shape[1]:
            passed = passed[:, columns]
        total = total + passed.astype(F32)
    refs[-1][...] = total.astype(BF16)


def total_kernel(ids_ref, levels_ref, pick_ref, *refs):
    term_refs, passed_refs, (grad_ref, router_ref) = refs[:3], refs[3:-2], refs[-2:]
    fanout, rows = ids_ref.shape
    features = grad_ref.shape[1]
    passed = jnp.concatenate([ref[...] for ref in passed_refs], axis=1)
    total = dot(pick_ref[...], joined(term_refs), ((0,), (0,))) + passed.astype(F32)
    grad_ref[...] = total[:, :features].astype(BF16)
    router = total[:, features:].T
    expert = lax.broadcasted_iota(jnp.int32, (LANES, rows), 0)
    for k in range(fanout):
        own = jnp.where(ids_ref[k : k + 1, :] == expert, router, 0.0)
        own = jnp.sum(own, axis=0, keepdims=True)
        own = own * (256.0 / levels_ref[k : k + 1, :].astype(F32))
        router_ref[k : k + 1, :] = own.astype(BF16)


def delta_kernel(chunks, *refs):
    x_refs, d_refs = refs[: 3 * chunks], refs[3 * chunks : 6 * chunks]
    grads_refs, hidden_refs = refs[6 * chunks : 7 * chunks], refs[7 * chunks : 8 * chunks]
    gate_ref, up_ref, down_ref, done_ref, x_all, d_all = refs[8 * chunks :]
    done_ref[...] = jnp.zeros_like(done_ref)
    features, units = gate_ref.shape
    start = 0
    for x_ref, d_ref in zip(x_refs, d_refs):
        rows = x_ref.shape[0]
        x_all[start : start + rows, :] = x_ref[...]
        d_all[start : start + rows, :] = d_ref[...]
        start += rows
    grads = jnp.concatenate([ref[...] for ref in grads_refs], axis=0)
    hidden = jnp.concatenate([ref[...] for ref in hidden_refs], axis=0)
    step = 512

    @pl.loop(0, features // step)
    def _(i):
        cols = pl.ds(pl.multiple_of(i * step, step), step)
        both = dot(x_all[:, cols], grads, ((0,), (0,))).astype(BF16)
        gate_ref[cols, :] = both[:, :units]
        up_ref[cols, :] = both[:, units:]
        down_ref[:, cols] = dot(hidden, d_all[:, cols], ((0,), (0,))).astype(BF16)


def staged(tokens, cotangent, expert_ids, gate_levels, w_gate, w_up, w_down):
    devices = lax.axis_size("expert")
    planes = devices // PLANE
    tok_rows, fanout = expert_ids.shape
    features = tokens.shape[1]
    units = w_gate.shape[2]
    capacity = 3 * tok_rows * fanout // (2 * devices)
    wide = features + LANES
    rows = PLANE * capacity
    me = lax.axis_index("expert").reshape(1)
    ids, levels = expert_ids.T, gate_levels.T
    gate_mat, up_mat, down_mat = w_gate[0], w_up[0], w_down[0]
    run = Chain()

    def along(array):
        return lax.ppermute(array, "expert", [(i, (i + PLANE) % devices) for i in range(devices)])

    def across(array):
        return lax.ppermute(array, "expert", [(i, i ^ 2) for i in range(devices)])

    def cores(array):
        return lax.ppermute(array, "expert", [(i, i ^ 1) for i in range(devices)])

    def swap(blocks, pieces):
        own, near, far, diagonal = blocks
        size = -(-capacity // 16 // pieces) * 16
        passing = [cores(diagonal[i : i + size]) for i in range(0, capacity, size)]
        near = cores(near)
        return own, near, far, passing

    def send(own, near, far, passing, wait=True):
        after = run.pending + ([near] if wait else [])
        run.pending = [] if wait else [near]
        (both,) = run(
            join_kernel,
            [((2 * capacity, far.shape[1]), BF16)],
            "join",
            far,
            *passing,
            after=after,
        )
        return [own, near, across(both)]

    def spread(blocks, pieces=1):
        return send(*swap(blocks, pieces), wait=pieces == 1)

    pick, scaled, rows_x, rows_d, grads, hidden, terms = ({} for _ in range(7))

    def slots_x(s, x, pieces=1):
        pick[s], scaled[s], *blocks = run(
            functools.partial(slot_kernel, capacity),
            [((rows, tok_rows), BF16)] * 2 + [((capacity, features), BF16)] * PLANE,
            "slots_x",
            me,
            x,
            smem=1,
        )
        rows_x[s] = spread(blocks, pieces)

    def slots_d(s, d):
        blocks = run(
            functools.partial(gather_kernel, capacity),
            [((capacity, features), BF16)] * PLANE,
            "slots_d",
            scaled[s],
            d,
        )
        rows_d[s] = spread(blocks)

    def expert(s, after=()):
        grads[s], hidden[s], *terms[s] = run(
            expert_kernel,
            [((rows, 2 * units), BF16), ((rows, units), BF16)]
            + [((capacity, wide), BF16)] * PLANE,
            "expert",
            me,
            *rows_x[s],
            *rows_d[s],
            gate_mat,
            up_mat,
            down_mat,
            smem=1,
            limit=30,
            after=after,
        )

    def home(s, columns, *passed):
        return along(
            run(
                functools.partial(home_kernel, columns),
                [((tok_rows, columns.stop - columns.start), BF16)],
                "home",
                pick[s],
                *terms[s],
                *passed,
            )[0]
        )

    (packed,) = run(
        pack_kernel,
        [((tok_rows, wide), BF16)],
        "pack",
        ids,
        levels,
        tokens,
        hbm=3,
        scratch=[pltpu.VMEM(ids.shape, jnp.int32)] * 2 + [pltpu.SemaphoreType.DMA((3,))],
        limit=60,
    )
    x, d = along(packed), along(cotangent)
    slots_x(0, packed, 2)
    slots_d(0, cotangent)
    last = planes - 1
    for s in range(1, planes):
        (here,) = run.hold(x, after=rows_x[s - 1][2:])
        if s < last:
            x = along(here)
        slots_x(s, here, 2 if s == last else 1)
        if s == last:
            expert(s - 1)
        (here,) = run.hold(d, after=rows_d[s - 1][2:])
        if s < last:
            d = along(here)
        slots_d(s, here)
        if s == 1:
            expert(0)
        if s == 2:
            expert(1, after=rows_x[2][2:])
            terms[1] = spread(terms[1], 2)
    passed = home(1, slice(0, wide))
    terms[2] = send(*swap(run.hold(*terms[2], after=rows_x[last][2:]), 2), wait=False)
    swapped = swap(run.hold(*terms[0]), 2)
    run.pending = [swapped[1], *swapped[3]]
    expert(last, after=[passed])
    terms[last] = spread(terms[last], 2)
    terms[0] = send(*swapped)
    cuts = [0, 896, 1664, wide]
    columns = [slice(start, end) for start, end in zip(cuts, cuts[1:])]
    passed = [home(2, part, passed) for part in columns]
    passed = [home(last, part, whole) for whole, part in zip(passed, columns)]
    order = range(planes)
    gate_delta, up_delta, down_delta, _ = run(
        functools.partial(delta_kernel, planes),
        [((features, units), BF16)] * 2 + [((units, features), BF16), ((8, LANES), F32)],
        "deltas",
        *[block for s in order for block in rows_x[s]],
        *[block for s in order for block in rows_d[s]],
        *[grads[s] for s in order],
        *[hidden[s] for s in order],
        scratch=[pltpu.VMEM((planes * rows, features), BF16)] * 2,
        limit=40,
    )
    input_grad, router_grad = run(
        total_kernel,
        [((tok_rows, features), BF16), ((fanout, tok_rows), BF16)],
        "total",
        ids,
        levels,
        pick[0],
        *terms[0],
        *passed,
    )
    return input_grad, router_grad.T, gate_delta[None], up_delta[None], down_delta[None]


def solution(mesh):
    devices = mesh.shape["expert"]
    tokens, experts = P(("groups", "expert"), None), P("expert", None, None)
    deltas = P(("groups", "expert"), None, None)

    def on_device(*arrays):
        tok_rows, fanout = arrays[2].shape
        capacity = 3 * tok_rows * fanout // (2 * devices)
        plan = staged if PLANE * capacity > tok_rows and devices % PLANE == 0 else direct
        return plan(*arrays)

    return jax.shard_map(
        on_device,
        mesh=mesh,
        in_specs=(tokens, tokens, tokens, tokens, experts, experts, experts),
        out_specs=(tokens, tokens, deltas, deltas, deltas),
        check_vma=False,
    )
```

time: 205 us -> 137 us (0.67)
  Pallas kernels: 70.6 us -> 26.5 us
  waiting for transfers between devices: 90.2 us -> 72.2 us
  starting transfers between devices: 38.4 us -> 35.6 us
  local copies, waits for them, and re-layouts: 3.91 us -> 1.21 us
    pallas_call x19 -> x42, Pallas kernels: 70.6 us -> 26.5 us  [the longest x34 26.5 us: __call__(): pl.pallas_call(body, out_shape=[jax.ShapeDtypeStruct(shape, kind) for sha...]
    ppermute x45 -> x55, waiting for transfers between devices: 90.2 us -> 72.2 us  [the longest x13 37.3 us: along(): lax.ppermute(array, 'expert', [(i, (i + PLANE) % devices) for i in range(...]
    unnamed x96 -> x14, local copies, waits for them, and re-layouts: 3.91 us -> 1.11 us
    ppermute x45 -> x55, starting transfers between devices: 38.4 us -> 35.6 us  [the longest x12 18.2 us: across(): return lax.ppermute(array, 'expert', [(i, i ^ 2) for i in range(devices)])]
  transfers between devices with their start and end apart: 45 -> 55, of which waited for: 20 -> 31; matrix products, arithmetic and copies ran while one was open for 0% -> 0% of each run, Pallas kernels for 32% -> 17%
where the time goes in v3:
time: 137 us
  waiting for transfers between devices  72.2 us (53%)
  starting transfers between devices  35.6 us (26%)
  Pallas kernels  26.5 us (19%)
    ppermute x13, waiting for transfers between devices, along(): lax.ppermute(array, 'expert', [(i, (i + PLANE) % devices) for i in range(...  37.3 us
    pallas_call x34, Pallas kernels, __call__(): pl.pallas_call(body, out_shape=[jax.ShapeDtypeStruct(shape, kind) for sha...  26.5 us
    ppermute x12, waiting for transfers between devices, across(): return lax.ppermute(array, 'expert', [(i, i ^ 2) for i in range(devices)])  24.6 us
    ppermute x12, starting transfers between devices, across(): return lax.ppermute(array, 'expert', [(i, i ^ 2) for i in range(devices)])  18.2 us
    ppermute x30, waiting for transfers between devices, cores(): return lax.ppermute(array, 'expert', [(i, i ^ 1) for i in range(devices)])  10.2 us
    ppermute x13, starting transfers between devices, along(): lax.ppermute(array, 'expert', [(i, (i + PLANE) % devices) for i in range(...  9.68 us
    ppermute x30, starting transfers between devices, cores(): return lax.ppermute(array, 'expert', [(i, i ^ 1) for i in range(devices)])  7.8 us
  transfers between devices with their start and end apart: 55, of which 31 were waited for; matrix products, arithmetic and copies ran while one was open for 0% of the time, Pallas kernels for 17%

profile of v3, /device:TPU:0, one launch (start us, length us, event | category | flops | bytes accessed | tf_op | source)
XLA Modules:
  0.0 136.5 jit_solution(12459092798494498503)
XLA Ops:
  0.6 2.0 %pack.1.refs_1_.refs_2_ = bf16[128,2176]{1,0:T(8,128)(2,1)} custom-call(s32[4,128]{1,0:T(4,128)} %bitcast.22, s32[4,128]{1,0:T(4,128)} %bitcast.24, bf16[128,2048]{1,0:T(8,128)(2,1)} %refs_2_.1), custom_call_target="tpu_custom_call" | custom-call | flops 1000 | bytes 1000 | tf_op jit(solution)/shard_map/pack/pallas_call | solution.py:130
  2.6 3.1 %collective-permute-start.7 = (bf16[128,2176]{1,0:T(8,128)(2,1)}, bf16[128,2176]{1,0:T(8,128)(2,1)S(1)}, u32[]{:S(2)}, u32[]{:S(2)}) collective-permute-start(bf16[128,2176]{1,0:T(8,128)(2,1)} %pack.1.refs_1_.refs_2_), channel_id=1, source_target_pairs={{0,4},{1,5},{2,6},{3,7},{4,8},{5,9},{6,10},{7,11},{8,12},{9,13},{1... | collective-permute-start | bytes 1671176 | tf_op jit(solution)/shard_map/ppermute | solution.py:321
  5.7 1.1 copy-done.3
  8.0 0.9 collective-permute-done.2.refs_2_
  8.9 1.6 %collective-permute-start.3 = (bf16[96,2048]{1,0:T(8,128)(2,1)S(1)}, bf16[96,2048]{1,0:T(8,128)(2,1)S(1)}, u32[]{:S(2)}, u32[]{:S(2)}) collective-permute-start(bf16[96,2048]{1,0:T(8,128)(2,1)S(1)} %join.12.refs_2_), channel_id=1, source_target_pairs={{0,2},{1,3},{2,0},{3,1},{4,6},{5,7},{6,4},{7,5},{8,10},{9,11},{10,... | collective-permute-start | bytes 1179656 | tf_op jit(solution)/shard_map/ppermute | solution.py:324
  12.0 1.6 %collective-permute-start.8 = (bf16[128,2048]{1,0:T(8,128)(2,1)S(1)}, bf16[128,2048]{1,0:T(8,128)(2,1)S(1)}, u32[]{:S(2)}, u32[]{:S(2)}) collective-permute-start(bf16[128,2048]{1,0:T(8,128)(2,1)S(1)} %copy-done.4), channel_id=1, source_target_pairs={{0,4},{1,5},{2,6},{3,7},{4,8},{5,9},{6,10},{7,11},{8,12},{9,13},{1... | collective-permute-start | bytes 1572872 | tf_op jit(solution)/shard_map/ppermute | solution.py:321
  14.2 6.8 %collective-permute-done.3.refs_2_.refs_3_ = bf16[96,2048]{1,0:T(8,128)(2,1)S(1)} collective-permute-done((bf16[96,2048]{1,0:T(8,128)(2,1)S(1)}, bf16[96,2048]{1,0:T(8,128)(2,1)S(1)}, u32[]{:S(2)}, u32[]{:S(2)}) %collective-permute-start.3) | collective-permute-done | bytes 393248 | tf_op jit(solution)/shard_map/ppermute | solution.py:324
  22.6 1.1 collective-permute-start.13
  23.8 1.8 %collective-permute-start.14 = (bf16[96,2048]{1,0:T(8,128)(2,1)S(1)}, bf16[96,2048]{1,0:T(8,128)(2,1)S(1)}, u32[]{:S(2)}, u32[]{:S(2)}) collective-permute-start(bf16[96,2048]{1,0:T(8,128)(2,1)S(1)} %join.14.refs_1_), channel_id=1, source_target_pairs={{0,2},{1,3},{2,0},{3,1},{4,6},{5,7},{6,4},{7,5},{8,10},{9,11},{10,... | collective-permute-start | bytes 1179656 | tf_op jit(solution)/shard_map/ppermute | solution.py:324
  25.6 7.0 %collective-permute-done.8.refs_0_ = bf16[128,2048]{1,0:T(8,128)(2,1)S(1)} collective-permute-done((bf16[128,2048]{1,0:T(8,128)(2,1)S(1)}, bf16[128,2048]{1,0:T(8,128)(2,1)S(1)}, u32[]{:S(2)}, u32[]{:S(2)}) %collective-permute-start.8) | collective-permute-done | bytes 524320 | tf_op jit(solution)/shard_map/ppermute | solution.py:321
  33.6 0.9 collective-permute-done.11.refs_1_
  34.8 1.8 %collective-permute-start.19 = (bf16[96,2048]{1,0:T(8,128)(2,1)S(1)}, bf16[96,2048]{1,0:T(8,128)(2,1)S(1)}, u32[]{:S(2)}, u32[]{:S(2)}) collective-permute-start(bf16[96,2048]{1,0:T(8,128)(2,1)S(1)} %join.15.refs_10_), channel_id=1, source_target_pairs={{0,2},{1,3},{2,0},{3,1},{4,6},{5,7},{6,4},{7,5},{8,10},{9,11},{10,... | collective-permute-start | bytes 1179656 | tf_op jit(solution)/shard_map/ppermute | solution.py:324
  36.6 2.6 %expert.4 = (bf16[192,768]{1,0:T(8,128)(2,1)S(1)}, bf16[192,384]{1,0:T(8,128)(2,1)S(1)}, bf16[48,2176]{1,0:T(8,128)(2,1)S(1)}, bf16[48,2176]{1,0:T(8,128)(2,1)S(...) custom-call(s32[1]{0:T(128)} %bitcast.2.refs_0_, bf16[48,2048]{1,0:T(8,128)(2,1)S(1)} %get-tuple-element.84.refs_1_.refs_0_, ...), custom_call_target="tpu_custom_call" | custom-call | flops 1000 | bytes 1000 | tf_op jit(solution)/shard_map/expert/pallas_call | solution.py:130
  39.3 5.3 %collective-permute-done.13.refs_0_ = bf16[128,2176]{1,0:T(8,128)(2,1)S(1)} collective-permute-done((bf16[128,2176]{1,0:T(8,128)(2,1)S(1)}, bf16[128,2176]{1,0:T(8,128)(2,1)S(1)}, u32[]{:S(2)}, u32[]{:S(2)}) %collective-permute-start.13) | collective-permute-done | bytes 557088 | tf_op jit(solution)/shard_map/ppermute | solution.py:321
  45.7 0.9 collective-permute-done.15.refs_3_.refs_2_.refs_7_
  47.0 1.8 %collective-permute-start.17 = (bf16[96,2048]{1,0:T(8,128)(2,1)S(1)}, bf16[96,2048]{1,0:T(8,128)(2,1)S(1)}, u32[]{:S(2)}, u32[]{:S(2)}) collective-permute-start(bf16[96,2048]{1,0:T(8,128)(2,1)S(1)} %join.16.refs_1_), channel_id=1, source_target_pairs={{0,2},{1,3},{2,0},{3,1},{4,6},{5,7},{6,4},{7,5},{8,10},{9,11},{10,... | collective-permute-start | bytes 1179656 | tf_op jit(solution)/shard_map/ppermute | solution.py:324
  48.8 7.0 %collective-permute-done.18.refs_0_ = bf16[128,2048]{1,0:T(8,128)(2,1)S(1)} collective-permute-done((bf16[128,2048]{1,0:T(8,128)(2,1)S(1)}, bf16[128,2048]{1,0:T(8,128)(2,1)S(1)}, u32[]{:S(2)}, u32[]{:S(2)}) %collective-permute-start.18) | collective-permute-done | bytes 524320 | tf_op jit(solution)/shard_map/ppermute | solution.py:321
  56.8 0.9 collective-permute-done.20.refs_3_.refs_5_.refs_19_
  58.3 2.6 %expert.5 = (bf16[192,768]{1,0:T(8,128)(2,1)S(1)}, bf16[192,384]{1,0:T(8,128)(2,1)S(1)}, bf16[48,2176]{1,0:T(8,128)(2,1)S(1)}, bf16[48,2176]{1,0:T(8,128)(2,1)S(...) custom-call(s32[1]{0:T(128)} %bitcast.2.refs_0_, ...), custom_call_target="tpu_custom_call" | custom-call | flops 1000 | bytes 1000 | tf_op jit(solution)/shard_map/expert/pallas_call | solution.py:130
  61.5 1.7 %collective-permute-start.22 = (bf16[96,2048]{1,0:T(8,128)(2,1)S(1)}, bf16[96,2048]{1,0:T(8,128)(2,1)S(1)}, u32[]{:S(2)}, u32[]{:S(2)}) collective-permute-start(bf16[96,2048]{1,0:T(8,128)(2,1)S(1)} %join.17.refs_10_), channel_id=1, source_target_pairs={{0,2},{1,3},{2,0},{3,1},{4,6},{5,7},{6,4},{7,5},{8,10},{9,11},{10,... | collective-permute-start | bytes 1179656 | tf_op jit(solution)/shard_map/ppermute | solution.py:324
  63.4 1.3 collective-permute-done.24.refs_1_
  64.8 0.7 collective-permute-start.29
  65.5 2.2 %collective-permute-done.23.refs_0_ = bf16[128,2176]{1,0:T(8,128)(2,1)S(1)} collective-permute-done((bf16[128,2176]{1,0:T(8,128)(2,1)S(1)}, bf16[128,2176]{1,0:T(8,128)(2,1)S(1)}, u32[]{:S(2)}, u32[]{:S(2)}) %collective-permute-start.23) | collective-permute-done | bytes 557088 | tf_op jit(solution)/shard_map/ppermute | solution.py:321
  68.9 0.7 collective-permute-done.28.refs_2_
  69.8 1.2 collective-permute-done.27.refs_1_
  71.0 2.5 %collective-permute-done.22.refs_6_.refs_3_.refs_20_ = bf16[96,2048]{1,0:T(8,128)(2,1)S(1)} collective-permute-done((bf16[96,2048]{1,0:T(8,128)(2,1)S(1)}, bf16[96,2048]{1,0:T(8,128)(2,1)S(1)}, u32[]{:S(2)}, u32[]{:S(2)}) %collective-permute-start.22) | collective-permute-done | bytes 393248 | tf_op jit(solution)/shard_map/ppermute | solution.py:324
  73.5 2.6 %expert.6 = (bf16[192,768]{1,0:T(8,128)(2,1)S(1)}, bf16[192,384]{1,0:T(8,128)(2,1)S(1)}, bf16[48,2176]{1,0:T(8,128)(2,1)S(1)}, bf16[48,2176]{1,0:T(8,128)(2,1)S(...) custom-call(s32[1]{0:T(128)} %bitcast.2.refs_0_, ...), custom_call_target="tpu_custom_call" | custom-call | flops 1000 | bytes 1000 | tf_op jit(solution)/shard_map/expert/pallas_call | solution.py:130
  76.1 2.0 %collective-permute-done.30.refs_0_ = bf16[128,2048]{1,0:T(8,128)(2,1)S(1)} collective-permute-done((bf16[128,2048]{1,0:T(8,128)(2,1)S(1)}, bf16[128,2048]{1,0:T(8,128)(2,1)S(1)}, u32[]{:S(2)}, u32[]{:S(2)}) %collective-permute-start.30) | collective-permute-done | bytes 524320 | tf_op jit(solution)/shard_map/ppermute | solution.py:321
  79.1 1.5 %collective-permute-start.34 = (bf16[96,2048]{1,0:T(8,128)(2,1)S(1)}, bf16[96,2048]{1,0:T(8,128)(2,1)S(1)}, u32[]{:S(2)}, u32[]{:S(2)}) collective-permute-start(bf16[96,2048]{1,0:T(8,128)(2,1)S(1)} %join.19.refs_10_), channel_id=1, source_target_pairs={{0,2},{1,3},{2,0},{3,1},{4,6},{5,7},{6,4},{7,5},{8,10},{9,11},{10,... | collective-permute-start | bytes 1179656 | tf_op jit(solution)/shard_map/ppermute | solution.py:324
  80.6 1.0 collective-permute-done.29.refs_3_
  82.2 1.6 %collective-permute-start.41 = (bf16[96,2048]{1,0:T(8,128)(2,1)S(1)}, bf16[96,2048]{1,0:T(8,128)(2,1)S(1)}, u32[]{:S(2)}, u32[]{:S(2)}) collective-permute-start(bf16[96,2048]{1,0:T(8,128)(2,1)S(1)} %join.20.refs_4_), channel_id=1, source_target_pairs={{0,2},{1,3},{2,0},{3,1},{4,6},{5,7},{6,4},{7,5},{8,10},{9,11},{10,... | collective-permute-start | bytes 1179656 | tf_op jit(solution)/shard_map/ppermute | solution.py:324
  83.8 7.2 %collective-permute-done.34.refs_5_.refs_3_.refs_11_ = bf16[96,2048]{1,0:T(8,128)(2,1)S(1)} collective-permute-done((bf16[96,2048]{1,0:T(8,128)(2,1)S(1)}, bf16[96,2048]{1,0:T(8,128)(2,1)S(1)}, u32[]{:S(2)}, u32[]{:S(2)}) %collective-permute-start.34) | collective-permute-done | bytes 393248 | tf_op jit(solution)/shard_map/ppermute | solution.py:324
  91.7 1.2 collective-permute-done.36.refs_2_
  92.9 1.6 %collective-permute-start.48 = (bf16[96,2176]{1,0:T(8,128)(2,1)S(1)}, bf16[96,2176]{1,0:T(8,128)(2,1)S(1)}, u32[]{:S(2)}, u32[]{:S(2)}) collective-permute-start(bf16[96,2176]{1,0:T(8,128)(2,1)S(1)} %join.21.refs_4_), channel_id=1, source_target_pairs={{0,2},{1,3},{2,0},{3,1},{4,6},{5,7},{6,4},{7,5},{8,10},{9,11},{10,... | collective-permute-start | bytes 1253384 | tf_op jit(solution)/shard_map/ppermute | solution.py:324
  95.1 4.3 %collective-permute-done.41.refs_6_.refs_23_ = bf16[96,2048]{1,0:T(8,128)(2,1)S(1)} collective-permute-done((bf16[96,2048]{1,0:T(8,128)(2,1)S(1)}, bf16[96,2048]{1,0:T(8,128)(2,1)S(1)}, u32[]{:S(2)}, u32[]{:S(2)}) %collective-permute-start.41) | collective-permute-done | bytes 393248 | tf_op jit(solution)/shard_map/ppermute | solution.py:324
  99.5 2.6 %expert.7 = (bf16[192,768]{1,0:T(8,128)(2,1)S(1)}, bf16[192,384]{1,0:T(8,128)(2,1)S(1)}, bf16[48,2176]{1,0:T(8,128)(2,1)S(1)}, bf16[48,2176]{1,0:T(8,128)(2,1)S(...) custom-call(s32[1]{0:T(128)} %bitcast.2.refs_0_, ...), custom_call_target="tpu_custom_call" | custom-call | flops 1000 | bytes 1000 | tf_op jit(solution)/shard_map/expert/pallas_call | solution.py:130
  103.3 0.7 collective-permute-done.44.refs_2_
  104.1 1.6 %collective-permute-start.47 = (bf16[96,2176]{1,0:T(8,128)(2,1)S(1)}, bf16[96,2176]{1,0:T(8,128)(2,1)S(1)}, u32[]{:S(2)}, u32[]{:S(2)}) collective-permute-start(bf16[96,2176]{1,0:T(8,128)(2,1)S(1)} %join.22.refs_3_), channel_id=1, source_target_pairs={{0,2},{1,3},{2,0},{3,1},{4,6},{5,7},{6,4},{7,5},{8,10},{9,11},{10,... | collective-permute-start | bytes 1253384 | tf_op jit(solution)/shard_map/ppermute | solution.py:324
  105.7 2.5 %collective-permute-done.48.refs_3_ = bf16[96,2176]{1,0:T(8,128)(2,1)S(1)} collective-permute-done((bf16[96,2176]{1,0:T(8,128)(2,1)S(1)}, bf16[96,2176]{1,0:T(8,128)(2,1)S(1)}, u32[]{:S(2)}, u32[]{:S(2)}) %collective-permute-start.48) | collective-permute-done | bytes 417824 | tf_op jit(solution)/shard_map/ppermute | solution.py:324
  108.5 1.7 %collective-permute-start.46 = (bf16[96,2176]{1,0:T(8,128)(2,1)S(1)}, bf16[96,2176]{1,0:T(8,128)(2,1)S(1)}, u32[]{:S(2)}, u32[]{:S(2)}) collective-permute-start(bf16[96,2176]{1,0:T(8,128)(2,1)S(1)} %join.23.refs_5_), channel_id=1, source_target_pairs={{0,2},{1,3},{2,0},{3,1},{4,6},{5,7},{6,4},{7,5},{8,10},{9,11},{10,... | collective-permute-start | bytes 1253384 | tf_op jit(solution)/shard_map/ppermute | solution.py:324
  110.4 1.4 %collective-permute-start.51 = (bf16[128,768]{1,0:T(8,128)(2,1)S(1)}, bf16[128,768]{1,0:T(8,128)(2,1)S(1)}, u32[]{:S(2)}, u32[]{:S(2)}) collective-permute-start(bf16[128,768]{1,0:T(8,128)(2,1)S(1)} %home.9.refs_5_), channel_id=1, source_target_pairs={{0,4},{1,5},{2,6},{3,7},{4,8},{5,9},{6,10},{7,11},{8,12},{9,13},{1... | collective-permute-start | bytes 589832 | tf_op jit(solution)/shard_map/ppermute | solution.py:321
  112.0 2.0 %collective-permute-start.53 = (bf16[128,512]{1,0:T(8,128)(2,1)S(1)}, bf16[128,512]{1,0:T(8,128)(2,1)S(1)}, u32[]{:S(2)}, u32[]{:S(2)}) collective-permute-start(bf16[128,512]{1,0:T(8,128)(2,1)S(1)} %home.10.refs_5_), channel_id=1, source_target_pairs={{0,4},{1,5},{2,6},{3,7},{4,8},{5,9},{6,10},{7,11},{8,12},{9,13},{1... | collective-permute-start | bytes 393224 | tf_op jit(solution)/shard_map/ppermute | solution.py:321
  114.0 4.8 %collective-permute-done.49.refs_4_ = bf16[128,896]{1,0:T(8,128)(2,1)S(1)} collective-permute-done((bf16[128,896]{1,0:T(8,128)(2,1)S(1)}, bf16[128,896]{1,0:T(8,128)(2,1)S(1)}, u32[]{:S(2)}, u32[]{:S(2)}) %collective-permute-start.49) | collective-permute-done | bytes 229408 | tf_op jit(solution)/shard_map/ppermute | solution.py:321
  119.2 3.9 %collective-permute-done.51.refs_4_ = bf16[128,768]{1,0:T(8,128)(2,1)S(1)} collective-permute-done((bf16[128,768]{1,0:T(8,128)(2,1)S(1)}, bf16[128,768]{1,0:T(8,128)(2,1)S(1)}, u32[]{:S(2)}, u32[]{:S(2)}) %collective-permute-start.51) | collective-permute-done | bytes 196640 | tf_op jit(solution)/shard_map/ppermute | solution.py:321
  123.3 2.5 %collective-permute-done.53.refs_4_ = bf16[128,512]{1,0:T(8,128)(2,1)S(1)} collective-permute-done((bf16[128,512]{1,0:T(8,128)(2,1)S(1)}, bf16[128,512]{1,0:T(8,128)(2,1)S(1)}, u32[]{:S(2)}, u32[]{:S(2)}) %collective-permute-start.53) | collective-permute-done | bytes 131104 | tf_op jit(solution)/shard_map/ppermute | solution.py:321
  126.2 7.0 %deltas.1 = (bf16[2048,384]{1,0:T(8,128)(2,1)}, bf16[2048,384]{1,0:T(8,128)(2,1)}, bf16[384,2048]{1,0:T(8,128)(2,1)}, f32[8,128]{1,0:T(8,128)S(1)}) custom-call(bf16[48,2048]{1,0:T(8,128)(2,1)S(1)} %get-tuple-element.84.refs_1_.refs_0_, bf16[48,2048]{1,0:T(8,128)(2,1)S(1)} %collective-permute-done.refs_3_.refs_2_.refs_1_, ...), custom_call_target="tpu_custom_call" | custom-call | flops 1000 | bytes 1000 | tf_op jit(solution)/shard_map/deltas/pallas_call | solution.py:130
  133.2 2.2 %collective-permute-done.54.refs_8_ = bf16[128,512]{1,0:T(8,128)(2,1)S(1)} collective-permute-done((bf16[128,512]{1,0:T(8,128)(2,1)S(1)}, bf16[128,512]{1,0:T(8,128)(2,1)S(1)}, u32[]{:S(2)}, u32[]{:S(2)}) %collective-permute-start.54) | collective-permute-done | bytes 131104 | tf_op jit(solution)/shard_map/ppermute | solution.py:321
  135.4 1.2 total.1
  (130 shorter events, 17.1 us)
Async XLA Ops:
  2.6 18.8 %collective-permute-start.7 = (bf16[128,2176]{1,0:T(8,128)(2,1)}, bf16[128,2176]{1,0:T(8,128)(2,1)S(1)}, u32[]{:S(2)}, u32[]{:S(2)}) collective-permute-start(bf16[128,2176]{1,0:T(8,128)(2,1)} %pack.1.refs_1_.refs_2_), channel_id=1, source_target_pairs={{0,4},{1,5},{2,6},{3,7},{4,8},{5,9},{6,10},{7,11},{8,12},{9,13},{1... | collective-permute-start | bytes 1671176 | tf_op jit(solution)/shard_map/ppermute | solution.py:321
  7.4 1.5 %collective-permute-start.1 = (bf16[32,2048]{1,0:T(8,128)(2,1)S(1)}, bf16[32,2048]{1,0:T(8,128)(2,1)S(1)}, u32[]{:S(2)}, u32[]{:S(2)}) collective-permute-start(bf16[32,2048]{1,0:T(8,128)(2,1)S(1)} %slice.36), channel_id=1, source_target_pairs={{0,1},{1,0},{2,3},{3,2},{4,5},{5,4},{6,7},{7,6},{8,9},{9,8},{10,11... | collective-permute-start | bytes 393224 | tf_op jit(solution)/shard_map/ppermute | solution.py:327
  8.9 12.0 %collective-permute-start.3 = (bf16[96,2048]{1,0:T(8,128)(2,1)S(1)}, bf16[96,2048]{1,0:T(8,128)(2,1)S(1)}, u32[]{:S(2)}, u32[]{:S(2)}) collective-permute-start(bf16[96,2048]{1,0:T(8,128)(2,1)S(1)} %join.12.refs_2_), channel_id=1, source_target_pairs={{0,2},{1,3},{2,0},{3,1},{4,6},{5,7},{6,4},{7,5},{8,10},{9,11},{10,... | collective-permute-start | bytes 1179656 | tf_op jit(solution)/shard_map/ppermute | solution.py:324
  10.9 2.6 %collective-permute-start.4 = (bf16[48,2048]{1,0:T(8,128)(2,1)S(1)}, bf16[48,2048]{1,0:T(8,128)(2,1)S(1)}, u32[]{:S(2)}, u32[]{:S(2)}) collective-permute-start(bf16[48,2048]{1,0:T(8,128)(2,1)S(1)} %get-tuple-element.90), channel_id=1, source_target_pairs={{0,1},{1,0},{2,3},{3,2},{4,5},{5,4},{6,7},{7,6},{8,9},{9,8},{10,11... | collective-permute-start | bytes 589832 | tf_op jit(solution)/shard_map/ppermute | solution.py:327
  11.5 2.1 %collective-permute-start.5 = (bf16[48,2048]{1,0:T(8,128)(2,1)S(1)}, bf16[48,2048]{1,0:T(8,128)(2,1)S(1)}, u32[]{:S(2)}, u32[]{:S(2)}) collective-permute-start(bf16[48,2048]{1,0:T(8,128)(2,1)S(1)} %get-tuple-element.92), channel_id=1, source_target_pairs={{0,1},{1,0},{2,3},{3,2},{4,5},{5,4},{6,7},{7,6},{8,9},{9,8},{10,11... | collective-permute-start | bytes 589832 | tf_op jit(solution)/shard_map/ppermute | solution.py:327
  12.0 20.6 %collective-permute-start.8 = (bf16[128,2048]{1,0:T(8,128)(2,1)S(1)}, bf16[128,2048]{1,0:T(8,128)(2,1)S(1)}, u32[]{:S(2)}, u32[]{:S(2)}) collective-permute-start(bf16[128,2048]{1,0:T(8,128)(2,1)S(1)} %copy-done.4), channel_id=1, source_target_pairs={{0,4},{1,5},{2,6},{3,7},{4,8},{5,9},{6,10},{7,11},{8,12},{9,13},{1... | collective-permute-start | bytes 1572872 | tf_op jit(solution)/shard_map/ppermute | solution.py:321
  13.6 19.0 %collective-permute-start.6 = (bf16[96,2048]{1,0:T(8,128)(2,1)S(1)}, bf16[96,2048]{1,0:T(8,128)(2,1)S(1)}, u32[]{:S(2)}, u32[]{:S(2)}) collective-permute-start(bf16[96,2048]{1,0:T(8,128)(2,1)S(1)} %join.13.refs_1_), channel_id=1, source_target_pairs={{0,2},{1,3},{2,0},{3,1},{4,6},{5,7},{6,4},{7,5},{8,10},{9,11},{10,... | collective-permute-start | bytes 1179656 | tf_op jit(solution)/shard_map/ppermute | solution.py:324
  22.0 1.7 %collective-permute-start.9 = (bf16[48,2048]{1,0:T(8,128)(2,1)S(1)}, bf16[48,2048]{1,0:T(8,128)(2,1)S(1)}, u32[]{:S(2)}, u32[]{:S(2)}) collective-permute-start(bf16[48,2048]{1,0:T(8,128)(2,1)S(1)} %get-tuple-element.95), channel_id=1, source_target_pairs={{0,1},{1,0},{2,3},{3,2},{4,5},{5,4},{6,7},{7,6},{8,9},{9,8},{10,11... | collective-permute-start | bytes 589832 | tf_op jit(solution)/shard_map/ppermute | solution.py:327
  22.1 1.7 %collective-permute-start.10 = (bf16[48,2048]{1,0:T(8,128)(2,1)S(1)}, bf16[48,2048]{1,0:T(8,128)(2,1)S(1)}, u32[]{:S(2)}, u32[]{:S(2)}) collective-permute-start(bf16[48,2048]{1,0:T(8,128)(2,1)S(1)} %get-tuple-element.97), channel_id=1, source_target_pairs={{0,1},{1,0},{2,3},{3,2},{4,5},{5,4},{6,7},{7,6},{8,9},{9,8},{10,11... | collective-permute-start | bytes 589832 | tf_op jit(solution)/shard_map/ppermute | solution.py:327
  22.6 22.0 %collective-permute-start.13 = (bf16[128,2176]{1,0:T(8,128)(2,1)S(1)}, bf16[128,2176]{1,0:T(8,128)(2,1)S(1)}, u32[]{:S(2)}, u32[]{:S(2)}) collective-permute-start(bf16[128,2176]{1,0:T(8,128)(2,1)S(1)} %hold.8.refs_1_.refs_2_), channel_id=1, source_target_pairs={{0,4},{1,5},{2,6},{3,7},{4,8},{5,9},{6,10},{7,11},{8,12},{9,13},{1... | collective-permute-start | bytes 1671176 | tf_op jit(solution)/shard_map/ppermute | solution.py:321
  23.8 20.7 %collective-permute-start.14 = (bf16[96,2048]{1,0:T(8,128)(2,1)S(1)}, bf16[96,2048]{1,0:T(8,128)(2,1)S(1)}, u32[]{:S(2)}, u32[]{:S(2)}) collective-permute-start(bf16[96,2048]{1,0:T(8,128)(2,1)S(1)} %join.14.refs_1_), channel_id=1, source_target_pairs={{0,2},{1,3},{2,0},{3,1},{4,6},{5,7},{6,4},{7,5},{8,10},{9,11},{10,... | collective-permute-start | bytes 1179656 | tf_op jit(solution)/shard_map/ppermute | solution.py:324
  33.0 1.5 %collective-permute-start.11 = (bf16[48,2048]{1,0:T(8,128)(2,1)S(1)}, bf16[48,2048]{1,0:T(8,128)(2,1)S(1)}, u32[]{:S(2)}, u32[]{:S(2)}) collective-permute-start(bf16[48,2048]{1,0:T(8,128)(2,1)S(1)} %get-tuple-element.99), channel_id=1, source_target_pairs={{0,1},{1,0},{2,3},{3,2},{4,5},{5,4},{6,7},{7,6},{8,9},{9,8},{10,11... | collective-permute-start | bytes 589832 | tf_op jit(solution)/shard_map/ppermute | solution.py:327
  33.1 1.7 %collective-permute-start.12 = (bf16[48,2048]{1,0:T(8,128)(2,1)S(1)}, bf16[48,2048]{1,0:T(8,128)(2,1)S(1)}, u32[]{:S(2)}, u32[]{:S(2)}) collective-permute-start(bf16[48,2048]{1,0:T(8,128)(2,1)S(1)} %get-tuple-element.101), channel_id=1, source_target_pairs={{0,1},{1,0},{2,3},{3,2},{4,5},{5,4},{6,7},{7,6},{8,9},{9,8},{10,11... | collective-permute-start | bytes 589832 | tf_op jit(solution)/shard_map/ppermute | solution.py:327
  33.6 22.2 %collective-permute-start.18 = (bf16[128,2048]{1,0:T(8,128)(2,1)S(1)}, bf16[128,2048]{1,0:T(8,128)(2,1)S(1)}, u32[]{:S(2)}, u32[]{:S(2)}) collective-permute-start(bf16[128,2048]{1,0:T(8,128)(2,1)S(1)} %hold.9.refs_1_.refs_2_), channel_id=1, source_target_pairs={{0,4},{1,5},{2,6},{3,7},{4,8},{5,9},{6,10},{7,11},{8,12},{9,13},{1... | collective-permute-start | bytes 1572872 | tf_op jit(solution)/shard_map/ppermute | solution.py:321
  34.8 21.0 %collective-permute-start.19 = (bf16[96,2048]{1,0:T(8,128)(2,1)S(1)}, bf16[96,2048]{1,0:T(8,128)(2,1)S(1)}, u32[]{:S(2)}, u32[]{:S(2)}) collective-permute-start(bf16[96,2048]{1,0:T(8,128)(2,1)S(1)} %join.15.refs_10_), channel_id=1, source_target_pairs={{0,2},{1,3},{2,0},{3,1},{4,6},{5,7},{6,4},{7,5},{8,10},{9,11},{10,... | collective-permute-start | bytes 1179656 | tf_op jit(solution)/shard_map/ppermute | solution.py:324
  45.2 1.5 %collective-permute-start.15 = (bf16[48,2048]{1,0:T(8,128)(2,1)S(1)}, bf16[48,2048]{1,0:T(8,128)(2,1)S(1)}, u32[]{:S(2)}, u32[]{:S(2)}) collective-permute-start(bf16[48,2048]{1,0:T(8,128)(2,1)S(1)} %get-tuple-element.108), channel_id=1, source_target_pairs={{0,1},{1,0},{2,3},{3,2},{4,5},{5,4},{6,7},{7,6},{8,9},{9,8},{10,11... | collective-permute-start | bytes 589832 | tf_op jit(solution)/shard_map/ppermute | solution.py:327
  45.2 1.7 %collective-permute-start.16 = (bf16[48,2048]{1,0:T(8,128)(2,1)S(1)}, bf16[48,2048]{1,0:T(8,128)(2,1)S(1)}, u32[]{:S(2)}, u32[]{:S(2)}) collective-permute-start(bf16[48,2048]{1,0:T(8,128)(2,1)S(1)} %get-tuple-element.110), channel_id=1, source_target_pairs={{0,1},{1,0},{2,3},{3,2},{4,5},{5,4},{6,7},{7,6},{8,9},{9,8},{10,11... | collective-permute-start | bytes 589832 | tf_op jit(solution)/shard_map/ppermute | solution.py:327
  47.0 11.3 %collective-permute-start.17 = (bf16[96,2048]{1,0:T(8,128)(2,1)S(1)}, bf16[96,2048]{1,0:T(8,128)(2,1)S(1)}, u32[]{:S(2)}, u32[]{:S(2)}) collective-permute-start(bf16[96,2048]{1,0:T(8,128)(2,1)S(1)} %join.16.refs_1_), channel_id=1, source_target_pairs={{0,2},{1,3},{2,0},{3,1},{4,6},{5,7},{6,4},{7,5},{8,10},{9,11},{10,... | collective-permute-start | bytes 1179656 | tf_op jit(solution)/shard_map/ppermute | solution.py:324
  48.8 18.9 %collective-permute-start.23 = (bf16[128,2176]{1,0:T(8,128)(2,1)S(1)}, bf16[128,2176]{1,0:T(8,128)(2,1)S(1)}, u32[]{:S(2)}, u32[]{:S(2)}) collective-permute-start(bf16[128,2176]{1,0:T(8,128)(2,1)S(1)} %hold.10.refs_1_.refs_2_), channel_id=1, source_target_pairs={{0,4},{1,5},{2,6},{3,7},{4,8},{5,9},{6,10},{7,11},{8,12},{9,13},{1... | collective-permute-start | bytes 1671176 | tf_op jit(solution)/shard_map/ppermute | solution.py:321
  56.2 1.5 %collective-permute-start.20 = (bf16[48,2048]{1,0:T(8,128)(2,1)S(1)}, bf16[48,2048]{1,0:T(8,128)(2,1)S(1)}, u32[]{:S(2)}, u32[]{:S(2)}) collective-permute-start(bf16[48,2048]{1,0:T(8,128)(2,1)S(1)} %get-tuple-element.114), channel_id=1, source_target_pairs={{0,1},{1,0},{2,3},{3,2},{4,5},{5,4},{6,7},{7,6},{8,9},{9,8},{10,11... | collective-permute-start | bytes 589832 | tf_op jit(solution)/shard_map/ppermute | solution.py:327
  56.2 1.7 %collective-permute-start.21 = (bf16[48,2048]{1,0:T(8,128)(2,1)S(1)}, bf16[48,2048]{1,0:T(8,128)(2,1)S(1)}, u32[]{:S(2)}, u32[]{:S(2)}) collective-permute-start(bf16[48,2048]{1,0:T(8,128)(2,1)S(1)} %get-tuple-element.116), channel_id=1, source_target_pairs={{0,1},{1,0},{2,3},{3,2},{4,5},{5,4},{6,7},{7,6},{8,9},{9,8},{10,11... | collective-permute-start | bytes 589832 | tf_op jit(solution)/shard_map/ppermute | solution.py:327
  56.7 21.4 %collective-permute-start.30 = (bf16[128,2048]{1,0:T(8,128)(2,1)S(1)}, bf16[128,2048]{1,0:T(8,128)(2,1)S(1)}, u32[]{:S(2)}, u32[]{:S(2)}) collective-permute-start(bf16[128,2048]{1,0:T(8,128)(2,1)S(1)} %hold.11.refs_1_.refs_2_), channel_id=1, source_target_pairs={{0,4},{1,5},{2,6},{3,7},{4,8},{5,9},{6,10},{7,11},{8,12},{9,13},{1... | collective-permute-start | bytes 1572872 | tf_op jit(solution)/shard_map/ppermute | solution.py:321
  61.0 2.3 %collective-permute-start.25 = (bf16[16,2176]{1,0:T(8,128)(2,1)S(1)}, bf16[16,2176]{1,0:T(8,128)(2,1)S(1)}, u32[]{:S(2)}, u32[]{:S(2)}) collective-permute-start(bf16[16,2176]{1,0:T(8,128)(2,1)S(1)} %slice.39), channel_id=1, source_target_pairs={{0,1},{1,0},{2,3},{3,2},{4,5},{5,4},{6,7},{7,6},{8,9},{9,8},{10,11... | collective-permute-start | bytes 208904 | tf_op jit(solution)/shard_map/ppermute | solution.py:327
  61.0 6.7 %collective-permute-start.26 = (bf16[48,2176]{1,0:T(8,128)(2,1)S(1)}, bf16[48,2176]{1,0:T(8,128)(2,1)S(1)}, u32[]{:S(2)}, u32[]{:S(2)}) collective-permute-start(bf16[48,2176]{1,0:T(8,128)(2,1)S(1)} %get-tuple-element.121), channel_id=1, source_target_pairs={{0,1},{1,0},{2,3},{3,2},{4,5},{5,4},{6,7},{7,6},{8,9},{9,8},{10,11... | collective-permute-start | bytes 626696 | tf_op jit(solution)/shard_map/ppermute | solution.py:327
  61.5 12.0 %collective-permute-start.22 = (bf16[96,2048]{1,0:T(8,128)(2,1)S(1)}, bf16[96,2048]{1,0:T(8,128)(2,1)S(1)}, u32[]{:S(2)}, u32[]{:S(2)}) collective-permute-start(bf16[96,2048]{1,0:T(8,128)(2,1)S(1)} %join.17.refs_10_), channel_id=1, source_target_pairs={{0,2},{1,3},{2,0},{3,1},{4,6},{5,7},{6,4},{7,5},{8,10},{9,11},{10,... | collective-permute-start | bytes 1179656 | tf_op jit(solution)/shard_map/ppermute | solution.py:324
  64.8 16.8 %collective-permute-start.29 = (bf16[96,2176]{1,0:T(8,128)(2,1)S(1)}, bf16[96,2176]{1,0:T(8,128)(2,1)S(1)}, u32[]{:S(2)}, u32[]{:S(2)}) collective-permute-start(bf16[96,2176]{1,0:T(8,128)(2,1)S(1)} %join.18.refs_1_), channel_id=1, source_target_pairs={{0,2},{1,3},{2,0},{3,1},{4,6},{5,7},{6,4},{7,5},{8,10},{9,11},{10,... | collective-permute-start | bytes 1253384 | tf_op jit(solution)/shard_map/ppermute | solution.py:324
  68.4 9.7 %collective-permute-start.31 = (bf16[48,2048]{1,0:T(8,128)(2,1)S(1)}, bf16[48,2048]{1,0:T(8,128)(2,1)S(1)}, u32[]{:S(2)}, u32[]{:S(2)}) collective-permute-start(bf16[48,2048]{1,0:T(8,128)(2,1)S(1)} %get-tuple-element.132), channel_id=1, source_target_pairs={{0,1},{1,0},{2,3},{3,2},{4,5},{5,4},{6,7},{7,6},{8,9},{9,8},{10,11... | collective-permute-start | bytes 589832 | tf_op jit(solution)/shard_map/ppermute | solution.py:327
  78.5 2.1 %collective-permute-start.32 = (bf16[48,2048]{1,0:T(8,128)(2,1)S(1)}, bf16[48,2048]{1,0:T(8,128)(2,1)S(1)}, u32[]{:S(2)}, u32[]{:S(2)}) collective-permute-start(bf16[48,2048]{1,0:T(8,128)(2,1)S(1)} %get-tuple-element.134), channel_id=1, source_target_pairs={{0,1},{1,0},{2,3},{3,2},{4,5},{5,4},{6,7},{7,6},{8,9},{9,8},{10,11... | collective-permute-start | bytes 589832 | tf_op jit(solution)/shard_map/ppermute | solution.py:327
  78.6 2.0 %collective-permute-start.33 = (bf16[48,2048]{1,0:T(8,128)(2,1)S(1)}, bf16[48,2048]{1,0:T(8,128)(2,1)S(1)}, u32[]{:S(2)}, u32[]{:S(2)}) collective-permute-start(bf16[48,2048]{1,0:T(8,128)(2,1)S(1)} %get-tuple-element.136), channel_id=1, source_target_pairs={{0,1},{1,0},{2,3},{3,2},{4,5},{5,4},{6,7},{7,6},{8,9},{9,8},{10,11... | collective-permute-start | bytes 589832 | tf_op jit(solution)/shard_map/ppermute | solution.py:327
  79.1 12.0 %collective-permute-start.34 = (bf16[96,2048]{1,0:T(8,128)(2,1)S(1)}, bf16[96,2048]{1,0:T(8,128)(2,1)S(1)}, u32[]{:S(2)}, u32[]{:S(2)}) collective-permute-start(bf16[96,2048]{1,0:T(8,128)(2,1)S(1)} %join.19.refs_10_), channel_id=1, source_target_pairs={{0,2},{1,3},{2,0},{3,1},{4,6},{5,7},{6,4},{7,5},{8,10},{9,11},{10,... | collective-permute-start | bytes 1179656 | tf_op jit(solution)/shard_map/ppermute | solution.py:324
  81.9 17.5 %collective-permute-start.42 = (bf16[128,2176]{1,0:T(8,128)(2,1)S(1)}, bf16[128,2176]{1,0:T(8,128)(2,1)S(1)}, u32[]{:S(2)}, u32[]{:S(2)}) collective-permute-start(bf16[128,2176]{1,0:T(8,128)(2,1)S(1)} %home.7.refs_4_), channel_id=1, source_target_pairs={{0,4},{1,5},{2,6},{3,7},{4,8},{5,9},{6,10},{7,11},{8,12},{9,13},{1... | collective-permute-start | bytes 1671176 | tf_op jit(solution)/shard_map/ppermute | solution.py:321
  82.2 17.3 %collective-permute-start.41 = (bf16[96,2048]{1,0:T(8,128)(2,1)S(1)}, bf16[96,2048]{1,0:T(8,128)(2,1)S(1)}, u32[]{:S(2)}, u32[]{:S(2)}) collective-permute-start(bf16[96,2048]{1,0:T(8,128)(2,1)S(1)} %join.20.refs_4_), channel_id=1, source_target_pairs={{0,2},{1,3},{2,0},{3,1},{4,6},{5,7},{6,4},{7,5},{8,10},{9,11},{10,... | collective-permute-start | bytes 1179656 | tf_op jit(solution)/shard_map/ppermute | solution.py:324
  91.0 3.5 %collective-permute-start.37 = (bf16[48,2176]{1,0:T(8,128)(2,1)S(1)}, bf16[48,2176]{1,0:T(8,128)(2,1)S(1)}, u32[]{:S(2)}, u32[]{:S(2)}) collective-permute-start(bf16[48,2176]{1,0:T(8,128)(2,1)S(1)} %get-tuple-element.140), channel_id=1, source_target_pairs={{0,1},{1,0},{2,3},{3,2},{4,5},{5,4},{6,7},{7,6},{8,9},{9,8},{10,11... | collective-permute-start | bytes 626696 | tf_op jit(solution)/shard_map/ppermute | solution.py:327
  91.1 1.8 %collective-permute-start.35 = (bf16[32,2176]{1,0:T(8,128)(2,1)S(1)}, bf16[32,2176]{1,0:T(8,128)(2,1)S(1)}, u32[]{:S(2)}, u32[]{:S(2)}) collective-permute-start(bf16[32,2176]{1,0:T(8,128)(2,1)S(1)} %slice.42), channel_id=1, source_target_pairs={{0,1},{1,0},{2,3},{3,2},{4,5},{5,4},{6,7},{7,6},{8,9},{9,8},{10,11... | collective-permute-start | bytes 417800 | tf_op jit(solution)/shard_map/ppermute | solution.py:327
  92.9 15.2 %collective-permute-start.48 = (bf16[96,2176]{1,0:T(8,128)(2,1)S(1)}, bf16[96,2176]{1,0:T(8,128)(2,1)S(1)}, u32[]{:S(2)}, u32[]{:S(2)}) collective-permute-start(bf16[96,2176]{1,0:T(8,128)(2,1)S(1)} %join.21.refs_4_), channel_id=1, source_target_pairs={{0,2},{1,3},{2,0},{3,1},{4,6},{5,7},{6,4},{7,5},{8,10},{9,11},{10,... | collective-permute-start | bytes 1253384 | tf_op jit(solution)/shard_map/ppermute | solution.py:324
  94.5 8.8 %collective-permute-start.38 = (bf16[48,2176]{1,0:T(8,128)(2,1)S(1)}, bf16[48,2176]{1,0:T(8,128)(2,1)S(1)}, u32[]{:S(2)}, u32[]{:S(2)}) collective-permute-start(bf16[48,2176]{1,0:T(8,128)(2,1)S(1)} %get-tuple-element.142), channel_id=1, source_target_pairs={{0,1},{1,0},{2,3},{3,2},{4,5},{5,4},{6,7},{7,6},{8,9},{9,8},{10,11... | collective-permute-start | bytes 626696 | tf_op jit(solution)/shard_map/ppermute | solution.py:327
  94.5 8.2 %collective-permute-start.39 = (bf16[32,2176]{1,0:T(8,128)(2,1)S(1)}, bf16[32,2176]{1,0:T(8,128)(2,1)S(1)}, u32[]{:S(2)}, u32[]{:S(2)}) collective-permute-start(bf16[32,2176]{1,0:T(8,128)(2,1)S(1)} %slice.44), channel_id=1, source_target_pairs={{0,1},{1,0},{2,3},{3,2},{4,5},{5,4},{6,7},{7,6},{8,9},{9,8},{10,11... | collective-permute-start | bytes 417800 | tf_op jit(solution)/shard_map/ppermute | solution.py:327
  99.5 3.2 %collective-permute-start.40 = (bf16[16,2176]{1,0:T(8,128)(2,1)S(1)}, bf16[16,2176]{1,0:T(8,128)(2,1)S(1)}, u32[]{:S(2)}, u32[]{:S(2)}) collective-permute-start(bf16[16,2176]{1,0:T(8,128)(2,1)S(1)} %slice.45), channel_id=1, source_target_pairs={{0,1},{1,0},{2,3},{3,2},{4,5},{5,4},{6,7},{7,6},{8,9},{9,8},{10,11... | collective-permute-start | bytes 208904 | tf_op jit(solution)/shard_map/ppermute | solution.py:327
  102.1 1.9 %collective-permute-start.43 = (bf16[32,2176]{1,0:T(8,128)(2,1)S(1)}, bf16[32,2176]{1,0:T(8,128)(2,1)S(1)}, u32[]{:S(2)}, u32[]{:S(2)}) collective-permute-start(bf16[32,2176]{1,0:T(8,128)(2,1)S(1)} %slice.46), channel_id=1, source_target_pairs={{0,1},{1,0},{2,3},{3,2},{4,5},{5,4},{6,7},{7,6},{8,9},{9,8},{10,11... | collective-permute-start | bytes 417800 | tf_op jit(solution)/shard_map/ppermute | solution.py:327
  102.8 2.9 %collective-permute-start.45 = (bf16[48,2176]{1,0:T(8,128)(2,1)S(1)}, bf16[48,2176]{1,0:T(8,128)(2,1)S(1)}, u32[]{:S(2)}, u32[]{:S(2)}) collective-permute-start(bf16[48,2176]{1,0:T(8,128)(2,1)S(1)} %get-tuple-element.149), channel_id=1, source_target_pairs={{0,1},{1,0},{2,3},{3,2},{4,5},{5,4},{6,7},{7,6},{8,9},{9,8},{10,11... | collective-permute-start | bytes 626696 | tf_op jit(solution)/shard_map/ppermute | solution.py:327
  104.1 14.8 %collective-permute-start.47 = (bf16[96,2176]{1,0:T(8,128)(2,1)S(1)}, bf16[96,2176]{1,0:T(8,128)(2,1)S(1)}, u32[]{:S(2)}, u32[]{:S(2)}) collective-permute-start(bf16[96,2176]{1,0:T(8,128)(2,1)S(1)} %join.22.refs_3_), channel_id=1, source_target_pairs={{0,2},{1,3},{2,0},{3,1},{4,6},{5,7},{6,4},{7,5},{8,10},{9,11},{10,... | collective-permute-start | bytes 1253384 | tf_op jit(solution)/shard_map/ppermute | solution.py:324
  108.4 10.4 %collective-permute-start.49 = (bf16[128,896]{1,0:T(8,128)(2,1)S(1)}, bf16[128,896]{1,0:T(8,128)(2,1)S(1)}, u32[]{:S(2)}, u32[]{:S(2)}) collective-permute-start(bf16[128,896]{1,0:T(8,128)(2,1)S(1)} %home.8.refs_5_), channel_id=1, source_target_pairs={{0,4},{1,5},{2,6},{3,7},{4,8},{5,9},{6,10},{7,11},{8,12},{9,13},{1... | collective-permute-start | bytes 688136 | tf_op jit(solution)/shard_map/ppermute | solution.py:321
  108.5 24.7 %collective-permute-start.46 = (bf16[96,2176]{1,0:T(8,128)(2,1)S(1)}, bf16[96,2176]{1,0:T(8,128)(2,1)S(1)}, u32[]{:S(2)}, u32[]{:S(2)}) collective-permute-start(bf16[96,2176]{1,0:T(8,128)(2,1)S(1)} %join.23.refs_5_), channel_id=1, source_target_pairs={{0,2},{1,3},{2,0},{3,1},{4,6},{5,7},{6,4},{7,5},{8,10},{9,11},{10,... | collective-permute-start | bytes 1253384 | tf_op jit(solution)/shard_map/ppermute | solution.py:324
  110.4 12.6 %collective-permute-start.51 = (bf16[128,768]{1,0:T(8,128)(2,1)S(1)}, bf16[128,768]{1,0:T(8,128)(2,1)S(1)}, u32[]{:S(2)}, u32[]{:S(2)}) collective-permute-start(bf16[128,768]{1,0:T(8,128)(2,1)S(1)} %home.9.refs_5_), channel_id=1, source_target_pairs={{0,4},{1,5},{2,6},{3,7},{4,8},{5,9},{6,10},{7,11},{8,12},{9,13},{1... | collective-permute-start | bytes 589832 | tf_op jit(solution)/shard_map/ppermute | solution.py:321
  112.0 13.8 %collective-permute-start.53 = (bf16[128,512]{1,0:T(8,128)(2,1)S(1)}, bf16[128,512]{1,0:T(8,128)(2,1)S(1)}, u32[]{:S(2)}, u32[]{:S(2)}) collective-permute-start(bf16[128,512]{1,0:T(8,128)(2,1)S(1)} %home.10.refs_5_), channel_id=1, source_target_pairs={{0,4},{1,5},{2,6},{3,7},{4,8},{5,9},{6,10},{7,11},{8,12},{9,13},{1... | collective-permute-start | bytes 393224 | tf_op jit(solution)/shard_map/ppermute | solution.py:321
  119.1 16.3 %collective-permute-start.50 = (bf16[128,896]{1,0:T(8,128)(2,1)S(1)}, bf16[128,896]{1,0:T(8,128)(2,1)S(1)}, u32[]{:S(2)}, u32[]{:S(2)}) collective-permute-start(bf16[128,896]{1,0:T(8,128)(2,1)S(1)} %home.11.refs_5_), channel_id=1, source_target_pairs={{0,4},{1,5},{2,6},{3,7},{4,8},{5,9},{6,10},{7,11},{8,12},{9,13},{1... | collective-permute-start | bytes 688136 | tf_op jit(solution)/shard_map/ppermute | solution.py:321
  123.3 12.1 %collective-permute-start.52 = (bf16[128,768]{1,0:T(8,128)(2,1)S(1)}, bf16[128,768]{1,0:T(8,128)(2,1)S(1)}, u32[]{:S(2)}, u32[]{:S(2)}) collective-permute-start(bf16[128,768]{1,0:T(8,128)(2,1)S(1)} %home.12.refs_5_), channel_id=1, source_target_pairs={{0,4},{1,5},{2,6},{3,7},{4,8},{5,9},{6,10},{7,11},{8,12},{9,13},{1... | collective-permute-start | bytes 589832 | tf_op jit(solution)/shard_map/ppermute | solution.py:321
  126.1 9.3 %collective-permute-start.54 = (bf16[128,512]{1,0:T(8,128)(2,1)S(1)}, bf16[128,512]{1,0:T(8,128)(2,1)S(1)}, u32[]{:S(2)}, u32[]{:S(2)}) collective-permute-start(bf16[128,512]{1,0:T(8,128)(2,1)S(1)} %home.13.refs_32_), channel_id=1, source_target_pairs={{0,4},{1,5},{2,6},{3,7},{4,8},{5,9},{6,10},{7,11},{8,12},{9,13},{1... | collective-permute-start | bytes 393224 | tf_op jit(solution)/shard_map/ppermute | solution.py:321
  (14 other events, 59.9 us)

commit v4 on v3

--- a/solution.py
+++ b/solution.py
@@ -362,13 +362,14 @@
         )
         rows_x[s] = spread(blocks, pieces)
 
-    def slots_d(s, d):
+    def slots_d(s, d, after=()):
         blocks = run(
             functools.partial(gather_kernel, capacity),
             [((capacity, features), BF16)] * PLANE,
             "slots_d",
             scaled[s],
             d,
+            after=after,
         )
         rows_d[s] = spread(blocks)
 
@@ -417,26 +418,31 @@
     slots_d(0, cotangent)
     last = planes - 1
     for s in range(1, planes):
-        (here,) = run.hold(x, after=rows_x[s - 1][2:])
+        (here,) = run.hold(x, after=terms[1][1:] if s == last else rows_x[s - 1][2:])
         if s < last:
             x = along(here)
         slots_x(s, here, 2 if s == last else 1)
-        if s == last:
+        if s > 1:
             expert(s - 1)
+        if s == 2:
+            terms[1] = spread(terms[1], 2)
+            run.pending = []
         (here,) = run.hold(d, after=rows_d[s - 1][2:])
-        if s < last:
+        if s == 1:
             d = along(here)
+        if s == 2:
+            run.pending += rows_x[s][2:]
         slots_d(s, here)
         if s == 1:
             expert(0)
         if s == 2:
-            expert(1, after=rows_x[2][2:])
-            terms[1] = spread(terms[1], 2)
+            (here,) = run.hold(here)
+            d = along(here)
     passed = home(1, slice(0, wide))
     terms[2] = send(*swap(run.hold(*terms[2], after=rows_x[last][2:]), 2), wait=False)
     swapped = swap(run.hold(*terms[0]), 2)
     run.pending = [swapped[1], *swapped[3]]
-    expert(last, after=[passed])
+    expert(last)
     terms[last] = spread(terms[last], 2)
     terms[0] = send(*swapped)
     cuts = [0, 896, 1664, wide]

time: 137 us -> 132 us (0.964)
  waiting for transfers between devices: 72.2 us -> 66.8 us
    ppermute x12, waiting for transfers between devices: 24.6 us -> 21.4 us  [across(): return lax.ppermute(array, 'expert', [(i, i ^ 2) for i in range(devices)])]
  transfers between devices with their start and end apart: 55 -> 55, of which waited for: 31 -> 27; matrix products, arithmetic and copies ran while one was open for 0% -> 0% of each run, Pallas kernels for 17% -> 18%
where the time goes in v4:
time: 132 us; the launch traced here: 131 us
  waiting for transfers between devices  66.8 us (51%)
  starting transfers between devices  35.7 us (27%)
  Pallas kernels  26.5 us (20%)
    ppermute x13, waiting for transfers between devices, along(): lax.ppermute(array, 'expert', [(i, (i + PLANE) % devices) for i in range(...  36.4 us
    pallas_call x34, Pallas kernels, __call__(): pl.pallas_call(body, out_shape=[jax.ShapeDtypeStruct(shape, kind) for sha...  26.5 us
    ppermute x12, waiting for transfers between devices, across(): return lax.ppermute(array, 'expert', [(i, i ^ 2) for i in range(devices)])  21.4 us
    ppermute x12, starting transfers between devices, across(): return lax.ppermute(array, 'expert', [(i, i ^ 2) for i in range(devices)])  17.7 us
    ppermute x13, starting transfers between devices, along(): lax.ppermute(array, 'expert', [(i, (i + PLANE) % devices) for i in range(...  10.5 us
    ppermute x30, waiting for transfers between devices, cores(): return lax.ppermute(array, 'expert', [(i, i ^ 1) for i in range(devices)])  8.96 us
    ppermute x30, starting transfers between devices, cores(): return lax.ppermute(array, 'expert', [(i, i ^ 1) for i in range(devices)])  7.48 us
  transfers between devices with their start and end apart: 55, of which 27 were waited for; matrix products, arithmetic and copies ran while one was open for 0% of the time, Pallas kernels for 18%

profile of v4, /device:TPU:0, one launch (start us, length us, event | category | flops | bytes accessed | tf_op | source)
XLA Modules:
  0.0 131.3 jit_solution(16994781748151026561)
XLA Ops:
  0.6 2.0 %pack.1.refs_1_.refs_2_ = bf16[128,2176]{1,0:T(8,128)(2,1)} custom-call(s32[4,128]{1,0:T(4,128)} %bitcast.22, s32[4,128]{1,0:T(4,128)} %bitcast.24, bf16[128,2048]{1,0:T(8,128)(2,1)} %refs_2_.1), custom_call_target="tpu_custom_call" | custom-call | flops 1000 | bytes 1000 | tf_op jit(solution)/shard_map/pack/pallas_call | solution.py:130
  2.6 3.1 %collective-permute-start.7 = (bf16[128,2176]{1,0:T(8,128)(2,1)}, bf16[128,2176]{1,0:T(8,128)(2,1)S(1)}, u32[]{:S(2)}, u32[]{:S(2)}) collective-permute-start(bf16[128,2176]{1,0:T(8,128)(2,1)} %pack.1.refs_1_.refs_2_), channel_id=1, source_target_pairs={{0,4},{1,5},{2,6},{3,7},{4,8},{5,9},{6,10},{7,11},{8,12},{9,13},{1... | collective-permute-start | bytes 1671176 | tf_op jit(solution)/shard_map/ppermute | solution.py:321
  5.7 1.1 copy-done.3
  6.8 0.6 slots_x.4
  8.1 1.2 collective-permute-done.2.refs_2_
  9.3 1.6 %collective-permute-start.3 = (bf16[96,2048]{1,0:T(8,128)(2,1)S(1)}, bf16[96,2048]{1,0:T(8,128)(2,1)S(1)}, u32[]{:S(2)}, u32[]{:S(2)}) collective-permute-start(bf16[96,2048]{1,0:T(8,128)(2,1)S(1)} %join.12.refs_2_), channel_id=1, source_target_pairs={{0,2},{1,3},{2,0},{3,1},{4,6},{5,7},{6,4},{7,5},{8,10},{9,11},{10,... | collective-permute-start | bytes 1179656 | tf_op jit(solution)/shard_map/ppermute | solution.py:324
  11.8 1.6 %collective-permute-start.8 = (bf16[128,2048]{1,0:T(8,128)(2,1)S(1)}, bf16[128,2048]{1,0:T(8,128)(2,1)S(1)}, u32[]{:S(2)}, u32[]{:S(2)}) collective-permute-start(bf16[128,2048]{1,0:T(8,128)(2,1)S(1)} %copy-done.4), channel_id=1, source_target_pairs={{0,4},{1,5},{2,6},{3,7},{4,8},{5,9},{6,10},{7,11},{8,12},{9,13},{1... | collective-permute-start | bytes 1572872 | tf_op jit(solution)/shard_map/ppermute | solution.py:321
  14.0 7.3 %collective-permute-done.3.refs_2_.refs_3_ = bf16[96,2048]{1,0:T(8,128)(2,1)S(1)} collective-permute-done((bf16[96,2048]{1,0:T(8,128)(2,1)S(1)}, bf16[96,2048]{1,0:T(8,128)(2,1)S(1)}, u32[]{:S(2)}, u32[]{:S(2)}) %collective-permute-start.3) | collective-permute-done | bytes 393248 | tf_op jit(solution)/shard_map/ppermute | solution.py:324
  22.6 1.5 %collective-permute-start.13 = (bf16[128,2176]{1,0:T(8,128)(2,1)S(1)}, bf16[128,2176]{1,0:T(8,128)(2,1)S(1)}, u32[]{:S(2)}, u32[]{:S(2)}) collective-permute-start(bf16[128,2176]{1,0:T(8,128)(2,1)S(1)} %hold.9.refs_1_.refs_2_), channel_id=1, source_target_pairs={{0,4},{1,5},{2,6},{3,7},{4,8},{5,9},{6,10},{7,11},{8,12},{9,13},{1... | collective-permute-start | bytes 1671176 | tf_op jit(solution)/shard_map/ppermute | solution.py:321
  24.1 1.6 %collective-permute-start.14 = (bf16[96,2048]{1,0:T(8,128)(2,1)S(1)}, bf16[96,2048]{1,0:T(8,128)(2,1)S(1)}, u32[]{:S(2)}, u32[]{:S(2)}) collective-permute-start(bf16[96,2048]{1,0:T(8,128)(2,1)S(1)} %join.14.refs_1_), channel_id=1, source_target_pairs={{0,2},{1,3},{2,0},{3,1},{4,6},{5,7},{6,4},{7,5},{8,10},{9,11},{10,... | collective-permute-start | bytes 1179656 | tf_op jit(solution)/shard_map/ppermute | solution.py:324
  25.7 6.9 %collective-permute-done.8.refs_0_ = bf16[128,2048]{1,0:T(8,128)(2,1)S(1)} collective-permute-done((bf16[128,2048]{1,0:T(8,128)(2,1)S(1)}, bf16[128,2048]{1,0:T(8,128)(2,1)S(1)}, u32[]{:S(2)}, u32[]{:S(2)}) %collective-permute-start.8) | collective-permute-done | bytes 524320 | tf_op jit(solution)/shard_map/ppermute | solution.py:321
  33.6 0.9 collective-permute-done.11.refs_1_
  34.8 1.8 %collective-permute-start.19 = (bf16[96,2048]{1,0:T(8,128)(2,1)S(1)}, bf16[96,2048]{1,0:T(8,128)(2,1)S(1)}, u32[]{:S(2)}, u32[]{:S(2)}) collective-permute-start(bf16[96,2048]{1,0:T(8,128)(2,1)S(1)} %join.15.refs_10_), channel_id=1, source_target_pairs={{0,2},{1,3},{2,0},{3,1},{4,6},{5,7},{6,4},{7,5},{8,10},{9,11},{10,... | collective-permute-start | bytes 1179656 | tf_op jit(solution)/shard_map/ppermute | solution.py:324
  36.6 2.6 %expert.4 = (bf16[192,768]{1,0:T(8,128)(2,1)S(1)}, bf16[192,384]{1,0:T(8,128)(2,1)S(1)}, bf16[48,2176]{1,0:T(8,128)(2,1)S(1)}, bf16[48,2176]{1,0:T(8,128)(2,1)S(...) custom-call(s32[1]{0:T(128)} %bitcast.2.refs_0_, bf16[48,2048]{1,0:T(8,128)(2,1)S(1)} %get-tuple-element.84.refs_1_.refs_0_, ...), custom_call_target="tpu_custom_call" | custom-call | flops 1000 | bytes 1000 | tf_op jit(solution)/shard_map/expert/pallas_call | solution.py:130
  39.3 5.3 %collective-permute-done.13.refs_0_ = bf16[128,2176]{1,0:T(8,128)(2,1)S(1)} collective-permute-done((bf16[128,2176]{1,0:T(8,128)(2,1)S(1)}, bf16[128,2176]{1,0:T(8,128)(2,1)S(1)}, u32[]{:S(2)}, u32[]{:S(2)}) %collective-permute-start.13) | collective-permute-done | bytes 557088 | tf_op jit(solution)/shard_map/ppermute | solution.py:321
  45.7 0.9 collective-permute-done.15.refs_3_.refs_2_.refs_7_
  47.0 1.8 %collective-permute-start.17 = (bf16[96,2048]{1,0:T(8,128)(2,1)S(1)}, bf16[96,2048]{1,0:T(8,128)(2,1)S(1)}, u32[]{:S(2)}, u32[]{:S(2)}) collective-permute-start(bf16[96,2048]{1,0:T(8,128)(2,1)S(1)} %join.16.refs_10_), channel_id=1, source_target_pairs={{0,2},{1,3},{2,0},{3,1},{4,6},{5,7},{6,4},{7,5},{8,10},{9,11},{10,... | collective-permute-start | bytes 1179656 | tf_op jit(solution)/shard_map/ppermute | solution.py:324
  48.8 2.6 %expert.5 = (bf16[192,768]{1,0:T(8,128)(2,1)S(1)}, bf16[192,384]{1,0:T(8,128)(2,1)S(1)}, bf16[48,2176]{1,0:T(8,128)(2,1)S(1)}, bf16[48,2176]{1,0:T(8,128)(2,1)S(...) custom-call(s32[1]{0:T(128)} %bitcast.2.refs_0_, ...), custom_call_target="tpu_custom_call" | custom-call | flops 1000 | bytes 1000 | tf_op jit(solution)/shard_map/expert/pallas_call | solution.py:130
  52.0 0.9 collective-permute-done.21.refs_2_
  53.0 1.9 %collective-permute-done.18.refs_0_ = bf16[128,2048]{1,0:T(8,128)(2,1)S(1)} collective-permute-done((bf16[128,2048]{1,0:T(8,128)(2,1)S(1)}, bf16[128,2048]{1,0:T(8,128)(2,1)S(1)}, u32[]{:S(2)}, u32[]{:S(2)}) %collective-permute-start.18) | collective-permute-done | bytes 524320 | tf_op jit(solution)/shard_map/ppermute | solution.py:321
  55.9 1.5 %collective-permute-start.27 = (bf16[96,2176]{1,0:T(8,128)(2,1)S(1)}, bf16[96,2176]{1,0:T(8,128)(2,1)S(1)}, u32[]{:S(2)}, u32[]{:S(2)}) collective-permute-start(bf16[96,2176]{1,0:T(8,128)(2,1)S(1)} %join.17.refs_1_), channel_id=1, source_target_pairs={{0,2},{1,3},{2,0},{3,1},{4,6},{5,7},{6,4},{7,5},{8,10},{9,11},{10,... | collective-permute-start | bytes 1253384 | tf_op jit(solution)/shard_map/ppermute | solution.py:324
  57.4 0.9 collective-permute-done.17.refs_3_.refs_8_
  58.7 1.8 %collective-permute-start.24 = (bf16[96,2048]{1,0:T(8,128)(2,1)S(1)}, bf16[96,2048]{1,0:T(8,128)(2,1)S(1)}, u32[]{:S(2)}, u32[]{:S(2)}) collective-permute-start(bf16[96,2048]{1,0:T(8,128)(2,1)S(1)} %join.18.refs_1_), channel_id=1, source_target_pairs={{0,2},{1,3},{2,0},{3,1},{4,6},{5,7},{6,4},{7,5},{8,10},{9,11},{10,... | collective-permute-start | bytes 1179656 | tf_op jit(solution)/shard_map/ppermute | solution.py:324
  60.5 8.8 %collective-permute-done.25.refs_0_ = bf16[128,2176]{1,0:T(8,128)(2,1)S(1)} collective-permute-done((bf16[128,2176]{1,0:T(8,128)(2,1)S(1)}, bf16[128,2176]{1,0:T(8,128)(2,1)S(1)}, u32[]{:S(2)}, u32[]{:S(2)}) %collective-permute-start.25) | collective-permute-done | bytes 557088 | tf_op jit(solution)/shard_map/ppermute | solution.py:321
  69.3 0.6 slots_x.7
  70.7 1.2 collective-permute-done.29.refs_2_
  71.9 0.6 collective-permute-start.34
  72.5 4.3 %collective-permute-done.24.refs_6_.refs_3_.refs_20_ = bf16[96,2048]{1,0:T(8,128)(2,1)S(1)} collective-permute-done((bf16[96,2048]{1,0:T(8,128)(2,1)S(1)}, bf16[96,2048]{1,0:T(8,128)(2,1)S(1)}, u32[]{:S(2)}, u32[]{:S(2)}) %collective-permute-start.24) | collective-permute-done | bytes 393248 | tf_op jit(solution)/shard_map/ppermute | solution.py:324
  76.8 2.6 %expert.6 = (bf16[192,768]{1,0:T(8,128)(2,1)S(1)}, bf16[192,384]{1,0:T(8,128)(2,1)S(1)}, bf16[48,2176]{1,0:T(8,128)(2,1)S(1)}, bf16[48,2176]{1,0:T(8,128)(2,1)S(...) custom-call(s32[1]{0:T(128)} %bitcast.2.refs_0_, ...), custom_call_target="tpu_custom_call" | custom-call | flops 1000 | bytes 1000 | tf_op jit(solution)/shard_map/expert/pallas_call | solution.py:130
  80.6 0.9 collective-permute-done.32.refs_1_
  81.9 1.4 %collective-permute-start.41 = (bf16[96,2048]{1,0:T(8,128)(2,1)S(1)}, bf16[96,2048]{1,0:T(8,128)(2,1)S(1)}, u32[]{:S(2)}, u32[]{:S(2)}) collective-permute-start(bf16[96,2048]{1,0:T(8,128)(2,1)S(1)} %join.20.refs_4_), channel_id=1, source_target_pairs={{0,2},{1,3},{2,0},{3,1},{4,6},{5,7},{6,4},{7,5},{8,10},{9,11},{10,... | collective-permute-start | bytes 1179656 | tf_op jit(solution)/shard_map/ppermute | solution.py:324
  83.6 0.8 collective-permute-done.34.refs_5_.refs_3_.refs_11_
  85.3 1.3 collective-permute-done.36.refs_2_
  86.9 1.7 %collective-permute-start.47 = (bf16[96,2176]{1,0:T(8,128)(2,1)S(1)}, bf16[96,2176]{1,0:T(8,128)(2,1)S(1)}, u32[]{:S(2)}, u32[]{:S(2)}) collective-permute-start(bf16[96,2176]{1,0:T(8,128)(2,1)S(1)} %join.21.refs_4_), channel_id=1, source_target_pairs={{0,2},{1,3},{2,0},{3,1},{4,6},{5,7},{6,4},{7,5},{8,10},{9,11},{10,... | collective-permute-start | bytes 1253384 | tf_op jit(solution)/shard_map/ppermute | solution.py:324
  88.8 5.1 %collective-permute-done.41.refs_6_.refs_23_ = bf16[96,2048]{1,0:T(8,128)(2,1)S(1)} collective-permute-done((bf16[96,2048]{1,0:T(8,128)(2,1)S(1)}, bf16[96,2048]{1,0:T(8,128)(2,1)S(1)}, u32[]{:S(2)}, u32[]{:S(2)}) %collective-permute-start.41) | collective-permute-done | bytes 393248 | tf_op jit(solution)/shard_map/ppermute | solution.py:324
  93.9 2.6 %expert.7 = (bf16[192,768]{1,0:T(8,128)(2,1)S(1)}, bf16[192,384]{1,0:T(8,128)(2,1)S(1)}, bf16[48,2176]{1,0:T(8,128)(2,1)S(1)}, bf16[48,2176]{1,0:T(8,128)(2,1)S(...) custom-call(s32[1]{0:T(128)} %bitcast.2.refs_0_, ...), custom_call_target="tpu_custom_call" | custom-call | flops 1000 | bytes 1000 | tf_op jit(solution)/shard_map/expert/pallas_call | solution.py:130
  97.7 0.7 collective-permute-done.43.refs_2_
  98.5 1.4 %collective-permute-start.46 = (bf16[96,2176]{1,0:T(8,128)(2,1)S(1)}, bf16[96,2176]{1,0:T(8,128)(2,1)S(1)}, u32[]{:S(2)}, u32[]{:S(2)}) collective-permute-start(bf16[96,2176]{1,0:T(8,128)(2,1)S(1)} %join.22.refs_3_), channel_id=1, source_target_pairs={{0,2},{1,3},{2,0},{3,1},{4,6},{5,7},{6,4},{7,5},{8,10},{9,11},{10,... | collective-permute-start | bytes 1253384 | tf_op jit(solution)/shard_map/ppermute | solution.py:324
  99.9 3.0 %collective-permute-done.47.refs_3_ = bf16[96,2176]{1,0:T(8,128)(2,1)S(1)} collective-permute-done((bf16[96,2176]{1,0:T(8,128)(2,1)S(1)}, bf16[96,2176]{1,0:T(8,128)(2,1)S(1)}, u32[]{:S(2)}, u32[]{:S(2)}) %collective-permute-start.47) | collective-permute-done | bytes 417824 | tf_op jit(solution)/shard_map/ppermute | solution.py:324
  103.2 1.9 %collective-permute-start.45 = (bf16[96,2176]{1,0:T(8,128)(2,1)S(1)}, bf16[96,2176]{1,0:T(8,128)(2,1)S(1)}, u32[]{:S(2)}, u32[]{:S(2)}) collective-permute-start(bf16[96,2176]{1,0:T(8,128)(2,1)S(1)} %join.23.refs_5_), channel_id=1, source_target_pairs={{0,2},{1,3},{2,0},{3,1},{4,6},{5,7},{6,4},{7,5},{8,10},{9,11},{10,... | collective-permute-start | bytes 1253384 | tf_op jit(solution)/shard_map/ppermute | solution.py:324
  105.3 1.9 %collective-permute-start.51 = (bf16[128,768]{1,0:T(8,128)(2,1)S(1)}, bf16[128,768]{1,0:T(8,128)(2,1)S(1)}, u32[]{:S(2)}, u32[]{:S(2)}) collective-permute-start(bf16[128,768]{1,0:T(8,128)(2,1)S(1)} %home.9.refs_5_), channel_id=1, source_target_pairs={{0,4},{1,5},{2,6},{3,7},{4,8},{5,9},{6,10},{7,11},{8,12},{9,13},{1... | collective-permute-start | bytes 589832 | tf_op jit(solution)/shard_map/ppermute | solution.py:321
  107.4 1.6 %collective-permute-start.53 = (bf16[128,512]{1,0:T(8,128)(2,1)S(1)}, bf16[128,512]{1,0:T(8,128)(2,1)S(1)}, u32[]{:S(2)}, u32[]{:S(2)}) collective-permute-start(bf16[128,512]{1,0:T(8,128)(2,1)S(1)} %home.10.refs_5_), channel_id=1, source_target_pairs={{0,4},{1,5},{2,6},{3,7},{4,8},{5,9},{6,10},{7,11},{8,12},{9,13},{1... | collective-permute-start | bytes 393224 | tf_op jit(solution)/shard_map/ppermute | solution.py:321
  109.0 4.5 %collective-permute-done.49.refs_4_ = bf16[128,896]{1,0:T(8,128)(2,1)S(1)} collective-permute-done((bf16[128,896]{1,0:T(8,128)(2,1)S(1)}, bf16[128,896]{1,0:T(8,128)(2,1)S(1)}, u32[]{:S(2)}, u32[]{:S(2)}) %collective-permute-start.49) | collective-permute-done | bytes 229408 | tf_op jit(solution)/shard_map/ppermute | solution.py:321
  113.8 3.9 %collective-permute-done.51.refs_4_ = bf16[128,768]{1,0:T(8,128)(2,1)S(1)} collective-permute-done((bf16[128,768]{1,0:T(8,128)(2,1)S(1)}, bf16[128,768]{1,0:T(8,128)(2,1)S(1)}, u32[]{:S(2)}, u32[]{:S(2)}) %collective-permute-start.51) | collective-permute-done | bytes 196640 | tf_op jit(solution)/shard_map/ppermute | solution.py:321
  118.0 2.5 %collective-permute-done.53.refs_4_ = bf16[128,512]{1,0:T(8,128)(2,1)S(1)} collective-permute-done((bf16[128,512]{1,0:T(8,128)(2,1)S(1)}, bf16[128,512]{1,0:T(8,128)(2,1)S(1)}, u32[]{:S(2)}, u32[]{:S(2)}) %collective-permute-start.53) | collective-permute-done | bytes 131104 | tf_op jit(solution)/shard_map/ppermute | solution.py:321
  120.8 7.0 %deltas.1 = (bf16[2048,384]{1,0:T(8,128)(2,1)}, bf16[2048,384]{1,0:T(8,128)(2,1)}, bf16[384,2048]{1,0:T(8,128)(2,1)}, f32[8,128]{1,0:T(8,128)S(1)}) custom-call(bf16[48,2048]{1,0:T(8,128)(2,1)S(1)} %get-tuple-element.84.refs_1_.refs_0_, bf16[48,2048]{1,0:T(8,128)(2,1)S(1)} %collective-permute-done.refs_3_.refs_2_.refs_1_, ...), custom_call_target="tpu_custom_call" | custom-call | flops 1000 | bytes 1000 | tf_op jit(solution)/shard_map/deltas/pallas_call | solution.py:130
  127.8 2.3 %collective-permute-done.54.refs_8_ = bf16[128,512]{1,0:T(8,128)(2,1)S(1)} collective-permute-done((bf16[128,512]{1,0:T(8,128)(2,1)S(1)}, bf16[128,512]{1,0:T(8,128)(2,1)S(1)}, u32[]{:S(2)}, u32[]{:S(2)}) %collective-permute-start.54) | collective-permute-done | bytes 131104 | tf_op jit(solution)/shard_map/ppermute | solution.py:321
  130.2 1.2 total.1
  (131 shorter events, 15.0 us)
Async XLA Ops:
  2.6 18.8 %collective-permute-start.7 = (bf16[128,2176]{1,0:T(8,128)(2,1)}, bf16[128,2176]{1,0:T(8,128)(2,1)S(1)}, u32[]{:S(2)}, u32[]{:S(2)}) collective-permute-start(bf16[128,2176]{1,0:T(8,128)(2,1)} %pack.1.refs_1_.refs_2_), channel_id=1, source_target_pairs={{0,4},{1,5},{2,6},{3,7},{4,8},{5,9},{6,10},{7,11},{8,12},{9,13},{1... | collective-permute-start | bytes 1671176 | tf_op jit(solution)/shard_map/ppermute | solution.py:321
  7.4 1.8 %collective-permute-start.1 = (bf16[32,2048]{1,0:T(8,128)(2,1)S(1)}, bf16[32,2048]{1,0:T(8,128)(2,1)S(1)}, u32[]{:S(2)}, u32[]{:S(2)}) collective-permute-start(bf16[32,2048]{1,0:T(8,128)(2,1)S(1)} %slice.36), channel_id=1, source_target_pairs={{0,1},{1,0},{2,3},{3,2},{4,5},{5,4},{6,7},{7,6},{8,9},{9,8},{10,11... | collective-permute-start | bytes 393224 | tf_op jit(solution)/shard_map/ppermute | solution.py:327
  7.5 4.3 %collective-permute-start = (bf16[48,2048]{1,0:T(8,128)(2,1)S(1)}, bf16[48,2048]{1,0:T(8,128)(2,1)S(1)}, u32[]{:S(2)}, u32[]{:S(2)}) collective-permute-start(bf16[48,2048]{1,0:T(8,128)(2,1)S(1)} %get-tuple-element.85), channel_id=1, source_target_pairs={{0,1},{1,0},{2,3},{3,2},{4,5},{5,4},{6,7},{7,6},{8,9},{9,8},{10,11... | collective-permute-start | bytes 589832 | tf_op jit(solution)/shard_map/ppermute | solution.py:327
  9.3 12.0 %collective-permute-start.3 = (bf16[96,2048]{1,0:T(8,128)(2,1)S(1)}, bf16[96,2048]{1,0:T(8,128)(2,1)S(1)}, u32[]{:S(2)}, u32[]{:S(2)}) collective-permute-start(bf16[96,2048]{1,0:T(8,128)(2,1)S(1)} %join.12.refs_2_), channel_id=1, source_target_pairs={{0,2},{1,3},{2,0},{3,1},{4,6},{5,7},{6,4},{7,5},{8,10},{9,11},{10,... | collective-permute-start | bytes 1179656 | tf_op jit(solution)/shard_map/ppermute | solution.py:324
  11.2 2.2 %collective-permute-start.4 = (bf16[48,2048]{1,0:T(8,128)(2,1)S(1)}, bf16[48,2048]{1,0:T(8,128)(2,1)S(1)}, u32[]{:S(2)}, u32[]{:S(2)}) collective-permute-start(bf16[48,2048]{1,0:T(8,128)(2,1)S(1)} %get-tuple-element.90), channel_id=1, source_target_pairs={{0,1},{1,0},{2,3},{3,2},{4,5},{5,4},{6,7},{7,6},{8,9},{9,8},{10,11... | collective-permute-start | bytes 589832 | tf_op jit(solution)/shard_map/ppermute | solution.py:327
  11.3 2.1 %collective-permute-start.5 = (bf16[48,2048]{1,0:T(8,128)(2,1)S(1)}, bf16[48,2048]{1,0:T(8,128)(2,1)S(1)}, u32[]{:S(2)}, u32[]{:S(2)}) collective-permute-start(bf16[48,2048]{1,0:T(8,128)(2,1)S(1)} %get-tuple-element.92), channel_id=1, source_target_pairs={{0,1},{1,0},{2,3},{3,2},{4,5},{5,4},{6,7},{7,6},{8,9},{9,8},{10,11... | collective-permute-start | bytes 589832 | tf_op jit(solution)/shard_map/ppermute | solution.py:327
  11.8 20.8 %collective-permute-start.8 = (bf16[128,2048]{1,0:T(8,128)(2,1)S(1)}, bf16[128,2048]{1,0:T(8,128)(2,1)S(1)}, u32[]{:S(2)}, u32[]{:S(2)}) collective-permute-start(bf16[128,2048]{1,0:T(8,128)(2,1)S(1)} %copy-done.4), channel_id=1, source_target_pairs={{0,4},{1,5},{2,6},{3,7},{4,8},{5,9},{6,10},{7,11},{8,12},{9,13},{1... | collective-permute-start | bytes 1572872 | tf_op jit(solution)/shard_map/ppermute | solution.py:321
  13.4 19.2 %collective-permute-start.6 = (bf16[96,2048]{1,0:T(8,128)(2,1)S(1)}, bf16[96,2048]{1,0:T(8,128)(2,1)S(1)}, u32[]{:S(2)}, u32[]{:S(2)}) collective-permute-start(bf16[96,2048]{1,0:T(8,128)(2,1)S(1)} %join.13.refs_1_), channel_id=1, source_target_pairs={{0,2},{1,3},{2,0},{3,1},{4,6},{5,7},{6,4},{7,5},{8,10},{9,11},{10,... | collective-permute-start | bytes 1179656 | tf_op jit(solution)/shard_map/ppermute | solution.py:324
  22.0 2.1 %collective-permute-start.9 = (bf16[48,2048]{1,0:T(8,128)(2,1)S(1)}, bf16[48,2048]{1,0:T(8,128)(2,1)S(1)}, u32[]{:S(2)}, u32[]{:S(2)}) collective-permute-start(bf16[48,2048]{1,0:T(8,128)(2,1)S(1)} %get-tuple-element.95), channel_id=1, source_target_pairs={{0,1},{1,0},{2,3},{3,2},{4,5},{5,4},{6,7},{7,6},{8,9},{9,8},{10,11... | collective-permute-start | bytes 589832 | tf_op jit(solution)/shard_map/ppermute | solution.py:327
  22.1 2.0 %collective-permute-start.10 = (bf16[48,2048]{1,0:T(8,128)(2,1)S(1)}, bf16[48,2048]{1,0:T(8,128)(2,1)S(1)}, u32[]{:S(2)}, u32[]{:S(2)}) collective-permute-start(bf16[48,2048]{1,0:T(8,128)(2,1)S(1)} %get-tuple-element.97), channel_id=1, source_target_pairs={{0,1},{1,0},{2,3},{3,2},{4,5},{5,4},{6,7},{7,6},{8,9},{9,8},{10,11... | collective-permute-start | bytes 589832 | tf_op jit(solution)/shard_map/ppermute | solution.py:327
  22.6 22.0 %collective-permute-start.13 = (bf16[128,2176]{1,0:T(8,128)(2,1)S(1)}, bf16[128,2176]{1,0:T(8,128)(2,1)S(1)}, u32[]{:S(2)}, u32[]{:S(2)}) collective-permute-start(bf16[128,2176]{1,0:T(8,128)(2,1)S(1)} %hold.9.refs_1_.refs_2_), channel_id=1, source_target_pairs={{0,4},{1,5},{2,6},{3,7},{4,8},{5,9},{6,10},{7,11},{8,12},{9,13},{1... | collective-permute-start | bytes 1671176 | tf_op jit(solution)/shard_map/ppermute | solution.py:321
  24.1 20.5 %collective-permute-start.14 = (bf16[96,2048]{1,0:T(8,128)(2,1)S(1)}, bf16[96,2048]{1,0:T(8,128)(2,1)S(1)}, u32[]{:S(2)}, u32[]{:S(2)}) collective-permute-start(bf16[96,2048]{1,0:T(8,128)(2,1)S(1)} %join.14.refs_1_), channel_id=1, source_target_pairs={{0,2},{1,3},{2,0},{3,1},{4,6},{5,7},{6,4},{7,5},{8,10},{9,11},{10,... | collective-permute-start | bytes 1179656 | tf_op jit(solution)/shard_map/ppermute | solution.py:324
  33.0 1.5 %collective-permute-start.11 = (bf16[48,2048]{1,0:T(8,128)(2,1)S(1)}, bf16[48,2048]{1,0:T(8,128)(2,1)S(1)}, u32[]{:S(2)}, u32[]{:S(2)}) collective-permute-start(bf16[48,2048]{1,0:T(8,128)(2,1)S(1)} %get-tuple-element.99), channel_id=1, source_target_pairs={{0,1},{1,0},{2,3},{3,2},{4,5},{5,4},{6,7},{7,6},{8,9},{9,8},{10,11... | collective-permute-start | bytes 589832 | tf_op jit(solution)/shard_map/ppermute | solution.py:327
  33.1 1.7 %collective-permute-start.12 = (bf16[48,2048]{1,0:T(8,128)(2,1)S(1)}, bf16[48,2048]{1,0:T(8,128)(2,1)S(1)}, u32[]{:S(2)}, u32[]{:S(2)}) collective-permute-start(bf16[48,2048]{1,0:T(8,128)(2,1)S(1)} %get-tuple-element.101), channel_id=1, source_target_pairs={{0,1},{1,0},{2,3},{3,2},{4,5},{5,4},{6,7},{7,6},{8,9},{9,8},{10,11... | collective-permute-start | bytes 589832 | tf_op jit(solution)/shard_map/ppermute | solution.py:327
  34.8 14.0 %collective-permute-start.19 = (bf16[96,2048]{1,0:T(8,128)(2,1)S(1)}, bf16[96,2048]{1,0:T(8,128)(2,1)S(1)}, u32[]{:S(2)}, u32[]{:S(2)}) collective-permute-start(bf16[96,2048]{1,0:T(8,128)(2,1)S(1)} %join.15.refs_10_), channel_id=1, source_target_pairs={{0,2},{1,3},{2,0},{3,1},{4,6},{5,7},{6,4},{7,5},{8,10},{9,11},{10,... | collective-permute-start | bytes 1179656 | tf_op jit(solution)/shard_map/ppermute | solution.py:324
  36.6 18.3 %collective-permute-start.18 = (bf16[128,2048]{1,0:T(8,128)(2,1)S(1)}, bf16[128,2048]{1,0:T(8,128)(2,1)S(1)}, u32[]{:S(2)}, u32[]{:S(2)}) collective-permute-start(bf16[128,2048]{1,0:T(8,128)(2,1)S(1)} %hold.10.refs_1_.refs_2_), channel_id=1, source_target_pairs={{0,4},{1,5},{2,6},{3,7},{4,8},{5,9},{6,10},{7,11},{8,12},{9,13},{1... | collective-permute-start | bytes 1572872 | tf_op jit(solution)/shard_map/ppermute | solution.py:321
  45.2 1.7 %collective-permute-start.16 = (bf16[48,2048]{1,0:T(8,128)(2,1)S(1)}, bf16[48,2048]{1,0:T(8,128)(2,1)S(1)}, u32[]{:S(2)}, u32[]{:S(2)}) collective-permute-start(bf16[48,2048]{1,0:T(8,128)(2,1)S(1)} %get-tuple-element.110), channel_id=1, source_target_pairs={{0,1},{1,0},{2,3},{3,2},{4,5},{5,4},{6,7},{7,6},{8,9},{9,8},{10,11... | collective-permute-start | bytes 589832 | tf_op jit(solution)/shard_map/ppermute | solution.py:327
  47.0 11.3 %collective-permute-start.17 = (bf16[96,2048]{1,0:T(8,128)(2,1)S(1)}, bf16[96,2048]{1,0:T(8,128)(2,1)S(1)}, u32[]{:S(2)}, u32[]{:S(2)}) collective-permute-start(bf16[96,2048]{1,0:T(8,128)(2,1)S(1)} %join.16.refs_10_), channel_id=1, source_target_pairs={{0,2},{1,3},{2,0},{3,1},{4,6},{5,7},{6,4},{7,5},{8,10},{9,11},{10,... | collective-permute-start | bytes 1179656 | tf_op jit(solution)/shard_map/ppermute | solution.py:324
  51.5 1.5 %collective-permute-start.20 = (bf16[32,2176]{1,0:T(8,128)(2,1)S(1)}, bf16[32,2176]{1,0:T(8,128)(2,1)S(1)}, u32[]{:S(2)}, u32[]{:S(2)}) collective-permute-start(bf16[32,2176]{1,0:T(8,128)(2,1)S(1)} %slice.38), channel_id=1, source_target_pairs={{0,1},{1,0},{2,3},{3,2},{4,5},{5,4},{6,7},{7,6},{8,9},{9,8},{10,11... | collective-permute-start | bytes 417800 | tf_op jit(solution)/shard_map/ppermute | solution.py:327
  52.0 17.3 %collective-permute-start.25 = (bf16[128,2176]{1,0:T(8,128)(2,1)S(1)}, bf16[128,2176]{1,0:T(8,128)(2,1)S(1)}, u32[]{:S(2)}, u32[]{:S(2)}) collective-permute-start(bf16[128,2176]{1,0:T(8,128)(2,1)S(1)} %hold.11.refs_1_.refs_2_), channel_id=1, source_target_pairs={{0,4},{1,5},{2,6},{3,7},{4,8},{5,9},{6,10},{7,11},{8,12},{9,13},{1... | collective-permute-start | bytes 1671176 | tf_op jit(solution)/shard_map/ppermute | solution.py:321
  55.3 2.1 %collective-permute-start.22 = (bf16[48,2048]{1,0:T(8,128)(2,1)S(1)}, bf16[48,2048]{1,0:T(8,128)(2,1)S(1)}, u32[]{:S(2)}, u32[]{:S(2)}) collective-permute-start(bf16[48,2048]{1,0:T(8,128)(2,1)S(1)} %get-tuple-element.118), channel_id=1, source_target_pairs={{0,1},{1,0},{2,3},{3,2},{4,5},{5,4},{6,7},{7,6},{8,9},{9,8},{10,11... | collective-permute-start | bytes 589832 | tf_op jit(solution)/shard_map/ppermute | solution.py:327
  55.4 2.0 %collective-permute-start.23 = (bf16[48,2048]{1,0:T(8,128)(2,1)S(1)}, bf16[48,2048]{1,0:T(8,128)(2,1)S(1)}, u32[]{:S(2)}, u32[]{:S(2)}) collective-permute-start(bf16[48,2048]{1,0:T(8,128)(2,1)S(1)} %get-tuple-element.120), channel_id=1, source_target_pairs={{0,1},{1,0},{2,3},{3,2},{4,5},{5,4},{6,7},{7,6},{8,9},{9,8},{10,11... | collective-permute-start | bytes 589832 | tf_op jit(solution)/shard_map/ppermute | solution.py:327
  55.9 13.4 %collective-permute-start.27 = (bf16[96,2176]{1,0:T(8,128)(2,1)S(1)}, bf16[96,2176]{1,0:T(8,128)(2,1)S(1)}, u32[]{:S(2)}, u32[]{:S(2)}) collective-permute-start(bf16[96,2176]{1,0:T(8,128)(2,1)S(1)} %join.17.refs_1_), channel_id=1, source_target_pairs={{0,2},{1,3},{2,0},{3,1},{4,6},{5,7},{6,4},{7,5},{8,10},{9,11},{10,... | collective-permute-start | bytes 1253384 | tf_op jit(solution)/shard_map/ppermute | solution.py:324
  58.4 21.3 %collective-permute-start.30 = (bf16[128,2048]{1,0:T(8,128)(2,1)S(1)}, bf16[128,2048]{1,0:T(8,128)(2,1)S(1)}, u32[]{:S(2)}, u32[]{:S(2)}) collective-permute-start(bf16[128,2048]{1,0:T(8,128)(2,1)S(1)} %hold.13.refs_1_), channel_id=1, source_target_pairs={{0,4},{1,5},{2,6},{3,7},{4,8},{5,9},{6,10},{7,11},{8,12},{9,13},{1... | collective-permute-start | bytes 1572872 | tf_op jit(solution)/shard_map/ppermute | solution.py:321
  58.6 1.9 %collective-permute-start.26 = (bf16[48,2176]{1,0:T(8,128)(2,1)S(1)}, bf16[48,2176]{1,0:T(8,128)(2,1)S(1)}, u32[]{:S(2)}, u32[]{:S(2)}) collective-permute-start(bf16[48,2176]{1,0:T(8,128)(2,1)S(1)} %get-tuple-element.121), channel_id=1, source_target_pairs={{0,1},{1,0},{2,3},{3,2},{4,5},{5,4},{6,7},{7,6},{8,9},{9,8},{10,11... | collective-permute-start | bytes 626696 | tf_op jit(solution)/shard_map/ppermute | solution.py:327
  58.7 18.1 %collective-permute-start.24 = (bf16[96,2048]{1,0:T(8,128)(2,1)S(1)}, bf16[96,2048]{1,0:T(8,128)(2,1)S(1)}, u32[]{:S(2)}, u32[]{:S(2)}) collective-permute-start(bf16[96,2048]{1,0:T(8,128)(2,1)S(1)} %join.18.refs_1_), channel_id=1, source_target_pairs={{0,2},{1,3},{2,0},{3,1},{4,6},{5,7},{6,4},{7,5},{8,10},{9,11},{10,... | collective-permute-start | bytes 1179656 | tf_op jit(solution)/shard_map/ppermute | solution.py:324
  69.9 9.5 %collective-permute-start.31 = (bf16[48,2048]{1,0:T(8,128)(2,1)S(1)}, bf16[48,2048]{1,0:T(8,128)(2,1)S(1)}, u32[]{:S(2)}, u32[]{:S(2)}) collective-permute-start(bf16[48,2048]{1,0:T(8,128)(2,1)S(1)} %get-tuple-element.132), channel_id=1, source_target_pairs={{0,1},{1,0},{2,3},{3,2},{4,5},{5,4},{6,7},{7,6},{8,9},{9,8},{10,11... | collective-permute-start | bytes 589832 | tf_op jit(solution)/shard_map/ppermute | solution.py:327
  70.0 1.8 %collective-permute-start.28 = (bf16[32,2048]{1,0:T(8,128)(2,1)S(1)}, bf16[32,2048]{1,0:T(8,128)(2,1)S(1)}, u32[]{:S(2)}, u32[]{:S(2)}) collective-permute-start(bf16[32,2048]{1,0:T(8,128)(2,1)S(1)} %slice.40), channel_id=1, source_target_pairs={{0,1},{1,0},{2,3},{3,2},{4,5},{5,4},{6,7},{7,6},{8,9},{9,8},{10,11... | collective-permute-start | bytes 393224 | tf_op jit(solution)/shard_map/ppermute | solution.py:327
  71.9 12.5 %collective-permute-start.34 = (bf16[96,2048]{1,0:T(8,128)(2,1)S(1)}, bf16[96,2048]{1,0:T(8,128)(2,1)S(1)}, u32[]{:S(2)}, u32[]{:S(2)}) collective-permute-start(bf16[96,2048]{1,0:T(8,128)(2,1)S(1)} %join.19.refs_10_), channel_id=1, source_target_pairs={{0,2},{1,3},{2,0},{3,1},{4,6},{5,7},{6,4},{7,5},{8,10},{9,11},{10,... | collective-permute-start | bytes 1179656 | tf_op jit(solution)/shard_map/ppermute | solution.py:324
  80.1 1.7 %collective-permute-start.33 = (bf16[48,2048]{1,0:T(8,128)(2,1)S(1)}, bf16[48,2048]{1,0:T(8,128)(2,1)S(1)}, u32[]{:S(2)}, u32[]{:S(2)}) collective-permute-start(bf16[48,2048]{1,0:T(8,128)(2,1)S(1)} %get-tuple-element.136), channel_id=1, source_target_pairs={{0,1},{1,0},{2,3},{3,2},{4,5},{5,4},{6,7},{7,6},{8,9},{9,8},{10,11... | collective-permute-start | bytes 589832 | tf_op jit(solution)/shard_map/ppermute | solution.py:327
  81.9 12.0 %collective-permute-start.41 = (bf16[96,2048]{1,0:T(8,128)(2,1)S(1)}, bf16[96,2048]{1,0:T(8,128)(2,1)S(1)}, u32[]{:S(2)}, u32[]{:S(2)}) collective-permute-start(bf16[96,2048]{1,0:T(8,128)(2,1)S(1)} %join.20.refs_4_), channel_id=1, source_target_pairs={{0,2},{1,3},{2,0},{3,1},{4,6},{5,7},{6,4},{7,5},{8,10},{9,11},{10,... | collective-permute-start | bytes 1179656 | tf_op jit(solution)/shard_map/ppermute | solution.py:324
  84.4 2.2 %collective-permute-start.37 = (bf16[48,2176]{1,0:T(8,128)(2,1)S(1)}, bf16[48,2176]{1,0:T(8,128)(2,1)S(1)}, u32[]{:S(2)}, u32[]{:S(2)}) collective-permute-start(bf16[48,2176]{1,0:T(8,128)(2,1)S(1)} %get-tuple-element.140), channel_id=1, source_target_pairs={{0,1},{1,0},{2,3},{3,2},{4,5},{5,4},{6,7},{7,6},{8,9},{9,8},{10,11... | collective-permute-start | bytes 626696 | tf_op jit(solution)/shard_map/ppermute | solution.py:327
  84.4 2.2 %collective-permute-start.35 = (bf16[32,2176]{1,0:T(8,128)(2,1)S(1)}, bf16[32,2176]{1,0:T(8,128)(2,1)S(1)}, u32[]{:S(2)}, u32[]{:S(2)}) collective-permute-start(bf16[32,2176]{1,0:T(8,128)(2,1)S(1)} %slice.42), channel_id=1, source_target_pairs={{0,1},{1,0},{2,3},{3,2},{4,5},{5,4},{6,7},{7,6},{8,9},{9,8},{10,11... | collective-permute-start | bytes 417800 | tf_op jit(solution)/shard_map/ppermute | solution.py:327
  85.0 17.9 %collective-permute-start.48 = (bf16[128,2176]{1,0:T(8,128)(2,1)S(1)}, bf16[128,2176]{1,0:T(8,128)(2,1)S(1)}, u32[]{:S(2)}, u32[]{:S(2)}) collective-permute-start(bf16[128,2176]{1,0:T(8,128)(2,1)S(1)} %home.7.refs_4_), channel_id=1, source_target_pairs={{0,4},{1,5},{2,6},{3,7},{4,8},{5,9},{6,10},{7,11},{8,12},{9,13},{1... | collective-permute-start | bytes 1671176 | tf_op jit(solution)/shard_map/ppermute | solution.py:321
  86.6 10.6 %collective-permute-start.38 = (bf16[48,2176]{1,0:T(8,128)(2,1)S(1)}, bf16[48,2176]{1,0:T(8,128)(2,1)S(1)}, u32[]{:S(2)}, u32[]{:S(2)}) collective-permute-start(bf16[48,2176]{1,0:T(8,128)(2,1)S(1)} %get-tuple-element.142), channel_id=1, source_target_pairs={{0,1},{1,0},{2,3},{3,2},{4,5},{5,4},{6,7},{7,6},{8,9},{9,8},{10,11... | collective-permute-start | bytes 626696 | tf_op jit(solution)/shard_map/ppermute | solution.py:327
  86.9 16.0 %collective-permute-start.47 = (bf16[96,2176]{1,0:T(8,128)(2,1)S(1)}, bf16[96,2176]{1,0:T(8,128)(2,1)S(1)}, u32[]{:S(2)}, u32[]{:S(2)}) collective-permute-start(bf16[96,2176]{1,0:T(8,128)(2,1)S(1)} %join.21.refs_4_), channel_id=1, source_target_pairs={{0,2},{1,3},{2,0},{3,1},{4,6},{5,7},{6,4},{7,5},{8,10},{9,11},{10,... | collective-permute-start | bytes 1253384 | tf_op jit(solution)/shard_map/ppermute | solution.py:324
  88.6 8.5 %collective-permute-start.39 = (bf16[32,2176]{1,0:T(8,128)(2,1)S(1)}, bf16[32,2176]{1,0:T(8,128)(2,1)S(1)}, u32[]{:S(2)}, u32[]{:S(2)}) collective-permute-start(bf16[32,2176]{1,0:T(8,128)(2,1)S(1)} %slice.44), channel_id=1, source_target_pairs={{0,1},{1,0},{2,3},{3,2},{4,5},{5,4},{6,7},{7,6},{8,9},{9,8},{10,11... | collective-permute-start | bytes 417800 | tf_op jit(solution)/shard_map/ppermute | solution.py:327
  93.9 2.6 %collective-permute-start.40 = (bf16[16,2176]{1,0:T(8,128)(2,1)S(1)}, bf16[16,2176]{1,0:T(8,128)(2,1)S(1)}, u32[]{:S(2)}, u32[]{:S(2)}) collective-permute-start(bf16[16,2176]{1,0:T(8,128)(2,1)S(1)} %slice.45), channel_id=1, source_target_pairs={{0,1},{1,0},{2,3},{3,2},{4,5},{5,4},{6,7},{7,6},{8,9},{9,8},{10,11... | collective-permute-start | bytes 208904 | tf_op jit(solution)/shard_map/ppermute | solution.py:327
  96.5 1.9 %collective-permute-start.42 = (bf16[32,2176]{1,0:T(8,128)(2,1)S(1)}, bf16[32,2176]{1,0:T(8,128)(2,1)S(1)}, u32[]{:S(2)}, u32[]{:S(2)}) collective-permute-start(bf16[32,2176]{1,0:T(8,128)(2,1)S(1)} %slice.46), channel_id=1, source_target_pairs={{0,1},{1,0},{2,3},{3,2},{4,5},{5,4},{6,7},{7,6},{8,9},{9,8},{10,11... | collective-permute-start | bytes 417800 | tf_op jit(solution)/shard_map/ppermute | solution.py:327
  97.2 2.6 %collective-permute-start.44 = (bf16[48,2176]{1,0:T(8,128)(2,1)S(1)}, bf16[48,2176]{1,0:T(8,128)(2,1)S(1)}, u32[]{:S(2)}, u32[]{:S(2)}) collective-permute-start(bf16[48,2176]{1,0:T(8,128)(2,1)S(1)} %get-tuple-element.149), channel_id=1, source_target_pairs={{0,1},{1,0},{2,3},{3,2},{4,5},{5,4},{6,7},{7,6},{8,9},{9,8},{10,11... | collective-permute-start | bytes 626696 | tf_op jit(solution)/shard_map/ppermute | solution.py:327
  98.5 15.0 %collective-permute-start.46 = (bf16[96,2176]{1,0:T(8,128)(2,1)S(1)}, bf16[96,2176]{1,0:T(8,128)(2,1)S(1)}, u32[]{:S(2)}, u32[]{:S(2)}) collective-permute-start(bf16[96,2176]{1,0:T(8,128)(2,1)S(1)} %join.22.refs_3_), channel_id=1, source_target_pairs={{0,2},{1,3},{2,0},{3,1},{4,6},{5,7},{6,4},{7,5},{8,10},{9,11},{10,... | collective-permute-start | bytes 1253384 | tf_op jit(solution)/shard_map/ppermute | solution.py:324
  103.1 10.4 %collective-permute-start.49 = (bf16[128,896]{1,0:T(8,128)(2,1)S(1)}, bf16[128,896]{1,0:T(8,128)(2,1)S(1)}, u32[]{:S(2)}, u32[]{:S(2)}) collective-permute-start(bf16[128,896]{1,0:T(8,128)(2,1)S(1)} %home.8.refs_5_), channel_id=1, source_target_pairs={{0,4},{1,5},{2,6},{3,7},{4,8},{5,9},{6,10},{7,11},{8,12},{9,13},{1... | collective-permute-start | bytes 688136 | tf_op jit(solution)/shard_map/ppermute | solution.py:321
  103.2 24.7 %collective-permute-start.45 = (bf16[96,2176]{1,0:T(8,128)(2,1)S(1)}, bf16[96,2176]{1,0:T(8,128)(2,1)S(1)}, u32[]{:S(2)}, u32[]{:S(2)}) collective-permute-start(bf16[96,2176]{1,0:T(8,128)(2,1)S(1)} %join.23.refs_5_), channel_id=1, source_target_pairs={{0,2},{1,3},{2,0},{3,1},{4,6},{5,7},{6,4},{7,5},{8,10},{9,11},{10,... | collective-permute-start | bytes 1253384 | tf_op jit(solution)/shard_map/ppermute | solution.py:324
  105.3 12.4 %collective-permute-start.51 = (bf16[128,768]{1,0:T(8,128)(2,1)S(1)}, bf16[128,768]{1,0:T(8,128)(2,1)S(1)}, u32[]{:S(2)}, u32[]{:S(2)}) collective-permute-start(bf16[128,768]{1,0:T(8,128)(2,1)S(1)} %home.9.refs_5_), channel_id=1, source_target_pairs={{0,4},{1,5},{2,6},{3,7},{4,8},{5,9},{6,10},{7,11},{8,12},{9,13},{1... | collective-permute-start | bytes 589832 | tf_op jit(solution)/shard_map/ppermute | solution.py:321
  107.4 13.1 %collective-permute-start.53 = (bf16[128,512]{1,0:T(8,128)(2,1)S(1)}, bf16[128,512]{1,0:T(8,128)(2,1)S(1)}, u32[]{:S(2)}, u32[]{:S(2)}) collective-permute-start(bf16[128,512]{1,0:T(8,128)(2,1)S(1)} %home.10.refs_5_), channel_id=1, source_target_pairs={{0,4},{1,5},{2,6},{3,7},{4,8},{5,9},{6,10},{7,11},{8,12},{9,13},{1... | collective-permute-start | bytes 393224 | tf_op jit(solution)/shard_map/ppermute | solution.py:321
  113.8 16.4 %collective-permute-start.50 = (bf16[128,896]{1,0:T(8,128)(2,1)S(1)}, bf16[128,896]{1,0:T(8,128)(2,1)S(1)}, u32[]{:S(2)}, u32[]{:S(2)}) collective-permute-start(bf16[128,896]{1,0:T(8,128)(2,1)S(1)} %home.11.refs_5_), channel_id=1, source_target_pairs={{0,4},{1,5},{2,6},{3,7},{4,8},{5,9},{6,10},{7,11},{8,12},{9,13},{1... | collective-permute-start | bytes 688136 | tf_op jit(solution)/shard_map/ppermute | solution.py:321
  117.9 12.2 %collective-permute-start.52 = (bf16[128,768]{1,0:T(8,128)(2,1)S(1)}, bf16[128,768]{1,0:T(8,128)(2,1)S(1)}, u32[]{:S(2)}, u32[]{:S(2)}) collective-permute-start(bf16[128,768]{1,0:T(8,128)(2,1)S(1)} %home.12.refs_5_), channel_id=1, source_target_pairs={{0,4},{1,5},{2,6},{3,7},{4,8},{5,9},{6,10},{7,11},{8,12},{9,13},{1... | collective-permute-start | bytes 589832 | tf_op jit(solution)/shard_map/ppermute | solution.py:321
  120.7 9.4 %collective-permute-start.54 = (bf16[128,512]{1,0:T(8,128)(2,1)S(1)}, bf16[128,512]{1,0:T(8,128)(2,1)S(1)}, u32[]{:S(2)}, u32[]{:S(2)}) collective-permute-start(bf16[128,512]{1,0:T(8,128)(2,1)S(1)} %home.13.refs_32_), channel_id=1, source_target_pairs={{0,4},{1,5},{2,6},{3,7},{4,8},{5,9},{6,10},{7,11},{8,12},{9,13},{1... | collective-permute-start | bytes 393224 | tf_op jit(solution)/shard_map/ppermute | solution.py:321
  (14 other events, 60.2 us)

commit v5 on v4

--- a/solution.py
+++ b/solution.py
@@ -317,8 +317,12 @@
     gate_mat, up_mat, down_mat = w_gate[0], w_up[0], w_down[0]
     run = Chain()
 
+    ring = [*range(0, planes, 2), *range(1, planes, 2)[::-1]]
+    follows = dict(zip(ring, ring[1:] + ring[:1]))
+
     def along(array):
-        return lax.ppermute(array, "expert", [(i, (i + PLANE) % devices) for i in range(devices)])
+        pairs = [(i, follows[i // PLANE] * PLANE + i % PLANE) for i in range(devices)]
+        return lax.ppermute(array, "expert", pairs)
 
     def across(array):
         return lax.ppermute(array, "expert", [(i, i ^ 2) for i in range(devices)])

time: 132 us -> 129 us (0.977)
  waiting for transfers between devices: 66.8 us -> 42.3 us
  starting transfers between devices: 35.7 us -> 57.9 us
    ppermute x13, starting transfers between devices: 10.5 us -> 34.5 us  [along(): return lax.ppermute(array, 'expert', pairs)]
    ppermute x13, waiting for transfers between devices: 36.4 us -> 13.3 us  [along(): return lax.ppermute(array, 'expert', pairs)]
    ppermute x12, starting transfers between devices: 17.7 us -> 16 us  [across(): return lax.ppermute(array, 'expert', [(i, i ^ 2) for i in range(devices)])]
  transfers between devices with their start and end apart: 55 -> 55, of which waited for: 27 -> 24; matrix products, arithmetic and copies ran while one was open for 0% -> 0% of each run, Pallas kernels for 18% -> 18%
where the time goes in v5:
time: 129 us
  starting transfers between devices  57.9 us (45%)
  waiting for transfers between devices  42.3 us (33%)
  Pallas kernels  26.4 us (20%)
    ppermute x13, starting transfers between devices, along(): return lax.ppermute(array, 'expert', pairs)  34.5 us
    pallas_call x34, Pallas kernels, __call__(): pl.pallas_call(body, out_shape=[jax.ShapeDtypeStruct(shape, kind) for sha...  26.4 us
    ppermute x12, waiting for transfers between devices, across(): return lax.ppermute(array, 'expert', [(i, i ^ 2) for i in range(devices)])  20.9 us
    ppermute x12, starting transfers between devices, across(): return lax.ppermute(array, 'expert', [(i, i ^ 2) for i in range(devices)])  16 us
    ppermute x13, waiting for transfers between devices, along(): return lax.ppermute(array, 'expert', pairs)  13.3 us
    ppermute x30, waiting for transfers between devices, cores(): return lax.ppermute(array, 'expert', [(i, i ^ 1) for i in range(devices)])  8.11 us
    ppermute x30, starting transfers between devices, cores(): return lax.ppermute(array, 'expert', [(i, i ^ 1) for i in range(devices)])  7.41 us
  transfers between devices with their start and end apart: 55, of which 24 were waited for; matrix products, arithmetic and copies ran while one was open for 0% of the time, Pallas kernels for 18%

profile of v5, /device:TPU:0, one launch (start us, length us, event | category | flops | bytes accessed | tf_op | source)
XLA Modules:
  0.0 128.9 jit_solution(10091944828754099039)
XLA Ops:
  0.6 2.0 %pack.1.refs_1_.refs_2_ = bf16[128,2176]{1,0:T(8,128)(2,1)} custom-call(s32[4,128]{1,0:T(4,128)} %bitcast.22, s32[4,128]{1,0:T(4,128)} %bitcast.24, bf16[128,2048]{1,0:T(8,128)(2,1)} %refs_2_.1), custom_call_target="tpu_custom_call" | custom-call | flops 1000 | bytes 1000 | tf_op jit(solution)/shard_map/pack/pallas_call | solution.py:130
  2.6 4.1 %collective-permute-start.7 = (bf16[128,2176]{1,0:T(8,128)(2,1)}, bf16[128,2176]{1,0:T(8,128)(2,1)S(1)}, u32[]{:S(2)}, u32[]{:S(2)}) collective-permute-start(bf16[128,2176]{1,0:T(8,128)(2,1)} %pack.1.refs_1_.refs_2_), channel_id=1, source_target_pairs={{0,8},{1,9},{2,10},{3,11},{4,0},{5,1},{6,2},{7,3},{8,12},{9,13},{1... | collective-permute-start | bytes 1671176 | tf_op jit(solution)/shard_map/ppermute | solution.py:325
  6.7 1.1 copy-done.3
  9.1 1.2 collective-permute-done.2.refs_2_
  10.3 1.6 %collective-permute-start.3 = (bf16[96,2048]{1,0:T(8,128)(2,1)S(1)}, bf16[96,2048]{1,0:T(8,128)(2,1)S(1)}, u32[]{:S(2)}, u32[]{:S(2)}) collective-permute-start(bf16[96,2048]{1,0:T(8,128)(2,1)S(1)} %join.12.refs_2_), channel_id=1, source_target_pairs={{0,2},{1,3},{2,0},{3,1},{4,6},{5,7},{6,4},{7,5},{8,10},{9,11},{10,... | collective-permute-start | bytes 1179656 | tf_op jit(solution)/shard_map/ppermute | solution.py:328
  12.8 1.6 %collective-permute-start.8 = (bf16[128,2048]{1,0:T(8,128)(2,1)S(1)}, bf16[128,2048]{1,0:T(8,128)(2,1)S(1)}, u32[]{:S(2)}, u32[]{:S(2)}) collective-permute-start(bf16[128,2048]{1,0:T(8,128)(2,1)S(1)} %copy-done.4), channel_id=1, source_target_pairs={{0,8},{1,9},{2,10},{3,11},{4,0},{5,1},{6,2},{7,3},{8,12},{9,13},{1... | collective-permute-start | bytes 1572872 | tf_op jit(solution)/shard_map/ppermute | solution.py:325
  15.0 7.3 %collective-permute-done.3.refs_2_.refs_3_ = bf16[96,2048]{1,0:T(8,128)(2,1)S(1)} collective-permute-done((bf16[96,2048]{1,0:T(8,128)(2,1)S(1)}, bf16[96,2048]{1,0:T(8,128)(2,1)S(1)}, u32[]{:S(2)}, u32[]{:S(2)}) %collective-permute-start.3) | collective-permute-done | bytes 393248 | tf_op jit(solution)/shard_map/ppermute | solution.py:328
  23.5 1.6 %collective-permute-start.13 = (bf16[128,2176]{1,0:T(8,128)(2,1)S(1)}, bf16[128,2176]{1,0:T(8,128)(2,1)S(1)}, u32[]{:S(2)}, u32[]{:S(2)}) collective-permute-start(bf16[128,2176]{1,0:T(8,128)(2,1)S(1)} %hold.9.refs_1_.refs_2_), channel_id=1, source_target_pairs={{0,8},{1,9},{2,10},{3,11},{4,0},{5,1},{6,2},{7,3},{8,12},{9,13},{1... | collective-permute-start | bytes 1671176 | tf_op jit(solution)/shard_map/ppermute | solution.py:325
  25.1 1.6 %collective-permute-start.14 = (bf16[96,2048]{1,0:T(8,128)(2,1)S(1)}, bf16[96,2048]{1,0:T(8,128)(2,1)S(1)}, u32[]{:S(2)}, u32[]{:S(2)}) collective-permute-start(bf16[96,2048]{1,0:T(8,128)(2,1)S(1)} %join.14.refs_1_), channel_id=1, source_target_pairs={{0,2},{1,3},{2,0},{3,1},{4,6},{5,7},{6,4},{7,5},{8,10},{9,11},{10,... | collective-permute-start | bytes 1179656 | tf_op jit(solution)/shard_map/ppermute | solution.py:328
  26.7 4.5 %collective-permute-done.8.refs_0_ = bf16[128,2048]{1,0:T(8,128)(2,1)S(1)} collective-permute-done((bf16[128,2048]{1,0:T(8,128)(2,1)S(1)}, bf16[128,2048]{1,0:T(8,128)(2,1)S(1)}, u32[]{:S(2)}, u32[]{:S(2)}) %collective-permute-start.8) | collective-permute-done | bytes 524320 | tf_op jit(solution)/shard_map/ppermute | solution.py:325
  32.1 0.9 collective-permute-done.11.refs_1_
  33.4 1.6 %collective-permute-start.19 = (bf16[96,2048]{1,0:T(8,128)(2,1)S(1)}, bf16[96,2048]{1,0:T(8,128)(2,1)S(1)}, u32[]{:S(2)}, u32[]{:S(2)}) collective-permute-start(bf16[96,2048]{1,0:T(8,128)(2,1)S(1)} %join.15.refs_10_), channel_id=1, source_target_pairs={{0,2},{1,3},{2,0},{3,1},{4,6},{5,7},{6,4},{7,5},{8,10},{9,11},{10,... | collective-permute-start | bytes 1179656 | tf_op jit(solution)/shard_map/ppermute | solution.py:328
  34.9 3.4 %collective-permute-start.18 = (bf16[128,2048]{1,0:T(8,128)(2,1)S(1)}, bf16[128,2048]{1,0:T(8,128)(2,1)S(1)}, u32[]{:S(2)}, u32[]{:S(2)}) collective-permute-start(bf16[128,2048]{1,0:T(8,128)(2,1)S(1)} %hold.10.refs_1_.refs_2_), channel_id=1, source_target_pairs={{0,8},{1,9},{2,10},{3,11},{4,0},{5,1},{6,2},{7,3},{8,12},{9,13},{1... | collective-permute-start | bytes 1572872 | tf_op jit(solution)/shard_map/ppermute | solution.py:325
  38.3 2.6 %expert.4 = (bf16[192,768]{1,0:T(8,128)(2,1)S(1)}, bf16[192,384]{1,0:T(8,128)(2,1)S(1)}, bf16[48,2176]{1,0:T(8,128)(2,1)S(1)}, bf16[48,2176]{1,0:T(8,128)(2,1)S(...) custom-call(s32[1]{0:T(128)} %bitcast.2.refs_0_, bf16[48,2048]{1,0:T(8,128)(2,1)S(1)} %get-tuple-element.84.refs_1_.refs_0_, ...), custom_call_target="tpu_custom_call" | custom-call | flops 1000 | bytes 1000 | tf_op jit(solution)/shard_map/expert/pallas_call | solution.py:130
  41.0 2.2 %collective-permute-done.13.refs_0_ = bf16[128,2176]{1,0:T(8,128)(2,1)S(1)} collective-permute-done((bf16[128,2176]{1,0:T(8,128)(2,1)S(1)}, bf16[128,2176]{1,0:T(8,128)(2,1)S(1)}, u32[]{:S(2)}, u32[]{:S(2)}) %collective-permute-start.13) | collective-permute-done | bytes 557088 | tf_op jit(solution)/shard_map/ppermute | solution.py:325
  44.3 0.9 collective-permute-done.15.refs_3_.refs_2_.refs_7_
  45.5 1.6 %collective-permute-start.17 = (bf16[96,2048]{1,0:T(8,128)(2,1)S(1)}, bf16[96,2048]{1,0:T(8,128)(2,1)S(1)}, u32[]{:S(2)}, u32[]{:S(2)}) collective-permute-start(bf16[96,2048]{1,0:T(8,128)(2,1)S(1)} %join.16.refs_10_), channel_id=1, source_target_pairs={{0,2},{1,3},{2,0},{3,1},{4,6},{5,7},{6,4},{7,5},{8,10},{9,11},{10,... | collective-permute-start | bytes 1179656 | tf_op jit(solution)/shard_map/ppermute | solution.py:328
  47.1 2.6 %expert.5 = (bf16[192,768]{1,0:T(8,128)(2,1)S(1)}, bf16[192,384]{1,0:T(8,128)(2,1)S(1)}, bf16[48,2176]{1,0:T(8,128)(2,1)S(1)}, bf16[48,2176]{1,0:T(8,128)(2,1)S(...) custom-call(s32[1]{0:T(128)} %bitcast.2.refs_0_, ...), custom_call_target="tpu_custom_call" | custom-call | flops 1000 | bytes 1000 | tf_op jit(solution)/shard_map/expert/pallas_call | solution.py:130
  50.4 3.4 %collective-permute-start.25 = (bf16[128,2176]{1,0:T(8,128)(2,1)S(1)}, bf16[128,2176]{1,0:T(8,128)(2,1)S(1)}, u32[]{:S(2)}, u32[]{:S(2)}) collective-permute-start(bf16[128,2176]{1,0:T(8,128)(2,1)S(1)} %hold.11.refs_1_.refs_2_), channel_id=1, source_target_pairs={{0,8},{1,9},{2,10},{3,11},{4,0},{5,1},{6,2},{7,3},{8,12},{9,13},{1... | collective-permute-start | bytes 1671176 | tf_op jit(solution)/shard_map/ppermute | solution.py:325
  54.7 1.1 collective-permute-start.27
  56.0 0.9 collective-permute-done.17.refs_3_.refs_8_
  56.9 3.6 %collective-permute-start.30 = (bf16[128,2048]{1,0:T(8,128)(2,1)S(1)}, bf16[128,2048]{1,0:T(8,128)(2,1)S(1)}, u32[]{:S(2)}, u32[]{:S(2)}) collective-permute-start(bf16[128,2048]{1,0:T(8,128)(2,1)S(1)} %hold.13.refs_1_), channel_id=1, source_target_pairs={{0,8},{1,9},{2,10},{3,11},{4,0},{5,1},{6,2},{7,3},{8,12},{9,13},{1... | collective-permute-start | bytes 1572872 | tf_op jit(solution)/shard_map/ppermute | solution.py:325
  60.5 1.5 %collective-permute-start.24 = (bf16[96,2048]{1,0:T(8,128)(2,1)S(1)}, bf16[96,2048]{1,0:T(8,128)(2,1)S(1)}, u32[]{:S(2)}, u32[]{:S(2)}) collective-permute-start(bf16[96,2048]{1,0:T(8,128)(2,1)S(1)} %join.18.refs_1_), channel_id=1, source_target_pairs={{0,2},{1,3},{2,0},{3,1},{4,6},{5,7},{6,4},{7,5},{8,10},{9,11},{10,... | collective-permute-start | bytes 1179656 | tf_op jit(solution)/shard_map/ppermute | solution.py:328
  62.0 4.7 %collective-permute-done.25.refs_0_ = bf16[128,2176]{1,0:T(8,128)(2,1)S(1)} collective-permute-done((bf16[128,2176]{1,0:T(8,128)(2,1)S(1)}, bf16[128,2176]{1,0:T(8,128)(2,1)S(1)}, u32[]{:S(2)}, u32[]{:S(2)}) %collective-permute-start.25) | collective-permute-done | bytes 557088 | tf_op jit(solution)/shard_map/ppermute | solution.py:325
  68.6 1.2 collective-permute-done.29.refs_2_
  69.8 1.2 collective-permute-start.34
  71.0 4.7 %collective-permute-done.24.refs_6_.refs_3_.refs_20_ = bf16[96,2048]{1,0:T(8,128)(2,1)S(1)} collective-permute-done((bf16[96,2048]{1,0:T(8,128)(2,1)S(1)}, bf16[96,2048]{1,0:T(8,128)(2,1)S(1)}, u32[]{:S(2)}, u32[]{:S(2)}) %collective-permute-start.24) | collective-permute-done | bytes 393248 | tf_op jit(solution)/shard_map/ppermute | solution.py:328
  75.7 2.6 %expert.6 = (bf16[192,768]{1,0:T(8,128)(2,1)S(1)}, bf16[192,384]{1,0:T(8,128)(2,1)S(1)}, bf16[48,2176]{1,0:T(8,128)(2,1)S(1)}, bf16[48,2176]{1,0:T(8,128)(2,1)S(...) custom-call(s32[1]{0:T(128)} %bitcast.2.refs_0_, ...), custom_call_target="tpu_custom_call" | custom-call | flops 1000 | bytes 1000 | tf_op jit(solution)/shard_map/expert/pallas_call | solution.py:130
  79.2 0.9 collective-permute-done.32.refs_1_
  80.5 1.2 collective-permute-start.41
  82.0 1.2 collective-permute-done.34.refs_5_.refs_3_.refs_11_
  83.8 2.8 %collective-permute-start.48 = (bf16[128,2176]{1,0:T(8,128)(2,1)S(1)}, bf16[128,2176]{1,0:T(8,128)(2,1)S(1)}, u32[]{:S(2)}, u32[]{:S(2)}) collective-permute-start(bf16[128,2176]{1,0:T(8,128)(2,1)S(1)} %home.7.refs_4_), channel_id=1, source_target_pairs={{0,8},{1,9},{2,10},{3,11},{4,0},{5,1},{6,2},{7,3},{8,12},{9,13},{1... | collective-permute-start | bytes 1671176 | tf_op jit(solution)/shard_map/ppermute | solution.py:325
  86.7 1.3 collective-permute-done.36.refs_2_
  88.2 1.7 %collective-permute-start.47 = (bf16[96,2176]{1,0:T(8,128)(2,1)S(1)}, bf16[96,2176]{1,0:T(8,128)(2,1)S(1)}, u32[]{:S(2)}, u32[]{:S(2)}) collective-permute-start(bf16[96,2176]{1,0:T(8,128)(2,1)S(1)} %join.21.refs_4_), channel_id=1, source_target_pairs={{0,2},{1,3},{2,0},{3,1},{4,6},{5,7},{6,4},{7,5},{8,10},{9,11},{10,... | collective-permute-start | bytes 1253384 | tf_op jit(solution)/shard_map/ppermute | solution.py:328
  90.0 2.4 %collective-permute-done.41.refs_6_.refs_23_ = bf16[96,2048]{1,0:T(8,128)(2,1)S(1)} collective-permute-done((bf16[96,2048]{1,0:T(8,128)(2,1)S(1)}, bf16[96,2048]{1,0:T(8,128)(2,1)S(1)}, u32[]{:S(2)}, u32[]{:S(2)}) %collective-permute-start.41) | collective-permute-done | bytes 393248 | tf_op jit(solution)/shard_map/ppermute | solution.py:328
  92.4 2.6 %expert.7 = (bf16[192,768]{1,0:T(8,128)(2,1)S(1)}, bf16[192,384]{1,0:T(8,128)(2,1)S(1)}, bf16[48,2176]{1,0:T(8,128)(2,1)S(1)}, bf16[48,2176]{1,0:T(8,128)(2,1)S(...) custom-call(s32[1]{0:T(128)} %bitcast.2.refs_0_, ...), custom_call_target="tpu_custom_call" | custom-call | flops 1000 | bytes 1000 | tf_op jit(solution)/shard_map/expert/pallas_call | solution.py:130
  96.2 0.7 collective-permute-done.43.refs_2_
  97.0 0.6 collective-permute-start.46
  97.7 3.7 %collective-permute-done.47.refs_3_ = bf16[96,2176]{1,0:T(8,128)(2,1)S(1)} collective-permute-done((bf16[96,2176]{1,0:T(8,128)(2,1)S(1)}, bf16[96,2176]{1,0:T(8,128)(2,1)S(1)}, u32[]{:S(2)}, u32[]{:S(2)}) %collective-permute-start.47) | collective-permute-done | bytes 417824 | tf_op jit(solution)/shard_map/ppermute | solution.py:328
  101.6 2.9 %collective-permute-start.49 = (bf16[128,896]{1,0:T(8,128)(2,1)S(1)}, bf16[128,896]{1,0:T(8,128)(2,1)S(1)}, u32[]{:S(2)}, u32[]{:S(2)}) collective-permute-start(bf16[128,896]{1,0:T(8,128)(2,1)S(1)} %home.8.refs_5_), channel_id=1, source_target_pairs={{0,8},{1,9},{2,10},{3,11},{4,0},{5,1},{6,2},{7,3},{8,12},{9,13},{1... | collective-permute-start | bytes 688136 | tf_op jit(solution)/shard_map/ppermute | solution.py:325
  104.5 1.7 %collective-permute-start.45 = (bf16[96,2176]{1,0:T(8,128)(2,1)S(1)}, bf16[96,2176]{1,0:T(8,128)(2,1)S(1)}, u32[]{:S(2)}, u32[]{:S(2)}) collective-permute-start(bf16[96,2176]{1,0:T(8,128)(2,1)S(1)} %join.23.refs_5_), channel_id=1, source_target_pairs={{0,2},{1,3},{2,0},{3,1},{4,6},{5,7},{6,4},{7,5},{8,10},{9,11},{10,... | collective-permute-start | bytes 1253384 | tf_op jit(solution)/shard_map/ppermute | solution.py:328
  106.5 1.7 %collective-permute-start.51 = (bf16[128,768]{1,0:T(8,128)(2,1)S(1)}, bf16[128,768]{1,0:T(8,128)(2,1)S(1)}, u32[]{:S(2)}, u32[]{:S(2)}) collective-permute-start(bf16[128,768]{1,0:T(8,128)(2,1)S(1)} %home.9.refs_5_), channel_id=1, source_target_pairs={{0,8},{1,9},{2,10},{3,11},{4,0},{5,1},{6,2},{7,3},{8,12},{9,13},{1... | collective-permute-start | bytes 589832 | tf_op jit(solution)/shard_map/ppermute | solution.py:325
  108.8 1.4 %collective-permute-done.49.refs_4_ = bf16[128,896]{1,0:T(8,128)(2,1)S(1)} collective-permute-done((bf16[128,896]{1,0:T(8,128)(2,1)S(1)}, bf16[128,896]{1,0:T(8,128)(2,1)S(1)}, u32[]{:S(2)}, u32[]{:S(2)}) %collective-permute-start.49) | collective-permute-done | bytes 229408 | tf_op jit(solution)/shard_map/ppermute | solution.py:325
  110.6 3.2 %collective-permute-start.50 = (bf16[128,896]{1,0:T(8,128)(2,1)S(1)}, bf16[128,896]{1,0:T(8,128)(2,1)S(1)}, u32[]{:S(2)}, u32[]{:S(2)}) collective-permute-start(bf16[128,896]{1,0:T(8,128)(2,1)S(1)} %home.11.refs_5_), channel_id=1, source_target_pairs={{0,8},{1,9},{2,10},{3,11},{4,0},{5,1},{6,2},{7,3},{8,12},{9,13},{1... | collective-permute-start | bytes 688136 | tf_op jit(solution)/shard_map/ppermute | solution.py:325
  114.7 3.3 %collective-permute-start.52 = (bf16[128,768]{1,0:T(8,128)(2,1)S(1)}, bf16[128,768]{1,0:T(8,128)(2,1)S(1)}, u32[]{:S(2)}, u32[]{:S(2)}) collective-permute-start(bf16[128,768]{1,0:T(8,128)(2,1)S(1)} %home.12.refs_5_), channel_id=1, source_target_pairs={{0,8},{1,9},{2,10},{3,11},{4,0},{5,1},{6,2},{7,3},{8,12},{9,13},{1... | collective-permute-start | bytes 589832 | tf_op jit(solution)/shard_map/ppermute | solution.py:325
  118.2 2.6 %collective-permute-start.54 = (bf16[128,512]{1,0:T(8,128)(2,1)S(1)}, bf16[128,512]{1,0:T(8,128)(2,1)S(1)}, u32[]{:S(2)}, u32[]{:S(2)}) collective-permute-start(bf16[128,512]{1,0:T(8,128)(2,1)S(1)} %home.13.refs_32_), channel_id=1, source_target_pairs={{0,8},{1,9},{2,10},{3,11},{4,0},{5,1},{6,2},{7,3},{8,12},{9,13},{1... | collective-permute-start | bytes 393224 | tf_op jit(solution)/shard_map/ppermute | solution.py:325
  120.8 7.0 %deltas.1 = (bf16[2048,384]{1,0:T(8,128)(2,1)}, bf16[2048,384]{1,0:T(8,128)(2,1)}, bf16[384,2048]{1,0:T(8,128)(2,1)}, f32[8,128]{1,0:T(8,128)S(1)}) custom-call(bf16[48,2048]{1,0:T(8,128)(2,1)S(1)} %get-tuple-element.84.refs_1_.refs_0_, bf16[48,2048]{1,0:T(8,128)(2,1)S(1)} %collective-permute-done.refs_3_.refs_2_.refs_1_, ...), custom_call_target="tpu_custom_call" | custom-call | flops 1000 | bytes 1000 | tf_op jit(solution)/shard_map/deltas/pallas_call | solution.py:130
  127.8 1.1 total.1
  (131 shorter events, 16.7 us)
Async XLA Ops:
  2.6 19.7 %collective-permute-start.7 = (bf16[128,2176]{1,0:T(8,128)(2,1)}, bf16[128,2176]{1,0:T(8,128)(2,1)S(1)}, u32[]{:S(2)}, u32[]{:S(2)}) collective-permute-start(bf16[128,2176]{1,0:T(8,128)(2,1)} %pack.1.refs_1_.refs_2_), channel_id=1, source_target_pairs={{0,8},{1,9},{2,10},{3,11},{4,0},{5,1},{6,2},{7,3},{8,12},{9,13},{1... | collective-permute-start | bytes 1671176 | tf_op jit(solution)/shard_map/ppermute | solution.py:325
  8.4 1.8 %collective-permute-start.1 = (bf16[32,2048]{1,0:T(8,128)(2,1)S(1)}, bf16[32,2048]{1,0:T(8,128)(2,1)S(1)}, u32[]{:S(2)}, u32[]{:S(2)}) collective-permute-start(bf16[32,2048]{1,0:T(8,128)(2,1)S(1)} %slice.36), channel_id=1, source_target_pairs={{0,1},{1,0},{2,3},{3,2},{4,5},{5,4},{6,7},{7,6},{8,9},{9,8},{10,11... | collective-permute-start | bytes 393224 | tf_op jit(solution)/shard_map/ppermute | solution.py:331
  8.5 4.3 %collective-permute-start = (bf16[48,2048]{1,0:T(8,128)(2,1)S(1)}, bf16[48,2048]{1,0:T(8,128)(2,1)S(1)}, u32[]{:S(2)}, u32[]{:S(2)}) collective-permute-start(bf16[48,2048]{1,0:T(8,128)(2,1)S(1)} %get-tuple-element.85), channel_id=1, source_target_pairs={{0,1},{1,0},{2,3},{3,2},{4,5},{5,4},{6,7},{7,6},{8,9},{9,8},{10,11... | collective-permute-start | bytes 589832 | tf_op jit(solution)/shard_map/ppermute | solution.py:331
  10.3 12.0 %collective-permute-start.3 = (bf16[96,2048]{1,0:T(8,128)(2,1)S(1)}, bf16[96,2048]{1,0:T(8,128)(2,1)S(1)}, u32[]{:S(2)}, u32[]{:S(2)}) collective-permute-start(bf16[96,2048]{1,0:T(8,128)(2,1)S(1)} %join.12.refs_2_), channel_id=1, source_target_pairs={{0,2},{1,3},{2,0},{3,1},{4,6},{5,7},{6,4},{7,5},{8,10},{9,11},{10,... | collective-permute-start | bytes 1179656 | tf_op jit(solution)/shard_map/ppermute | solution.py:328
  12.2 2.2 %collective-permute-start.4 = (bf16[48,2048]{1,0:T(8,128)(2,1)S(1)}, bf16[48,2048]{1,0:T(8,128)(2,1)S(1)}, u32[]{:S(2)}, u32[]{:S(2)}) collective-permute-start(bf16[48,2048]{1,0:T(8,128)(2,1)S(1)} %get-tuple-element.90), channel_id=1, source_target_pairs={{0,1},{1,0},{2,3},{3,2},{4,5},{5,4},{6,7},{7,6},{8,9},{9,8},{10,11... | collective-permute-start | bytes 589832 | tf_op jit(solution)/shard_map/ppermute | solution.py:331
  12.3 2.1 %collective-permute-start.5 = (bf16[48,2048]{1,0:T(8,128)(2,1)S(1)}, bf16[48,2048]{1,0:T(8,128)(2,1)S(1)}, u32[]{:S(2)}, u32[]{:S(2)}) collective-permute-start(bf16[48,2048]{1,0:T(8,128)(2,1)S(1)} %get-tuple-element.92), channel_id=1, source_target_pairs={{0,1},{1,0},{2,3},{3,2},{4,5},{5,4},{6,7},{7,6},{8,9},{9,8},{10,11... | collective-permute-start | bytes 589832 | tf_op jit(solution)/shard_map/ppermute | solution.py:331
  12.8 18.4 %collective-permute-start.8 = (bf16[128,2048]{1,0:T(8,128)(2,1)S(1)}, bf16[128,2048]{1,0:T(8,128)(2,1)S(1)}, u32[]{:S(2)}, u32[]{:S(2)}) collective-permute-start(bf16[128,2048]{1,0:T(8,128)(2,1)S(1)} %copy-done.4), channel_id=1, source_target_pairs={{0,8},{1,9},{2,10},{3,11},{4,0},{5,1},{6,2},{7,3},{8,12},{9,13},{1... | collective-permute-start | bytes 1572872 | tf_op jit(solution)/shard_map/ppermute | solution.py:325
  14.4 16.8 %collective-permute-start.6 = (bf16[96,2048]{1,0:T(8,128)(2,1)S(1)}, bf16[96,2048]{1,0:T(8,128)(2,1)S(1)}, u32[]{:S(2)}, u32[]{:S(2)}) collective-permute-start(bf16[96,2048]{1,0:T(8,128)(2,1)S(1)} %join.13.refs_1_), channel_id=1, source_target_pairs={{0,2},{1,3},{2,0},{3,1},{4,6},{5,7},{6,4},{7,5},{8,10},{9,11},{10,... | collective-permute-start | bytes 1179656 | tf_op jit(solution)/shard_map/ppermute | solution.py:328
  22.9 2.2 %collective-permute-start.9 = (bf16[48,2048]{1,0:T(8,128)(2,1)S(1)}, bf16[48,2048]{1,0:T(8,128)(2,1)S(1)}, u32[]{:S(2)}, u32[]{:S(2)}) collective-permute-start(bf16[48,2048]{1,0:T(8,128)(2,1)S(1)} %get-tuple-element.95), channel_id=1, source_target_pairs={{0,1},{1,0},{2,3},{3,2},{4,5},{5,4},{6,7},{7,6},{8,9},{9,8},{10,11... | collective-permute-start | bytes 589832 | tf_op jit(solution)/shard_map/ppermute | solution.py:331
  23.0 2.1 %collective-permute-start.10 = (bf16[48,2048]{1,0:T(8,128)(2,1)S(1)}, bf16[48,2048]{1,0:T(8,128)(2,1)S(1)}, u32[]{:S(2)}, u32[]{:S(2)}) collective-permute-start(bf16[48,2048]{1,0:T(8,128)(2,1)S(1)} %get-tuple-element.97), channel_id=1, source_target_pairs={{0,1},{1,0},{2,3},{3,2},{4,5},{5,4},{6,7},{7,6},{8,9},{9,8},{10,11... | collective-permute-start | bytes 589832 | tf_op jit(solution)/shard_map/ppermute | solution.py:331
  23.5 19.6 %collective-permute-start.13 = (bf16[128,2176]{1,0:T(8,128)(2,1)S(1)}, bf16[128,2176]{1,0:T(8,128)(2,1)S(1)}, u32[]{:S(2)}, u32[]{:S(2)}) collective-permute-start(bf16[128,2176]{1,0:T(8,128)(2,1)S(1)} %hold.9.refs_1_.refs_2_), channel_id=1, source_target_pairs={{0,8},{1,9},{2,10},{3,11},{4,0},{5,1},{6,2},{7,3},{8,12},{9,13},{1... | collective-permute-start | bytes 1671176 | tf_op jit(solution)/shard_map/ppermute | solution.py:325
  25.1 18.0 %collective-permute-start.14 = (bf16[96,2048]{1,0:T(8,128)(2,1)S(1)}, bf16[96,2048]{1,0:T(8,128)(2,1)S(1)}, u32[]{:S(2)}, u32[]{:S(2)}) collective-permute-start(bf16[96,2048]{1,0:T(8,128)(2,1)S(1)} %join.14.refs_1_), channel_id=1, source_target_pairs={{0,2},{1,3},{2,0},{3,1},{4,6},{5,7},{6,4},{7,5},{8,10},{9,11},{10,... | collective-permute-start | bytes 1179656 | tf_op jit(solution)/shard_map/ppermute | solution.py:328
  31.6 1.7 %collective-permute-start.12 = (bf16[48,2048]{1,0:T(8,128)(2,1)S(1)}, bf16[48,2048]{1,0:T(8,128)(2,1)S(1)}, u32[]{:S(2)}, u32[]{:S(2)}) collective-permute-start(bf16[48,2048]{1,0:T(8,128)(2,1)S(1)} %get-tuple-element.101), channel_id=1, source_target_pairs={{0,1},{1,0},{2,3},{3,2},{4,5},{5,4},{6,7},{7,6},{8,9},{9,8},{10,11... | collective-permute-start | bytes 589832 | tf_op jit(solution)/shard_map/ppermute | solution.py:331
  33.4 13.8 %collective-permute-start.19 = (bf16[96,2048]{1,0:T(8,128)(2,1)S(1)}, bf16[96,2048]{1,0:T(8,128)(2,1)S(1)}, u32[]{:S(2)}, u32[]{:S(2)}) collective-permute-start(bf16[96,2048]{1,0:T(8,128)(2,1)S(1)} %join.15.refs_10_), channel_id=1, source_target_pairs={{0,2},{1,3},{2,0},{3,1},{4,6},{5,7},{6,4},{7,5},{8,10},{9,11},{10,... | collective-permute-start | bytes 1179656 | tf_op jit(solution)/shard_map/ppermute | solution.py:328
  34.9 18.8 %collective-permute-start.18 = (bf16[128,2048]{1,0:T(8,128)(2,1)S(1)}, bf16[128,2048]{1,0:T(8,128)(2,1)S(1)}, u32[]{:S(2)}, u32[]{:S(2)}) collective-permute-start(bf16[128,2048]{1,0:T(8,128)(2,1)S(1)} %hold.10.refs_1_.refs_2_), channel_id=1, source_target_pairs={{0,8},{1,9},{2,10},{3,11},{4,0},{5,1},{6,2},{7,3},{8,12},{9,13},{1... | collective-permute-start | bytes 1572872 | tf_op jit(solution)/shard_map/ppermute | solution.py:325
  43.8 1.7 %collective-permute-start.16 = (bf16[48,2048]{1,0:T(8,128)(2,1)S(1)}, bf16[48,2048]{1,0:T(8,128)(2,1)S(1)}, u32[]{:S(2)}, u32[]{:S(2)}) collective-permute-start(bf16[48,2048]{1,0:T(8,128)(2,1)S(1)} %get-tuple-element.110), channel_id=1, source_target_pairs={{0,1},{1,0},{2,3},{3,2},{4,5},{5,4},{6,7},{7,6},{8,9},{9,8},{10,11... | collective-permute-start | bytes 589832 | tf_op jit(solution)/shard_map/ppermute | solution.py:331
  45.5 11.3 %collective-permute-start.17 = (bf16[96,2048]{1,0:T(8,128)(2,1)S(1)}, bf16[96,2048]{1,0:T(8,128)(2,1)S(1)}, u32[]{:S(2)}, u32[]{:S(2)}) collective-permute-start(bf16[96,2048]{1,0:T(8,128)(2,1)S(1)} %join.16.refs_10_), channel_id=1, source_target_pairs={{0,2},{1,3},{2,0},{3,1},{4,6},{5,7},{6,4},{7,5},{8,10},{9,11},{10,... | collective-permute-start | bytes 1179656 | tf_op jit(solution)/shard_map/ppermute | solution.py:328
  49.8 4.0 %collective-permute-start.20 = (bf16[32,2176]{1,0:T(8,128)(2,1)S(1)}, bf16[32,2176]{1,0:T(8,128)(2,1)S(1)}, u32[]{:S(2)}, u32[]{:S(2)}) collective-permute-start(bf16[32,2176]{1,0:T(8,128)(2,1)S(1)} %slice.38), channel_id=1, source_target_pairs={{0,1},{1,0},{2,3},{3,2},{4,5},{5,4},{6,7},{7,6},{8,9},{9,8},{10,11... | collective-permute-start | bytes 417800 | tf_op jit(solution)/shard_map/ppermute | solution.py:331
  49.9 3.9 %collective-permute-start.21 = (bf16[16,2176]{1,0:T(8,128)(2,1)S(1)}, bf16[16,2176]{1,0:T(8,128)(2,1)S(1)}, u32[]{:S(2)}, u32[]{:S(2)}) collective-permute-start(bf16[16,2176]{1,0:T(8,128)(2,1)S(1)} %slice.39), channel_id=1, source_target_pairs={{0,1},{1,0},{2,3},{3,2},{4,5},{5,4},{6,7},{7,6},{8,9},{9,8},{10,11... | collective-permute-start | bytes 208904 | tf_op jit(solution)/shard_map/ppermute | solution.py:331
  50.4 16.4 %collective-permute-start.25 = (bf16[128,2176]{1,0:T(8,128)(2,1)S(1)}, bf16[128,2176]{1,0:T(8,128)(2,1)S(1)}, u32[]{:S(2)}, u32[]{:S(2)}) collective-permute-start(bf16[128,2176]{1,0:T(8,128)(2,1)S(1)} %hold.11.refs_1_.refs_2_), channel_id=1, source_target_pairs={{0,8},{1,9},{2,10},{3,11},{4,0},{5,1},{6,2},{7,3},{8,12},{9,13},{1... | collective-permute-start | bytes 1671176 | tf_op jit(solution)/shard_map/ppermute | solution.py:325
  54.2 1.7 %collective-permute-start.22 = (bf16[48,2048]{1,0:T(8,128)(2,1)S(1)}, bf16[48,2048]{1,0:T(8,128)(2,1)S(1)}, u32[]{:S(2)}, u32[]{:S(2)}) collective-permute-start(bf16[48,2048]{1,0:T(8,128)(2,1)S(1)} %get-tuple-element.118), channel_id=1, source_target_pairs={{0,1},{1,0},{2,3},{3,2},{4,5},{5,4},{6,7},{7,6},{8,9},{9,8},{10,11... | collective-permute-start | bytes 589832 | tf_op jit(solution)/shard_map/ppermute | solution.py:331
  54.2 1.7 %collective-permute-start.23 = (bf16[48,2048]{1,0:T(8,128)(2,1)S(1)}, bf16[48,2048]{1,0:T(8,128)(2,1)S(1)}, u32[]{:S(2)}, u32[]{:S(2)}) collective-permute-start(bf16[48,2048]{1,0:T(8,128)(2,1)S(1)} %get-tuple-element.120), channel_id=1, source_target_pairs={{0,1},{1,0},{2,3},{3,2},{4,5},{5,4},{6,7},{7,6},{8,9},{9,8},{10,11... | collective-permute-start | bytes 589832 | tf_op jit(solution)/shard_map/ppermute | solution.py:331
  54.7 12.5 %collective-permute-start.27 = (bf16[96,2176]{1,0:T(8,128)(2,1)S(1)}, bf16[96,2176]{1,0:T(8,128)(2,1)S(1)}, u32[]{:S(2)}, u32[]{:S(2)}) collective-permute-start(bf16[96,2176]{1,0:T(8,128)(2,1)S(1)} %join.17.refs_1_), channel_id=1, source_target_pairs={{0,2},{1,3},{2,0},{3,1},{4,6},{5,7},{6,4},{7,5},{8,10},{9,11},{10,... | collective-permute-start | bytes 1253384 | tf_op jit(solution)/shard_map/ppermute | solution.py:328
  56.9 21.4 %collective-permute-start.30 = (bf16[128,2048]{1,0:T(8,128)(2,1)S(1)}, bf16[128,2048]{1,0:T(8,128)(2,1)S(1)}, u32[]{:S(2)}, u32[]{:S(2)}) collective-permute-start(bf16[128,2048]{1,0:T(8,128)(2,1)S(1)} %hold.13.refs_1_), channel_id=1, source_target_pairs={{0,8},{1,9},{2,10},{3,11},{4,0},{5,1},{6,2},{7,3},{8,12},{9,13},{1... | collective-permute-start | bytes 1572872 | tf_op jit(solution)/shard_map/ppermute | solution.py:325
  60.5 1.5 %collective-permute-start.26 = (bf16[48,2176]{1,0:T(8,128)(2,1)S(1)}, bf16[48,2176]{1,0:T(8,128)(2,1)S(1)}, u32[]{:S(2)}, u32[]{:S(2)}) collective-permute-start(bf16[48,2176]{1,0:T(8,128)(2,1)S(1)} %get-tuple-element.121), channel_id=1, source_target_pairs={{0,1},{1,0},{2,3},{3,2},{4,5},{5,4},{6,7},{7,6},{8,9},{9,8},{10,11... | collective-permute-start | bytes 626696 | tf_op jit(solution)/shard_map/ppermute | solution.py:331
  60.5 15.1 %collective-permute-start.24 = (bf16[96,2048]{1,0:T(8,128)(2,1)S(1)}, bf16[96,2048]{1,0:T(8,128)(2,1)S(1)}, u32[]{:S(2)}, u32[]{:S(2)}) collective-permute-start(bf16[96,2048]{1,0:T(8,128)(2,1)S(1)} %join.18.refs_1_), channel_id=1, source_target_pairs={{0,2},{1,3},{2,0},{3,1},{4,6},{5,7},{6,4},{7,5},{8,10},{9,11},{10,... | collective-permute-start | bytes 1179656 | tf_op jit(solution)/shard_map/ppermute | solution.py:328
  67.8 10.4 %collective-permute-start.31 = (bf16[48,2048]{1,0:T(8,128)(2,1)S(1)}, bf16[48,2048]{1,0:T(8,128)(2,1)S(1)}, u32[]{:S(2)}, u32[]{:S(2)}) collective-permute-start(bf16[48,2048]{1,0:T(8,128)(2,1)S(1)} %get-tuple-element.132), channel_id=1, source_target_pairs={{0,1},{1,0},{2,3},{3,2},{4,5},{5,4},{6,7},{7,6},{8,9},{9,8},{10,11... | collective-permute-start | bytes 589832 | tf_op jit(solution)/shard_map/ppermute | solution.py:331
  67.9 1.8 %collective-permute-start.28 = (bf16[32,2048]{1,0:T(8,128)(2,1)S(1)}, bf16[32,2048]{1,0:T(8,128)(2,1)S(1)}, u32[]{:S(2)}, u32[]{:S(2)}) collective-permute-start(bf16[32,2048]{1,0:T(8,128)(2,1)S(1)} %slice.40), channel_id=1, source_target_pairs={{0,1},{1,0},{2,3},{3,2},{4,5},{5,4},{6,7},{7,6},{8,9},{9,8},{10,11... | collective-permute-start | bytes 393224 | tf_op jit(solution)/shard_map/ppermute | solution.py:331
  69.8 13.4 %collective-permute-start.34 = (bf16[96,2048]{1,0:T(8,128)(2,1)S(1)}, bf16[96,2048]{1,0:T(8,128)(2,1)S(1)}, u32[]{:S(2)}, u32[]{:S(2)}) collective-permute-start(bf16[96,2048]{1,0:T(8,128)(2,1)S(1)} %join.19.refs_10_), channel_id=1, source_target_pairs={{0,2},{1,3},{2,0},{3,1},{4,6},{5,7},{6,4},{7,5},{8,10},{9,11},{10,... | collective-permute-start | bytes 1179656 | tf_op jit(solution)/shard_map/ppermute | solution.py:328
  78.8 1.7 %collective-permute-start.33 = (bf16[48,2048]{1,0:T(8,128)(2,1)S(1)}, bf16[48,2048]{1,0:T(8,128)(2,1)S(1)}, u32[]{:S(2)}, u32[]{:S(2)}) collective-permute-start(bf16[48,2048]{1,0:T(8,128)(2,1)S(1)} %get-tuple-element.136), channel_id=1, source_target_pairs={{0,1},{1,0},{2,3},{3,2},{4,5},{5,4},{6,7},{7,6},{8,9},{9,8},{10,11... | collective-permute-start | bytes 589832 | tf_op jit(solution)/shard_map/ppermute | solution.py:331
  80.5 11.9 %collective-permute-start.41 = (bf16[96,2048]{1,0:T(8,128)(2,1)S(1)}, bf16[96,2048]{1,0:T(8,128)(2,1)S(1)}, u32[]{:S(2)}, u32[]{:S(2)}) collective-permute-start(bf16[96,2048]{1,0:T(8,128)(2,1)S(1)} %join.20.refs_4_), channel_id=1, source_target_pairs={{0,2},{1,3},{2,0},{3,1},{4,6},{5,7},{6,4},{7,5},{8,10},{9,11},{10,... | collective-permute-start | bytes 1179656 | tf_op jit(solution)/shard_map/ppermute | solution.py:328
  83.2 4.7 %collective-permute-start.37 = (bf16[48,2176]{1,0:T(8,128)(2,1)S(1)}, bf16[48,2176]{1,0:T(8,128)(2,1)S(1)}, u32[]{:S(2)}, u32[]{:S(2)}) collective-permute-start(bf16[48,2176]{1,0:T(8,128)(2,1)S(1)} %get-tuple-element.140), channel_id=1, source_target_pairs={{0,1},{1,0},{2,3},{3,2},{4,5},{5,4},{6,7},{7,6},{8,9},{9,8},{10,11... | collective-permute-start | bytes 626696 | tf_op jit(solution)/shard_map/ppermute | solution.py:331
  83.2 4.7 %collective-permute-start.35 = (bf16[32,2176]{1,0:T(8,128)(2,1)S(1)}, bf16[32,2176]{1,0:T(8,128)(2,1)S(1)}, u32[]{:S(2)}, u32[]{:S(2)}) collective-permute-start(bf16[32,2176]{1,0:T(8,128)(2,1)S(1)} %slice.42), channel_id=1, source_target_pairs={{0,1},{1,0},{2,3},{3,2},{4,5},{5,4},{6,7},{7,6},{8,9},{9,8},{10,11... | collective-permute-start | bytes 417800 | tf_op jit(solution)/shard_map/ppermute | solution.py:331
  83.8 17.6 %collective-permute-start.48 = (bf16[128,2176]{1,0:T(8,128)(2,1)S(1)}, bf16[128,2176]{1,0:T(8,128)(2,1)S(1)}, u32[]{:S(2)}, u32[]{:S(2)}) collective-permute-start(bf16[128,2176]{1,0:T(8,128)(2,1)S(1)} %home.7.refs_4_), channel_id=1, source_target_pairs={{0,8},{1,9},{2,10},{3,11},{4,0},{5,1},{6,2},{7,3},{8,12},{9,13},{1... | collective-permute-start | bytes 1671176 | tf_op jit(solution)/shard_map/ppermute | solution.py:325
  88.0 7.8 %collective-permute-start.38 = (bf16[48,2176]{1,0:T(8,128)(2,1)S(1)}, bf16[48,2176]{1,0:T(8,128)(2,1)S(1)}, u32[]{:S(2)}, u32[]{:S(2)}) collective-permute-start(bf16[48,2176]{1,0:T(8,128)(2,1)S(1)} %get-tuple-element.142), channel_id=1, source_target_pairs={{0,1},{1,0},{2,3},{3,2},{4,5},{5,4},{6,7},{7,6},{8,9},{9,8},{10,11... | collective-permute-start | bytes 626696 | tf_op jit(solution)/shard_map/ppermute | solution.py:331
  88.2 13.2 %collective-permute-start.47 = (bf16[96,2176]{1,0:T(8,128)(2,1)S(1)}, bf16[96,2176]{1,0:T(8,128)(2,1)S(1)}, u32[]{:S(2)}, u32[]{:S(2)}) collective-permute-start(bf16[96,2176]{1,0:T(8,128)(2,1)S(1)} %join.21.refs_4_), channel_id=1, source_target_pairs={{0,2},{1,3},{2,0},{3,1},{4,6},{5,7},{6,4},{7,5},{8,10},{9,11},{10,... | collective-permute-start | bytes 1253384 | tf_op jit(solution)/shard_map/ppermute | solution.py:328
  89.9 5.7 %collective-permute-start.39 = (bf16[32,2176]{1,0:T(8,128)(2,1)S(1)}, bf16[32,2176]{1,0:T(8,128)(2,1)S(1)}, u32[]{:S(2)}, u32[]{:S(2)}) collective-permute-start(bf16[32,2176]{1,0:T(8,128)(2,1)S(1)} %slice.44), channel_id=1, source_target_pairs={{0,1},{1,0},{2,3},{3,2},{4,5},{5,4},{6,7},{7,6},{8,9},{9,8},{10,11... | collective-permute-start | bytes 417800 | tf_op jit(solution)/shard_map/ppermute | solution.py:331
  92.4 2.6 %collective-permute-start.40 = (bf16[16,2176]{1,0:T(8,128)(2,1)S(1)}, bf16[16,2176]{1,0:T(8,128)(2,1)S(1)}, u32[]{:S(2)}, u32[]{:S(2)}) collective-permute-start(bf16[16,2176]{1,0:T(8,128)(2,1)S(1)} %slice.45), channel_id=1, source_target_pairs={{0,1},{1,0},{2,3},{3,2},{4,5},{5,4},{6,7},{7,6},{8,9},{9,8},{10,11... | collective-permute-start | bytes 208904 | tf_op jit(solution)/shard_map/ppermute | solution.py:331
  95.1 1.9 %collective-permute-start.42 = (bf16[32,2176]{1,0:T(8,128)(2,1)S(1)}, bf16[32,2176]{1,0:T(8,128)(2,1)S(1)}, u32[]{:S(2)}, u32[]{:S(2)}) collective-permute-start(bf16[32,2176]{1,0:T(8,128)(2,1)S(1)} %slice.46), channel_id=1, source_target_pairs={{0,1},{1,0},{2,3},{3,2},{4,5},{5,4},{6,7},{7,6},{8,9},{9,8},{10,11... | collective-permute-start | bytes 417800 | tf_op jit(solution)/shard_map/ppermute | solution.py:331
  95.7 1.9 %collective-permute-start.44 = (bf16[48,2176]{1,0:T(8,128)(2,1)S(1)}, bf16[48,2176]{1,0:T(8,128)(2,1)S(1)}, u32[]{:S(2)}, u32[]{:S(2)}) collective-permute-start(bf16[48,2176]{1,0:T(8,128)(2,1)S(1)} %get-tuple-element.149), channel_id=1, source_target_pairs={{0,1},{1,0},{2,3},{3,2},{4,5},{5,4},{6,7},{7,6},{8,9},{9,8},{10,11... | collective-permute-start | bytes 626696 | tf_op jit(solution)/shard_map/ppermute | solution.py:331
  97.0 13.3 %collective-permute-start.46 = (bf16[96,2176]{1,0:T(8,128)(2,1)S(1)}, bf16[96,2176]{1,0:T(8,128)(2,1)S(1)}, u32[]{:S(2)}, u32[]{:S(2)}) collective-permute-start(bf16[96,2176]{1,0:T(8,128)(2,1)S(1)} %join.22.refs_3_), channel_id=1, source_target_pairs={{0,2},{1,3},{2,0},{3,1},{4,6},{5,7},{6,4},{7,5},{8,10},{9,11},{10,... | collective-permute-start | bytes 1253384 | tf_op jit(solution)/shard_map/ppermute | solution.py:328
  101.6 8.5 %collective-permute-start.49 = (bf16[128,896]{1,0:T(8,128)(2,1)S(1)}, bf16[128,896]{1,0:T(8,128)(2,1)S(1)}, u32[]{:S(2)}, u32[]{:S(2)}) collective-permute-start(bf16[128,896]{1,0:T(8,128)(2,1)S(1)} %home.8.refs_5_), channel_id=1, source_target_pairs={{0,8},{1,9},{2,10},{3,11},{4,0},{5,1},{6,2},{7,3},{8,12},{9,13},{1... | collective-permute-start | bytes 688136 | tf_op jit(solution)/shard_map/ppermute | solution.py:325
  104.5 23.2 %collective-permute-start.45 = (bf16[96,2176]{1,0:T(8,128)(2,1)S(1)}, bf16[96,2176]{1,0:T(8,128)(2,1)S(1)}, u32[]{:S(2)}, u32[]{:S(2)}) collective-permute-start(bf16[96,2176]{1,0:T(8,128)(2,1)S(1)} %join.23.refs_5_), channel_id=1, source_target_pairs={{0,2},{1,3},{2,0},{3,1},{4,6},{5,7},{6,4},{7,5},{8,10},{9,11},{10,... | collective-permute-start | bytes 1253384 | tf_op jit(solution)/shard_map/ppermute | solution.py:328
  106.5 7.9 %collective-permute-start.51 = (bf16[128,768]{1,0:T(8,128)(2,1)S(1)}, bf16[128,768]{1,0:T(8,128)(2,1)S(1)}, u32[]{:S(2)}, u32[]{:S(2)}) collective-permute-start(bf16[128,768]{1,0:T(8,128)(2,1)S(1)} %home.9.refs_5_), channel_id=1, source_target_pairs={{0,8},{1,9},{2,10},{3,11},{4,0},{5,1},{6,2},{7,3},{8,12},{9,13},{1... | collective-permute-start | bytes 589832 | tf_op jit(solution)/shard_map/ppermute | solution.py:325
  108.4 9.6 %collective-permute-start.53 = (bf16[128,512]{1,0:T(8,128)(2,1)S(1)}, bf16[128,512]{1,0:T(8,128)(2,1)S(1)}, u32[]{:S(2)}, u32[]{:S(2)}) collective-permute-start(bf16[128,512]{1,0:T(8,128)(2,1)S(1)} %home.10.refs_5_), channel_id=1, source_target_pairs={{0,8},{1,9},{2,10},{3,11},{4,0},{5,1},{6,2},{7,3},{8,12},{9,13},{1... | collective-permute-start | bytes 393224 | tf_op jit(solution)/shard_map/ppermute | solution.py:325
  110.6 17.2 %collective-permute-start.50 = (bf16[128,896]{1,0:T(8,128)(2,1)S(1)}, bf16[128,896]{1,0:T(8,128)(2,1)S(1)}, u32[]{:S(2)}, u32[]{:S(2)}) collective-permute-start(bf16[128,896]{1,0:T(8,128)(2,1)S(1)} %home.11.refs_5_), channel_id=1, source_target_pairs={{0,8},{1,9},{2,10},{3,11},{4,0},{5,1},{6,2},{7,3},{8,12},{9,13},{1... | collective-permute-start | bytes 688136 | tf_op jit(solution)/shard_map/ppermute | solution.py:325
  114.7 13.1 %collective-permute-start.52 = (bf16[128,768]{1,0:T(8,128)(2,1)S(1)}, bf16[128,768]{1,0:T(8,128)(2,1)S(1)}, u32[]{:S(2)}, u32[]{:S(2)}) collective-permute-start(bf16[128,768]{1,0:T(8,128)(2,1)S(1)} %home.12.refs_5_), channel_id=1, source_target_pairs={{0,8},{1,9},{2,10},{3,11},{4,0},{5,1},{6,2},{7,3},{8,12},{9,13},{1... | collective-permute-start | bytes 589832 | tf_op jit(solution)/shard_map/ppermute | solution.py:325
  118.2 9.5 %collective-permute-start.54 = (bf16[128,512]{1,0:T(8,128)(2,1)S(1)}, bf16[128,512]{1,0:T(8,128)(2,1)S(1)}, u32[]{:S(2)}, u32[]{:S(2)}) collective-permute-start(bf16[128,512]{1,0:T(8,128)(2,1)S(1)} %home.13.refs_32_), channel_id=1, source_target_pairs={{0,8},{1,9},{2,10},{3,11},{4,0},{5,1},{6,2},{7,3},{8,12},{9,13},{1... | collective-permute-start | bytes 393224 | tf_op jit(solution)/shard_map/ppermute | solution.py:325
  (14 other events, 63.5 us)

commit v6 on v5

--- a/solution.py
+++ b/solution.py
@@ -161,10 +161,23 @@
         return held
 
 
+def joined(refs):
+    return jnp.concatenate([ref[...] for ref in refs], axis=0)
+
+
+def unstacked(ref, rows, start, stop):
+    blocks = range(start // LANES, stop // LANES)
+    return jnp.concatenate([ref[rows * i : rows * (i + 1), :] for i in blocks], axis=1)
+
+
 def pack_kernel(ids_ref, levels_ref, x_ref, out_ref, ids_here, levels_here, sems):
     fanout, rows = ids_ref.shape
     features = x_ref.shape[1]
-    moves = [(ids_ref, ids_here), (levels_ref, levels_here), (x_ref, out_ref.at[:, :features])]
+    experts = out_ref.shape[0] - rows * features // LANES
+    moves = [(ids_ref, ids_here), (levels_ref, levels_here)]
+    for i in range(features // LANES):
+        source = x_ref.at[:, LANES * i : LANES * (i + 1)]
+        moves.append((source, out_ref.at[rows * i : rows * (i + 1), :]))
     copies = [
         pltpu.make_async_copy(source, target, sems.at[i])
         for i, (source, target) in enumerate(moves)
@@ -173,26 +186,25 @@
         copy.start()
     for copy in copies[:2]:
         copy.wait()
-    expert = lax.broadcasted_iota(jnp.int32, (LANES, rows), 0)
-    gates = jnp.zeros((LANES, rows), F32)
+    expert = lax.broadcasted_iota(jnp.int32, (experts, rows), 0)
+    gates = jnp.zeros((experts, rows), F32)
     for k in range(fanout):
         value = levels_here[k : k + 1, :].astype(F32) * (1.0 / 256.0)
         gates = gates + jnp.where(ids_here[k : k + 1, :] == expert, value, 0.0)
-    out_ref[:, features:] = gates.T.astype(BF16)
-    copies[2].wait()
-
-
-def joined(refs):
-    return jnp.concatenate([ref[...] for ref in refs], axis=0)
+    out_ref[out_ref.shape[0] - experts :, :] = gates.astype(BF16)
+    for copy in copies[2:]:
+        copy.wait()
 
 
 def slot_kernel(capacity, me_ref, x_ref, pick_ref, scaled_ref, *block_refs):
-    rows = x_ref.shape[0]
-    features = x_ref.shape[1] - LANES
-    expert = lax.broadcasted_iota(jnp.int32, (8, LANES), 1)
-    wanted = jnp.bitwise_xor(lax.broadcasted_iota(jnp.int32, (8, LANES), 0), me_ref[0])
+    features = block_refs[0].shape[1]
+    rows = pick_ref.shape[1]
+    table = x_ref[rows * features // LANES :, :]
+    experts = table.shape[0]
+    expert = lax.broadcasted_iota(jnp.int32, (8, experts), 1)
+    wanted = jnp.bitwise_xor(lax.broadcasted_iota(jnp.int32, (8, experts), 0), me_ref[0])
     chooser = jnp.where(expert == wanted, 1.0, 0.0).astype(BF16)
-    gates = dot(chooser, x_ref[:, features:], ((1,), (1,)))
+    gates = dot(chooser, table)
     routed = jnp.where(gates > 0.0, 1.0, 0.0)
     before = lax.broadcasted_iota(jnp.int32, (rows, rows), 0)
     after = lax.broadcasted_iota(jnp.int32, (rows, rows), 1)
@@ -206,7 +218,7 @@
     scaled_ref[...] = jnp.concatenate(
         [jnp.where(here, gates[i : i + 1, :], 0.0) for i, here in enumerate(chosen)], axis=0
     ).astype(BF16)
-    picked = dot(pick, x_ref[:, :features]).astype(BF16)
+    picked = dot(pick, unstacked(x_ref, rows, 0, features)).astype(BF16)
     for i, block_ref in enumerate(block_refs):
         block_ref[...] = picked[capacity * i : capacity * (i + 1), :]
 
@@ -219,6 +231,19 @@
 
 def join_kernel(*refs):
     refs[-1][...] = joined(refs[:-1])
+
+
+def stack_kernel(features, *refs):
+    *block_refs, out_ref = refs
+    rows = sum(ref.shape[0] for ref in block_refs)
+    for i in range(features // LANES):
+        blocks = [ref[:, LANES * i : LANES * (i + 1)] for ref in block_refs]
+        out_ref[rows * i : rows * (i + 1), :] = jnp.concatenate(blocks, axis=0)
+    lanes = jnp.concatenate([ref[:, features:] for ref in block_refs], axis=0).astype(F32)
+    blank = jnp.zeros((LANES - rows, LANES), F32)
+    experts = out_ref.shape[0] - rows * features // LANES
+    router = jnp.concatenate([lanes, blank], axis=0).T[:experts, :]
+    out_ref[rows * features // LANES :, :] = router.astype(BF16)
 
 
 def expert_kernel(me_ref, *refs):
@@ -251,26 +276,54 @@
         term_ref[:, features:] = router[part, :]
 
 
-def home_kernel(columns, pick_ref, *refs):
-    terms = jnp.concatenate([ref[:, columns] for ref in refs[:3]], axis=0)
+def plane_sum(pick_ref, term_refs, features, columns, experts):
+    own_ref, near_ref, far_ref = term_refs
+    half = pick_ref.shape[0] // 2
+    terms = jnp.concatenate(
+        [
+            own_ref[:, columns],
+            near_ref[:, columns],
+            unstacked(far_ref, half, columns.start, columns.stop),
+        ],
+        axis=0,
+    )
     total = dot(pick_ref[...], terms, ((0,), (0,)))
-    for passed_ref in refs[3:-1]:
-        passed = passed_ref[...]
-        if passed.shape[1] > terms.shape[1]:
+    if not experts:
+        return total, None
+    lanes = jnp.concatenate([own_ref[:, features:], near_ref[:, features:]], axis=0)
+    router = dot(lanes, pick_ref[:half, :], ((0,), (0,)))[:experts, :]
+    router = router + dot(far_ref[half * features // LANES :, :half], pick_ref[half:, :])
+    return total, router
+
+
+def home_kernel(features, columns, pick_ref, *refs):
+    *refs, out_ref = refs
+    rows = pick_ref.shape[1]
+    experts = out_ref.shape[0] - rows
+    total, router = plane_sum(pick_ref, refs[:3], features, columns, experts)
+    for passed_ref in refs[3:]:
+        passed = passed_ref[:rows, :]
+        if passed.shape[1] > total.shape[1]:
             passed = passed[:, columns]
         total = total + passed.astype(F32)
-    refs[-1][...] = total.astype(BF16)
+        if experts:
+            router = router + passed_ref[rows:, :LANES].astype(F32)
+    out_ref[:rows, :] = total.astype(BF16)
+    if experts:
+        rest = jnp.zeros((experts, out_ref.shape[1] - rows), F32)
+        out_ref[rows:, :] = jnp.concatenate([router, rest], axis=1).astype(BF16)
 
 
 def total_kernel(ids_ref, levels_ref, pick_ref, *refs):
     term_refs, passed_refs, (grad_ref, router_ref) = refs[:3], refs[3:-2], refs[-2:]
     fanout, rows = ids_ref.shape
     features = grad_ref.shape[1]
-    passed = jnp.concatenate([ref[...] for ref in passed_refs], axis=1)
-    total = dot(pick_ref[...], joined(term_refs), ((0,), (0,))) + passed.astype(F32)
-    grad_ref[...] = total[:, :features].astype(BF16)
-    router = total[:, features:].T
-    expert = lax.broadcasted_iota(jnp.int32, (LANES, rows), 0)
+    experts = passed_refs[-1].shape[0] - rows
+    passed = jnp.concatenate([ref[:rows, :] for ref in passed_refs], axis=1)
+    total, router = plane_sum(pick_ref, term_refs, features, slice(0, features), experts)
+    grad_ref[...] = (total + passed.astype(F32)).astype(BF16)
+    router = router + passed_refs[-1][rows:, :LANES].astype(F32)
+    expert = lax.broadcasted_iota(jnp.int32, (experts, rows), 0)
     for k in range(fanout):
         own = jnp.where(ids_ref[k : k + 1, :] == expert, router, 0.0)
         own = jnp.sum(own, axis=0, keepdims=True)
@@ -278,20 +331,34 @@
         router_ref[k : k + 1, :] = own.astype(BF16)
 
 
-def delta_kernel(chunks, *refs):
-    x_refs, d_refs = refs[: 3 * chunks], refs[3 * chunks : 6 * chunks]
-    grads_refs, hidden_refs = refs[6 * chunks : 7 * chunks], refs[7 * chunks : 8 * chunks]
-    gate_ref, up_ref, down_ref, done_ref, x_all, d_all = refs[8 * chunks :]
+def stacked(refs, whole_ref):
+    start = 0
+    for ref in refs:
+        whole_ref[start : start + ref.shape[0], :] = ref[...]
+        start += ref.shape[0]
+
+
+def down_kernel(chunks, *refs):
+    *d_refs, down_ref, done_ref, d_all = refs
+    hidden_refs, d_refs = d_refs[:chunks], d_refs[chunks:]
     done_ref[...] = jnp.zeros_like(done_ref)
+    stacked(d_refs, d_all)
+    hidden = joined(hidden_refs)
+    step = 512
+
+    @pl.loop(0, down_ref.shape[1] // step)
+    def _(i):
+        cols = pl.ds(pl.multiple_of(i * step, step), step)
+        down_ref[:, cols] = dot(hidden, d_all[:, cols], ((0,), (0,))).astype(BF16)
+
+
+def gate_up_kernel(chunks, *refs):
+    *x_refs, gate_ref, up_ref, done_ref, x_all = refs
+    grads_refs, x_refs = x_refs[:chunks], x_refs[chunks:]
+    done_ref[...] = jnp.zeros_like(done_ref)
+    stacked(x_refs, x_all)
+    grads = joined(grads_refs)
     features, units = gate_ref.shape
-    start = 0
-    for x_ref, d_ref in zip(x_refs, d_refs):
-        rows = x_ref.shape[0]
-        x_all[start : start + rows, :] = x_ref[...]
-        d_all[start : start + rows, :] = d_ref[...]
-        start += rows
-    grads = jnp.concatenate([ref[...] for ref in grads_refs], axis=0)
-    hidden = jnp.concatenate([ref[...] for ref in hidden_refs], axis=0)
     step = 512
 
     @pl.loop(0, features // step)
@@ -300,7 +367,6 @@
         both = dot(x_all[:, cols], grads, ((0,), (0,))).astype(BF16)
         gate_ref[cols, :] = both[:, :units]
         up_ref[cols, :] = both[:, units:]
-        down_ref[:, cols] = dot(hidden, d_all[:, cols], ((0,), (0,))).astype(BF16)
 
 
 def staged(tokens, cotangent, expert_ids, gate_levels, w_gate, w_up, w_down):
@@ -340,9 +406,14 @@
     def send(own, near, far, passing, wait=True):
         after = run.pending + ([near] if wait else [])
         run.pending = [] if wait else [near]
+        if far.shape[1] > features:
+            kernel = functools.partial(stack_kernel, features)
+            shape = (2 * capacity * features // LANES + devices, LANES)
+        else:
+            kernel, shape = join_kernel, (2 * capacity, features)
         (both,) = run(
-            join_kernel,
-            [((2 * capacity, far.shape[1]), BF16)],
+            kernel,
+            [(shape, BF16)],
             "join",
             far,
             *passing,
@@ -397,8 +468,16 @@
     def home(s, columns, *passed):
         return along(
             run(
-                functools.partial(home_kernel, columns),
-                [((tok_rows, columns.stop - columns.start), BF16)],
+                functools.partial(home_kernel, features, columns),
+                [
+                    (
+                        (
+                            tok_rows + (devices if columns.stop == features else 0),
+                            columns.stop - columns.start,
+                        ),
+                        BF16,
+                    )
+                ],
                 "home",
                 pick[s],
                 *terms[s],
@@ -408,13 +487,14 @@
 
     (packed,) = run(
         pack_kernel,
-        [((tok_rows, wide), BF16)],
+        [((tok_rows * features // LANES + devices, tok_rows), BF16)],
         "pack",
         ids,
         levels,
         tokens,
         hbm=3,
-        scratch=[pltpu.VMEM(ids.shape, jnp.int32)] * 2 + [pltpu.SemaphoreType.DMA((3,))],
+        scratch=[pltpu.VMEM(ids.shape, jnp.int32)] * 2
+        + [pltpu.SemaphoreType.DMA((2 + features // LANES,))],
         limit=60,
     )
     x, d = along(packed), along(cotangent)
@@ -426,11 +506,12 @@
         if s < last:
             x = along(here)
         slots_x(s, here, 2 if s == last else 1)
-        if s > 1:
-            expert(s - 1)
         if s == 2:
+            expert(1)
             terms[1] = spread(terms[1], 2)
             run.pending = []
+        if s == last:
+            passed = home(1, slice(0, features))
         (here,) = run.hold(d, after=rows_d[s - 1][2:])
         if s == 1:
             d = along(here)
@@ -442,28 +523,33 @@
         if s == 2:
             (here,) = run.hold(here)
             d = along(here)
-    passed = home(1, slice(0, wide))
+    expert(2)
     terms[2] = send(*swap(run.hold(*terms[2], after=rows_x[last][2:]), 2), wait=False)
-    swapped = swap(run.hold(*terms[0]), 2)
+    swapped = swap(run.hold(*terms[0], after=[passed]), 2)
     run.pending = [swapped[1], *swapped[3]]
     expert(last)
     terms[last] = spread(terms[last], 2)
     terms[0] = send(*swapped)
-    cuts = [0, 896, 1664, wide]
+    order = range(planes)
+    down_delta, _ = run(
+        functools.partial(down_kernel, planes),
+        [((units, features), BF16), ((8, LANES), F32)],
+        "down_delta",
+        *[hidden[s] for s in order],
+        *[block for s in order for block in rows_d[s]],
+        scratch=[pltpu.VMEM((planes * rows, features), BF16)],
+    )
+    cuts = [0, 896, 1536, features]
     columns = [slice(start, end) for start, end in zip(cuts, cuts[1:])]
     passed = [home(2, part, passed) for part in columns]
     passed = [home(last, part, whole) for whole, part in zip(passed, columns)]
-    order = range(planes)
-    gate_delta, up_delta, down_delta, _ = run(
-        functools.partial(delta_kernel, planes),
-        [((features, units), BF16)] * 2 + [((units, features), BF16), ((8, LANES), F32)],
-        "deltas",
+    gate_delta, up_delta, _ = run(
+        functools.partial(gate_up_kernel, planes),
+        [((features, units), BF16)] * 2 + [((8, LANES), F32)],
+        "gate_up_delta",
+        *[grads[s] for s in order],
         *[block for s in order for block in rows_x[s]],
-        *[block for s in order for block in rows_d[s]],
-        *[grads[s] for s in order],
-        *[hidden[s] for s in order],
-        scratch=[pltpu.VMEM((planes * rows, features), BF16)] * 2,
-        limit=40,
+        scratch=[pltpu.VMEM((planes * rows, features), BF16)],
     )
     input_grad, router_grad = run(
         total_kernel,

time: 129 us -> 128 us (level)
  Pallas kernels: 26.4 us -> 28.6 us
  waiting for transfers between devices: 42.3 us -> 40.2 us
    ppermute x12, waiting for transfers between devices: 20.9 us -> 12.6 us  [across(): return lax.ppermute(array, 'expert', [(i, i ^ 2) for i in range(devices)])]
    ppermute x13, waiting for transfers between devices: 13.3 us -> 19.3 us  [along(): return lax.ppermute(array, 'expert', pairs)]
    pallas_call x34 -> x35, Pallas kernels: 26.4 us -> 28.6 us  [__call__(): pl.pallas_call(body, out_shape=[jax.ShapeDtypeStruct(shape, kind) for sha...]
  transfers between devices with their start and end apart: 55 -> 55, of which waited for: 24 -> 25; matrix products, arithmetic and copies ran while one was open for 0% -> 0% of each run, Pallas kernels for 18% -> 20%
where the time goes in v6:
time: 128 us
  starting transfers between devices  56.8 us (44%)
  waiting for transfers between devices  40.2 us (31%)
  Pallas kernels  28.6 us (22%)
    ppermute x13, starting transfers between devices, along(): return lax.ppermute(array, 'expert', pairs)  34.7 us
    pallas_call x35, Pallas kernels, __call__(): pl.pallas_call(body, out_shape=[jax.ShapeDtypeStruct(shape, kind) for sha...  28.6 us
    ppermute x13, waiting for transfers between devices, along(): return lax.ppermute(array, 'expert', pairs)  19.3 us
    ppermute x12, starting transfers between devices, across(): return lax.ppermute(array, 'expert', [(i, i ^ 2) for i in range(devices)])  14.8 us
    ppermute x12, waiting for transfers between devices, across(): return lax.ppermute(array, 'expert', [(i, i ^ 2) for i in range(devices)])  12.6 us
    ppermute x30, waiting for transfers between devices, cores(): return lax.ppermute(array, 'expert', [(i, i ^ 1) for i in range(devices)])  8.34 us
    ppermute x30, starting transfers between devices, cores(): return lax.ppermute(array, 'expert', [(i, i ^ 1) for i in range(devices)])  7.34 us
  transfers between devices with their start and end apart: 55, of which 25 were waited for; matrix products, arithmetic and copies ran while one was open for 0% of the time, Pallas kernels for 20%

profile of v6, /device:TPU:0, one launch (start us, length us, event | category | flops | bytes accessed | tf_op | source)
XLA Modules:
  0.0 127.9 jit_solution(14632291881884266572)
XLA Ops:
  0.6 2.0 %pack.1.refs_1_.refs_2_ = bf16[2064,128]{1,0:T(8,128)(2,1)} custom-call(s32[4,128]{1,0:T(4,128)} %bitcast.22, s32[4,128]{1,0:T(4,128)} %bitcast.24, bf16[128,2048]{1,0:T(8,128)(2,1)} %refs_2_.1), custom_call_target="tpu_custom_call" | custom-call | flops 1000 | bytes 1000 | tf_op jit(solution)/shard_map/pack/pallas_call | solution.py:130
  2.7 4.1 %collective-permute-start.7 = (bf16[2064,128]{1,0:T(8,128)(2,1)}, bf16[2064,128]{1,0:T(8,128)(2,1)S(1)}, u32[]{:S(2)}, u32[]{:S(2)}) collective-permute-start(bf16[2064,128]{1,0:T(8,128)(2,1)} %pack.1.refs_1_.refs_2_), channel_id=1, source_target_pairs={{0,8},{1,9},{2,10},{3,11},{4,0},{5,1},{6,2},{7,3},{8,12},{9,13},{1... | collective-permute-start | bytes 1585160 | tf_op jit(solution)/shard_map/ppermute | solution.py:391
  6.8 1.1 copy-done.3
  9.1 1.2 collective-permute-done.2.refs_2_
  10.3 1.6 %collective-permute-start.3 = (bf16[96,2048]{1,0:T(8,128)(2,1)S(1)}, bf16[96,2048]{1,0:T(8,128)(2,1)S(1)}, u32[]{:S(2)}, u32[]{:S(2)}) collective-permute-start(bf16[96,2048]{1,0:T(8,128)(2,1)S(1)} %join.12.refs_2_), channel_id=1, source_target_pairs={{0,2},{1,3},{2,0},{3,1},{4,6},{5,7},{6,4},{7,5},{8,10},{9,11},{10,... | collective-permute-start | bytes 1179656 | tf_op jit(solution)/shard_map/ppermute | solution.py:394
  12.9 1.6 %collective-permute-start.8 = (bf16[128,2048]{1,0:T(8,128)(2,1)S(1)}, bf16[128,2048]{1,0:T(8,128)(2,1)S(1)}, u32[]{:S(2)}, u32[]{:S(2)}) collective-permute-start(bf16[128,2048]{1,0:T(8,128)(2,1)S(1)} %copy-done.4), channel_id=1, source_target_pairs={{0,8},{1,9},{2,10},{3,11},{4,0},{5,1},{6,2},{7,3},{8,12},{9,13},{1... | collective-permute-start | bytes 1572872 | tf_op jit(solution)/shard_map/ppermute | solution.py:391
  15.0 7.3 %collective-permute-done.3.refs_2_.refs_3_.refs_6_ = bf16[96,2048]{1,0:T(8,128)(2,1)S(1)} collective-permute-done((bf16[96,2048]{1,0:T(8,128)(2,1)S(1)}, bf16[96,2048]{1,0:T(8,128)(2,1)S(1)}, u32[]{:S(2)}, u32[]{:S(2)}) %collective-permute-start.3) | collective-permute-done | bytes 393248 | tf_op jit(solution)/shard_map/ppermute | solution.py:394
  23.5 1.6 %collective-permute-start.13 = (bf16[2064,128]{1,0:T(8,128)(2,1)S(1)}, bf16[2064,128]{1,0:T(8,128)(2,1)S(1)}, u32[]{:S(2)}, u32[]{:S(2)}) collective-permute-start(bf16[2064,128]{1,0:T(8,128)(2,1)S(1)} %hold.9.refs_1_.refs_2_), channel_id=1, source_target_pairs={{0,8},{1,9},{2,10},{3,11},{4,0},{5,1},{6,2},{7,3},{8,12},{9,13},{1... | collective-permute-start | bytes 1585160 | tf_op jit(solution)/shard_map/ppermute | solution.py:391
  25.1 1.6 %collective-permute-start.14 = (bf16[96,2048]{1,0:T(8,128)(2,1)S(1)}, bf16[96,2048]{1,0:T(8,128)(2,1)S(1)}, u32[]{:S(2)}, u32[]{:S(2)}) collective-permute-start(bf16[96,2048]{1,0:T(8,128)(2,1)S(1)} %join.14.refs_1_), channel_id=1, source_target_pairs={{0,2},{1,3},{2,0},{3,1},{4,6},{5,7},{6,4},{7,5},{8,10},{9,11},{10,... | collective-permute-start | bytes 1179656 | tf_op jit(solution)/shard_map/ppermute | solution.py:394
  26.7 3.9 %collective-permute-done.8.refs_0_ = bf16[128,2048]{1,0:T(8,128)(2,1)S(1)} collective-permute-done((bf16[128,2048]{1,0:T(8,128)(2,1)S(1)}, bf16[128,2048]{1,0:T(8,128)(2,1)S(1)}, u32[]{:S(2)}, u32[]{:S(2)}) %collective-permute-start.8) | collective-permute-done | bytes 524320 | tf_op jit(solution)/shard_map/ppermute | solution.py:391
  31.7 0.9 collective-permute-done.11.refs_1_
  32.9 1.6 %collective-permute-start.19 = (bf16[96,2048]{1,0:T(8,128)(2,1)S(1)}, bf16[96,2048]{1,0:T(8,128)(2,1)S(1)}, u32[]{:S(2)}, u32[]{:S(2)}) collective-permute-start(bf16[96,2048]{1,0:T(8,128)(2,1)S(1)} %join.15.refs_10_), channel_id=1, source_target_pairs={{0,2},{1,3},{2,0},{3,1},{4,6},{5,7},{6,4},{7,5},{8,10},{9,11},{10,... | collective-permute-start | bytes 1179656 | tf_op jit(solution)/shard_map/ppermute | solution.py:394
  34.5 3.3 %collective-permute-start.18 = (bf16[128,2048]{1,0:T(8,128)(2,1)S(1)}, bf16[128,2048]{1,0:T(8,128)(2,1)S(1)}, u32[]{:S(2)}, u32[]{:S(2)}) collective-permute-start(bf16[128,2048]{1,0:T(8,128)(2,1)S(1)} %hold.10.refs_1_.refs_2_), channel_id=1, source_target_pairs={{0,8},{1,9},{2,10},{3,11},{4,0},{5,1},{6,2},{7,3},{8,12},{9,13},{1... | collective-permute-start | bytes 1572872 | tf_op jit(solution)/shard_map/ppermute | solution.py:391
  37.8 2.6 %expert.4 = (bf16[192,768]{1,0:T(8,128)(2,1)S(1)}, bf16[192,384]{1,0:T(8,128)(2,1)S(1)}, bf16[48,2176]{1,0:T(8,128)(2,1)S(1)}, bf16[48,2176]{1,0:T(8,128)(2,1)S(...) custom-call(s32[1]{0:T(128)} %bitcast.2.refs_0_, bf16[48,2048]{1,0:T(8,128)(2,1)S(1)} %get-tuple-element.85.refs_1_.refs_4_, ...), custom_call_target="tpu_custom_call" | custom-call | flops 1000 | bytes 1000 | tf_op jit(solution)/shard_map/expert/pallas_call | solution.py:130
  40.4 1.6 %collective-permute-done.13.refs_0_ = bf16[2064,128]{1,0:T(8,128)(2,1)S(1)} collective-permute-done((bf16[2064,128]{1,0:T(8,128)(2,1)S(1)}, bf16[2064,128]{1,0:T(8,128)(2,1)S(1)}, u32[]{:S(2)}, u32[]{:S(2)}) %collective-permute-start.13) | collective-permute-done | bytes 528416 | tf_op jit(solution)/shard_map/ppermute | solution.py:391
  43.1 0.9 collective-permute-done.15.refs_3_.refs_2_.refs_11_
  44.4 1.6 %collective-permute-start.17 = (bf16[96,2048]{1,0:T(8,128)(2,1)S(1)}, bf16[96,2048]{1,0:T(8,128)(2,1)S(1)}, u32[]{:S(2)}, u32[]{:S(2)}) collective-permute-start(bf16[96,2048]{1,0:T(8,128)(2,1)S(1)} %join.16.refs_10_), channel_id=1, source_target_pairs={{0,2},{1,3},{2,0},{3,1},{4,6},{5,7},{6,4},{7,5},{8,10},{9,11},{10,... | collective-permute-start | bytes 1179656 | tf_op jit(solution)/shard_map/ppermute | solution.py:394
  46.0 1.0 collective-permute-done.19.refs_6_.refs_2_.refs_9_
  47.0 2.6 %expert.5 = (bf16[192,768]{1,0:T(8,128)(2,1)S(1)}, bf16[192,384]{1,0:T(8,128)(2,1)S(1)}, bf16[48,2176]{1,0:T(8,128)(2,1)S(1)}, bf16[48,2176]{1,0:T(8,128)(2,1)S(...) custom-call(s32[1]{0:T(128)} %bitcast.2.refs_0_, ...), custom_call_target="tpu_custom_call" | custom-call | flops 1000 | bytes 1000 | tf_op jit(solution)/shard_map/expert/pallas_call | solution.py:130
  50.2 2.4 %collective-permute-start.25 = (bf16[2064,128]{1,0:T(8,128)(2,1)S(1)}, bf16[2064,128]{1,0:T(8,128)(2,1)S(1)}, u32[]{:S(2)}, u32[]{:S(2)}) collective-permute-start(bf16[2064,128]{1,0:T(8,128)(2,1)S(1)} %hold.11.refs_1_.refs_2_), channel_id=1, source_target_pairs={{0,8},{1,9},{2,10},{3,11},{4,0},{5,1},{6,2},{7,3},{8,12},{9,13},{1... | collective-permute-start | bytes 1585160 | tf_op jit(solution)/shard_map/ppermute | solution.py:391
  53.6 0.9 collective-permute-start.27
  54.8 0.9 collective-permute-done.17.refs_3_.refs_12_
  55.7 3.4 %collective-permute-start.28 = (bf16[128,2048]{1,0:T(8,128)(2,1)S(1)}, bf16[128,2048]{1,0:T(8,128)(2,1)S(1)}, u32[]{:S(2)}, u32[]{:S(2)}) collective-permute-start(bf16[128,2048]{1,0:T(8,128)(2,1)S(1)} %hold.13.refs_1_), channel_id=1, source_target_pairs={{0,8},{1,9},{2,10},{3,11},{4,0},{5,1},{6,2},{7,3},{8,12},{9,13},{1... | collective-permute-start | bytes 1572872 | tf_op jit(solution)/shard_map/ppermute | solution.py:391
  59.2 1.5 %collective-permute-start.24 = (bf16[96,2048]{1,0:T(8,128)(2,1)S(1)}, bf16[96,2048]{1,0:T(8,128)(2,1)S(1)}, u32[]{:S(2)}, u32[]{:S(2)}) collective-permute-start(bf16[96,2048]{1,0:T(8,128)(2,1)S(1)} %join.18.refs_1_), channel_id=1, source_target_pairs={{0,2},{1,3},{2,0},{3,1},{4,6},{5,7},{6,4},{7,5},{8,10},{9,11},{10,... | collective-permute-start | bytes 1179656 | tf_op jit(solution)/shard_map/ppermute | solution.py:394
  60.7 4.4 %collective-permute-done.25.refs_0_ = bf16[2064,128]{1,0:T(8,128)(2,1)S(1)} collective-permute-done((bf16[2064,128]{1,0:T(8,128)(2,1)S(1)}, bf16[2064,128]{1,0:T(8,128)(2,1)S(1)}, u32[]{:S(2)}, u32[]{:S(2)}) %collective-permute-start.25) | collective-permute-done | bytes 528416 | tf_op jit(solution)/shard_map/ppermute | solution.py:391
  66.9 1.2 collective-permute-done.30.refs_2_
  68.1 1.0 collective-permute-start.34
  69.5 3.6 %collective-permute-start.38 = (bf16[144,2048]{1,0:T(8,128)(2,1)S(1)}, bf16[144,2048]{1,0:T(8,128)(2,1)S(1)}, u32[]{:S(2)}, u32[]{:S(2)}) collective-permute-start(bf16[144,2048]{1,0:T(8,128)(2,1)S(1)} %home.7.refs_1_), channel_id=1, source_target_pairs={{0,8},{1,9},{2,10},{3,11},{4,0},{5,1},{6,2},{7,3},{8,12},{9,13},{1... | collective-permute-start | bytes 1769480 | tf_op jit(solution)/shard_map/ppermute | solution.py:391
  73.1 1.0 collective-permute-done.24.refs_3_.refs_6_.refs_12_
  74.1 2.2 %collective-permute-done.28.refs_0_ = bf16[128,2048]{1,0:T(8,128)(2,1)S(1)} collective-permute-done((bf16[128,2048]{1,0:T(8,128)(2,1)S(1)}, bf16[128,2048]{1,0:T(8,128)(2,1)S(1)}, u32[]{:S(2)}, u32[]{:S(2)}) %collective-permute-start.28) | collective-permute-done | bytes 524320 | tf_op jit(solution)/shard_map/ppermute | solution.py:391
  77.2 0.9 collective-permute-done.32.refs_1_
  78.5 1.6 %collective-permute-start.42 = (bf16[96,2048]{1,0:T(8,128)(2,1)S(1)}, bf16[96,2048]{1,0:T(8,128)(2,1)S(1)}, u32[]{:S(2)}, u32[]{:S(2)}) collective-permute-start(bf16[96,2048]{1,0:T(8,128)(2,1)S(1)} %join.20.refs_10_), channel_id=1, source_target_pairs={{0,2},{1,3},{2,0},{3,1},{4,6},{5,7},{6,4},{7,5},{8,10},{9,11},{10,... | collective-permute-start | bytes 1179656 | tf_op jit(solution)/shard_map/ppermute | solution.py:394
  80.1 2.6 %expert.6 = (bf16[192,768]{1,0:T(8,128)(2,1)S(1)}, bf16[192,384]{1,0:T(8,128)(2,1)S(1)}, bf16[48,2176]{1,0:T(8,128)(2,1)S(1)}, bf16[48,2176]{1,0:T(8,128)(2,1)S(...) custom-call(s32[1]{0:T(128)} %bitcast.2.refs_0_, ...), custom_call_target="tpu_custom_call" | custom-call | flops 1000 | bytes 1000 | tf_op jit(solution)/shard_map/expert/pallas_call | solution.py:130
  83.4 1.2 collective-permute-done.36.refs_2_
  85.2 2.8 %collective-permute-done.38.refs_6_.refs_4_ = bf16[144,2048]{1,0:T(8,128)(2,1)S(1)} collective-permute-done((bf16[144,2048]{1,0:T(8,128)(2,1)S(1)}, bf16[144,2048]{1,0:T(8,128)(2,1)S(1)}, u32[]{:S(2)}, u32[]{:S(2)}) %collective-permute-start.38) | collective-permute-done | bytes 589856 | tf_op jit(solution)/shard_map/ppermute | solution.py:391
  88.7 1.7 %collective-permute-done.42.refs_6_.refs_15_ = bf16[96,2048]{1,0:T(8,128)(2,1)S(1)} collective-permute-done((bf16[96,2048]{1,0:T(8,128)(2,1)S(1)}, bf16[96,2048]{1,0:T(8,128)(2,1)S(1)}, u32[]{:S(2)}, u32[]{:S(2)}) %collective-permute-start.42) | collective-permute-done | bytes 393248 | tf_op jit(solution)/shard_map/ppermute | solution.py:394
  90.5 2.6 %expert.7 = (bf16[192,768]{1,0:T(8,128)(2,1)S(1)}, bf16[192,384]{1,0:T(8,128)(2,1)S(1)}, bf16[48,2176]{1,0:T(8,128)(2,1)S(1)}, bf16[48,2176]{1,0:T(8,128)(2,1)S(...) custom-call(s32[1]{0:T(128)} %bitcast.2.refs_0_, ...), custom_call_target="tpu_custom_call" | custom-call | flops 1000 | bytes 1000 | tf_op jit(solution)/shard_map/expert/pallas_call | solution.py:130
  94.8 1.6 %collective-permute-start.47 = (bf16[1552,128]{1,0:T(8,128)(2,1)S(1)}, bf16[1552,128]{1,0:T(8,128)(2,1)S(1)}, u32[]{:S(2)}, u32[]{:S(2)}) collective-permute-start(bf16[1552,128]{1,0:T(8,128)(2,1)S(1)} %join.22.refs_3_), channel_id=1, source_target_pairs={{0,2},{1,3},{2,0},{3,1},{4,6},{5,7},{6,4},{7,5},{8,10},{9,11},{10,... | collective-permute-start | bytes 1191944 | tf_op jit(solution)/shard_map/ppermute | solution.py:394
  96.5 3.4 %down_delta.1 = (bf16[384,2048]{1,0:T(8,128)(2,1)}, f32[8,128]{1,0:T(8,128)S(1)}) custom-call(bf16[192,384]{1,0:T(8,128)(2,1)S(1)} %get-tuple-element.107.refs_1_.refs_0_, bf16[192,384]{1,0:T(8,128)(2,1)S(1)} %get-tuple-element.117.refs_3_.refs_1_, bf16[192,384]{1,0:T(8,128)(2,1)S(1)} %get-tuple-element.137.refs_4_.refs_2_, ...), custom_call_target="tpu_custom_call" | custom-call | flops 1000 | bytes 1000 | tf_op jit(solution)/shard_map/down_delta/pallas_call | solution.py:130
  100.1 3.0 %collective-permute-start.49 = (bf16[128,896]{1,0:T(8,128)(2,1)S(1)}, bf16[128,896]{1,0:T(8,128)(2,1)S(1)}, u32[]{:S(2)}, u32[]{:S(2)}) collective-permute-start(bf16[128,896]{1,0:T(8,128)(2,1)S(1)} %home.8.refs_5_), channel_id=1, source_target_pairs={{0,8},{1,9},{2,10},{3,11},{4,0},{5,1},{6,2},{7,3},{8,12},{9,13},{1... | collective-permute-start | bytes 688136 | tf_op jit(solution)/shard_map/ppermute | solution.py:391
  104.2 1.7 %collective-permute-start.51 = (bf16[128,640]{1,0:T(8,128)(2,1)S(1)}, bf16[128,640]{1,0:T(8,128)(2,1)S(1)}, u32[]{:S(2)}, u32[]{:S(2)}) collective-permute-start(bf16[128,640]{1,0:T(8,128)(2,1)S(1)} %home.9.refs_5_), channel_id=1, source_target_pairs={{0,8},{1,9},{2,10},{3,11},{4,0},{5,1},{6,2},{7,3},{8,12},{9,13},{1... | collective-permute-start | bytes 491528 | tf_op jit(solution)/shard_map/ppermute | solution.py:391
  106.6 2.5 %collective-permute-done.49.refs_4_ = bf16[128,896]{1,0:T(8,128)(2,1)S(1)} collective-permute-done((bf16[128,896]{1,0:T(8,128)(2,1)S(1)}, bf16[128,896]{1,0:T(8,128)(2,1)S(1)}, u32[]{:S(2)}, u32[]{:S(2)}) %collective-permute-start.49) | collective-permute-done | bytes 229408 | tf_op jit(solution)/shard_map/ppermute | solution.py:391
  109.4 3.4 %collective-permute-start.50 = (bf16[128,896]{1,0:T(8,128)(2,1)S(1)}, bf16[128,896]{1,0:T(8,128)(2,1)S(1)}, u32[]{:S(2)}, u32[]{:S(2)}) collective-permute-start(bf16[128,896]{1,0:T(8,128)(2,1)S(1)} %home.11.refs_5_), channel_id=1, source_target_pairs={{0,8},{1,9},{2,10},{3,11},{4,0},{5,1},{6,2},{7,3},{8,12},{9,13},{1... | collective-permute-start | bytes 688136 | tf_op jit(solution)/shard_map/ppermute | solution.py:391
  113.0 3.2 %collective-permute-start.52 = (bf16[128,640]{1,0:T(8,128)(2,1)S(1)}, bf16[128,640]{1,0:T(8,128)(2,1)S(1)}, u32[]{:S(2)}, u32[]{:S(2)}) collective-permute-start(bf16[128,640]{1,0:T(8,128)(2,1)S(1)} %home.12.refs_5_), channel_id=1, source_target_pairs={{0,8},{1,9},{2,10},{3,11},{4,0},{5,1},{6,2},{7,3},{8,12},{9,13},{1... | collective-permute-start | bytes 491528 | tf_op jit(solution)/shard_map/ppermute | solution.py:391
  116.5 2.9 %collective-permute-start.54 = (bf16[144,512]{1,0:T(8,128)(2,1)S(1)}, bf16[144,512]{1,0:T(8,128)(2,1)S(1)}, u32[]{:S(2)}, u32[]{:S(2)}) collective-permute-start(bf16[144,512]{1,0:T(8,128)(2,1)S(1)} %home.13.refs_16_), channel_id=1, source_target_pairs={{0,8},{1,9},{2,10},{3,11},{4,0},{5,1},{6,2},{7,3},{8,12},{9,13},{1... | collective-permute-start | bytes 442376 | tf_op jit(solution)/shard_map/ppermute | solution.py:391
  119.5 5.4 %gate_up_delta.1 = (bf16[2048,384]{1,0:T(8,128)(2,1)}, bf16[2048,384]{1,0:T(8,128)(2,1)}, f32[8,128]{1,0:T(8,128)S(1)}) custom-call(bf16[192,768]{1,0:T(8,128)(2,1)S(1)} %get-tuple-element.153.refs_0_, bf16[192,768]{1,0:T(8,128)(2,1)S(1)} %get-tuple-element.154.refs_1_, bf16[192,768]{1,0:T(8,128)(2,1)S(1)} %get-tuple-element.155.refs_2_, ...), custom_call_target="tpu_custom_call" | custom-call | flops 1000 | bytes 1000 | tf_op jit(solution)/shard_map/gate_up_delta/pallas_call | solution.py:130
  124.9 1.9 %collective-permute-done.54.refs_8_ = bf16[144,512]{1,0:T(8,128)(2,1)S(1)} collective-permute-done((bf16[144,512]{1,0:T(8,128)(2,1)S(1)}, bf16[144,512]{1,0:T(8,128)(2,1)S(1)}, u32[]{:S(2)}, u32[]{:S(2)}) %collective-permute-start.54) | collective-permute-done | bytes 147488 | tf_op jit(solution)/shard_map/ppermute | solution.py:391
  126.8 1.1 total.1
  (132 shorter events, 18.7 us)
Async XLA Ops:
  2.7 19.6 %collective-permute-start.7 = (bf16[2064,128]{1,0:T(8,128)(2,1)}, bf16[2064,128]{1,0:T(8,128)(2,1)S(1)}, u32[]{:S(2)}, u32[]{:S(2)}) collective-permute-start(bf16[2064,128]{1,0:T(8,128)(2,1)} %pack.1.refs_1_.refs_2_), channel_id=1, source_target_pairs={{0,8},{1,9},{2,10},{3,11},{4,0},{5,1},{6,2},{7,3},{8,12},{9,13},{1... | collective-permute-start | bytes 1585160 | tf_op jit(solution)/shard_map/ppermute | solution.py:391
  8.5 1.8 %collective-permute-start.1 = (bf16[32,2048]{1,0:T(8,128)(2,1)S(1)}, bf16[32,2048]{1,0:T(8,128)(2,1)S(1)}, u32[]{:S(2)}, u32[]{:S(2)}) collective-permute-start(bf16[32,2048]{1,0:T(8,128)(2,1)S(1)} %slice.36), channel_id=1, source_target_pairs={{0,1},{1,0},{2,3},{3,2},{4,5},{5,4},{6,7},{7,6},{8,9},{9,8},{10,11... | collective-permute-start | bytes 393224 | tf_op jit(solution)/shard_map/ppermute | solution.py:397
  8.5 4.3 %collective-permute-start = (bf16[48,2048]{1,0:T(8,128)(2,1)S(1)}, bf16[48,2048]{1,0:T(8,128)(2,1)S(1)}, u32[]{:S(2)}, u32[]{:S(2)}) collective-permute-start(bf16[48,2048]{1,0:T(8,128)(2,1)S(1)} %get-tuple-element.86), channel_id=1, source_target_pairs={{0,1},{1,0},{2,3},{3,2},{4,5},{5,4},{6,7},{7,6},{8,9},{9,8},{10,11... | collective-permute-start | bytes 589832 | tf_op jit(solution)/shard_map/ppermute | solution.py:397
  10.3 12.0 %collective-permute-start.3 = (bf16[96,2048]{1,0:T(8,128)(2,1)S(1)}, bf16[96,2048]{1,0:T(8,128)(2,1)S(1)}, u32[]{:S(2)}, u32[]{:S(2)}) collective-permute-start(bf16[96,2048]{1,0:T(8,128)(2,1)S(1)} %join.12.refs_2_), channel_id=1, source_target_pairs={{0,2},{1,3},{2,0},{3,1},{4,6},{5,7},{6,4},{7,5},{8,10},{9,11},{10,... | collective-permute-start | bytes 1179656 | tf_op jit(solution)/shard_map/ppermute | solution.py:394
  12.3 2.2 %collective-permute-start.4 = (bf16[48,2048]{1,0:T(8,128)(2,1)S(1)}, bf16[48,2048]{1,0:T(8,128)(2,1)S(1)}, u32[]{:S(2)}, u32[]{:S(2)}) collective-permute-start(bf16[48,2048]{1,0:T(8,128)(2,1)S(1)} %get-tuple-element.91), channel_id=1, source_target_pairs={{0,1},{1,0},{2,3},{3,2},{4,5},{5,4},{6,7},{7,6},{8,9},{9,8},{10,11... | collective-permute-start | bytes 589832 | tf_op jit(solution)/shard_map/ppermute | solution.py:397
  12.4 2.1 %collective-permute-start.5 = (bf16[48,2048]{1,0:T(8,128)(2,1)S(1)}, bf16[48,2048]{1,0:T(8,128)(2,1)S(1)}, u32[]{:S(2)}, u32[]{:S(2)}) collective-permute-start(bf16[48,2048]{1,0:T(8,128)(2,1)S(1)} %get-tuple-element.93), channel_id=1, source_target_pairs={{0,1},{1,0},{2,3},{3,2},{4,5},{5,4},{6,7},{7,6},{8,9},{9,8},{10,11... | collective-permute-start | bytes 589832 | tf_op jit(solution)/shard_map/ppermute | solution.py:397
  12.9 17.8 %collective-permute-start.8 = (bf16[128,2048]{1,0:T(8,128)(2,1)S(1)}, bf16[128,2048]{1,0:T(8,128)(2,1)S(1)}, u32[]{:S(2)}, u32[]{:S(2)}) collective-permute-start(bf16[128,2048]{1,0:T(8,128)(2,1)S(1)} %copy-done.4), channel_id=1, source_target_pairs={{0,8},{1,9},{2,10},{3,11},{4,0},{5,1},{6,2},{7,3},{8,12},{9,13},{1... | collective-permute-start | bytes 1572872 | tf_op jit(solution)/shard_map/ppermute | solution.py:391
  14.5 16.3 %collective-permute-start.6 = (bf16[96,2048]{1,0:T(8,128)(2,1)S(1)}, bf16[96,2048]{1,0:T(8,128)(2,1)S(1)}, u32[]{:S(2)}, u32[]{:S(2)}) collective-permute-start(bf16[96,2048]{1,0:T(8,128)(2,1)S(1)} %join.13.refs_1_), channel_id=1, source_target_pairs={{0,2},{1,3},{2,0},{3,1},{4,6},{5,7},{6,4},{7,5},{8,10},{9,11},{10,... | collective-permute-start | bytes 1179656 | tf_op jit(solution)/shard_map/ppermute | solution.py:394
  22.9 2.2 %collective-permute-start.9 = (bf16[48,2048]{1,0:T(8,128)(2,1)S(1)}, bf16[48,2048]{1,0:T(8,128)(2,1)S(1)}, u32[]{:S(2)}, u32[]{:S(2)}) collective-permute-start(bf16[48,2048]{1,0:T(8,128)(2,1)S(1)} %get-tuple-element.96), channel_id=1, source_target_pairs={{0,1},{1,0},{2,3},{3,2},{4,5},{5,4},{6,7},{7,6},{8,9},{9,8},{10,11... | collective-permute-start | bytes 589832 | tf_op jit(solution)/shard_map/ppermute | solution.py:397
  23.0 2.1 %collective-permute-start.10 = (bf16[48,2048]{1,0:T(8,128)(2,1)S(1)}, bf16[48,2048]{1,0:T(8,128)(2,1)S(1)}, u32[]{:S(2)}, u32[]{:S(2)}) collective-permute-start(bf16[48,2048]{1,0:T(8,128)(2,1)S(1)} %get-tuple-element.98), channel_id=1, source_target_pairs={{0,1},{1,0},{2,3},{3,2},{4,5},{5,4},{6,7},{7,6},{8,9},{9,8},{10,11... | collective-permute-start | bytes 589832 | tf_op jit(solution)/shard_map/ppermute | solution.py:397
  23.5 18.5 %collective-permute-start.13 = (bf16[2064,128]{1,0:T(8,128)(2,1)S(1)}, bf16[2064,128]{1,0:T(8,128)(2,1)S(1)}, u32[]{:S(2)}, u32[]{:S(2)}) collective-permute-start(bf16[2064,128]{1,0:T(8,128)(2,1)S(1)} %hold.9.refs_1_.refs_2_), channel_id=1, source_target_pairs={{0,8},{1,9},{2,10},{3,11},{4,0},{5,1},{6,2},{7,3},{8,12},{9,13},{1... | collective-permute-start | bytes 1585160 | tf_op jit(solution)/shard_map/ppermute | solution.py:391
  25.1 16.9 %collective-permute-start.14 = (bf16[96,2048]{1,0:T(8,128)(2,1)S(1)}, bf16[96,2048]{1,0:T(8,128)(2,1)S(1)}, u32[]{:S(2)}, u32[]{:S(2)}) collective-permute-start(bf16[96,2048]{1,0:T(8,128)(2,1)S(1)} %join.14.refs_1_), channel_id=1, source_target_pairs={{0,2},{1,3},{2,0},{3,1},{4,6},{5,7},{6,4},{7,5},{8,10},{9,11},{10,... | collective-permute-start | bytes 1179656 | tf_op jit(solution)/shard_map/ppermute | solution.py:394
  31.2 1.7 %collective-permute-start.12 = (bf16[48,2048]{1,0:T(8,128)(2,1)S(1)}, bf16[48,2048]{1,0:T(8,128)(2,1)S(1)}, u32[]{:S(2)}, u32[]{:S(2)}) collective-permute-start(bf16[48,2048]{1,0:T(8,128)(2,1)S(1)} %get-tuple-element.102), channel_id=1, source_target_pairs={{0,1},{1,0},{2,3},{3,2},{4,5},{5,4},{6,7},{7,6},{8,9},{9,8},{10,11... | collective-permute-start | bytes 589832 | tf_op jit(solution)/shard_map/ppermute | solution.py:397
  32.9 14.0 %collective-permute-start.19 = (bf16[96,2048]{1,0:T(8,128)(2,1)S(1)}, bf16[96,2048]{1,0:T(8,128)(2,1)S(1)}, u32[]{:S(2)}, u32[]{:S(2)}) collective-permute-start(bf16[96,2048]{1,0:T(8,128)(2,1)S(1)} %join.15.refs_10_), channel_id=1, source_target_pairs={{0,2},{1,3},{2,0},{3,1},{4,6},{5,7},{6,4},{7,5},{8,10},{9,11},{10,... | collective-permute-start | bytes 1179656 | tf_op jit(solution)/shard_map/ppermute | solution.py:394
  34.5 18.1 %collective-permute-start.18 = (bf16[128,2048]{1,0:T(8,128)(2,1)S(1)}, bf16[128,2048]{1,0:T(8,128)(2,1)S(1)}, u32[]{:S(2)}, u32[]{:S(2)}) collective-permute-start(bf16[128,2048]{1,0:T(8,128)(2,1)S(1)} %hold.10.refs_1_.refs_2_), channel_id=1, source_target_pairs={{0,8},{1,9},{2,10},{3,11},{4,0},{5,1},{6,2},{7,3},{8,12},{9,13},{1... | collective-permute-start | bytes 1572872 | tf_op jit(solution)/shard_map/ppermute | solution.py:391
  42.6 1.7 %collective-permute-start.16 = (bf16[48,2048]{1,0:T(8,128)(2,1)S(1)}, bf16[48,2048]{1,0:T(8,128)(2,1)S(1)}, u32[]{:S(2)}, u32[]{:S(2)}) collective-permute-start(bf16[48,2048]{1,0:T(8,128)(2,1)S(1)} %get-tuple-element.111), channel_id=1, source_target_pairs={{0,1},{1,0},{2,3},{3,2},{4,5},{5,4},{6,7},{7,6},{8,9},{9,8},{10,11... | collective-permute-start | bytes 589832 | tf_op jit(solution)/shard_map/ppermute | solution.py:397
  44.4 11.3 %collective-permute-start.17 = (bf16[96,2048]{1,0:T(8,128)(2,1)S(1)}, bf16[96,2048]{1,0:T(8,128)(2,1)S(1)}, u32[]{:S(2)}, u32[]{:S(2)}) collective-permute-start(bf16[96,2048]{1,0:T(8,128)(2,1)S(1)} %join.16.refs_10_), channel_id=1, source_target_pairs={{0,2},{1,3},{2,0},{3,1},{4,6},{5,7},{6,4},{7,5},{8,10},{9,11},{10,... | collective-permute-start | bytes 1179656 | tf_op jit(solution)/shard_map/ppermute | solution.py:394
  49.6 3.0 %collective-permute-start.20 = (bf16[32,2176]{1,0:T(8,128)(2,1)S(1)}, bf16[32,2176]{1,0:T(8,128)(2,1)S(1)}, u32[]{:S(2)}, u32[]{:S(2)}) collective-permute-start(bf16[32,2176]{1,0:T(8,128)(2,1)S(1)} %slice.38), channel_id=1, source_target_pairs={{0,1},{1,0},{2,3},{3,2},{4,5},{5,4},{6,7},{7,6},{8,9},{9,8},{10,11... | collective-permute-start | bytes 417800 | tf_op jit(solution)/shard_map/ppermute | solution.py:397
  49.7 2.9 %collective-permute-start.21 = (bf16[16,2176]{1,0:T(8,128)(2,1)S(1)}, bf16[16,2176]{1,0:T(8,128)(2,1)S(1)}, u32[]{:S(2)}, u32[]{:S(2)}) collective-permute-start(bf16[16,2176]{1,0:T(8,128)(2,1)S(1)} %slice.39), channel_id=1, source_target_pairs={{0,1},{1,0},{2,3},{3,2},{4,5},{5,4},{6,7},{7,6},{8,9},{9,8},{10,11... | collective-permute-start | bytes 208904 | tf_op jit(solution)/shard_map/ppermute | solution.py:397
  50.2 14.9 %collective-permute-start.25 = (bf16[2064,128]{1,0:T(8,128)(2,1)S(1)}, bf16[2064,128]{1,0:T(8,128)(2,1)S(1)}, u32[]{:S(2)}, u32[]{:S(2)}) collective-permute-start(bf16[2064,128]{1,0:T(8,128)(2,1)S(1)} %hold.11.refs_1_.refs_2_), channel_id=1, source_target_pairs={{0,8},{1,9},{2,10},{3,11},{4,0},{5,1},{6,2},{7,3},{8,12},{9,13},{1... | collective-permute-start | bytes 1585160 | tf_op jit(solution)/shard_map/ppermute | solution.py:391
  53.0 1.5 %collective-permute-start.22 = (bf16[48,2048]{1,0:T(8,128)(2,1)S(1)}, bf16[48,2048]{1,0:T(8,128)(2,1)S(1)}, u32[]{:S(2)}, u32[]{:S(2)}) collective-permute-start(bf16[48,2048]{1,0:T(8,128)(2,1)S(1)} %get-tuple-element.119), channel_id=1, source_target_pairs={{0,1},{1,0},{2,3},{3,2},{4,5},{5,4},{6,7},{7,6},{8,9},{9,8},{10,11... | collective-permute-start | bytes 589832 | tf_op jit(solution)/shard_map/ppermute | solution.py:397
  53.1 1.7 %collective-permute-start.23 = (bf16[48,2048]{1,0:T(8,128)(2,1)S(1)}, bf16[48,2048]{1,0:T(8,128)(2,1)S(1)}, u32[]{:S(2)}, u32[]{:S(2)}) collective-permute-start(bf16[48,2048]{1,0:T(8,128)(2,1)S(1)} %get-tuple-element.121), channel_id=1, source_target_pairs={{0,1},{1,0},{2,3},{3,2},{4,5},{5,4},{6,7},{7,6},{8,9},{9,8},{10,11... | collective-permute-start | bytes 589832 | tf_op jit(solution)/shard_map/ppermute | solution.py:397
  53.6 12.1 %collective-permute-start.27 = (bf16[1552,128]{1,0:T(8,128)(2,1)S(1)}, bf16[1552,128]{1,0:T(8,128)(2,1)S(1)}, u32[]{:S(2)}, u32[]{:S(2)}) collective-permute-start(bf16[1552,128]{1,0:T(8,128)(2,1)S(1)} %join.17.refs_1_), channel_id=1, source_target_pairs={{0,2},{1,3},{2,0},{3,1},{4,6},{5,7},{6,4},{7,5},{8,10},{9,11},{10,... | collective-permute-start | bytes 1191944 | tf_op jit(solution)/shard_map/ppermute | solution.py:394
  55.7 20.6 %collective-permute-start.28 = (bf16[128,2048]{1,0:T(8,128)(2,1)S(1)}, bf16[128,2048]{1,0:T(8,128)(2,1)S(1)}, u32[]{:S(2)}, u32[]{:S(2)}) collective-permute-start(bf16[128,2048]{1,0:T(8,128)(2,1)S(1)} %hold.13.refs_1_), channel_id=1, source_target_pairs={{0,8},{1,9},{2,10},{3,11},{4,0},{5,1},{6,2},{7,3},{8,12},{9,13},{1... | collective-permute-start | bytes 1572872 | tf_op jit(solution)/shard_map/ppermute | solution.py:391
  59.2 1.5 %collective-permute-start.26 = (bf16[48,2176]{1,0:T(8,128)(2,1)S(1)}, bf16[48,2176]{1,0:T(8,128)(2,1)S(1)}, u32[]{:S(2)}, u32[]{:S(2)}) collective-permute-start(bf16[48,2176]{1,0:T(8,128)(2,1)S(1)} %get-tuple-element.122), channel_id=1, source_target_pairs={{0,1},{1,0},{2,3},{3,2},{4,5},{5,4},{6,7},{7,6},{8,9},{9,8},{10,11... | collective-permute-start | bytes 626696 | tf_op jit(solution)/shard_map/ppermute | solution.py:397
  59.2 14.9 %collective-permute-start.24 = (bf16[96,2048]{1,0:T(8,128)(2,1)S(1)}, bf16[96,2048]{1,0:T(8,128)(2,1)S(1)}, u32[]{:S(2)}, u32[]{:S(2)}) collective-permute-start(bf16[96,2048]{1,0:T(8,128)(2,1)S(1)} %join.18.refs_1_), channel_id=1, source_target_pairs={{0,2},{1,3},{2,0},{3,1},{4,6},{5,7},{6,4},{7,5},{8,10},{9,11},{10,... | collective-permute-start | bytes 1179656 | tf_op jit(solution)/shard_map/ppermute | solution.py:394
  66.3 1.8 %collective-permute-start.29 = (bf16[32,2048]{1,0:T(8,128)(2,1)S(1)}, bf16[32,2048]{1,0:T(8,128)(2,1)S(1)}, u32[]{:S(2)}, u32[]{:S(2)}) collective-permute-start(bf16[32,2048]{1,0:T(8,128)(2,1)S(1)} %slice.40), channel_id=1, source_target_pairs={{0,1},{1,0},{2,3},{3,2},{4,5},{5,4},{6,7},{7,6},{8,9},{9,8},{10,11... | collective-permute-start | bytes 393224 | tf_op jit(solution)/shard_map/ppermute | solution.py:397
  66.4 6.8 %collective-permute-start.31 = (bf16[48,2048]{1,0:T(8,128)(2,1)S(1)}, bf16[48,2048]{1,0:T(8,128)(2,1)S(1)}, u32[]{:S(2)}, u32[]{:S(2)}) collective-permute-start(bf16[48,2048]{1,0:T(8,128)(2,1)S(1)} %get-tuple-element.128), channel_id=1, source_target_pairs={{0,1},{1,0},{2,3},{3,2},{4,5},{5,4},{6,7},{7,6},{8,9},{9,8},{10,11... | collective-permute-start | bytes 589832 | tf_op jit(solution)/shard_map/ppermute | solution.py:397
  68.1 14.5 %collective-permute-start.34 = (bf16[96,2048]{1,0:T(8,128)(2,1)S(1)}, bf16[96,2048]{1,0:T(8,128)(2,1)S(1)}, u32[]{:S(2)}, u32[]{:S(2)}) collective-permute-start(bf16[96,2048]{1,0:T(8,128)(2,1)S(1)} %join.19.refs_4_), channel_id=1, source_target_pairs={{0,2},{1,3},{2,0},{3,1},{4,6},{5,7},{6,4},{7,5},{8,10},{9,11},{10,... | collective-permute-start | bytes 1179656 | tf_op jit(solution)/shard_map/ppermute | solution.py:394
  69.5 18.6 %collective-permute-start.38 = (bf16[144,2048]{1,0:T(8,128)(2,1)S(1)}, bf16[144,2048]{1,0:T(8,128)(2,1)S(1)}, u32[]{:S(2)}, u32[]{:S(2)}) collective-permute-start(bf16[144,2048]{1,0:T(8,128)(2,1)S(1)} %home.7.refs_1_), channel_id=1, source_target_pairs={{0,8},{1,9},{2,10},{3,11},{4,0},{5,1},{6,2},{7,3},{8,12},{9,13},{1... | collective-permute-start | bytes 1769480 | tf_op jit(solution)/shard_map/ppermute | solution.py:391
  76.7 1.7 %collective-permute-start.33 = (bf16[48,2048]{1,0:T(8,128)(2,1)S(1)}, bf16[48,2048]{1,0:T(8,128)(2,1)S(1)}, u32[]{:S(2)}, u32[]{:S(2)}) collective-permute-start(bf16[48,2048]{1,0:T(8,128)(2,1)S(1)} %get-tuple-element.132), channel_id=1, source_target_pairs={{0,1},{1,0},{2,3},{3,2},{4,5},{5,4},{6,7},{7,6},{8,9},{9,8},{10,11... | collective-permute-start | bytes 589832 | tf_op jit(solution)/shard_map/ppermute | solution.py:397
  78.5 12.0 %collective-permute-start.42 = (bf16[96,2048]{1,0:T(8,128)(2,1)S(1)}, bf16[96,2048]{1,0:T(8,128)(2,1)S(1)}, u32[]{:S(2)}, u32[]{:S(2)}) collective-permute-start(bf16[96,2048]{1,0:T(8,128)(2,1)S(1)} %join.20.refs_10_), channel_id=1, source_target_pairs={{0,2},{1,3},{2,0},{3,1},{4,6},{5,7},{6,4},{7,5},{8,10},{9,11},{10,... | collective-permute-start | bytes 1179656 | tf_op jit(solution)/shard_map/ppermute | solution.py:394
  82.7 5.4 %collective-permute-start.37 = (bf16[48,2176]{1,0:T(8,128)(2,1)S(1)}, bf16[48,2176]{1,0:T(8,128)(2,1)S(1)}, u32[]{:S(2)}, u32[]{:S(2)}) collective-permute-start(bf16[48,2176]{1,0:T(8,128)(2,1)S(1)} %get-tuple-element.141), channel_id=1, source_target_pairs={{0,1},{1,0},{2,3},{3,2},{4,5},{5,4},{6,7},{7,6},{8,9},{9,8},{10,11... | collective-permute-start | bytes 626696 | tf_op jit(solution)/shard_map/ppermute | solution.py:397
  82.8 1.8 %collective-permute-start.35 = (bf16[32,2176]{1,0:T(8,128)(2,1)S(1)}, bf16[32,2176]{1,0:T(8,128)(2,1)S(1)}, u32[]{:S(2)}, u32[]{:S(2)}) collective-permute-start(bf16[32,2176]{1,0:T(8,128)(2,1)S(1)} %slice.42), channel_id=1, source_target_pairs={{0,1},{1,0},{2,3},{3,2},{4,5},{5,4},{6,7},{7,6},{8,9},{9,8},{10,11... | collective-permute-start | bytes 417800 | tf_op jit(solution)/shard_map/ppermute | solution.py:397
  84.7 15.1 %collective-permute-start.48 = (bf16[1552,128]{1,0:T(8,128)(2,1)S(1)}, bf16[1552,128]{1,0:T(8,128)(2,1)S(1)}, u32[]{:S(2)}, u32[]{:S(2)}) collective-permute-start(bf16[1552,128]{1,0:T(8,128)(2,1)S(1)} %join.21.refs_4_), channel_id=1, source_target_pairs={{0,2},{1,3},{2,0},{3,1},{4,6},{5,7},{6,4},{7,5},{8,10},{9,11},{10,... | collective-permute-start | bytes 1191944 | tf_op jit(solution)/shard_map/ppermute | solution.py:394
  88.1 5.8 %collective-permute-start.39 = (bf16[48,2176]{1,0:T(8,128)(2,1)S(1)}, bf16[48,2176]{1,0:T(8,128)(2,1)S(1)}, u32[]{:S(2)}, u32[]{:S(2)}) collective-permute-start(bf16[48,2176]{1,0:T(8,128)(2,1)S(1)} %get-tuple-element.143), channel_id=1, source_target_pairs={{0,1},{1,0},{2,3},{3,2},{4,5},{5,4},{6,7},{7,6},{8,9},{9,8},{10,11... | collective-permute-start | bytes 626696 | tf_op jit(solution)/shard_map/ppermute | solution.py:397
  88.1 5.7 %collective-permute-start.40 = (bf16[32,2176]{1,0:T(8,128)(2,1)S(1)}, bf16[32,2176]{1,0:T(8,128)(2,1)S(1)}, u32[]{:S(2)}, u32[]{:S(2)}) collective-permute-start(bf16[32,2176]{1,0:T(8,128)(2,1)S(1)} %slice.44), channel_id=1, source_target_pairs={{0,1},{1,0},{2,3},{3,2},{4,5},{5,4},{6,7},{7,6},{8,9},{9,8},{10,11... | collective-permute-start | bytes 417800 | tf_op jit(solution)/shard_map/ppermute | solution.py:397
  88.7 4.5 %collective-permute-start.41 = (bf16[16,2176]{1,0:T(8,128)(2,1)S(1)}, bf16[16,2176]{1,0:T(8,128)(2,1)S(1)}, u32[]{:S(2)}, u32[]{:S(2)}) collective-permute-start(bf16[16,2176]{1,0:T(8,128)(2,1)S(1)} %slice.45), channel_id=1, source_target_pairs={{0,1},{1,0},{2,3},{3,2},{4,5},{5,4},{6,7},{7,6},{8,9},{9,8},{10,11... | collective-permute-start | bytes 208904 | tf_op jit(solution)/shard_map/ppermute | solution.py:397
  93.1 1.6 %collective-permute-start.43 = (bf16[32,2176]{1,0:T(8,128)(2,1)S(1)}, bf16[32,2176]{1,0:T(8,128)(2,1)S(1)}, u32[]{:S(2)}, u32[]{:S(2)}) collective-permute-start(bf16[32,2176]{1,0:T(8,128)(2,1)S(1)} %slice.46), channel_id=1, source_target_pairs={{0,1},{1,0},{2,3},{3,2},{4,5},{5,4},{6,7},{7,6},{8,9},{9,8},{10,11... | collective-permute-start | bytes 417800 | tf_op jit(solution)/shard_map/ppermute | solution.py:397
  93.8 2.6 %collective-permute-start.45 = (bf16[48,2176]{1,0:T(8,128)(2,1)S(1)}, bf16[48,2176]{1,0:T(8,128)(2,1)S(1)}, u32[]{:S(2)}, u32[]{:S(2)}) collective-permute-start(bf16[48,2176]{1,0:T(8,128)(2,1)S(1)} %get-tuple-element.150), channel_id=1, source_target_pairs={{0,1},{1,0},{2,3},{3,2},{4,5},{5,4},{6,7},{7,6},{8,9},{9,8},{10,11... | collective-permute-start | bytes 626696 | tf_op jit(solution)/shard_map/ppermute | solution.py:397
  94.8 14.3 %collective-permute-start.47 = (bf16[1552,128]{1,0:T(8,128)(2,1)S(1)}, bf16[1552,128]{1,0:T(8,128)(2,1)S(1)}, u32[]{:S(2)}, u32[]{:S(2)}) collective-permute-start(bf16[1552,128]{1,0:T(8,128)(2,1)S(1)} %join.22.refs_3_), channel_id=1, source_target_pairs={{0,2},{1,3},{2,0},{3,1},{4,6},{5,7},{6,4},{7,5},{8,10},{9,11},{10,... | collective-permute-start | bytes 1191944 | tf_op jit(solution)/shard_map/ppermute | solution.py:394
  100.1 9.0 %collective-permute-start.49 = (bf16[128,896]{1,0:T(8,128)(2,1)S(1)}, bf16[128,896]{1,0:T(8,128)(2,1)S(1)}, u32[]{:S(2)}, u32[]{:S(2)}) collective-permute-start(bf16[128,896]{1,0:T(8,128)(2,1)S(1)} %home.8.refs_5_), channel_id=1, source_target_pairs={{0,8},{1,9},{2,10},{3,11},{4,0},{5,1},{6,2},{7,3},{8,12},{9,13},{1... | collective-permute-start | bytes 688136 | tf_op jit(solution)/shard_map/ppermute | solution.py:391
  103.1 21.8 %collective-permute-start.46 = (bf16[1552,128]{1,0:T(8,128)(2,1)S(1)}, bf16[1552,128]{1,0:T(8,128)(2,1)S(1)}, u32[]{:S(2)}, u32[]{:S(2)}) collective-permute-start(bf16[1552,128]{1,0:T(8,128)(2,1)S(1)} %join.23.refs_16_), channel_id=1, source_target_pairs={{0,2},{1,3},{2,0},{3,1},{4,6},{5,7},{6,4},{7,5},{8,10},{9,11},{10,... | collective-permute-start | bytes 1191944 | tf_op jit(solution)/shard_map/ppermute | solution.py:394
  104.2 8.6 %collective-permute-start.51 = (bf16[128,640]{1,0:T(8,128)(2,1)S(1)}, bf16[128,640]{1,0:T(8,128)(2,1)S(1)}, u32[]{:S(2)}, u32[]{:S(2)}) collective-permute-start(bf16[128,640]{1,0:T(8,128)(2,1)S(1)} %home.9.refs_5_), channel_id=1, source_target_pairs={{0,8},{1,9},{2,10},{3,11},{4,0},{5,1},{6,2},{7,3},{8,12},{9,13},{1... | collective-permute-start | bytes 491528 | tf_op jit(solution)/shard_map/ppermute | solution.py:391
  106.2 10.1 %collective-permute-start.53 = (bf16[144,512]{1,0:T(8,128)(2,1)S(1)}, bf16[144,512]{1,0:T(8,128)(2,1)S(1)}, u32[]{:S(2)}, u32[]{:S(2)}) collective-permute-start(bf16[144,512]{1,0:T(8,128)(2,1)S(1)} %home.10.refs_5_), channel_id=1, source_target_pairs={{0,8},{1,9},{2,10},{3,11},{4,0},{5,1},{6,2},{7,3},{8,12},{9,13},{1... | collective-permute-start | bytes 442376 | tf_op jit(solution)/shard_map/ppermute | solution.py:391
  109.4 17.4 %collective-permute-start.50 = (bf16[128,896]{1,0:T(8,128)(2,1)S(1)}, bf16[128,896]{1,0:T(8,128)(2,1)S(1)}, u32[]{:S(2)}, u32[]{:S(2)}) collective-permute-start(bf16[128,896]{1,0:T(8,128)(2,1)S(1)} %home.11.refs_5_), channel_id=1, source_target_pairs={{0,8},{1,9},{2,10},{3,11},{4,0},{5,1},{6,2},{7,3},{8,12},{9,13},{1... | collective-permute-start | bytes 688136 | tf_op jit(solution)/shard_map/ppermute | solution.py:391
  113.0 13.7 %collective-permute-start.52 = (bf16[128,640]{1,0:T(8,128)(2,1)S(1)}, bf16[128,640]{1,0:T(8,128)(2,1)S(1)}, u32[]{:S(2)}, u32[]{:S(2)}) collective-permute-start(bf16[128,640]{1,0:T(8,128)(2,1)S(1)} %home.12.refs_5_), channel_id=1, source_target_pairs={{0,8},{1,9},{2,10},{3,11},{4,0},{5,1},{6,2},{7,3},{8,12},{9,13},{1... | collective-permute-start | bytes 491528 | tf_op jit(solution)/shard_map/ppermute | solution.py:391
  116.5 10.2 %collective-permute-start.54 = (bf16[144,512]{1,0:T(8,128)(2,1)S(1)}, bf16[144,512]{1,0:T(8,128)(2,1)S(1)}, u32[]{:S(2)}, u32[]{:S(2)}) collective-permute-start(bf16[144,512]{1,0:T(8,128)(2,1)S(1)} %home.13.refs_16_), channel_id=1, source_target_pairs={{0,8},{1,9},{2,10},{3,11},{4,0},{5,1},{6,2},{7,3},{8,12},{9,13},{1... | collective-permute-start | bytes 442376 | tf_op jit(solution)/shard_map/ppermute | solution.py:391
  (14 other events, 63.5 us)

commit v7 on v6

--- a/solution.py
+++ b/solution.py
@@ -531,6 +531,9 @@
     terms[last] = spread(terms[last], 2)
     terms[0] = send(*swapped)
     order = range(planes)
+    cuts = [0, 896, 1536, features]
+    columns = [slice(start, end) for start, end in zip(cuts, cuts[1:])]
+    passed = [home(2, part, passed) for part in columns]
     down_delta, _ = run(
         functools.partial(down_kernel, planes),
         [((units, features), BF16), ((8, LANES), F32)],
@@ -539,9 +542,6 @@
         *[block for s in order for block in rows_d[s]],
         scratch=[pltpu.VMEM((planes * rows, features), BF16)],
     )
-    cuts = [0, 896, 1536, features]
-    columns = [slice(start, end) for start, end in zip(cuts, cuts[1:])]
-    passed = [home(2, part, passed) for part in columns]
     passed = [home(last, part, whole) for whole, part in zip(passed, columns)]
     gate_delta, up_delta, _ = run(
         functools.partial(gate_up_kernel, planes),

time: 128 us -> 126 us (0.984)
  waiting for transfers between devices: 40.2 us -> 38.8 us
    ppermute x13, waiting for transfers between devices: 19.3 us -> 15.3 us  [along(): return lax.ppermute(array, 'expert', pairs)]
    ppermute x12, waiting for transfers between devices: 12.6 us -> 15.2 us  [across(): return lax.ppermute(array, 'expert', [(i, i ^ 2) for i in range(devices)])]
    ppermute x13, starting transfers between devices: 34.7 us -> 33.4 us  [along(): return lax.ppermute(array, 'expert', pairs)]
where the time goes in v7:
time: 126 us
  starting transfers between devices  56.1 us (45%)
  waiting for transfers between devices  38.8 us (31%)
  Pallas kernels  28.6 us (23%)
    ppermute x13, starting transfers between devices, along(): return lax.ppermute(array, 'expert', pairs)  33.4 us
    pallas_call x35, Pallas kernels, __call__(): pl.pallas_call(body, out_shape=[jax.ShapeDtypeStruct(shape, kind) for sha...  28.6 us
    ppermute x12, starting transfers between devices, across(): return lax.ppermute(array, 'expert', [(i, i ^ 2) for i in range(devices)])  15.4 us
    ppermute x13, waiting for transfers between devices, along(): return lax.ppermute(array, 'expert', pairs)  15.3 us
    ppermute x12, waiting for transfers between devices, across(): return lax.ppermute(array, 'expert', [(i, i ^ 2) for i in range(devices)])  15.2 us
    ppermute x30, waiting for transfers between devices, cores(): return lax.ppermute(array, 'expert', [(i, i ^ 1) for i in range(devices)])  8.34 us
    ppermute x30, starting transfers between devices, cores(): return lax.ppermute(array, 'expert', [(i, i ^ 1) for i in range(devices)])  7.34 us
  transfers between devices with their start and end apart: 55, of which 25 were waited for; matrix products, arithmetic and copies ran while one was open for 0% of the time, Pallas kernels for 20%

profile of v7, /device:TPU:0, one launch (start us, length us, event | category | flops | bytes accessed | tf_op | source)
XLA Modules:
  0.0 125.7 jit_solution(17651540217422681631)
XLA Ops:
  0.6 2.0 %pack.1.refs_1_.refs_2_ = bf16[2064,128]{1,0:T(8,128)(2,1)} custom-call(s32[4,128]{1,0:T(4,128)} %bitcast.22, s32[4,128]{1,0:T(4,128)} %bitcast.24, bf16[128,2048]{1,0:T(8,128)(2,1)} %refs_2_.1), custom_call_target="tpu_custom_call" | custom-call | flops 1000 | bytes 1000 | tf_op jit(solution)/shard_map/pack/pallas_call | solution.py:130
  2.7 4.1 %collective-permute-start.7 = (bf16[2064,128]{1,0:T(8,128)(2,1)}, bf16[2064,128]{1,0:T(8,128)(2,1)S(1)}, u32[]{:S(2)}, u32[]{:S(2)}) collective-permute-start(bf16[2064,128]{1,0:T(8,128)(2,1)} %pack.1.refs_1_.refs_2_), channel_id=1, source_target_pairs={{0,8},{1,9},{2,10},{3,11},{4,0},{5,1},{6,2},{7,3},{8,12},{9,13},{1... | collective-permute-start | bytes 1585160 | tf_op jit(solution)/shard_map/ppermute | solution.py:391
  6.8 1.1 copy-done.3
  9.1 1.2 collective-permute-done.2.refs_2_
  10.3 1.6 %collective-permute-start.3 = (bf16[96,2048]{1,0:T(8,128)(2,1)S(1)}, bf16[96,2048]{1,0:T(8,128)(2,1)S(1)}, u32[]{:S(2)}, u32[]{:S(2)}) collective-permute-start(bf16[96,2048]{1,0:T(8,128)(2,1)S(1)} %join.12.refs_2_), channel_id=1, source_target_pairs={{0,2},{1,3},{2,0},{3,1},{4,6},{5,7},{6,4},{7,5},{8,10},{9,11},{10,... | collective-permute-start | bytes 1179656 | tf_op jit(solution)/shard_map/ppermute | solution.py:394
  12.9 1.6 %collective-permute-start.8 = (bf16[128,2048]{1,0:T(8,128)(2,1)S(1)}, bf16[128,2048]{1,0:T(8,128)(2,1)S(1)}, u32[]{:S(2)}, u32[]{:S(2)}) collective-permute-start(bf16[128,2048]{1,0:T(8,128)(2,1)S(1)} %copy-done.4), channel_id=1, source_target_pairs={{0,8},{1,9},{2,10},{3,11},{4,0},{5,1},{6,2},{7,3},{8,12},{9,13},{1... | collective-permute-start | bytes 1572872 | tf_op jit(solution)/shard_map/ppermute | solution.py:391
  15.0 7.3 %collective-permute-done.3.refs_2_.refs_3_.refs_6_ = bf16[96,2048]{1,0:T(8,128)(2,1)S(1)} collective-permute-done((bf16[96,2048]{1,0:T(8,128)(2,1)S(1)}, bf16[96,2048]{1,0:T(8,128)(2,1)S(1)}, u32[]{:S(2)}, u32[]{:S(2)}) %collective-permute-start.3) | collective-permute-done | bytes 393248 | tf_op jit(solution)/shard_map/ppermute | solution.py:394
  23.5 1.6 %collective-permute-start.13 = (bf16[2064,128]{1,0:T(8,128)(2,1)S(1)}, bf16[2064,128]{1,0:T(8,128)(2,1)S(1)}, u32[]{:S(2)}, u32[]{:S(2)}) collective-permute-start(bf16[2064,128]{1,0:T(8,128)(2,1)S(1)} %hold.9.refs_1_.refs_2_), channel_id=1, source_target_pairs={{0,8},{1,9},{2,10},{3,11},{4,0},{5,1},{6,2},{7,3},{8,12},{9,13},{1... | collective-permute-start | bytes 1585160 | tf_op jit(solution)/shard_map/ppermute | solution.py:391
  25.1 1.6 %collective-permute-start.14 = (bf16[96,2048]{1,0:T(8,128)(2,1)S(1)}, bf16[96,2048]{1,0:T(8,128)(2,1)S(1)}, u32[]{:S(2)}, u32[]{:S(2)}) collective-permute-start(bf16[96,2048]{1,0:T(8,128)(2,1)S(1)} %join.14.refs_1_), channel_id=1, source_target_pairs={{0,2},{1,3},{2,0},{3,1},{4,6},{5,7},{6,4},{7,5},{8,10},{9,11},{10,... | collective-permute-start | bytes 1179656 | tf_op jit(solution)/shard_map/ppermute | solution.py:394
  26.7 3.9 %collective-permute-done.8.refs_0_ = bf16[128,2048]{1,0:T(8,128)(2,1)S(1)} collective-permute-done((bf16[128,2048]{1,0:T(8,128)(2,1)S(1)}, bf16[128,2048]{1,0:T(8,128)(2,1)S(1)}, u32[]{:S(2)}, u32[]{:S(2)}) %collective-permute-start.8) | collective-permute-done | bytes 524320 | tf_op jit(solution)/shard_map/ppermute | solution.py:391
  31.7 0.9 collective-permute-done.11.refs_1_
  32.9 1.6 %collective-permute-start.19 = (bf16[96,2048]{1,0:T(8,128)(2,1)S(1)}, bf16[96,2048]{1,0:T(8,128)(2,1)S(1)}, u32[]{:S(2)}, u32[]{:S(2)}) collective-permute-start(bf16[96,2048]{1,0:T(8,128)(2,1)S(1)} %join.15.refs_10_), channel_id=1, source_target_pairs={{0,2},{1,3},{2,0},{3,1},{4,6},{5,7},{6,4},{7,5},{8,10},{9,11},{10,... | collective-permute-start | bytes 1179656 | tf_op jit(solution)/shard_map/ppermute | solution.py:394
  34.5 3.3 %collective-permute-start.18 = (bf16[128,2048]{1,0:T(8,128)(2,1)S(1)}, bf16[128,2048]{1,0:T(8,128)(2,1)S(1)}, u32[]{:S(2)}, u32[]{:S(2)}) collective-permute-start(bf16[128,2048]{1,0:T(8,128)(2,1)S(1)} %hold.10.refs_1_.refs_2_), channel_id=1, source_target_pairs={{0,8},{1,9},{2,10},{3,11},{4,0},{5,1},{6,2},{7,3},{8,12},{9,13},{1... | collective-permute-start | bytes 1572872 | tf_op jit(solution)/shard_map/ppermute | solution.py:391
  37.8 2.6 %expert.4 = (bf16[192,768]{1,0:T(8,128)(2,1)S(1)}, bf16[192,384]{1,0:T(8,128)(2,1)S(1)}, bf16[48,2176]{1,0:T(8,128)(2,1)S(1)}, bf16[48,2176]{1,0:T(8,128)(2,1)S(...) custom-call(s32[1]{0:T(128)} %bitcast.2.refs_0_, bf16[48,2048]{1,0:T(8,128)(2,1)S(1)} %get-tuple-element.85.refs_1_.refs_4_, ...), custom_call_target="tpu_custom_call" | custom-call | flops 1000 | bytes 1000 | tf_op jit(solution)/shard_map/expert/pallas_call | solution.py:130
  40.4 1.6 %collective-permute-done.13.refs_0_ = bf16[2064,128]{1,0:T(8,128)(2,1)S(1)} collective-permute-done((bf16[2064,128]{1,0:T(8,128)(2,1)S(1)}, bf16[2064,128]{1,0:T(8,128)(2,1)S(1)}, u32[]{:S(2)}, u32[]{:S(2)}) %collective-permute-start.13) | collective-permute-done | bytes 528416 | tf_op jit(solution)/shard_map/ppermute | solution.py:391
  43.1 0.9 collective-permute-done.15.refs_3_.refs_2_.refs_11_
  44.4 1.6 %collective-permute-start.17 = (bf16[96,2048]{1,0:T(8,128)(2,1)S(1)}, bf16[96,2048]{1,0:T(8,128)(2,1)S(1)}, u32[]{:S(2)}, u32[]{:S(2)}) collective-permute-start(bf16[96,2048]{1,0:T(8,128)(2,1)S(1)} %join.16.refs_10_), channel_id=1, source_target_pairs={{0,2},{1,3},{2,0},{3,1},{4,6},{5,7},{6,4},{7,5},{8,10},{9,11},{10,... | collective-permute-start | bytes 1179656 | tf_op jit(solution)/shard_map/ppermute | solution.py:394
  46.0 1.0 collective-permute-done.19.refs_6_.refs_2_.refs_9_
  47.0 2.6 %expert.5 = (bf16[192,768]{1,0:T(8,128)(2,1)S(1)}, bf16[192,384]{1,0:T(8,128)(2,1)S(1)}, bf16[48,2176]{1,0:T(8,128)(2,1)S(1)}, bf16[48,2176]{1,0:T(8,128)(2,1)S(...) custom-call(s32[1]{0:T(128)} %bitcast.2.refs_0_, ...), custom_call_target="tpu_custom_call" | custom-call | flops 1000 | bytes 1000 | tf_op jit(solution)/shard_map/expert/pallas_call | solution.py:130
  50.2 2.4 %collective-permute-start.25 = (bf16[2064,128]{1,0:T(8,128)(2,1)S(1)}, bf16[2064,128]{1,0:T(8,128)(2,1)S(1)}, u32[]{:S(2)}, u32[]{:S(2)}) collective-permute-start(bf16[2064,128]{1,0:T(8,128)(2,1)S(1)} %hold.11.refs_1_.refs_2_), channel_id=1, source_target_pairs={{0,8},{1,9},{2,10},{3,11},{4,0},{5,1},{6,2},{7,3},{8,12},{9,13},{1... | collective-permute-start | bytes 1585160 | tf_op jit(solution)/shard_map/ppermute | solution.py:391
  53.6 0.9 collective-permute-start.27
  54.8 0.9 collective-permute-done.17.refs_3_.refs_12_
  55.7 3.4 %collective-permute-start.28 = (bf16[128,2048]{1,0:T(8,128)(2,1)S(1)}, bf16[128,2048]{1,0:T(8,128)(2,1)S(1)}, u32[]{:S(2)}, u32[]{:S(2)}) collective-permute-start(bf16[128,2048]{1,0:T(8,128)(2,1)S(1)} %hold.13.refs_1_), channel_id=1, source_target_pairs={{0,8},{1,9},{2,10},{3,11},{4,0},{5,1},{6,2},{7,3},{8,12},{9,13},{1... | collective-permute-start | bytes 1572872 | tf_op jit(solution)/shard_map/ppermute | solution.py:391
  59.2 1.5 %collective-permute-start.24 = (bf16[96,2048]{1,0:T(8,128)(2,1)S(1)}, bf16[96,2048]{1,0:T(8,128)(2,1)S(1)}, u32[]{:S(2)}, u32[]{:S(2)}) collective-permute-start(bf16[96,2048]{1,0:T(8,128)(2,1)S(1)} %join.18.refs_1_), channel_id=1, source_target_pairs={{0,2},{1,3},{2,0},{3,1},{4,6},{5,7},{6,4},{7,5},{8,10},{9,11},{10,... | collective-permute-start | bytes 1179656 | tf_op jit(solution)/shard_map/ppermute | solution.py:394
  60.7 4.4 %collective-permute-done.25.refs_0_ = bf16[2064,128]{1,0:T(8,128)(2,1)S(1)} collective-permute-done((bf16[2064,128]{1,0:T(8,128)(2,1)S(1)}, bf16[2064,128]{1,0:T(8,128)(2,1)S(1)}, u32[]{:S(2)}, u32[]{:S(2)}) %collective-permute-start.25) | collective-permute-done | bytes 528416 | tf_op jit(solution)/shard_map/ppermute | solution.py:391
  66.9 1.2 collective-permute-done.30.refs_2_
  68.1 1.0 collective-permute-start.34
  69.5 3.6 %collective-permute-start.38 = (bf16[144,2048]{1,0:T(8,128)(2,1)S(1)}, bf16[144,2048]{1,0:T(8,128)(2,1)S(1)}, u32[]{:S(2)}, u32[]{:S(2)}) collective-permute-start(bf16[144,2048]{1,0:T(8,128)(2,1)S(1)} %home.7.refs_1_), channel_id=1, source_target_pairs={{0,8},{1,9},{2,10},{3,11},{4,0},{5,1},{6,2},{7,3},{8,12},{9,13},{1... | collective-permute-start | bytes 1769480 | tf_op jit(solution)/shard_map/ppermute | solution.py:391
  73.1 1.0 collective-permute-done.24.refs_3_.refs_6_.refs_12_
  74.1 2.2 %collective-permute-done.28.refs_0_ = bf16[128,2048]{1,0:T(8,128)(2,1)S(1)} collective-permute-done((bf16[128,2048]{1,0:T(8,128)(2,1)S(1)}, bf16[128,2048]{1,0:T(8,128)(2,1)S(1)}, u32[]{:S(2)}, u32[]{:S(2)}) %collective-permute-start.28) | collective-permute-done | bytes 524320 | tf_op jit(solution)/shard_map/ppermute | solution.py:391
  77.2 0.9 collective-permute-done.32.refs_1_
  78.4 1.6 %collective-permute-start.42 = (bf16[96,2048]{1,0:T(8,128)(2,1)S(1)}, bf16[96,2048]{1,0:T(8,128)(2,1)S(1)}, u32[]{:S(2)}, u32[]{:S(2)}) collective-permute-start(bf16[96,2048]{1,0:T(8,128)(2,1)S(1)} %join.20.refs_10_), channel_id=1, source_target_pairs={{0,2},{1,3},{2,0},{3,1},{4,6},{5,7},{6,4},{7,5},{8,10},{9,11},{10,... | collective-permute-start | bytes 1179656 | tf_op jit(solution)/shard_map/ppermute | solution.py:394
  80.0 2.6 %expert.6 = (bf16[192,768]{1,0:T(8,128)(2,1)S(1)}, bf16[192,384]{1,0:T(8,128)(2,1)S(1)}, bf16[48,2176]{1,0:T(8,128)(2,1)S(1)}, bf16[48,2176]{1,0:T(8,128)(2,1)S(...) custom-call(s32[1]{0:T(128)} %bitcast.2.refs_0_, ...), custom_call_target="tpu_custom_call" | custom-call | flops 1000 | bytes 1000 | tf_op jit(solution)/shard_map/expert/pallas_call | solution.py:130
  83.4 1.2 collective-permute-done.36.refs_2_
  85.2 2.8 %collective-permute-done.38.refs_6_.refs_4_ = bf16[144,2048]{1,0:T(8,128)(2,1)S(1)} collective-permute-done((bf16[144,2048]{1,0:T(8,128)(2,1)S(1)}, bf16[144,2048]{1,0:T(8,128)(2,1)S(1)}, u32[]{:S(2)}, u32[]{:S(2)}) %collective-permute-start.38) | collective-permute-done | bytes 589856 | tf_op jit(solution)/shard_map/ppermute | solution.py:391
  88.7 1.7 %collective-permute-done.42.refs_6_.refs_15_ = bf16[96,2048]{1,0:T(8,128)(2,1)S(1)} collective-permute-done((bf16[96,2048]{1,0:T(8,128)(2,1)S(1)}, bf16[96,2048]{1,0:T(8,128)(2,1)S(1)}, u32[]{:S(2)}, u32[]{:S(2)}) %collective-permute-start.42) | collective-permute-done | bytes 393248 | tf_op jit(solution)/shard_map/ppermute | solution.py:394
  90.5 2.6 %expert.7 = (bf16[192,768]{1,0:T(8,128)(2,1)S(1)}, bf16[192,384]{1,0:T(8,128)(2,1)S(1)}, bf16[48,2176]{1,0:T(8,128)(2,1)S(1)}, bf16[48,2176]{1,0:T(8,128)(2,1)S(...) custom-call(s32[1]{0:T(128)} %bitcast.2.refs_0_, ...), custom_call_target="tpu_custom_call" | custom-call | flops 1000 | bytes 1000 | tf_op jit(solution)/shard_map/expert/pallas_call | solution.py:130
  94.8 1.5 %collective-permute-start.47 = (bf16[1552,128]{1,0:T(8,128)(2,1)S(1)}, bf16[1552,128]{1,0:T(8,128)(2,1)S(1)}, u32[]{:S(2)}, u32[]{:S(2)}) collective-permute-start(bf16[1552,128]{1,0:T(8,128)(2,1)S(1)} %join.22.refs_3_), channel_id=1, source_target_pairs={{0,2},{1,3},{2,0},{3,1},{4,6},{5,7},{6,4},{7,5},{8,10},{9,11},{10,... | collective-permute-start | bytes 1191944 | tf_op jit(solution)/shard_map/ppermute | solution.py:394
  96.4 2.5 %collective-permute-done.48.refs_3_ = bf16[1552,128]{1,0:T(8,128)(2,1)S(1)} collective-permute-done((bf16[1552,128]{1,0:T(8,128)(2,1)S(1)}, bf16[1552,128]{1,0:T(8,128)(2,1)S(1)}, u32[]{:S(2)}, u32[]{:S(2)}) %collective-permute-start.48) | collective-permute-done | bytes 397344 | tf_op jit(solution)/shard_map/ppermute | solution.py:394
  99.2 3.1 %collective-permute-start.49 = (bf16[128,896]{1,0:T(8,128)(2,1)S(1)}, bf16[128,896]{1,0:T(8,128)(2,1)S(1)}, u32[]{:S(2)}, u32[]{:S(2)}) collective-permute-start(bf16[128,896]{1,0:T(8,128)(2,1)S(1)} %home.8.refs_5_), channel_id=1, source_target_pairs={{0,8},{1,9},{2,10},{3,11},{4,0},{5,1},{6,2},{7,3},{8,12},{9,13},{1... | collective-permute-start | bytes 688136 | tf_op jit(solution)/shard_map/ppermute | solution.py:391
  102.3 1.5 %collective-permute-start.46 = (bf16[1552,128]{1,0:T(8,128)(2,1)S(1)}, bf16[1552,128]{1,0:T(8,128)(2,1)S(1)}, u32[]{:S(2)}, u32[]{:S(2)}) collective-permute-start(bf16[1552,128]{1,0:T(8,128)(2,1)S(1)} %join.23.refs_5_), channel_id=1, source_target_pairs={{0,2},{1,3},{2,0},{3,1},{4,6},{5,7},{6,4},{7,5},{8,10},{9,11},{10,... | collective-permute-start | bytes 1191944 | tf_op jit(solution)/shard_map/ppermute | solution.py:394
  104.0 1.6 %collective-permute-start.51 = (bf16[128,640]{1,0:T(8,128)(2,1)S(1)}, bf16[128,640]{1,0:T(8,128)(2,1)S(1)}, u32[]{:S(2)}, u32[]{:S(2)}) collective-permute-start(bf16[128,640]{1,0:T(8,128)(2,1)S(1)} %home.9.refs_5_), channel_id=1, source_target_pairs={{0,8},{1,9},{2,10},{3,11},{4,0},{5,1},{6,2},{7,3},{8,12},{9,13},{1... | collective-permute-start | bytes 491528 | tf_op jit(solution)/shard_map/ppermute | solution.py:391
  106.2 3.4 %down_delta.1 = (bf16[384,2048]{1,0:T(8,128)(2,1)}, f32[8,128]{1,0:T(8,128)S(1)}) custom-call(bf16[192,384]{1,0:T(8,128)(2,1)S(1)} %get-tuple-element.107.refs_1_.refs_0_, bf16[192,384]{1,0:T(8,128)(2,1)S(1)} %get-tuple-element.117.refs_3_.refs_1_, bf16[192,384]{1,0:T(8,128)(2,1)S(1)} %get-tuple-element.137.refs_4_.refs_2_, ...), custom_call_target="tpu_custom_call" | custom-call | flops 1000 | bytes 1000 | tf_op jit(solution)/shard_map/down_delta/pallas_call | solution.py:130
  109.9 2.2 %collective-permute-start.50 = (bf16[128,896]{1,0:T(8,128)(2,1)S(1)}, bf16[128,896]{1,0:T(8,128)(2,1)S(1)}, u32[]{:S(2)}, u32[]{:S(2)}) collective-permute-start(bf16[128,896]{1,0:T(8,128)(2,1)S(1)} %home.11.refs_5_), channel_id=1, source_target_pairs={{0,8},{1,9},{2,10},{3,11},{4,0},{5,1},{6,2},{7,3},{8,12},{9,13},{1... | collective-permute-start | bytes 688136 | tf_op jit(solution)/shard_map/ppermute | solution.py:391
  112.3 3.2 %collective-permute-start.52 = (bf16[128,640]{1,0:T(8,128)(2,1)S(1)}, bf16[128,640]{1,0:T(8,128)(2,1)S(1)}, u32[]{:S(2)}, u32[]{:S(2)}) collective-permute-start(bf16[128,640]{1,0:T(8,128)(2,1)S(1)} %home.12.refs_5_), channel_id=1, source_target_pairs={{0,8},{1,9},{2,10},{3,11},{4,0},{5,1},{6,2},{7,3},{8,12},{9,13},{1... | collective-permute-start | bytes 491528 | tf_op jit(solution)/shard_map/ppermute | solution.py:391
  115.8 2.9 %collective-permute-start.54 = (bf16[144,512]{1,0:T(8,128)(2,1)S(1)}, bf16[144,512]{1,0:T(8,128)(2,1)S(1)}, u32[]{:S(2)}, u32[]{:S(2)}) collective-permute-start(bf16[144,512]{1,0:T(8,128)(2,1)S(1)} %home.13.refs_16_), channel_id=1, source_target_pairs={{0,8},{1,9},{2,10},{3,11},{4,0},{5,1},{6,2},{7,3},{8,12},{9,13},{1... | collective-permute-start | bytes 442376 | tf_op jit(solution)/shard_map/ppermute | solution.py:391
  118.7 5.4 %gate_up_delta.1 = (bf16[2048,384]{1,0:T(8,128)(2,1)}, bf16[2048,384]{1,0:T(8,128)(2,1)}, f32[8,128]{1,0:T(8,128)S(1)}) custom-call(bf16[192,768]{1,0:T(8,128)(2,1)S(1)} %get-tuple-element.153.refs_0_, bf16[192,768]{1,0:T(8,128)(2,1)S(1)} %get-tuple-element.154.refs_1_, bf16[192,768]{1,0:T(8,128)(2,1)S(1)} %get-tuple-element.155.refs_2_, ...), custom_call_target="tpu_custom_call" | custom-call | flops 1000 | bytes 1000 | tf_op jit(solution)/shard_map/gate_up_delta/pallas_call | solution.py:130
  124.6 1.1 total.1
  (132 shorter events, 18.4 us)
Async XLA Ops:
  2.7 19.6 %collective-permute-start.7 = (bf16[2064,128]{1,0:T(8,128)(2,1)}, bf16[2064,128]{1,0:T(8,128)(2,1)S(1)}, u32[]{:S(2)}, u32[]{:S(2)}) collective-permute-start(bf16[2064,128]{1,0:T(8,128)(2,1)} %pack.1.refs_1_.refs_2_), channel_id=1, source_target_pairs={{0,8},{1,9},{2,10},{3,11},{4,0},{5,1},{6,2},{7,3},{8,12},{9,13},{1... | collective-permute-start | bytes 1585160 | tf_op jit(solution)/shard_map/ppermute | solution.py:391
  8.5 1.8 %collective-permute-start.1 = (bf16[32,2048]{1,0:T(8,128)(2,1)S(1)}, bf16[32,2048]{1,0:T(8,128)(2,1)S(1)}, u32[]{:S(2)}, u32[]{:S(2)}) collective-permute-start(bf16[32,2048]{1,0:T(8,128)(2,1)S(1)} %slice.36), channel_id=1, source_target_pairs={{0,1},{1,0},{2,3},{3,2},{4,5},{5,4},{6,7},{7,6},{8,9},{9,8},{10,11... | collective-permute-start | bytes 393224 | tf_op jit(solution)/shard_map/ppermute | solution.py:397
  8.5 4.3 %collective-permute-start = (bf16[48,2048]{1,0:T(8,128)(2,1)S(1)}, bf16[48,2048]{1,0:T(8,128)(2,1)S(1)}, u32[]{:S(2)}, u32[]{:S(2)}) collective-permute-start(bf16[48,2048]{1,0:T(8,128)(2,1)S(1)} %get-tuple-element.86), channel_id=1, source_target_pairs={{0,1},{1,0},{2,3},{3,2},{4,5},{5,4},{6,7},{7,6},{8,9},{9,8},{10,11... | collective-permute-start | bytes 589832 | tf_op jit(solution)/shard_map/ppermute | solution.py:397
  10.3 12.0 %collective-permute-start.3 = (bf16[96,2048]{1,0:T(8,128)(2,1)S(1)}, bf16[96,2048]{1,0:T(8,128)(2,1)S(1)}, u32[]{:S(2)}, u32[]{:S(2)}) collective-permute-start(bf16[96,2048]{1,0:T(8,128)(2,1)S(1)} %join.12.refs_2_), channel_id=1, source_target_pairs={{0,2},{1,3},{2,0},{3,1},{4,6},{5,7},{6,4},{7,5},{8,10},{9,11},{10,... | collective-permute-start | bytes 1179656 | tf_op jit(solution)/shard_map/ppermute | solution.py:394
  12.3 2.2 %collective-permute-start.4 = (bf16[48,2048]{1,0:T(8,128)(2,1)S(1)}, bf16[48,2048]{1,0:T(8,128)(2,1)S(1)}, u32[]{:S(2)}, u32[]{:S(2)}) collective-permute-start(bf16[48,2048]{1,0:T(8,128)(2,1)S(1)} %get-tuple-element.91), channel_id=1, source_target_pairs={{0,1},{1,0},{2,3},{3,2},{4,5},{5,4},{6,7},{7,6},{8,9},{9,8},{10,11... | collective-permute-start | bytes 589832 | tf_op jit(solution)/shard_map/ppermute | solution.py:397
  12.4 2.1 %collective-permute-start.5 = (bf16[48,2048]{1,0:T(8,128)(2,1)S(1)}, bf16[48,2048]{1,0:T(8,128)(2,1)S(1)}, u32[]{:S(2)}, u32[]{:S(2)}) collective-permute-start(bf16[48,2048]{1,0:T(8,128)(2,1)S(1)} %get-tuple-element.93), channel_id=1, source_target_pairs={{0,1},{1,0},{2,3},{3,2},{4,5},{5,4},{6,7},{7,6},{8,9},{9,8},{10,11... | collective-permute-start | bytes 589832 | tf_op jit(solution)/shard_map/ppermute | solution.py:397
  12.9 17.8 %collective-permute-start.8 = (bf16[128,2048]{1,0:T(8,128)(2,1)S(1)}, bf16[128,2048]{1,0:T(8,128)(2,1)S(1)}, u32[]{:S(2)}, u32[]{:S(2)}) collective-permute-start(bf16[128,2048]{1,0:T(8,128)(2,1)S(1)} %copy-done.4), channel_id=1, source_target_pairs={{0,8},{1,9},{2,10},{3,11},{4,0},{5,1},{6,2},{7,3},{8,12},{9,13},{1... | collective-permute-start | bytes 1572872 | tf_op jit(solution)/shard_map/ppermute | solution.py:391
  14.5 16.3 %collective-permute-start.6 = (bf16[96,2048]{1,0:T(8,128)(2,1)S(1)}, bf16[96,2048]{1,0:T(8,128)(2,1)S(1)}, u32[]{:S(2)}, u32[]{:S(2)}) collective-permute-start(bf16[96,2048]{1,0:T(8,128)(2,1)S(1)} %join.13.refs_1_), channel_id=1, source_target_pairs={{0,2},{1,3},{2,0},{3,1},{4,6},{5,7},{6,4},{7,5},{8,10},{9,11},{10,... | collective-permute-start | bytes 1179656 | tf_op jit(solution)/shard_map/ppermute | solution.py:394
  22.9 2.2 %collective-permute-start.9 = (bf16[48,2048]{1,0:T(8,128)(2,1)S(1)}, bf16[48,2048]{1,0:T(8,128)(2,1)S(1)}, u32[]{:S(2)}, u32[]{:S(2)}) collective-permute-start(bf16[48,2048]{1,0:T(8,128)(2,1)S(1)} %get-tuple-element.96), channel_id=1, source_target_pairs={{0,1},{1,0},{2,3},{3,2},{4,5},{5,4},{6,7},{7,6},{8,9},{9,8},{10,11... | collective-permute-start | bytes 589832 | tf_op jit(solution)/shard_map/ppermute | solution.py:397
  23.0 2.1 %collective-permute-start.10 = (bf16[48,2048]{1,0:T(8,128)(2,1)S(1)}, bf16[48,2048]{1,0:T(8,128)(2,1)S(1)}, u32[]{:S(2)}, u32[]{:S(2)}) collective-permute-start(bf16[48,2048]{1,0:T(8,128)(2,1)S(1)} %get-tuple-element.98), channel_id=1, source_target_pairs={{0,1},{1,0},{2,3},{3,2},{4,5},{5,4},{6,7},{7,6},{8,9},{9,8},{10,11... | collective-permute-start | bytes 589832 | tf_op jit(solution)/shard_map/ppermute | solution.py:397
  23.5 18.5 %collective-permute-start.13 = (bf16[2064,128]{1,0:T(8,128)(2,1)S(1)}, bf16[2064,128]{1,0:T(8,128)(2,1)S(1)}, u32[]{:S(2)}, u32[]{:S(2)}) collective-permute-start(bf16[2064,128]{1,0:T(8,128)(2,1)S(1)} %hold.9.refs_1_.refs_2_), channel_id=1, source_target_pairs={{0,8},{1,9},{2,10},{3,11},{4,0},{5,1},{6,2},{7,3},{8,12},{9,13},{1... | collective-permute-start | bytes 1585160 | tf_op jit(solution)/shard_map/ppermute | solution.py:391
  25.1 16.9 %collective-permute-start.14 = (bf16[96,2048]{1,0:T(8,128)(2,1)S(1)}, bf16[96,2048]{1,0:T(8,128)(2,1)S(1)}, u32[]{:S(2)}, u32[]{:S(2)}) collective-permute-start(bf16[96,2048]{1,0:T(8,128)(2,1)S(1)} %join.14.refs_1_), channel_id=1, source_target_pairs={{0,2},{1,3},{2,0},{3,1},{4,6},{5,7},{6,4},{7,5},{8,10},{9,11},{10,... | collective-permute-start | bytes 1179656 | tf_op jit(solution)/shard_map/ppermute | solution.py:394
  31.2 1.7 %collective-permute-start.12 = (bf16[48,2048]{1,0:T(8,128)(2,1)S(1)}, bf16[48,2048]{1,0:T(8,128)(2,1)S(1)}, u32[]{:S(2)}, u32[]{:S(2)}) collective-permute-start(bf16[48,2048]{1,0:T(8,128)(2,1)S(1)} %get-tuple-element.102), channel_id=1, source_target_pairs={{0,1},{1,0},{2,3},{3,2},{4,5},{5,4},{6,7},{7,6},{8,9},{9,8},{10,11... | collective-permute-start | bytes 589832 | tf_op jit(solution)/shard_map/ppermute | solution.py:397
  32.9 14.0 %collective-permute-start.19 = (bf16[96,2048]{1,0:T(8,128)(2,1)S(1)}, bf16[96,2048]{1,0:T(8,128)(2,1)S(1)}, u32[]{:S(2)}, u32[]{:S(2)}) collective-permute-start(bf16[96,2048]{1,0:T(8,128)(2,1)S(1)} %join.15.refs_10_), channel_id=1, source_target_pairs={{0,2},{1,3},{2,0},{3,1},{4,6},{5,7},{6,4},{7,5},{8,10},{9,11},{10,... | collective-permute-start | bytes 1179656 | tf_op jit(solution)/shard_map/ppermute | solution.py:394
  34.5 18.1 %collective-permute-start.18 = (bf16[128,2048]{1,0:T(8,128)(2,1)S(1)}, bf16[128,2048]{1,0:T(8,128)(2,1)S(1)}, u32[]{:S(2)}, u32[]{:S(2)}) collective-permute-start(bf16[128,2048]{1,0:T(8,128)(2,1)S(1)} %hold.10.refs_1_.refs_2_), channel_id=1, source_target_pairs={{0,8},{1,9},{2,10},{3,11},{4,0},{5,1},{6,2},{7,3},{8,12},{9,13},{1... | collective-permute-start | bytes 1572872 | tf_op jit(solution)/shard_map/ppermute | solution.py:391
  42.6 1.5 %collective-permute-start.15 = (bf16[48,2048]{1,0:T(8,128)(2,1)S(1)}, bf16[48,2048]{1,0:T(8,128)(2,1)S(1)}, u32[]{:S(2)}, u32[]{:S(2)}) collective-permute-start(bf16[48,2048]{1,0:T(8,128)(2,1)S(1)} %get-tuple-element.109), channel_id=1, source_target_pairs={{0,1},{1,0},{2,3},{3,2},{4,5},{5,4},{6,7},{7,6},{8,9},{9,8},{10,11... | collective-permute-start | bytes 589832 | tf_op jit(solution)/shard_map/ppermute | solution.py:397
  42.6 1.7 %collective-permute-start.16 = (bf16[48,2048]{1,0:T(8,128)(2,1)S(1)}, bf16[48,2048]{1,0:T(8,128)(2,1)S(1)}, u32[]{:S(2)}, u32[]{:S(2)}) collective-permute-start(bf16[48,2048]{1,0:T(8,128)(2,1)S(1)} %get-tuple-element.111), channel_id=1, source_target_pairs={{0,1},{1,0},{2,3},{3,2},{4,5},{5,4},{6,7},{7,6},{8,9},{9,8},{10,11... | collective-permute-start | bytes 589832 | tf_op jit(solution)/shard_map/ppermute | solution.py:397
  44.4 11.3 %collective-permute-start.17 = (bf16[96,2048]{1,0:T(8,128)(2,1)S(1)}, bf16[96,2048]{1,0:T(8,128)(2,1)S(1)}, u32[]{:S(2)}, u32[]{:S(2)}) collective-permute-start(bf16[96,2048]{1,0:T(8,128)(2,1)S(1)} %join.16.refs_10_), channel_id=1, source_target_pairs={{0,2},{1,3},{2,0},{3,1},{4,6},{5,7},{6,4},{7,5},{8,10},{9,11},{10,... | collective-permute-start | bytes 1179656 | tf_op jit(solution)/shard_map/ppermute | solution.py:394
  49.6 3.0 %collective-permute-start.20 = (bf16[32,2176]{1,0:T(8,128)(2,1)S(1)}, bf16[32,2176]{1,0:T(8,128)(2,1)S(1)}, u32[]{:S(2)}, u32[]{:S(2)}) collective-permute-start(bf16[32,2176]{1,0:T(8,128)(2,1)S(1)} %slice.38), channel_id=1, source_target_pairs={{0,1},{1,0},{2,3},{3,2},{4,5},{5,4},{6,7},{7,6},{8,9},{9,8},{10,11... | collective-permute-start | bytes 417800 | tf_op jit(solution)/shard_map/ppermute | solution.py:397
  49.7 2.9 %collective-permute-start.21 = (bf16[16,2176]{1,0:T(8,128)(2,1)S(1)}, bf16[16,2176]{1,0:T(8,128)(2,1)S(1)}, u32[]{:S(2)}, u32[]{:S(2)}) collective-permute-start(bf16[16,2176]{1,0:T(8,128)(2,1)S(1)} %slice.39), channel_id=1, source_target_pairs={{0,1},{1,0},{2,3},{3,2},{4,5},{5,4},{6,7},{7,6},{8,9},{9,8},{10,11... | collective-permute-start | bytes 208904 | tf_op jit(solution)/shard_map/ppermute | solution.py:397
  50.2 14.9 %collective-permute-start.25 = (bf16[2064,128]{1,0:T(8,128)(2,1)S(1)}, bf16[2064,128]{1,0:T(8,128)(2,1)S(1)}, u32[]{:S(2)}, u32[]{:S(2)}) collective-permute-start(bf16[2064,128]{1,0:T(8,128)(2,1)S(1)} %hold.11.refs_1_.refs_2_), channel_id=1, source_target_pairs={{0,8},{1,9},{2,10},{3,11},{4,0},{5,1},{6,2},{7,3},{8,12},{9,13},{1... | collective-permute-start | bytes 1585160 | tf_op jit(solution)/shard_map/ppermute | solution.py:391
  53.1 1.7 %collective-permute-start.23 = (bf16[48,2048]{1,0:T(8,128)(2,1)S(1)}, bf16[48,2048]{1,0:T(8,128)(2,1)S(1)}, u32[]{:S(2)}, u32[]{:S(2)}) collective-permute-start(bf16[48,2048]{1,0:T(8,128)(2,1)S(1)} %get-tuple-element.121), channel_id=1, source_target_pairs={{0,1},{1,0},{2,3},{3,2},{4,5},{5,4},{6,7},{7,6},{8,9},{9,8},{10,11... | collective-permute-start | bytes 589832 | tf_op jit(solution)/shard_map/ppermute | solution.py:397
  53.6 12.1 %collective-permute-start.27 = (bf16[1552,128]{1,0:T(8,128)(2,1)S(1)}, bf16[1552,128]{1,0:T(8,128)(2,1)S(1)}, u32[]{:S(2)}, u32[]{:S(2)}) collective-permute-start(bf16[1552,128]{1,0:T(8,128)(2,1)S(1)} %join.17.refs_1_), channel_id=1, source_target_pairs={{0,2},{1,3},{2,0},{3,1},{4,6},{5,7},{6,4},{7,5},{8,10},{9,11},{10,... | collective-permute-start | bytes 1191944 | tf_op jit(solution)/shard_map/ppermute | solution.py:394
  55.7 20.6 %collective-permute-start.28 = (bf16[128,2048]{1,0:T(8,128)(2,1)S(1)}, bf16[128,2048]{1,0:T(8,128)(2,1)S(1)}, u32[]{:S(2)}, u32[]{:S(2)}) collective-permute-start(bf16[128,2048]{1,0:T(8,128)(2,1)S(1)} %hold.13.refs_1_), channel_id=1, source_target_pairs={{0,8},{1,9},{2,10},{3,11},{4,0},{5,1},{6,2},{7,3},{8,12},{9,13},{1... | collective-permute-start | bytes 1572872 | tf_op jit(solution)/shard_map/ppermute | solution.py:391
  59.2 1.5 %collective-permute-start.26 = (bf16[48,2176]{1,0:T(8,128)(2,1)S(1)}, bf16[48,2176]{1,0:T(8,128)(2,1)S(1)}, u32[]{:S(2)}, u32[]{:S(2)}) collective-permute-start(bf16[48,2176]{1,0:T(8,128)(2,1)S(1)} %get-tuple-element.122), channel_id=1, source_target_pairs={{0,1},{1,0},{2,3},{3,2},{4,5},{5,4},{6,7},{7,6},{8,9},{9,8},{10,11... | collective-permute-start | bytes 626696 | tf_op jit(solution)/shard_map/ppermute | solution.py:397
  59.2 14.9 %collective-permute-start.24 = (bf16[96,2048]{1,0:T(8,128)(2,1)S(1)}, bf16[96,2048]{1,0:T(8,128)(2,1)S(1)}, u32[]{:S(2)}, u32[]{:S(2)}) collective-permute-start(bf16[96,2048]{1,0:T(8,128)(2,1)S(1)} %join.18.refs_1_), channel_id=1, source_target_pairs={{0,2},{1,3},{2,0},{3,1},{4,6},{5,7},{6,4},{7,5},{8,10},{9,11},{10,... | collective-permute-start | bytes 1179656 | tf_op jit(solution)/shard_map/ppermute | solution.py:394
  66.3 1.8 %collective-permute-start.29 = (bf16[32,2048]{1,0:T(8,128)(2,1)S(1)}, bf16[32,2048]{1,0:T(8,128)(2,1)S(1)}, u32[]{:S(2)}, u32[]{:S(2)}) collective-permute-start(bf16[32,2048]{1,0:T(8,128)(2,1)S(1)} %slice.40), channel_id=1, source_target_pairs={{0,1},{1,0},{2,3},{3,2},{4,5},{5,4},{6,7},{7,6},{8,9},{9,8},{10,11... | collective-permute-start | bytes 393224 | tf_op jit(solution)/shard_map/ppermute | solution.py:397
  66.4 6.8 %collective-permute-start.31 = (bf16[48,2048]{1,0:T(8,128)(2,1)S(1)}, bf16[48,2048]{1,0:T(8,128)(2,1)S(1)}, u32[]{:S(2)}, u32[]{:S(2)}) collective-permute-start(bf16[48,2048]{1,0:T(8,128)(2,1)S(1)} %get-tuple-element.128), channel_id=1, source_target_pairs={{0,1},{1,0},{2,3},{3,2},{4,5},{5,4},{6,7},{7,6},{8,9},{9,8},{10,11... | collective-permute-start | bytes 589832 | tf_op jit(solution)/shard_map/ppermute | solution.py:397
  68.1 14.5 %collective-permute-start.34 = (bf16[96,2048]{1,0:T(8,128)(2,1)S(1)}, bf16[96,2048]{1,0:T(8,128)(2,1)S(1)}, u32[]{:S(2)}, u32[]{:S(2)}) collective-permute-start(bf16[96,2048]{1,0:T(8,128)(2,1)S(1)} %join.19.refs_4_), channel_id=1, source_target_pairs={{0,2},{1,3},{2,0},{3,1},{4,6},{5,7},{6,4},{7,5},{8,10},{9,11},{10,... | collective-permute-start | bytes 1179656 | tf_op jit(solution)/shard_map/ppermute | solution.py:394
  69.5 18.6 %collective-permute-start.38 = (bf16[144,2048]{1,0:T(8,128)(2,1)S(1)}, bf16[144,2048]{1,0:T(8,128)(2,1)S(1)}, u32[]{:S(2)}, u32[]{:S(2)}) collective-permute-start(bf16[144,2048]{1,0:T(8,128)(2,1)S(1)} %home.7.refs_1_), channel_id=1, source_target_pairs={{0,8},{1,9},{2,10},{3,11},{4,0},{5,1},{6,2},{7,3},{8,12},{9,13},{1... | collective-permute-start | bytes 1769480 | tf_op jit(solution)/shard_map/ppermute | solution.py:391
  76.7 1.7 %collective-permute-start.33 = (bf16[48,2048]{1,0:T(8,128)(2,1)S(1)}, bf16[48,2048]{1,0:T(8,128)(2,1)S(1)}, u32[]{:S(2)}, u32[]{:S(2)}) collective-permute-start(bf16[48,2048]{1,0:T(8,128)(2,1)S(1)} %get-tuple-element.132), channel_id=1, source_target_pairs={{0,1},{1,0},{2,3},{3,2},{4,5},{5,4},{6,7},{7,6},{8,9},{9,8},{10,11... | collective-permute-start | bytes 589832 | tf_op jit(solution)/shard_map/ppermute | solution.py:397
  78.4 12.0 %collective-permute-start.42 = (bf16[96,2048]{1,0:T(8,128)(2,1)S(1)}, bf16[96,2048]{1,0:T(8,128)(2,1)S(1)}, u32[]{:S(2)}, u32[]{:S(2)}) collective-permute-start(bf16[96,2048]{1,0:T(8,128)(2,1)S(1)} %join.20.refs_10_), channel_id=1, source_target_pairs={{0,2},{1,3},{2,0},{3,1},{4,6},{5,7},{6,4},{7,5},{8,10},{9,11},{10,... | collective-permute-start | bytes 1179656 | tf_op jit(solution)/shard_map/ppermute | solution.py:394
  82.7 5.4 %collective-permute-start.37 = (bf16[48,2176]{1,0:T(8,128)(2,1)S(1)}, bf16[48,2176]{1,0:T(8,128)(2,1)S(1)}, u32[]{:S(2)}, u32[]{:S(2)}) collective-permute-start(bf16[48,2176]{1,0:T(8,128)(2,1)S(1)} %get-tuple-element.141), channel_id=1, source_target_pairs={{0,1},{1,0},{2,3},{3,2},{4,5},{5,4},{6,7},{7,6},{8,9},{9,8},{10,11... | collective-permute-start | bytes 626696 | tf_op jit(solution)/shard_map/ppermute | solution.py:397
  82.8 1.8 %collective-permute-start.35 = (bf16[32,2176]{1,0:T(8,128)(2,1)S(1)}, bf16[32,2176]{1,0:T(8,128)(2,1)S(1)}, u32[]{:S(2)}, u32[]{:S(2)}) collective-permute-start(bf16[32,2176]{1,0:T(8,128)(2,1)S(1)} %slice.42), channel_id=1, source_target_pairs={{0,1},{1,0},{2,3},{3,2},{4,5},{5,4},{6,7},{7,6},{8,9},{9,8},{10,11... | collective-permute-start | bytes 417800 | tf_op jit(solution)/shard_map/ppermute | solution.py:397
  84.7 14.3 %collective-permute-start.48 = (bf16[1552,128]{1,0:T(8,128)(2,1)S(1)}, bf16[1552,128]{1,0:T(8,128)(2,1)S(1)}, u32[]{:S(2)}, u32[]{:S(2)}) collective-permute-start(bf16[1552,128]{1,0:T(8,128)(2,1)S(1)} %join.21.refs_4_), channel_id=1, source_target_pairs={{0,2},{1,3},{2,0},{3,1},{4,6},{5,7},{6,4},{7,5},{8,10},{9,11},{10,... | collective-permute-start | bytes 1191944 | tf_op jit(solution)/shard_map/ppermute | solution.py:394
  88.1 5.8 %collective-permute-start.39 = (bf16[48,2176]{1,0:T(8,128)(2,1)S(1)}, bf16[48,2176]{1,0:T(8,128)(2,1)S(1)}, u32[]{:S(2)}, u32[]{:S(2)}) collective-permute-start(bf16[48,2176]{1,0:T(8,128)(2,1)S(1)} %get-tuple-element.143), channel_id=1, source_target_pairs={{0,1},{1,0},{2,3},{3,2},{4,5},{5,4},{6,7},{7,6},{8,9},{9,8},{10,11... | collective-permute-start | bytes 626696 | tf_op jit(solution)/shard_map/ppermute | solution.py:397
  88.1 5.7 %collective-permute-start.40 = (bf16[32,2176]{1,0:T(8,128)(2,1)S(1)}, bf16[32,2176]{1,0:T(8,128)(2,1)S(1)}, u32[]{:S(2)}, u32[]{:S(2)}) collective-permute-start(bf16[32,2176]{1,0:T(8,128)(2,1)S(1)} %slice.44), channel_id=1, source_target_pairs={{0,1},{1,0},{2,3},{3,2},{4,5},{5,4},{6,7},{7,6},{8,9},{9,8},{10,11... | collective-permute-start | bytes 417800 | tf_op jit(solution)/shard_map/ppermute | solution.py:397
  88.7 4.5 %collective-permute-start.41 = (bf16[16,2176]{1,0:T(8,128)(2,1)S(1)}, bf16[16,2176]{1,0:T(8,128)(2,1)S(1)}, u32[]{:S(2)}, u32[]{:S(2)}) collective-permute-start(bf16[16,2176]{1,0:T(8,128)(2,1)S(1)} %slice.45), channel_id=1, source_target_pairs={{0,1},{1,0},{2,3},{3,2},{4,5},{5,4},{6,7},{7,6},{8,9},{9,8},{10,11... | collective-permute-start | bytes 208904 | tf_op jit(solution)/shard_map/ppermute | solution.py:397
  93.1 1.6 %collective-permute-start.43 = (bf16[32,2176]{1,0:T(8,128)(2,1)S(1)}, bf16[32,2176]{1,0:T(8,128)(2,1)S(1)}, u32[]{:S(2)}, u32[]{:S(2)}) collective-permute-start(bf16[32,2176]{1,0:T(8,128)(2,1)S(1)} %slice.46), channel_id=1, source_target_pairs={{0,1},{1,0},{2,3},{3,2},{4,5},{5,4},{6,7},{7,6},{8,9},{9,8},{10,11... | collective-permute-start | bytes 417800 | tf_op jit(solution)/shard_map/ppermute | solution.py:397
  93.7 2.6 %collective-permute-start.45 = (bf16[48,2176]{1,0:T(8,128)(2,1)S(1)}, bf16[48,2176]{1,0:T(8,128)(2,1)S(1)}, u32[]{:S(2)}, u32[]{:S(2)}) collective-permute-start(bf16[48,2176]{1,0:T(8,128)(2,1)S(1)} %get-tuple-element.150), channel_id=1, source_target_pairs={{0,1},{1,0},{2,3},{3,2},{4,5},{5,4},{6,7},{7,6},{8,9},{9,8},{10,11... | collective-permute-start | bytes 626696 | tf_op jit(solution)/shard_map/ppermute | solution.py:397
  94.8 14.9 %collective-permute-start.47 = (bf16[1552,128]{1,0:T(8,128)(2,1)S(1)}, bf16[1552,128]{1,0:T(8,128)(2,1)S(1)}, u32[]{:S(2)}, u32[]{:S(2)}) collective-permute-start(bf16[1552,128]{1,0:T(8,128)(2,1)S(1)} %join.22.refs_3_), channel_id=1, source_target_pairs={{0,2},{1,3},{2,0},{3,1},{4,6},{5,7},{6,4},{7,5},{8,10},{9,11},{10,... | collective-permute-start | bytes 1191944 | tf_op jit(solution)/shard_map/ppermute | solution.py:394
  99.2 10.4 %collective-permute-start.49 = (bf16[128,896]{1,0:T(8,128)(2,1)S(1)}, bf16[128,896]{1,0:T(8,128)(2,1)S(1)}, u32[]{:S(2)}, u32[]{:S(2)}) collective-permute-start(bf16[128,896]{1,0:T(8,128)(2,1)S(1)} %home.8.refs_5_), channel_id=1, source_target_pairs={{0,8},{1,9},{2,10},{3,11},{4,0},{5,1},{6,2},{7,3},{8,12},{9,13},{1... | collective-permute-start | bytes 688136 | tf_op jit(solution)/shard_map/ppermute | solution.py:391
  102.3 21.8 %collective-permute-start.46 = (bf16[1552,128]{1,0:T(8,128)(2,1)S(1)}, bf16[1552,128]{1,0:T(8,128)(2,1)S(1)}, u32[]{:S(2)}, u32[]{:S(2)}) collective-permute-start(bf16[1552,128]{1,0:T(8,128)(2,1)S(1)} %join.23.refs_5_), channel_id=1, source_target_pairs={{0,2},{1,3},{2,0},{3,1},{4,6},{5,7},{6,4},{7,5},{8,10},{9,11},{10,... | collective-permute-start | bytes 1191944 | tf_op jit(solution)/shard_map/ppermute | solution.py:394
  104.0 8.1 %collective-permute-start.51 = (bf16[128,640]{1,0:T(8,128)(2,1)S(1)}, bf16[128,640]{1,0:T(8,128)(2,1)S(1)}, u32[]{:S(2)}, u32[]{:S(2)}) collective-permute-start(bf16[128,640]{1,0:T(8,128)(2,1)S(1)} %home.9.refs_5_), channel_id=1, source_target_pairs={{0,8},{1,9},{2,10},{3,11},{4,0},{5,1},{6,2},{7,3},{8,12},{9,13},{1... | collective-permute-start | bytes 491528 | tf_op jit(solution)/shard_map/ppermute | solution.py:391
  105.8 9.7 %collective-permute-start.53 = (bf16[144,512]{1,0:T(8,128)(2,1)S(1)}, bf16[144,512]{1,0:T(8,128)(2,1)S(1)}, u32[]{:S(2)}, u32[]{:S(2)}) collective-permute-start(bf16[144,512]{1,0:T(8,128)(2,1)S(1)} %home.10.refs_16_), channel_id=1, source_target_pairs={{0,8},{1,9},{2,10},{3,11},{4,0},{5,1},{6,2},{7,3},{8,12},{9,13},{1... | collective-permute-start | bytes 442376 | tf_op jit(solution)/shard_map/ppermute | solution.py:391
  109.9 14.7 %collective-permute-start.50 = (bf16[128,896]{1,0:T(8,128)(2,1)S(1)}, bf16[128,896]{1,0:T(8,128)(2,1)S(1)}, u32[]{:S(2)}, u32[]{:S(2)}) collective-permute-start(bf16[128,896]{1,0:T(8,128)(2,1)S(1)} %home.11.refs_5_), channel_id=1, source_target_pairs={{0,8},{1,9},{2,10},{3,11},{4,0},{5,1},{6,2},{7,3},{8,12},{9,13},{1... | collective-permute-start | bytes 688136 | tf_op jit(solution)/shard_map/ppermute | solution.py:391
  112.3 12.2 %collective-permute-start.52 = (bf16[128,640]{1,0:T(8,128)(2,1)S(1)}, bf16[128,640]{1,0:T(8,128)(2,1)S(1)}, u32[]{:S(2)}, u32[]{:S(2)}) collective-permute-start(bf16[128,640]{1,0:T(8,128)(2,1)S(1)} %home.12.refs_5_), channel_id=1, source_target_pairs={{0,8},{1,9},{2,10},{3,11},{4,0},{5,1},{6,2},{7,3},{8,12},{9,13},{1... | collective-permute-start | bytes 491528 | tf_op jit(solution)/shard_map/ppermute | solution.py:391
  115.8 8.7 %collective-permute-start.54 = (bf16[144,512]{1,0:T(8,128)(2,1)S(1)}, bf16[144,512]{1,0:T(8,128)(2,1)S(1)}, u32[]{:S(2)}, u32[]{:S(2)}) collective-permute-start(bf16[144,512]{1,0:T(8,128)(2,1)S(1)} %home.13.refs_16_), channel_id=1, source_target_pairs={{0,8},{1,9},{2,10},{3,11},{4,0},{5,1},{6,2},{7,3},{8,12},{9,13},{1... | collective-permute-start | bytes 442376 | tf_op jit(solution)/shard_map/ppermute | solution.py:391
  (14 other events, 60.6 us)

commit v8 on v7

--- a/solution.py
+++ b/solution.py
@@ -116,7 +116,7 @@
         self.last = []
         self.pending = []
 
-    def __call__(self, kernel, outs, name, *operands, after=(), scratch=(), smem=0, hbm=0, limit=16):
+    def __call__(self, kernel, outs, name, *operands, after=(), scratch=(), smem=0, hbm=0, hbm_out=(), limit=16):
         vmem = pl.BlockSpec(memory_space=pltpu.VMEM)
         scalar = pl.BlockSpec(memory_space=pltpu.SMEM)
         anywhere = pl.BlockSpec(memory_space=pl.ANY)
@@ -134,7 +134,7 @@
             + [outside] * hbm
             + [vmem] * (fixed - smem - hbm)
             + [anywhere] * len(unused),
-            out_specs=[vmem] * len(outs),
+            out_specs=[outside if i in hbm_out else vmem for i in range(len(outs))],
             scratch_shapes=list(scratch),
             name=name,
             compiler_params=pltpu.CompilerParams(vmem_limit_bytes=limit << 20),
@@ -314,15 +314,21 @@
         out_ref[rows:, :] = jnp.concatenate([router, rest], axis=1).astype(BF16)
 
 
-def total_kernel(ids_ref, levels_ref, pick_ref, *refs):
-    term_refs, passed_refs, (grad_ref, router_ref) = refs[:3], refs[3:-2], refs[-2:]
+def own_kernel(pick_ref, *refs):
+    *term_refs, sum_ref, rows_ref = refs
+    features = sum_ref.shape[1]
+    total, router = plane_sum(pick_ref, term_refs, features, slice(0, features), rows_ref.shape[0])
+    sum_ref[...] = total.astype(BF16)
+    rows_ref[...] = router
+
+
+def total_kernel(ids_ref, levels_ref, sum_ref, rows_ref, *refs):
+    passed_refs, (grad_ref, router_ref) = refs[:-2], refs[-2:]
     fanout, rows = ids_ref.shape
-    features = grad_ref.shape[1]
-    experts = passed_refs[-1].shape[0] - rows
+    experts = rows_ref.shape[0]
     passed = jnp.concatenate([ref[:rows, :] for ref in passed_refs], axis=1)
-    total, router = plane_sum(pick_ref, term_refs, features, slice(0, features), experts)
-    grad_ref[...] = (total + passed.astype(F32)).astype(BF16)
-    router = router + passed_refs[-1][rows:, :LANES].astype(F32)
+    grad_ref[...] = (sum_ref[...].astype(F32) + passed.astype(F32)).astype(BF16)
+    router = rows_ref[...] + passed_refs[-1][rows:, :LANES].astype(F32)
     expert = lax.broadcasted_iota(jnp.int32, (experts, rows), 0)
     for k in range(fanout):
         own = jnp.where(ids_ref[k : k + 1, :] == expert, router, 0.0)
@@ -339,34 +345,40 @@
 
 
 def down_kernel(chunks, *refs):
-    *d_refs, down_ref, done_ref, d_all = refs
+    *d_refs, down_ref, done_ref, d_all, parts, sems = refs
     hidden_refs, d_refs = d_refs[:chunks], d_refs[chunks:]
     done_ref[...] = jnp.zeros_like(done_ref)
     stacked(d_refs, d_all)
     hidden = joined(hidden_refs)
-    step = 512
-
-    @pl.loop(0, down_ref.shape[1] // step)
-    def _(i):
-        cols = pl.ds(pl.multiple_of(i * step, step), step)
-        down_ref[:, cols] = dot(hidden, d_all[:, cols], ((0,), (0,))).astype(BF16)
+    count, _, step = parts.shape
+    copies = []
+    for i in range(count):
+        cols = slice(step * i, step * (i + 1))
+        parts[i] = dot(hidden, d_all[:, cols], ((0,), (0,))).astype(BF16)
+        copies.append(pltpu.make_async_copy(parts.at[i], down_ref.at[:, cols], sems.at[i]))
+        copies[-1].start()
+    for copy in copies:
+        copy.wait()
 
 
 def gate_up_kernel(chunks, *refs):
-    *x_refs, gate_ref, up_ref, done_ref, x_all = refs
+    *x_refs, gate_ref, up_ref, done_ref, x_all, parts, sems = refs
     grads_refs, x_refs = x_refs[:chunks], x_refs[chunks:]
     done_ref[...] = jnp.zeros_like(done_ref)
     stacked(x_refs, x_all)
     grads = joined(grads_refs)
-    features, units = gate_ref.shape
-    step = 512
-
-    @pl.loop(0, features // step)
-    def _(i):
-        cols = pl.ds(pl.multiple_of(i * step, step), step)
+    count, _, step, units = parts.shape
+    copies = []
+    for i in range(count):
+        cols = slice(step * i, step * (i + 1))
         both = dot(x_all[:, cols], grads, ((0,), (0,))).astype(BF16)
-        gate_ref[cols, :] = both[:, :units]
-        up_ref[cols, :] = both[:, units:]
+        for j, out_ref in enumerate((gate_ref, up_ref)):
+            parts[i, j] = both[:, units * j : units * (j + 1)]
+            copy = pltpu.make_async_copy(parts.at[i, j], out_ref.at[cols, :], sems.at[i, j])
+            copy.start()
+            copies.append(copy)
+    for copy in copies:
+        copy.wait()
 
 
 def staged(tokens, cotangent, expert_ids, gate_levels, w_gate, w_up, w_down):
@@ -540,7 +552,12 @@
         "down_delta",
         *[hidden[s] for s in order],
         *[block for s in order for block in rows_d[s]],
-        scratch=[pltpu.VMEM((planes * rows, features), BF16)],
+        hbm_out=(0,),
+        scratch=[
+            pltpu.VMEM((planes * rows, features), BF16),
+            pltpu.VMEM((4, units, features // 4), BF16),
+            pltpu.SemaphoreType.DMA((4,)),
+        ],
     )
     passed = [home(last, part, whole) for whole, part in zip(passed, columns)]
     gate_delta, up_delta, _ = run(
@@ -549,7 +566,19 @@
         "gate_up_delta",
         *[grads[s] for s in order],
         *[block for s in order for block in rows_x[s]],
-        scratch=[pltpu.VMEM((planes * rows, features), BF16)],
+        hbm_out=(0, 1),
+        scratch=[
+            pltpu.VMEM((planes * rows, features), BF16),
+            pltpu.VMEM((4, 2, features // 4, units), BF16),
+            pltpu.SemaphoreType.DMA((4, 2)),
+        ],
+    )
+    own_sum, own_router = run(
+        own_kernel,
+        [((tok_rows, features), BF16), ((devices, tok_rows), F32)],
+        "own",
+        pick[0],
+        *terms[0],
     )
     input_grad, router_grad = run(
         total_kernel,
@@ -557,8 +586,8 @@
         "total",
         ids,
         levels,
-        pick[0],
-        *terms[0],
+        own_sum,
+        own_router,
         *passed,
     )
     return input_grad, router_grad.T, gate_delta[None], up_delta[None], down_delta[None]
@@ -572,7 +601,7 @@
     def on_device(*arrays):
         tok_rows, fanout = arrays[2].shape
         capacity = 3 * tok_rows * fanout // (2 * devices)
-        plan = staged if PLANE * capacity > tok_rows and devices % PLANE == 0 else direct
+        plan = staged if PLANE * capacity > tok_rows and devices == 4 * PLANE else direct
         return plan(*arrays)
 
     return jax.shard_map(

time: 126 us -> 126 us (level)
  Pallas kernels: 28.6 us -> 25.9 us
  waiting for transfers between devices: 38.8 us -> 40.1 us
    pallas_call x35 -> x36, Pallas kernels: 28.6 us -> 25.9 us  [__call__(): pl.pallas_call(body, out_shape=[jax.ShapeDtypeStruct(shape, kind) for sha...]
    ppermute x13, waiting for transfers between devices: 15.3 us -> 16.6 us  [along(): return lax.ppermute(array, 'expert', pairs)]
  transfers between devices with their start and end apart: 55 -> 55, of which waited for: 25 -> 25; matrix products, arithmetic and copies ran while one was open for 0% -> 0% of each run, Pallas kernels for 20% -> 18%
where the time goes in v8:
time: 126 us
  starting transfers between devices  57.3 us (45%)
  waiting for transfers between devices  40.1 us (32%)
  Pallas kernels  25.9 us (21%)
    ppermute x13, starting transfers between devices, along(): return lax.ppermute(array, 'expert', pairs)  34.5 us
    pallas_call x36, Pallas kernels, __call__(): pl.pallas_call(body, out_shape=[jax.ShapeDtypeStruct(shape, kind) for sha...  25.9 us
    ppermute x13, waiting for transfers between devices, along(): return lax.ppermute(array, 'expert', pairs)  16.6 us
    ppermute x12, starting transfers between devices, across(): return lax.ppermute(array, 'expert', [(i, i ^ 2) for i in range(devices)])  15.4 us
    ppermute x12, waiting for transfers between devices, across(): return lax.ppermute(array, 'expert', [(i, i ^ 2) for i in range(devices)])  15.2 us
    ppermute x30, waiting for transfers between devices, cores(): return lax.ppermute(array, 'expert', [(i, i ^ 1) for i in range(devices)])  8.34 us
    ppermute x30, starting transfers between devices, cores(): return lax.ppermute(array, 'expert', [(i, i ^ 1) for i in range(devices)])  7.34 us
  transfers between devices with their start and end apart: 55, of which 25 were waited for; matrix products, arithmetic and copies ran while one was open for 0% of the time, Pallas kernels for 18%

profile of v8, /device:TPU:0, one launch (start us, length us, event | category | flops | bytes accessed | tf_op | source)
XLA Modules:
  0.0 125.6 jit_solution(14332182098621644711)
XLA Ops:
  0.6 2.0 %pack.1.refs_1_.refs_2_ = bf16[2064,128]{1,0:T(8,128)(2,1)} custom-call(s32[4,128]{1,0:T(4,128)} %bitcast.22, s32[4,128]{1,0:T(4,128)} %bitcast.24, bf16[128,2048]{1,0:T(8,128)(2,1)} %refs_2_.1), custom_call_target="tpu_custom_call" | custom-call | flops 1000 | bytes 1000 | tf_op jit(solution)/shard_map/pack/pallas_call | solution.py:130
  2.7 4.1 %collective-permute-start.7 = (bf16[2064,128]{1,0:T(8,128)(2,1)}, bf16[2064,128]{1,0:T(8,128)(2,1)S(1)}, u32[]{:S(2)}, u32[]{:S(2)}) collective-permute-start(bf16[2064,128]{1,0:T(8,128)(2,1)} %pack.1.refs_1_.refs_2_), channel_id=1, source_target_pairs={{0,8},{1,9},{2,10},{3,11},{4,0},{5,1},{6,2},{7,3},{8,12},{9,13},{1... | collective-permute-start | bytes 1585160 | tf_op jit(solution)/shard_map/ppermute | solution.py:403
  6.8 1.1 copy-done.3
  9.1 1.2 collective-permute-done.2.refs_2_
  10.3 1.6 %collective-permute-start.3 = (bf16[96,2048]{1,0:T(8,128)(2,1)S(1)}, bf16[96,2048]{1,0:T(8,128)(2,1)S(1)}, u32[]{:S(2)}, u32[]{:S(2)}) collective-permute-start(bf16[96,2048]{1,0:T(8,128)(2,1)S(1)} %join.12.refs_2_), channel_id=1, source_target_pairs={{0,2},{1,3},{2,0},{3,1},{4,6},{5,7},{6,4},{7,5},{8,10},{9,11},{10,... | collective-permute-start | bytes 1179656 | tf_op jit(solution)/shard_map/ppermute | solution.py:406
  12.9 1.6 %collective-permute-start.8 = (bf16[128,2048]{1,0:T(8,128)(2,1)S(1)}, bf16[128,2048]{1,0:T(8,128)(2,1)S(1)}, u32[]{:S(2)}, u32[]{:S(2)}) collective-permute-start(bf16[128,2048]{1,0:T(8,128)(2,1)S(1)} %copy-done.4), channel_id=1, source_target_pairs={{0,8},{1,9},{2,10},{3,11},{4,0},{5,1},{6,2},{7,3},{8,12},{9,13},{1... | collective-permute-start | bytes 1572872 | tf_op jit(solution)/shard_map/ppermute | solution.py:403
  15.0 7.3 %collective-permute-done.3.refs_2_.refs_3_.refs_6_ = bf16[96,2048]{1,0:T(8,128)(2,1)S(1)} collective-permute-done((bf16[96,2048]{1,0:T(8,128)(2,1)S(1)}, bf16[96,2048]{1,0:T(8,128)(2,1)S(1)}, u32[]{:S(2)}, u32[]{:S(2)}) %collective-permute-start.3) | collective-permute-done | bytes 393248 | tf_op jit(solution)/shard_map/ppermute | solution.py:406
  23.5 1.6 %collective-permute-start.13 = (bf16[2064,128]{1,0:T(8,128)(2,1)S(1)}, bf16[2064,128]{1,0:T(8,128)(2,1)S(1)}, u32[]{:S(2)}, u32[]{:S(2)}) collective-permute-start(bf16[2064,128]{1,0:T(8,128)(2,1)S(1)} %hold.9.refs_1_.refs_2_), channel_id=1, source_target_pairs={{0,8},{1,9},{2,10},{3,11},{4,0},{5,1},{6,2},{7,3},{8,12},{9,13},{1... | collective-permute-start | bytes 1585160 | tf_op jit(solution)/shard_map/ppermute | solution.py:403
  25.1 1.6 %collective-permute-start.14 = (bf16[96,2048]{1,0:T(8,128)(2,1)S(1)}, bf16[96,2048]{1,0:T(8,128)(2,1)S(1)}, u32[]{:S(2)}, u32[]{:S(2)}) collective-permute-start(bf16[96,2048]{1,0:T(8,128)(2,1)S(1)} %join.14.refs_1_), channel_id=1, source_target_pairs={{0,2},{1,3},{2,0},{3,1},{4,6},{5,7},{6,4},{7,5},{8,10},{9,11},{10,... | collective-permute-start | bytes 1179656 | tf_op jit(solution)/shard_map/ppermute | solution.py:406
  26.7 3.9 %collective-permute-done.8.refs_0_ = bf16[128,2048]{1,0:T(8,128)(2,1)S(1)} collective-permute-done((bf16[128,2048]{1,0:T(8,128)(2,1)S(1)}, bf16[128,2048]{1,0:T(8,128)(2,1)S(1)}, u32[]{:S(2)}, u32[]{:S(2)}) %collective-permute-start.8) | collective-permute-done | bytes 524320 | tf_op jit(solution)/shard_map/ppermute | solution.py:403
  31.7 0.9 collective-permute-done.11.refs_1_
  32.9 1.6 %collective-permute-start.19 = (bf16[96,2048]{1,0:T(8,128)(2,1)S(1)}, bf16[96,2048]{1,0:T(8,128)(2,1)S(1)}, u32[]{:S(2)}, u32[]{:S(2)}) collective-permute-start(bf16[96,2048]{1,0:T(8,128)(2,1)S(1)} %join.15.refs_10_), channel_id=1, source_target_pairs={{0,2},{1,3},{2,0},{3,1},{4,6},{5,7},{6,4},{7,5},{8,10},{9,11},{10,... | collective-permute-start | bytes 1179656 | tf_op jit(solution)/shard_map/ppermute | solution.py:406
  34.5 3.3 %collective-permute-start.18 = (bf16[128,2048]{1,0:T(8,128)(2,1)S(1)}, bf16[128,2048]{1,0:T(8,128)(2,1)S(1)}, u32[]{:S(2)}, u32[]{:S(2)}) collective-permute-start(bf16[128,2048]{1,0:T(8,128)(2,1)S(1)} %hold.10.refs_1_.refs_2_), channel_id=1, source_target_pairs={{0,8},{1,9},{2,10},{3,11},{4,0},{5,1},{6,2},{7,3},{8,12},{9,13},{1... | collective-permute-start | bytes 1572872 | tf_op jit(solution)/shard_map/ppermute | solution.py:403
  37.8 2.6 %expert.4 = (bf16[192,768]{1,0:T(8,128)(2,1)S(1)}, bf16[192,384]{1,0:T(8,128)(2,1)S(1)}, bf16[48,2176]{1,0:T(8,128)(2,1)S(1)}, bf16[48,2176]{1,0:T(8,128)(2,1)S(...) custom-call(s32[1]{0:T(128)} %bitcast.2.refs_0_, bf16[48,2048]{1,0:T(8,128)(2,1)S(1)} %get-tuple-element.87.refs_1_.refs_4_, ...), custom_call_target="tpu_custom_call" | custom-call | flops 1000 | bytes 1000 | tf_op jit(solution)/shard_map/expert/pallas_call | solution.py:130
  40.4 1.6 %collective-permute-done.13.refs_0_ = bf16[2064,128]{1,0:T(8,128)(2,1)S(1)} collective-permute-done((bf16[2064,128]{1,0:T(8,128)(2,1)S(1)}, bf16[2064,128]{1,0:T(8,128)(2,1)S(1)}, u32[]{:S(2)}, u32[]{:S(2)}) %collective-permute-start.13) | collective-permute-done | bytes 528416 | tf_op jit(solution)/shard_map/ppermute | solution.py:403
  43.1 0.9 collective-permute-done.15.refs_3_.refs_2_.refs_11_
  44.4 1.6 %collective-permute-start.17 = (bf16[96,2048]{1,0:T(8,128)(2,1)S(1)}, bf16[96,2048]{1,0:T(8,128)(2,1)S(1)}, u32[]{:S(2)}, u32[]{:S(2)}) collective-permute-start(bf16[96,2048]{1,0:T(8,128)(2,1)S(1)} %join.16.refs_10_), channel_id=1, source_target_pairs={{0,2},{1,3},{2,0},{3,1},{4,6},{5,7},{6,4},{7,5},{8,10},{9,11},{10,... | collective-permute-start | bytes 1179656 | tf_op jit(solution)/shard_map/ppermute | solution.py:406
  46.0 1.0 collective-permute-done.19.refs_6_.refs_2_.refs_9_
  47.0 2.6 %expert.5 = (bf16[192,768]{1,0:T(8,128)(2,1)S(1)}, bf16[192,384]{1,0:T(8,128)(2,1)S(1)}, bf16[48,2176]{1,0:T(8,128)(2,1)S(1)}, bf16[48,2176]{1,0:T(8,128)(2,1)S(...) custom-call(s32[1]{0:T(128)} %bitcast.2.refs_0_, ...), custom_call_target="tpu_custom_call" | custom-call | flops 1000 | bytes 1000 | tf_op jit(solution)/shard_map/expert/pallas_call | solution.py:130
  50.2 2.4 %collective-permute-start.25 = (bf16[2064,128]{1,0:T(8,128)(2,1)S(1)}, bf16[2064,128]{1,0:T(8,128)(2,1)S(1)}, u32[]{:S(2)}, u32[]{:S(2)}) collective-permute-start(bf16[2064,128]{1,0:T(8,128)(2,1)S(1)} %hold.11.refs_1_.refs_2_), channel_id=1, source_target_pairs={{0,8},{1,9},{2,10},{3,11},{4,0},{5,1},{6,2},{7,3},{8,12},{9,13},{1... | collective-permute-start | bytes 1585160 | tf_op jit(solution)/shard_map/ppermute | solution.py:403
  53.6 0.9 collective-permute-start.27
  55.7 3.4 %collective-permute-start.28 = (bf16[128,2048]{1,0:T(8,128)(2,1)S(1)}, bf16[128,2048]{1,0:T(8,128)(2,1)S(1)}, u32[]{:S(2)}, u32[]{:S(2)}) collective-permute-start(bf16[128,2048]{1,0:T(8,128)(2,1)S(1)} %hold.13.refs_1_), channel_id=1, source_target_pairs={{0,8},{1,9},{2,10},{3,11},{4,0},{5,1},{6,2},{7,3},{8,12},{9,13},{1... | collective-permute-start | bytes 1572872 | tf_op jit(solution)/shard_map/ppermute | solution.py:403
  59.2 1.5 %collective-permute-start.24 = (bf16[96,2048]{1,0:T(8,128)(2,1)S(1)}, bf16[96,2048]{1,0:T(8,128)(2,1)S(1)}, u32[]{:S(2)}, u32[]{:S(2)}) collective-permute-start(bf16[96,2048]{1,0:T(8,128)(2,1)S(1)} %join.18.refs_1_), channel_id=1, source_target_pairs={{0,2},{1,3},{2,0},{3,1},{4,6},{5,7},{6,4},{7,5},{8,10},{9,11},{10,... | collective-permute-start | bytes 1179656 | tf_op jit(solution)/shard_map/ppermute | solution.py:406
  60.7 4.4 %collective-permute-done.25.refs_0_ = bf16[2064,128]{1,0:T(8,128)(2,1)S(1)} collective-permute-done((bf16[2064,128]{1,0:T(8,128)(2,1)S(1)}, bf16[2064,128]{1,0:T(8,128)(2,1)S(1)}, u32[]{:S(2)}, u32[]{:S(2)}) %collective-permute-start.25) | collective-permute-done | bytes 528416 | tf_op jit(solution)/shard_map/ppermute | solution.py:403
  66.9 1.2 collective-permute-done.30.refs_2_
  68.1 1.0 collective-permute-start.34
  69.5 3.6 %collective-permute-start.38 = (bf16[144,2048]{1,0:T(8,128)(2,1)S(1)}, bf16[144,2048]{1,0:T(8,128)(2,1)S(1)}, u32[]{:S(2)}, u32[]{:S(2)}) collective-permute-start(bf16[144,2048]{1,0:T(8,128)(2,1)S(1)} %home.7.refs_1_), channel_id=1, source_target_pairs={{0,8},{1,9},{2,10},{3,11},{4,0},{5,1},{6,2},{7,3},{8,12},{9,13},{1... | collective-permute-start | bytes 1769480 | tf_op jit(solution)/shard_map/ppermute | solution.py:403
  73.1 1.0 collective-permute-done.24.refs_3_.refs_6_.refs_12_
  74.1 2.2 %collective-permute-done.28.refs_0_ = bf16[128,2048]{1,0:T(8,128)(2,1)S(1)} collective-permute-done((bf16[128,2048]{1,0:T(8,128)(2,1)S(1)}, bf16[128,2048]{1,0:T(8,128)(2,1)S(1)}, u32[]{:S(2)}, u32[]{:S(2)}) %collective-permute-start.28) | collective-permute-done | bytes 524320 | tf_op jit(solution)/shard_map/ppermute | solution.py:403
  77.2 0.9 collective-permute-done.32.refs_1_
  78.4 1.6 %collective-permute-start.42 = (bf16[96,2048]{1,0:T(8,128)(2,1)S(1)}, bf16[96,2048]{1,0:T(8,128)(2,1)S(1)}, u32[]{:S(2)}, u32[]{:S(2)}) collective-permute-start(bf16[96,2048]{1,0:T(8,128)(2,1)S(1)} %join.20.refs_10_), channel_id=1, source_target_pairs={{0,2},{1,3},{2,0},{3,1},{4,6},{5,7},{6,4},{7,5},{8,10},{9,11},{10,... | collective-permute-start | bytes 1179656 | tf_op jit(solution)/shard_map/ppermute | solution.py:406
  80.0 2.6 %expert.6 = (bf16[192,768]{1,0:T(8,128)(2,1)S(1)}, bf16[192,384]{1,0:T(8,128)(2,1)S(1)}, bf16[48,2176]{1,0:T(8,128)(2,1)S(1)}, bf16[48,2176]{1,0:T(8,128)(2,1)S(...) custom-call(s32[1]{0:T(128)} %bitcast.2.refs_0_, ...), custom_call_target="tpu_custom_call" | custom-call | flops 1000 | bytes 1000 | tf_op jit(solution)/shard_map/expert/pallas_call | solution.py:130
  83.4 1.2 collective-permute-done.36.refs_2_
  85.2 2.8 %collective-permute-done.38.refs_6_.refs_4_ = bf16[144,2048]{1,0:T(8,128)(2,1)S(1)} collective-permute-done((bf16[144,2048]{1,0:T(8,128)(2,1)S(1)}, bf16[144,2048]{1,0:T(8,128)(2,1)S(1)}, u32[]{:S(2)}, u32[]{:S(2)}) %collective-permute-start.38) | collective-permute-done | bytes 589856 | tf_op jit(solution)/shard_map/ppermute | solution.py:403
  88.7 1.7 %collective-permute-done.42.refs_6_.refs_15_ = bf16[96,2048]{1,0:T(8,128)(2,1)S(1)} collective-permute-done((bf16[96,2048]{1,0:T(8,128)(2,1)S(1)}, bf16[96,2048]{1,0:T(8,128)(2,1)S(1)}, u32[]{:S(2)}, u32[]{:S(2)}) %collective-permute-start.42) | collective-permute-done | bytes 393248 | tf_op jit(solution)/shard_map/ppermute | solution.py:406
  90.5 2.6 %expert.7 = (bf16[192,768]{1,0:T(8,128)(2,1)S(1)}, bf16[192,384]{1,0:T(8,128)(2,1)S(1)}, bf16[48,2176]{1,0:T(8,128)(2,1)S(1)}, bf16[48,2176]{1,0:T(8,128)(2,1)S(...) custom-call(s32[1]{0:T(128)} %bitcast.2.refs_0_, ...), custom_call_target="tpu_custom_call" | custom-call | flops 1000 | bytes 1000 | tf_op jit(solution)/shard_map/expert/pallas_call | solution.py:130
  94.8 1.5 %collective-permute-start.47 = (bf16[1552,128]{1,0:T(8,128)(2,1)S(1)}, bf16[1552,128]{1,0:T(8,128)(2,1)S(1)}, u32[]{:S(2)}, u32[]{:S(2)}) collective-permute-start(bf16[1552,128]{1,0:T(8,128)(2,1)S(1)} %join.22.refs_3_), channel_id=1, source_target_pairs={{0,2},{1,3},{2,0},{3,1},{4,6},{5,7},{6,4},{7,5},{8,10},{9,11},{10,... | collective-permute-start | bytes 1191944 | tf_op jit(solution)/shard_map/ppermute | solution.py:406
  96.4 2.5 %collective-permute-done.48.refs_3_ = bf16[1552,128]{1,0:T(8,128)(2,1)S(1)} collective-permute-done((bf16[1552,128]{1,0:T(8,128)(2,1)S(1)}, bf16[1552,128]{1,0:T(8,128)(2,1)S(1)}, u32[]{:S(2)}, u32[]{:S(2)}) %collective-permute-start.48) | collective-permute-done | bytes 397344 | tf_op jit(solution)/shard_map/ppermute | solution.py:406
  99.2 3.1 %collective-permute-start.51 = (bf16[128,896]{1,0:T(8,128)(2,1)S(1)}, bf16[128,896]{1,0:T(8,128)(2,1)S(1)}, u32[]{:S(2)}, u32[]{:S(2)}) collective-permute-start(bf16[128,896]{1,0:T(8,128)(2,1)S(1)} %home.8.refs_5_), channel_id=1, source_target_pairs={{0,8},{1,9},{2,10},{3,11},{4,0},{5,1},{6,2},{7,3},{8,12},{9,13},{1... | collective-permute-start | bytes 688136 | tf_op jit(solution)/shard_map/ppermute | solution.py:403
  102.3 1.5 %collective-permute-start.46 = (bf16[1552,128]{1,0:T(8,128)(2,1)S(1)}, bf16[1552,128]{1,0:T(8,128)(2,1)S(1)}, u32[]{:S(2)}, u32[]{:S(2)}) collective-permute-start(bf16[1552,128]{1,0:T(8,128)(2,1)S(1)} %join.23.refs_5_), channel_id=1, source_target_pairs={{0,2},{1,3},{2,0},{3,1},{4,6},{5,7},{6,4},{7,5},{8,10},{9,11},{10,... | collective-permute-start | bytes 1191944 | tf_op jit(solution)/shard_map/ppermute | solution.py:406
  104.0 1.6 %collective-permute-start.50 = (bf16[128,640]{1,0:T(8,128)(2,1)S(1)}, bf16[128,640]{1,0:T(8,128)(2,1)S(1)}, u32[]{:S(2)}, u32[]{:S(2)}) collective-permute-start(bf16[128,640]{1,0:T(8,128)(2,1)S(1)} %home.9.refs_5_), channel_id=1, source_target_pairs={{0,8},{1,9},{2,10},{3,11},{4,0},{5,1},{6,2},{7,3},{8,12},{9,13},{1... | collective-permute-start | bytes 491528 | tf_op jit(solution)/shard_map/ppermute | solution.py:403
  106.2 2.2 %down_delta.1 = (bf16[384,2048]{1,0:T(8,128)(2,1)}, f32[8,128]{1,0:T(8,128)S(1)}) custom-call(bf16[192,384]{1,0:T(8,128)(2,1)S(1)} %get-tuple-element.109.refs_1_.refs_0_, bf16[192,384]{1,0:T(8,128)(2,1)S(1)} %get-tuple-element.119.refs_3_.refs_1_, bf16[192,384]{1,0:T(8,128)(2,1)S(1)} %get-tuple-element.139.refs_4_.refs_2_, ...), custom_call_target="tpu_custom_call" | custom-call | flops 1000 | bytes 1000 | tf_op jit(solution)/shard_map/down_delta/pallas_call | solution.py:130
  108.7 3.3 %collective-permute-start.52 = (bf16[128,896]{1,0:T(8,128)(2,1)S(1)}, bf16[128,896]{1,0:T(8,128)(2,1)S(1)}, u32[]{:S(2)}, u32[]{:S(2)}) collective-permute-start(bf16[128,896]{1,0:T(8,128)(2,1)S(1)} %home.11.refs_5_), channel_id=1, source_target_pairs={{0,8},{1,9},{2,10},{3,11},{4,0},{5,1},{6,2},{7,3},{8,12},{9,13},{1... | collective-permute-start | bytes 688136 | tf_op jit(solution)/shard_map/ppermute | solution.py:403
  112.3 3.2 %collective-permute-start.53 = (bf16[128,640]{1,0:T(8,128)(2,1)S(1)}, bf16[128,640]{1,0:T(8,128)(2,1)S(1)}, u32[]{:S(2)}, u32[]{:S(2)}) collective-permute-start(bf16[128,640]{1,0:T(8,128)(2,1)S(1)} %home.12.refs_5_), channel_id=1, source_target_pairs={{0,8},{1,9},{2,10},{3,11},{4,0},{5,1},{6,2},{7,3},{8,12},{9,13},{1... | collective-permute-start | bytes 491528 | tf_op jit(solution)/shard_map/ppermute | solution.py:403
  115.8 2.9 %collective-permute-start.54 = (bf16[144,512]{1,0:T(8,128)(2,1)S(1)}, bf16[144,512]{1,0:T(8,128)(2,1)S(1)}, u32[]{:S(2)}, u32[]{:S(2)}) collective-permute-start(bf16[144,512]{1,0:T(8,128)(2,1)S(1)} %home.13.refs_16_), channel_id=1, source_target_pairs={{0,8},{1,9},{2,10},{3,11},{4,0},{5,1},{6,2},{7,3},{8,12},{9,13},{1... | collective-permute-start | bytes 442376 | tf_op jit(solution)/shard_map/ppermute | solution.py:403
  118.7 3.7 %gate_up_delta.1 = (bf16[2048,384]{1,0:T(8,128)(2,1)}, bf16[2048,384]{1,0:T(8,128)(2,1)}, f32[8,128]{1,0:T(8,128)S(1)}) custom-call(bf16[192,768]{1,0:T(8,128)(2,1)S(1)} %get-tuple-element.153.refs_0_, bf16[192,768]{1,0:T(8,128)(2,1)S(1)} %get-tuple-element.154.refs_1_, bf16[192,768]{1,0:T(8,128)(2,1)S(1)} %get-tuple-element.155.refs_2_, ...), custom_call_target="tpu_custom_call" | custom-call | flops 1000 | bytes 1000 | tf_op jit(solution)/shard_map/gate_up_delta/pallas_call | solution.py:130
  122.8 1.7 %collective-permute-done.54.refs_6_ = bf16[144,512]{1,0:T(8,128)(2,1)S(1)} collective-permute-done((bf16[144,512]{1,0:T(8,128)(2,1)S(1)}, bf16[144,512]{1,0:T(8,128)(2,1)S(1)}, u32[]{:S(2)}, u32[]{:S(2)}) %collective-permute-start.54) | collective-permute-done | bytes 147488 | tf_op jit(solution)/shard_map/ppermute | solution.py:403
  124.6 1.0 total.1
  (133 shorter events, 19.1 us)
Async XLA Ops:
  2.7 19.6 %collective-permute-start.7 = (bf16[2064,128]{1,0:T(8,128)(2,1)}, bf16[2064,128]{1,0:T(8,128)(2,1)S(1)}, u32[]{:S(2)}, u32[]{:S(2)}) collective-permute-start(bf16[2064,128]{1,0:T(8,128)(2,1)} %pack.1.refs_1_.refs_2_), channel_id=1, source_target_pairs={{0,8},{1,9},{2,10},{3,11},{4,0},{5,1},{6,2},{7,3},{8,12},{9,13},{1... | collective-permute-start | bytes 1585160 | tf_op jit(solution)/shard_map/ppermute | solution.py:403
  8.5 1.8 %collective-permute-start.1 = (bf16[32,2048]{1,0:T(8,128)(2,1)S(1)}, bf16[32,2048]{1,0:T(8,128)(2,1)S(1)}, u32[]{:S(2)}, u32[]{:S(2)}) collective-permute-start(bf16[32,2048]{1,0:T(8,128)(2,1)S(1)} %slice.36), channel_id=1, source_target_pairs={{0,1},{1,0},{2,3},{3,2},{4,5},{5,4},{6,7},{7,6},{8,9},{9,8},{10,11... | collective-permute-start | bytes 393224 | tf_op jit(solution)/shard_map/ppermute | solution.py:409
  8.5 4.3 %collective-permute-start = (bf16[48,2048]{1,0:T(8,128)(2,1)S(1)}, bf16[48,2048]{1,0:T(8,128)(2,1)S(1)}, u32[]{:S(2)}, u32[]{:S(2)}) collective-permute-start(bf16[48,2048]{1,0:T(8,128)(2,1)S(1)} %get-tuple-element.88), channel_id=1, source_target_pairs={{0,1},{1,0},{2,3},{3,2},{4,5},{5,4},{6,7},{7,6},{8,9},{9,8},{10,11... | collective-permute-start | bytes 589832 | tf_op jit(solution)/shard_map/ppermute | solution.py:409
  10.3 12.0 %collective-permute-start.3 = (bf16[96,2048]{1,0:T(8,128)(2,1)S(1)}, bf16[96,2048]{1,0:T(8,128)(2,1)S(1)}, u32[]{:S(2)}, u32[]{:S(2)}) collective-permute-start(bf16[96,2048]{1,0:T(8,128)(2,1)S(1)} %join.12.refs_2_), channel_id=1, source_target_pairs={{0,2},{1,3},{2,0},{3,1},{4,6},{5,7},{6,4},{7,5},{8,10},{9,11},{10,... | collective-permute-start | bytes 1179656 | tf_op jit(solution)/shard_map/ppermute | solution.py:406
  12.3 2.2 %collective-permute-start.4 = (bf16[48,2048]{1,0:T(8,128)(2,1)S(1)}, bf16[48,2048]{1,0:T(8,128)(2,1)S(1)}, u32[]{:S(2)}, u32[]{:S(2)}) collective-permute-start(bf16[48,2048]{1,0:T(8,128)(2,1)S(1)} %get-tuple-element.93), channel_id=1, source_target_pairs={{0,1},{1,0},{2,3},{3,2},{4,5},{5,4},{6,7},{7,6},{8,9},{9,8},{10,11... | collective-permute-start | bytes 589832 | tf_op jit(solution)/shard_map/ppermute | solution.py:409
  12.4 2.1 %collective-permute-start.5 = (bf16[48,2048]{1,0:T(8,128)(2,1)S(1)}, bf16[48,2048]{1,0:T(8,128)(2,1)S(1)}, u32[]{:S(2)}, u32[]{:S(2)}) collective-permute-start(bf16[48,2048]{1,0:T(8,128)(2,1)S(1)} %get-tuple-element.95), channel_id=1, source_target_pairs={{0,1},{1,0},{2,3},{3,2},{4,5},{5,4},{6,7},{7,6},{8,9},{9,8},{10,11... | collective-permute-start | bytes 589832 | tf_op jit(solution)/shard_map/ppermute | solution.py:409
  12.9 17.8 %collective-permute-start.8 = (bf16[128,2048]{1,0:T(8,128)(2,1)S(1)}, bf16[128,2048]{1,0:T(8,128)(2,1)S(1)}, u32[]{:S(2)}, u32[]{:S(2)}) collective-permute-start(bf16[128,2048]{1,0:T(8,128)(2,1)S(1)} %copy-done.4), channel_id=1, source_target_pairs={{0,8},{1,9},{2,10},{3,11},{4,0},{5,1},{6,2},{7,3},{8,12},{9,13},{1... | collective-permute-start | bytes 1572872 | tf_op jit(solution)/shard_map/ppermute | solution.py:403
  14.5 16.3 %collective-permute-start.6 = (bf16[96,2048]{1,0:T(8,128)(2,1)S(1)}, bf16[96,2048]{1,0:T(8,128)(2,1)S(1)}, u32[]{:S(2)}, u32[]{:S(2)}) collective-permute-start(bf16[96,2048]{1,0:T(8,128)(2,1)S(1)} %join.13.refs_1_), channel_id=1, source_target_pairs={{0,2},{1,3},{2,0},{3,1},{4,6},{5,7},{6,4},{7,5},{8,10},{9,11},{10,... | collective-permute-start | bytes 1179656 | tf_op jit(solution)/shard_map/ppermute | solution.py:406
  22.9 2.2 %collective-permute-start.9 = (bf16[48,2048]{1,0:T(8,128)(2,1)S(1)}, bf16[48,2048]{1,0:T(8,128)(2,1)S(1)}, u32[]{:S(2)}, u32[]{:S(2)}) collective-permute-start(bf16[48,2048]{1,0:T(8,128)(2,1)S(1)} %get-tuple-element.98), channel_id=1, source_target_pairs={{0,1},{1,0},{2,3},{3,2},{4,5},{5,4},{6,7},{7,6},{8,9},{9,8},{10,11... | collective-permute-start | bytes 589832 | tf_op jit(solution)/shard_map/ppermute | solution.py:409
  23.0 2.1 %collective-permute-start.10 = (bf16[48,2048]{1,0:T(8,128)(2,1)S(1)}, bf16[48,2048]{1,0:T(8,128)(2,1)S(1)}, u32[]{:S(2)}, u32[]{:S(2)}) collective-permute-start(bf16[48,2048]{1,0:T(8,128)(2,1)S(1)} %get-tuple-element.100), channel_id=1, source_target_pairs={{0,1},{1,0},{2,3},{3,2},{4,5},{5,4},{6,7},{7,6},{8,9},{9,8},{10,11... | collective-permute-start | bytes 589832 | tf_op jit(solution)/shard_map/ppermute | solution.py:409
  23.5 18.5 %collective-permute-start.13 = (bf16[2064,128]{1,0:T(8,128)(2,1)S(1)}, bf16[2064,128]{1,0:T(8,128)(2,1)S(1)}, u32[]{:S(2)}, u32[]{:S(2)}) collective-permute-start(bf16[2064,128]{1,0:T(8,128)(2,1)S(1)} %hold.9.refs_1_.refs_2_), channel_id=1, source_target_pairs={{0,8},{1,9},{2,10},{3,11},{4,0},{5,1},{6,2},{7,3},{8,12},{9,13},{1... | collective-permute-start | bytes 1585160 | tf_op jit(solution)/shard_map/ppermute | solution.py:403
  25.1 16.9 %collective-permute-start.14 = (bf16[96,2048]{1,0:T(8,128)(2,1)S(1)}, bf16[96,2048]{1,0:T(8,128)(2,1)S(1)}, u32[]{:S(2)}, u32[]{:S(2)}) collective-permute-start(bf16[96,2048]{1,0:T(8,128)(2,1)S(1)} %join.14.refs_1_), channel_id=1, source_target_pairs={{0,2},{1,3},{2,0},{3,1},{4,6},{5,7},{6,4},{7,5},{8,10},{9,11},{10,... | collective-permute-start | bytes 1179656 | tf_op jit(solution)/shard_map/ppermute | solution.py:406
  31.2 1.7 %collective-permute-start.12 = (bf16[48,2048]{1,0:T(8,128)(2,1)S(1)}, bf16[48,2048]{1,0:T(8,128)(2,1)S(1)}, u32[]{:S(2)}, u32[]{:S(2)}) collective-permute-start(bf16[48,2048]{1,0:T(8,128)(2,1)S(1)} %get-tuple-element.104), channel_id=1, source_target_pairs={{0,1},{1,0},{2,3},{3,2},{4,5},{5,4},{6,7},{7,6},{8,9},{9,8},{10,11... | collective-permute-start | bytes 589832 | tf_op jit(solution)/shard_map/ppermute | solution.py:409
  32.9 14.0 %collective-permute-start.19 = (bf16[96,2048]{1,0:T(8,128)(2,1)S(1)}, bf16[96,2048]{1,0:T(8,128)(2,1)S(1)}, u32[]{:S(2)}, u32[]{:S(2)}) collective-permute-start(bf16[96,2048]{1,0:T(8,128)(2,1)S(1)} %join.15.refs_10_), channel_id=1, source_target_pairs={{0,2},{1,3},{2,0},{3,1},{4,6},{5,7},{6,4},{7,5},{8,10},{9,11},{10,... | collective-permute-start | bytes 1179656 | tf_op jit(solution)/shard_map/ppermute | solution.py:406
  34.5 18.1 %collective-permute-start.18 = (bf16[128,2048]{1,0:T(8,128)(2,1)S(1)}, bf16[128,2048]{1,0:T(8,128)(2,1)S(1)}, u32[]{:S(2)}, u32[]{:S(2)}) collective-permute-start(bf16[128,2048]{1,0:T(8,128)(2,1)S(1)} %hold.10.refs_1_.refs_2_), channel_id=1, source_target_pairs={{0,8},{1,9},{2,10},{3,11},{4,0},{5,1},{6,2},{7,3},{8,12},{9,13},{1... | collective-permute-start | bytes 1572872 | tf_op jit(solution)/shard_map/ppermute | solution.py:403
  42.6 1.5 %collective-permute-start.15 = (bf16[48,2048]{1,0:T(8,128)(2,1)S(1)}, bf16[48,2048]{1,0:T(8,128)(2,1)S(1)}, u32[]{:S(2)}, u32[]{:S(2)}) collective-permute-start(bf16[48,2048]{1,0:T(8,128)(2,1)S(1)} %get-tuple-element.111), channel_id=1, source_target_pairs={{0,1},{1,0},{2,3},{3,2},{4,5},{5,4},{6,7},{7,6},{8,9},{9,8},{10,11... | collective-permute-start | bytes 589832 | tf_op jit(solution)/shard_map/ppermute | solution.py:409
  42.6 1.7 %collective-permute-start.16 = (bf16[48,2048]{1,0:T(8,128)(2,1)S(1)}, bf16[48,2048]{1,0:T(8,128)(2,1)S(1)}, u32[]{:S(2)}, u32[]{:S(2)}) collective-permute-start(bf16[48,2048]{1,0:T(8,128)(2,1)S(1)} %get-tuple-element.113), channel_id=1, source_target_pairs={{0,1},{1,0},{2,3},{3,2},{4,5},{5,4},{6,7},{7,6},{8,9},{9,8},{10,11... | collective-permute-start | bytes 589832 | tf_op jit(solution)/shard_map/ppermute | solution.py:409
  44.4 11.3 %collective-permute-start.17 = (bf16[96,2048]{1,0:T(8,128)(2,1)S(1)}, bf16[96,2048]{1,0:T(8,128)(2,1)S(1)}, u32[]{:S(2)}, u32[]{:S(2)}) collective-permute-start(bf16[96,2048]{1,0:T(8,128)(2,1)S(1)} %join.16.refs_10_), channel_id=1, source_target_pairs={{0,2},{1,3},{2,0},{3,1},{4,6},{5,7},{6,4},{7,5},{8,10},{9,11},{10,... | collective-permute-start | bytes 1179656 | tf_op jit(solution)/shard_map/ppermute | solution.py:406
  49.6 3.0 %collective-permute-start.20 = (bf16[32,2176]{1,0:T(8,128)(2,1)S(1)}, bf16[32,2176]{1,0:T(8,128)(2,1)S(1)}, u32[]{:S(2)}, u32[]{:S(2)}) collective-permute-start(bf16[32,2176]{1,0:T(8,128)(2,1)S(1)} %slice.38), channel_id=1, source_target_pairs={{0,1},{1,0},{2,3},{3,2},{4,5},{5,4},{6,7},{7,6},{8,9},{9,8},{10,11... | collective-permute-start | bytes 417800 | tf_op jit(solution)/shard_map/ppermute | solution.py:409
  49.7 2.9 %collective-permute-start.21 = (bf16[16,2176]{1,0:T(8,128)(2,1)S(1)}, bf16[16,2176]{1,0:T(8,128)(2,1)S(1)}, u32[]{:S(2)}, u32[]{:S(2)}) collective-permute-start(bf16[16,2176]{1,0:T(8,128)(2,1)S(1)} %slice.39), channel_id=1, source_target_pairs={{0,1},{1,0},{2,3},{3,2},{4,5},{5,4},{6,7},{7,6},{8,9},{9,8},{10,11... | collective-permute-start | bytes 208904 | tf_op jit(solution)/shard_map/ppermute | solution.py:409
  50.2 14.9 %collective-permute-start.25 = (bf16[2064,128]{1,0:T(8,128)(2,1)S(1)}, bf16[2064,128]{1,0:T(8,128)(2,1)S(1)}, u32[]{:S(2)}, u32[]{:S(2)}) collective-permute-start(bf16[2064,128]{1,0:T(8,128)(2,1)S(1)} %hold.11.refs_1_.refs_2_), channel_id=1, source_target_pairs={{0,8},{1,9},{2,10},{3,11},{4,0},{5,1},{6,2},{7,3},{8,12},{9,13},{1... | collective-permute-start | bytes 1585160 | tf_op jit(solution)/shard_map/ppermute | solution.py:403
  53.1 1.7 %collective-permute-start.23 = (bf16[48,2048]{1,0:T(8,128)(2,1)S(1)}, bf16[48,2048]{1,0:T(8,128)(2,1)S(1)}, u32[]{:S(2)}, u32[]{:S(2)}) collective-permute-start(bf16[48,2048]{1,0:T(8,128)(2,1)S(1)} %get-tuple-element.123), channel_id=1, source_target_pairs={{0,1},{1,0},{2,3},{3,2},{4,5},{5,4},{6,7},{7,6},{8,9},{9,8},{10,11... | collective-permute-start | bytes 589832 | tf_op jit(solution)/shard_map/ppermute | solution.py:409
  53.6 12.1 %collective-permute-start.27 = (bf16[1552,128]{1,0:T(8,128)(2,1)S(1)}, bf16[1552,128]{1,0:T(8,128)(2,1)S(1)}, u32[]{:S(2)}, u32[]{:S(2)}) collective-permute-start(bf16[1552,128]{1,0:T(8,128)(2,1)S(1)} %join.17.refs_1_), channel_id=1, source_target_pairs={{0,2},{1,3},{2,0},{3,1},{4,6},{5,7},{6,4},{7,5},{8,10},{9,11},{10,... | collective-permute-start | bytes 1191944 | tf_op jit(solution)/shard_map/ppermute | solution.py:406
  55.7 20.6 %collective-permute-start.28 = (bf16[128,2048]{1,0:T(8,128)(2,1)S(1)}, bf16[128,2048]{1,0:T(8,128)(2,1)S(1)}, u32[]{:S(2)}, u32[]{:S(2)}) collective-permute-start(bf16[128,2048]{1,0:T(8,128)(2,1)S(1)} %hold.13.refs_1_), channel_id=1, source_target_pairs={{0,8},{1,9},{2,10},{3,11},{4,0},{5,1},{6,2},{7,3},{8,12},{9,13},{1... | collective-permute-start | bytes 1572872 | tf_op jit(solution)/shard_map/ppermute | solution.py:403
  59.2 1.5 %collective-permute-start.26 = (bf16[48,2176]{1,0:T(8,128)(2,1)S(1)}, bf16[48,2176]{1,0:T(8,128)(2,1)S(1)}, u32[]{:S(2)}, u32[]{:S(2)}) collective-permute-start(bf16[48,2176]{1,0:T(8,128)(2,1)S(1)} %get-tuple-element.124), channel_id=1, source_target_pairs={{0,1},{1,0},{2,3},{3,2},{4,5},{5,4},{6,7},{7,6},{8,9},{9,8},{10,11... | collective-permute-start | bytes 626696 | tf_op jit(solution)/shard_map/ppermute | solution.py:409
  59.2 14.9 %collective-permute-start.24 = (bf16[96,2048]{1,0:T(8,128)(2,1)S(1)}, bf16[96,2048]{1,0:T(8,128)(2,1)S(1)}, u32[]{:S(2)}, u32[]{:S(2)}) collective-permute-start(bf16[96,2048]{1,0:T(8,128)(2,1)S(1)} %join.18.refs_1_), channel_id=1, source_target_pairs={{0,2},{1,3},{2,0},{3,1},{4,6},{5,7},{6,4},{7,5},{8,10},{9,11},{10,... | collective-permute-start | bytes 1179656 | tf_op jit(solution)/shard_map/ppermute | solution.py:406
  66.3 1.8 %collective-permute-start.29 = (bf16[32,2048]{1,0:T(8,128)(2,1)S(1)}, bf16[32,2048]{1,0:T(8,128)(2,1)S(1)}, u32[]{:S(2)}, u32[]{:S(2)}) collective-permute-start(bf16[32,2048]{1,0:T(8,128)(2,1)S(1)} %slice.40), channel_id=1, source_target_pairs={{0,1},{1,0},{2,3},{3,2},{4,5},{5,4},{6,7},{7,6},{8,9},{9,8},{10,11... | collective-permute-start | bytes 393224 | tf_op jit(solution)/shard_map/ppermute | solution.py:409
  66.4 6.8 %collective-permute-start.31 = (bf16[48,2048]{1,0:T(8,128)(2,1)S(1)}, bf16[48,2048]{1,0:T(8,128)(2,1)S(1)}, u32[]{:S(2)}, u32[]{:S(2)}) collective-permute-start(bf16[48,2048]{1,0:T(8,128)(2,1)S(1)} %get-tuple-element.130), channel_id=1, source_target_pairs={{0,1},{1,0},{2,3},{3,2},{4,5},{5,4},{6,7},{7,6},{8,9},{9,8},{10,11... | collective-permute-start | bytes 589832 | tf_op jit(solution)/shard_map/ppermute | solution.py:409
  68.1 14.5 %collective-permute-start.34 = (bf16[96,2048]{1,0:T(8,128)(2,1)S(1)}, bf16[96,2048]{1,0:T(8,128)(2,1)S(1)}, u32[]{:S(2)}, u32[]{:S(2)}) collective-permute-start(bf16[96,2048]{1,0:T(8,128)(2,1)S(1)} %join.19.refs_4_), channel_id=1, source_target_pairs={{0,2},{1,3},{2,0},{3,1},{4,6},{5,7},{6,4},{7,5},{8,10},{9,11},{10,... | collective-permute-start | bytes 1179656 | tf_op jit(solution)/shard_map/ppermute | solution.py:406
  69.5 18.6 %collective-permute-start.38 = (bf16[144,2048]{1,0:T(8,128)(2,1)S(1)}, bf16[144,2048]{1,0:T(8,128)(2,1)S(1)}, u32[]{:S(2)}, u32[]{:S(2)}) collective-permute-start(bf16[144,2048]{1,0:T(8,128)(2,1)S(1)} %home.7.refs_1_), channel_id=1, source_target_pairs={{0,8},{1,9},{2,10},{3,11},{4,0},{5,1},{6,2},{7,3},{8,12},{9,13},{1... | collective-permute-start | bytes 1769480 | tf_op jit(solution)/shard_map/ppermute | solution.py:403
  76.7 1.7 %collective-permute-start.33 = (bf16[48,2048]{1,0:T(8,128)(2,1)S(1)}, bf16[48,2048]{1,0:T(8,128)(2,1)S(1)}, u32[]{:S(2)}, u32[]{:S(2)}) collective-permute-start(bf16[48,2048]{1,0:T(8,128)(2,1)S(1)} %get-tuple-element.134), channel_id=1, source_target_pairs={{0,1},{1,0},{2,3},{3,2},{4,5},{5,4},{6,7},{7,6},{8,9},{9,8},{10,11... | collective-permute-start | bytes 589832 | tf_op jit(solution)/shard_map/ppermute | solution.py:409
  78.4 12.0 %collective-permute-start.42 = (bf16[96,2048]{1,0:T(8,128)(2,1)S(1)}, bf16[96,2048]{1,0:T(8,128)(2,1)S(1)}, u32[]{:S(2)}, u32[]{:S(2)}) collective-permute-start(bf16[96,2048]{1,0:T(8,128)(2,1)S(1)} %join.20.refs_10_), channel_id=1, source_target_pairs={{0,2},{1,3},{2,0},{3,1},{4,6},{5,7},{6,4},{7,5},{8,10},{9,11},{10,... | collective-permute-start | bytes 1179656 | tf_op jit(solution)/shard_map/ppermute | solution.py:406
  82.7 5.4 %collective-permute-start.37 = (bf16[48,2176]{1,0:T(8,128)(2,1)S(1)}, bf16[48,2176]{1,0:T(8,128)(2,1)S(1)}, u32[]{:S(2)}, u32[]{:S(2)}) collective-permute-start(bf16[48,2176]{1,0:T(8,128)(2,1)S(1)} %get-tuple-element.143), channel_id=1, source_target_pairs={{0,1},{1,0},{2,3},{3,2},{4,5},{5,4},{6,7},{7,6},{8,9},{9,8},{10,11... | collective-permute-start | bytes 626696 | tf_op jit(solution)/shard_map/ppermute | solution.py:409
  82.8 1.8 %collective-permute-start.35 = (bf16[32,2176]{1,0:T(8,128)(2,1)S(1)}, bf16[32,2176]{1,0:T(8,128)(2,1)S(1)}, u32[]{:S(2)}, u32[]{:S(2)}) collective-permute-start(bf16[32,2176]{1,0:T(8,128)(2,1)S(1)} %slice.42), channel_id=1, source_target_pairs={{0,1},{1,0},{2,3},{3,2},{4,5},{5,4},{6,7},{7,6},{8,9},{9,8},{10,11... | collective-permute-start | bytes 417800 | tf_op jit(solution)/shard_map/ppermute | solution.py:409
  84.7 14.3 %collective-permute-start.48 = (bf16[1552,128]{1,0:T(8,128)(2,1)S(1)}, bf16[1552,128]{1,0:T(8,128)(2,1)S(1)}, u32[]{:S(2)}, u32[]{:S(2)}) collective-permute-start(bf16[1552,128]{1,0:T(8,128)(2,1)S(1)} %join.21.refs_4_), channel_id=1, source_target_pairs={{0,2},{1,3},{2,0},{3,1},{4,6},{5,7},{6,4},{7,5},{8,10},{9,11},{10,... | collective-permute-start | bytes 1191944 | tf_op jit(solution)/shard_map/ppermute | solution.py:406
  88.1 5.8 %collective-permute-start.39 = (bf16[48,2176]{1,0:T(8,128)(2,1)S(1)}, bf16[48,2176]{1,0:T(8,128)(2,1)S(1)}, u32[]{:S(2)}, u32[]{:S(2)}) collective-permute-start(bf16[48,2176]{1,0:T(8,128)(2,1)S(1)} %get-tuple-element.145), channel_id=1, source_target_pairs={{0,1},{1,0},{2,3},{3,2},{4,5},{5,4},{6,7},{7,6},{8,9},{9,8},{10,11... | collective-permute-start | bytes 626696 | tf_op jit(solution)/shard_map/ppermute | solution.py:409
  88.1 5.7 %collective-permute-start.40 = (bf16[32,2176]{1,0:T(8,128)(2,1)S(1)}, bf16[32,2176]{1,0:T(8,128)(2,1)S(1)}, u32[]{:S(2)}, u32[]{:S(2)}) collective-permute-start(bf16[32,2176]{1,0:T(8,128)(2,1)S(1)} %slice.44), channel_id=1, source_target_pairs={{0,1},{1,0},{2,3},{3,2},{4,5},{5,4},{6,7},{7,6},{8,9},{9,8},{10,11... | collective-permute-start | bytes 417800 | tf_op jit(solution)/shard_map/ppermute | solution.py:409
  88.7 4.5 %collective-permute-start.41 = (bf16[16,2176]{1,0:T(8,128)(2,1)S(1)}, bf16[16,2176]{1,0:T(8,128)(2,1)S(1)}, u32[]{:S(2)}, u32[]{:S(2)}) collective-permute-start(bf16[16,2176]{1,0:T(8,128)(2,1)S(1)} %slice.45), channel_id=1, source_target_pairs={{0,1},{1,0},{2,3},{3,2},{4,5},{5,4},{6,7},{7,6},{8,9},{9,8},{10,11... | collective-permute-start | bytes 208904 | tf_op jit(solution)/shard_map/ppermute | solution.py:409
  93.1 1.6 %collective-permute-start.43 = (bf16[32,2176]{1,0:T(8,128)(2,1)S(1)}, bf16[32,2176]{1,0:T(8,128)(2,1)S(1)}, u32[]{:S(2)}, u32[]{:S(2)}) collective-permute-start(bf16[32,2176]{1,0:T(8,128)(2,1)S(1)} %slice.46), channel_id=1, source_target_pairs={{0,1},{1,0},{2,3},{3,2},{4,5},{5,4},{6,7},{7,6},{8,9},{9,8},{10,11... | collective-permute-start | bytes 417800 | tf_op jit(solution)/shard_map/ppermute | solution.py:409
  93.7 2.6 %collective-permute-start.45 = (bf16[48,2176]{1,0:T(8,128)(2,1)S(1)}, bf16[48,2176]{1,0:T(8,128)(2,1)S(1)}, u32[]{:S(2)}, u32[]{:S(2)}) collective-permute-start(bf16[48,2176]{1,0:T(8,128)(2,1)S(1)} %get-tuple-element.152), channel_id=1, source_target_pairs={{0,1},{1,0},{2,3},{3,2},{4,5},{5,4},{6,7},{7,6},{8,9},{9,8},{10,11... | collective-permute-start | bytes 626696 | tf_op jit(solution)/shard_map/ppermute | solution.py:409
  94.8 13.7 %collective-permute-start.47 = (bf16[1552,128]{1,0:T(8,128)(2,1)S(1)}, bf16[1552,128]{1,0:T(8,128)(2,1)S(1)}, u32[]{:S(2)}, u32[]{:S(2)}) collective-permute-start(bf16[1552,128]{1,0:T(8,128)(2,1)S(1)} %join.22.refs_3_), channel_id=1, source_target_pairs={{0,2},{1,3},{2,0},{3,1},{4,6},{5,7},{6,4},{7,5},{8,10},{9,11},{10,... | collective-permute-start | bytes 1191944 | tf_op jit(solution)/shard_map/ppermute | solution.py:406
  99.2 9.2 %collective-permute-start.51 = (bf16[128,896]{1,0:T(8,128)(2,1)S(1)}, bf16[128,896]{1,0:T(8,128)(2,1)S(1)}, u32[]{:S(2)}, u32[]{:S(2)}) collective-permute-start(bf16[128,896]{1,0:T(8,128)(2,1)S(1)} %home.8.refs_5_), channel_id=1, source_target_pairs={{0,8},{1,9},{2,10},{3,11},{4,0},{5,1},{6,2},{7,3},{8,12},{9,13},{1... | collective-permute-start | bytes 688136 | tf_op jit(solution)/shard_map/ppermute | solution.py:403
  102.3 20.2 %collective-permute-start.46 = (bf16[1552,128]{1,0:T(8,128)(2,1)S(1)}, bf16[1552,128]{1,0:T(8,128)(2,1)S(1)}, u32[]{:S(2)}, u32[]{:S(2)}) collective-permute-start(bf16[1552,128]{1,0:T(8,128)(2,1)S(1)} %join.23.refs_5_), channel_id=1, source_target_pairs={{0,2},{1,3},{2,0},{3,1},{4,6},{5,7},{6,4},{7,5},{8,10},{9,11},{10,... | collective-permute-start | bytes 1191944 | tf_op jit(solution)/shard_map/ppermute | solution.py:406
  104.0 8.1 %collective-permute-start.50 = (bf16[128,640]{1,0:T(8,128)(2,1)S(1)}, bf16[128,640]{1,0:T(8,128)(2,1)S(1)}, u32[]{:S(2)}, u32[]{:S(2)}) collective-permute-start(bf16[128,640]{1,0:T(8,128)(2,1)S(1)} %home.9.refs_5_), channel_id=1, source_target_pairs={{0,8},{1,9},{2,10},{3,11},{4,0},{5,1},{6,2},{7,3},{8,12},{9,13},{1... | collective-permute-start | bytes 491528 | tf_op jit(solution)/shard_map/ppermute | solution.py:403
  105.8 9.7 %collective-permute-start.49 = (bf16[144,512]{1,0:T(8,128)(2,1)S(1)}, bf16[144,512]{1,0:T(8,128)(2,1)S(1)}, u32[]{:S(2)}, u32[]{:S(2)}) collective-permute-start(bf16[144,512]{1,0:T(8,128)(2,1)S(1)} %home.10.refs_16_), channel_id=1, source_target_pairs={{0,8},{1,9},{2,10},{3,11},{4,0},{5,1},{6,2},{7,3},{8,12},{9,13},{1... | collective-permute-start | bytes 442376 | tf_op jit(solution)/shard_map/ppermute | solution.py:403
  108.7 15.8 %collective-permute-start.52 = (bf16[128,896]{1,0:T(8,128)(2,1)S(1)}, bf16[128,896]{1,0:T(8,128)(2,1)S(1)}, u32[]{:S(2)}, u32[]{:S(2)}) collective-permute-start(bf16[128,896]{1,0:T(8,128)(2,1)S(1)} %home.11.refs_5_), channel_id=1, source_target_pairs={{0,8},{1,9},{2,10},{3,11},{4,0},{5,1},{6,2},{7,3},{8,12},{9,13},{1... | collective-permute-start | bytes 688136 | tf_op jit(solution)/shard_map/ppermute | solution.py:403
  112.3 12.2 %collective-permute-start.53 = (bf16[128,640]{1,0:T(8,128)(2,1)S(1)}, bf16[128,640]{1,0:T(8,128)(2,1)S(1)}, u32[]{:S(2)}, u32[]{:S(2)}) collective-permute-start(bf16[128,640]{1,0:T(8,128)(2,1)S(1)} %home.12.refs_5_), channel_id=1, source_target_pairs={{0,8},{1,9},{2,10},{3,11},{4,0},{5,1},{6,2},{7,3},{8,12},{9,13},{1... | collective-permute-start | bytes 491528 | tf_op jit(solution)/shard_map/ppermute | solution.py:403
  115.8 8.7 %collective-permute-start.54 = (bf16[144,512]{1,0:T(8,128)(2,1)S(1)}, bf16[144,512]{1,0:T(8,128)(2,1)S(1)}, u32[]{:S(2)}, u32[]{:S(2)}) collective-permute-start(bf16[144,512]{1,0:T(8,128)(2,1)S(1)} %home.13.refs_16_), channel_id=1, source_target_pairs={{0,8},{1,9},{2,10},{3,11},{4,0},{5,1},{6,2},{7,3},{8,12},{9,13},{1... | collective-permute-start | bytes 442376 | tf_op jit(solution)/shard_map/ppermute | solution.py:403
  (14 other events, 60.6 us)

commit v9 on v8

--- a/solution.py
+++ b/solution.py
@@ -449,16 +449,15 @@
         )
         rows_x[s] = spread(blocks, pieces)
 
-    def slots_d(s, d, after=()):
+    def slots_d(s, d, pieces=1):
         blocks = run(
             functools.partial(gather_kernel, capacity),
             [((capacity, features), BF16)] * PLANE,
             "slots_d",
             scaled[s],
             d,
-            after=after,
         )
-        rows_d[s] = spread(blocks)
+        rows_d[s] = spread(blocks, pieces)
 
     def expert(s, after=()):
         grads[s], hidden[s], *terms[s] = run(
@@ -514,7 +513,7 @@
     slots_d(0, cotangent)
     last = planes - 1
     for s in range(1, planes):
-        (here,) = run.hold(x, after=terms[1][1:] if s == last else rows_x[s - 1][2:])
+        (here,) = run.hold(x, after=terms[1][2:] if s == last else rows_x[s - 1][2:])
         if s < last:
             x = along(here)
         slots_x(s, here, 2 if s == last else 1)
@@ -529,10 +528,11 @@
             d = along(here)
         if s == 2:
             run.pending += rows_x[s][2:]
-        slots_d(s, here)
+        slots_d(s, here, 2 if s == 2 else 1)
         if s == 1:
             expert(0)
         if s == 2:
+            run.pending = []
             (here,) = run.hold(here)
             d = along(here)
     expert(2)

time: 126 us -> 126 us (level)
    ppermute x12, starting transfers between devices: 15.4 us -> 13.7 us  [across(): return lax.ppermute(array, 'expert', [(i, i ^ 2) for i in range(devices)])]
    ppermute x30 -> x31, waiting for transfers between devices: 8.34 us -> 9.28 us  [cores(): return lax.ppermute(array, 'expert', [(i, i ^ 1) for i in range(devices)])]
    ppermute x30 -> x31, starting transfers between devices: 7.34 us -> 7.18 us  [cores(): return lax.ppermute(array, 'expert', [(i, i ^ 1) for i in range(devices)])]
  transfers between devices with their start and end apart: 55 -> 56, of which waited for: 25 -> 26; matrix products, arithmetic and copies ran while one was open for 0% -> 0% of each run, Pallas kernels for 18% -> 18%
where the time goes in v9:
time: 126 us
  starting transfers between devices  56.2 us (45%)
  waiting for transfers between devices  41.3 us (33%)
  Pallas kernels  26 us (21%)
    ppermute x13, starting transfers between devices, along(): return lax.ppermute(array, 'expert', pairs)  35.3 us
    pallas_call x36, Pallas kernels, __call__(): pl.pallas_call(body, out_shape=[jax.ShapeDtypeStruct(shape, kind) for sha...  26 us
    ppermute x12, waiting for transfers between devices, across(): return lax.ppermute(array, 'expert', [(i, i ^ 2) for i in range(devices)])  16.4 us
    ppermute x13, waiting for transfers between devices, along(): return lax.ppermute(array, 'expert', pairs)  15.6 us
    ppermute x12, starting transfers between devices, across(): return lax.ppermute(array, 'expert', [(i, i ^ 2) for i in range(devices)])  13.7 us
    ppermute x31, waiting for transfers between devices, cores(): return lax.ppermute(array, 'expert', [(i, i ^ 1) for i in range(devices)])  9.28 us
    ppermute x31, starting transfers between devices, cores(): return lax.ppermute(array, 'expert', [(i, i ^ 1) for i in range(devices)])  7.18 us
  transfers between devices with their start and end apart: 56, of which 26 were waited for; matrix products, arithmetic and copies ran while one was open for 0% of the time, Pallas kernels for 18%

profile of v9, /device:TPU:0, one launch (start us, length us, event | category | flops | bytes accessed | tf_op | source)
XLA Modules:
  0.0 125.8 jit_solution(2118308043086076265)
XLA Ops:
  0.6 2.0 %pack.1.refs_1_.refs_2_ = bf16[2064,128]{1,0:T(8,128)(2,1)} custom-call(s32[4,128]{1,0:T(4,128)} %bitcast.22, s32[4,128]{1,0:T(4,128)} %bitcast.24, bf16[128,2048]{1,0:T(8,128)(2,1)} %refs_2_.1), custom_call_target="tpu_custom_call" | custom-call | flops 1000 | bytes 1000 | tf_op jit(solution)/shard_map/pack/pallas_call | solution.py:130
  2.7 4.1 %collective-permute-start.7 = (bf16[2064,128]{1,0:T(8,128)(2,1)}, bf16[2064,128]{1,0:T(8,128)(2,1)S(1)}, u32[]{:S(2)}, u32[]{:S(2)}) collective-permute-start(bf16[2064,128]{1,0:T(8,128)(2,1)} %pack.1.refs_1_.refs_2_), channel_id=1, source_target_pairs={{0,8},{1,9},{2,10},{3,11},{4,0},{5,1},{6,2},{7,3},{8,12},{9,13},{1... | collective-permute-start | bytes 1585160 | tf_op jit(solution)/shard_map/ppermute | solution.py:403
  6.8 1.1 copy-done.3
  9.1 0.8 collective-permute-done.2.refs_2_
  10.0 1.6 %collective-permute-start.3 = (bf16[96,2048]{1,0:T(8,128)(2,1)S(1)}, bf16[96,2048]{1,0:T(8,128)(2,1)S(1)}, u32[]{:S(2)}, u32[]{:S(2)}) collective-permute-start(bf16[96,2048]{1,0:T(8,128)(2,1)S(1)} %join.12.refs_2_), channel_id=1, source_target_pairs={{0,2},{1,3},{2,0},{3,1},{4,6},{5,7},{6,4},{7,5},{8,10},{9,11},{10,... | collective-permute-start | bytes 1179656 | tf_op jit(solution)/shard_map/ppermute | solution.py:406
  12.5 1.6 %collective-permute-start.8 = (bf16[128,2048]{1,0:T(8,128)(2,1)S(1)}, bf16[128,2048]{1,0:T(8,128)(2,1)S(1)}, u32[]{:S(2)}, u32[]{:S(2)}) collective-permute-start(bf16[128,2048]{1,0:T(8,128)(2,1)S(1)} %copy-done.4), channel_id=1, source_target_pairs={{0,8},{1,9},{2,10},{3,11},{4,0},{5,1},{6,2},{7,3},{8,12},{9,13},{1... | collective-permute-start | bytes 1572872 | tf_op jit(solution)/shard_map/ppermute | solution.py:403
  14.7 7.3 %collective-permute-done.3.refs_2_.refs_3_.refs_6_ = bf16[96,2048]{1,0:T(8,128)(2,1)S(1)} collective-permute-done((bf16[96,2048]{1,0:T(8,128)(2,1)S(1)}, bf16[96,2048]{1,0:T(8,128)(2,1)S(1)}, u32[]{:S(2)}, u32[]{:S(2)}) %collective-permute-start.3) | collective-permute-done | bytes 393248 | tf_op jit(solution)/shard_map/ppermute | solution.py:406
  23.2 1.6 %collective-permute-start.13 = (bf16[2064,128]{1,0:T(8,128)(2,1)S(1)}, bf16[2064,128]{1,0:T(8,128)(2,1)S(1)}, u32[]{:S(2)}, u32[]{:S(2)}) collective-permute-start(bf16[2064,128]{1,0:T(8,128)(2,1)S(1)} %hold.9.refs_1_.refs_2_), channel_id=1, source_target_pairs={{0,8},{1,9},{2,10},{3,11},{4,0},{5,1},{6,2},{7,3},{8,12},{9,13},{1... | collective-permute-start | bytes 1585160 | tf_op jit(solution)/shard_map/ppermute | solution.py:403
  24.8 1.6 %collective-permute-start.14 = (bf16[96,2048]{1,0:T(8,128)(2,1)S(1)}, bf16[96,2048]{1,0:T(8,128)(2,1)S(1)}, u32[]{:S(2)}, u32[]{:S(2)}) collective-permute-start(bf16[96,2048]{1,0:T(8,128)(2,1)S(1)} %join.14.refs_1_), channel_id=1, source_target_pairs={{0,2},{1,3},{2,0},{3,1},{4,6},{5,7},{6,4},{7,5},{8,10},{9,11},{10,... | collective-permute-start | bytes 1179656 | tf_op jit(solution)/shard_map/ppermute | solution.py:406
  26.4 4.3 %collective-permute-done.8.refs_0_ = bf16[128,2048]{1,0:T(8,128)(2,1)S(1)} collective-permute-done((bf16[128,2048]{1,0:T(8,128)(2,1)S(1)}, bf16[128,2048]{1,0:T(8,128)(2,1)S(1)}, u32[]{:S(2)}, u32[]{:S(2)}) %collective-permute-start.8) | collective-permute-done | bytes 524320 | tf_op jit(solution)/shard_map/ppermute | solution.py:403
  31.6 0.9 collective-permute-done.11.refs_1_
  32.8 1.6 %collective-permute-start.19 = (bf16[96,2048]{1,0:T(8,128)(2,1)S(1)}, bf16[96,2048]{1,0:T(8,128)(2,1)S(1)}, u32[]{:S(2)}, u32[]{:S(2)}) collective-permute-start(bf16[96,2048]{1,0:T(8,128)(2,1)S(1)} %join.15.refs_10_), channel_id=1, source_target_pairs={{0,2},{1,3},{2,0},{3,1},{4,6},{5,7},{6,4},{7,5},{8,10},{9,11},{10,... | collective-permute-start | bytes 1179656 | tf_op jit(solution)/shard_map/ppermute | solution.py:406
  34.4 3.4 %collective-permute-start.18 = (bf16[128,2048]{1,0:T(8,128)(2,1)S(1)}, bf16[128,2048]{1,0:T(8,128)(2,1)S(1)}, u32[]{:S(2)}, u32[]{:S(2)}) collective-permute-start(bf16[128,2048]{1,0:T(8,128)(2,1)S(1)} %hold.10.refs_1_.refs_2_), channel_id=1, source_target_pairs={{0,8},{1,9},{2,10},{3,11},{4,0},{5,1},{6,2},{7,3},{8,12},{9,13},{1... | collective-permute-start | bytes 1572872 | tf_op jit(solution)/shard_map/ppermute | solution.py:403
  37.8 2.6 %expert.4 = (bf16[192,768]{1,0:T(8,128)(2,1)S(1)}, bf16[192,384]{1,0:T(8,128)(2,1)S(1)}, bf16[48,2176]{1,0:T(8,128)(2,1)S(1)}, bf16[48,2176]{1,0:T(8,128)(2,1)S(...) custom-call(s32[1]{0:T(128)} %bitcast.2.refs_0_, bf16[48,2048]{1,0:T(8,128)(2,1)S(1)} %get-tuple-element.87.refs_1_.refs_4_, ...), custom_call_target="tpu_custom_call" | custom-call | flops 1000 | bytes 1000 | tf_op jit(solution)/shard_map/expert/pallas_call | solution.py:130
  40.4 1.5 %collective-permute-done.13.refs_0_ = bf16[2064,128]{1,0:T(8,128)(2,1)S(1)} collective-permute-done((bf16[2064,128]{1,0:T(8,128)(2,1)S(1)}, bf16[2064,128]{1,0:T(8,128)(2,1)S(1)}, u32[]{:S(2)}, u32[]{:S(2)}) %collective-permute-start.13) | collective-permute-done | bytes 528416 | tf_op jit(solution)/shard_map/ppermute | solution.py:403
  43.1 0.9 collective-permute-done.15.refs_3_.refs_2_.refs_11_
  44.4 1.6 %collective-permute-start.17 = (bf16[96,2048]{1,0:T(8,128)(2,1)S(1)}, bf16[96,2048]{1,0:T(8,128)(2,1)S(1)}, u32[]{:S(2)}, u32[]{:S(2)}) collective-permute-start(bf16[96,2048]{1,0:T(8,128)(2,1)S(1)} %join.16.refs_10_), channel_id=1, source_target_pairs={{0,2},{1,3},{2,0},{3,1},{4,6},{5,7},{6,4},{7,5},{8,10},{9,11},{10,... | collective-permute-start | bytes 1179656 | tf_op jit(solution)/shard_map/ppermute | solution.py:406
  46.7 2.6 %expert.5 = (bf16[192,768]{1,0:T(8,128)(2,1)S(1)}, bf16[192,384]{1,0:T(8,128)(2,1)S(1)}, bf16[48,2176]{1,0:T(8,128)(2,1)S(1)}, bf16[48,2176]{1,0:T(8,128)(2,1)S(...) custom-call(s32[1]{0:T(128)} %bitcast.2.refs_0_, ...), custom_call_target="tpu_custom_call" | custom-call | flops 1000 | bytes 1000 | tf_op jit(solution)/shard_map/expert/pallas_call | solution.py:130
  49.4 2.7 %collective-permute-start.26 = (bf16[2064,128]{1,0:T(8,128)(2,1)S(1)}, bf16[2064,128]{1,0:T(8,128)(2,1)S(1)}, u32[]{:S(2)}, u32[]{:S(2)}) collective-permute-start(bf16[2064,128]{1,0:T(8,128)(2,1)S(1)} %hold.11.refs_1_.refs_2_), channel_id=1, source_target_pairs={{0,8},{1,9},{2,10},{3,11},{4,0},{5,1},{6,2},{7,3},{8,12},{9,13},{1... | collective-permute-start | bytes 1585160 | tf_op jit(solution)/shard_map/ppermute | solution.py:403
  52.3 1.1 collective-permute-done.21.refs_2_
  55.0 0.9 collective-permute-done.24.refs_2_
  56.0 3.9 %collective-permute-start.28 = (bf16[128,2048]{1,0:T(8,128)(2,1)S(1)}, bf16[128,2048]{1,0:T(8,128)(2,1)S(1)}, u32[]{:S(2)}, u32[]{:S(2)}) collective-permute-start(bf16[128,2048]{1,0:T(8,128)(2,1)S(1)} %hold.13.refs_1_), channel_id=1, source_target_pairs={{0,8},{1,9},{2,10},{3,11},{4,0},{5,1},{6,2},{7,3},{8,12},{9,13},{1... | collective-permute-start | bytes 1572872 | tf_op jit(solution)/shard_map/ppermute | solution.py:403
  59.9 1.5 %collective-permute-start.25 = (bf16[96,2048]{1,0:T(8,128)(2,1)S(1)}, bf16[96,2048]{1,0:T(8,128)(2,1)S(1)}, u32[]{:S(2)}, u32[]{:S(2)}) collective-permute-start(bf16[96,2048]{1,0:T(8,128)(2,1)S(1)} %join.18.refs_1_), channel_id=1, source_target_pairs={{0,2},{1,3},{2,0},{3,1},{4,6},{5,7},{6,4},{7,5},{8,10},{9,11},{10,... | collective-permute-start | bytes 1179656 | tf_op jit(solution)/shard_map/ppermute | solution.py:406
  61.4 3.0 %collective-permute-done.26.refs_0_ = bf16[2064,128]{1,0:T(8,128)(2,1)S(1)} collective-permute-done((bf16[2064,128]{1,0:T(8,128)(2,1)S(1)}, bf16[2064,128]{1,0:T(8,128)(2,1)S(1)}, u32[]{:S(2)}, u32[]{:S(2)}) %collective-permute-start.26) | collective-permute-done | bytes 528416 | tf_op jit(solution)/shard_map/ppermute | solution.py:403
  64.4 1.1 collective-permute-done.27.refs_2_.refs_3_
  68.8 3.9 %collective-permute-start.39 = (bf16[144,2048]{1,0:T(8,128)(2,1)S(1)}, bf16[144,2048]{1,0:T(8,128)(2,1)S(1)}, u32[]{:S(2)}, u32[]{:S(2)}) collective-permute-start(bf16[144,2048]{1,0:T(8,128)(2,1)S(1)} %home.7.refs_1_), channel_id=1, source_target_pairs={{0,8},{1,9},{2,10},{3,11},{4,0},{5,1},{6,2},{7,3},{8,12},{9,13},{1... | collective-permute-start | bytes 1769480 | tf_op jit(solution)/shard_map/ppermute | solution.py:403
  72.7 1.2 collective-permute-done.25.refs_3_.refs_6_.refs_12_
  74.0 1.7 %collective-permute-done.28.refs_0_ = bf16[128,2048]{1,0:T(8,128)(2,1)S(1)} collective-permute-done((bf16[128,2048]{1,0:T(8,128)(2,1)S(1)}, bf16[128,2048]{1,0:T(8,128)(2,1)S(1)}, u32[]{:S(2)}, u32[]{:S(2)}) %collective-permute-start.28) | collective-permute-done | bytes 524320 | tf_op jit(solution)/shard_map/ppermute | solution.py:403
  76.7 0.9 collective-permute-done.33.refs_1_
  77.8 1.4 %collective-permute-start.43 = (bf16[96,2048]{1,0:T(8,128)(2,1)S(1)}, bf16[96,2048]{1,0:T(8,128)(2,1)S(1)}, u32[]{:S(2)}, u32[]{:S(2)}) collective-permute-start(bf16[96,2048]{1,0:T(8,128)(2,1)S(1)} %join.20.refs_10_), channel_id=1, source_target_pairs={{0,2},{1,3},{2,0},{3,1},{4,6},{5,7},{6,4},{7,5},{8,10},{9,11},{10,... | collective-permute-start | bytes 1179656 | tf_op jit(solution)/shard_map/ppermute | solution.py:406
  79.3 2.6 %expert.6 = (bf16[192,768]{1,0:T(8,128)(2,1)S(1)}, bf16[192,384]{1,0:T(8,128)(2,1)S(1)}, bf16[48,2176]{1,0:T(8,128)(2,1)S(1)}, bf16[48,2176]{1,0:T(8,128)(2,1)S(...) custom-call(s32[1]{0:T(128)} %bitcast.2.refs_0_, ...), custom_call_target="tpu_custom_call" | custom-call | flops 1000 | bytes 1000 | tf_op jit(solution)/shard_map/expert/pallas_call | solution.py:130
  83.1 1.2 collective-permute-done.37.refs_2_
  84.9 2.9 %collective-permute-done.39.refs_6_.refs_4_ = bf16[144,2048]{1,0:T(8,128)(2,1)S(1)} collective-permute-done((bf16[144,2048]{1,0:T(8,128)(2,1)S(1)}, bf16[144,2048]{1,0:T(8,128)(2,1)S(1)}, u32[]{:S(2)}, u32[]{:S(2)}) %collective-permute-start.39) | collective-permute-done | bytes 589856 | tf_op jit(solution)/shard_map/ppermute | solution.py:403
  88.5 2.3 %collective-permute-done.43.refs_6_.refs_15_ = bf16[96,2048]{1,0:T(8,128)(2,1)S(1)} collective-permute-done((bf16[96,2048]{1,0:T(8,128)(2,1)S(1)}, bf16[96,2048]{1,0:T(8,128)(2,1)S(1)}, u32[]{:S(2)}, u32[]{:S(2)}) %collective-permute-start.43) | collective-permute-done | bytes 393248 | tf_op jit(solution)/shard_map/ppermute | solution.py:406
  90.8 2.6 %expert.7 = (bf16[192,768]{1,0:T(8,128)(2,1)S(1)}, bf16[192,384]{1,0:T(8,128)(2,1)S(1)}, bf16[48,2176]{1,0:T(8,128)(2,1)S(1)}, bf16[48,2176]{1,0:T(8,128)(2,1)S(...) custom-call(s32[1]{0:T(128)} %bitcast.2.refs_0_, ...), custom_call_target="tpu_custom_call" | custom-call | flops 1000 | bytes 1000 | tf_op jit(solution)/shard_map/expert/pallas_call | solution.py:130
  94.2 0.8 collective-permute-done.45.refs_2_
  95.8 3.1 %collective-permute-done.49.refs_3_ = bf16[1552,128]{1,0:T(8,128)(2,1)S(1)} collective-permute-done((bf16[1552,128]{1,0:T(8,128)(2,1)S(1)}, bf16[1552,128]{1,0:T(8,128)(2,1)S(1)}, u32[]{:S(2)}, u32[]{:S(2)}) %collective-permute-start.49) | collective-permute-done | bytes 397344 | tf_op jit(solution)/shard_map/ppermute | solution.py:406
  99.2 2.8 %collective-permute-start.52 = (bf16[128,896]{1,0:T(8,128)(2,1)S(1)}, bf16[128,896]{1,0:T(8,128)(2,1)S(1)}, u32[]{:S(2)}, u32[]{:S(2)}) collective-permute-start(bf16[128,896]{1,0:T(8,128)(2,1)S(1)} %home.8.refs_5_), channel_id=1, source_target_pairs={{0,8},{1,9},{2,10},{3,11},{4,0},{5,1},{6,2},{7,3},{8,12},{9,13},{1... | collective-permute-start | bytes 688136 | tf_op jit(solution)/shard_map/ppermute | solution.py:403
  102.1 1.6 %collective-permute-start.47 = (bf16[1552,128]{1,0:T(8,128)(2,1)S(1)}, bf16[1552,128]{1,0:T(8,128)(2,1)S(1)}, u32[]{:S(2)}, u32[]{:S(2)}) collective-permute-start(bf16[1552,128]{1,0:T(8,128)(2,1)S(1)} %join.23.refs_5_), channel_id=1, source_target_pairs={{0,2},{1,3},{2,0},{3,1},{4,6},{5,7},{6,4},{7,5},{8,10},{9,11},{10,... | collective-permute-start | bytes 1191944 | tf_op jit(solution)/shard_map/ppermute | solution.py:406
  103.9 0.7 collective-permute-start.51
  104.9 1.3 %collective-permute-start.50 = (bf16[144,512]{1,0:T(8,128)(2,1)S(1)}, bf16[144,512]{1,0:T(8,128)(2,1)S(1)}, u32[]{:S(2)}, u32[]{:S(2)}) collective-permute-start(bf16[144,512]{1,0:T(8,128)(2,1)S(1)} %home.10.refs_16_), channel_id=1, source_target_pairs={{0,8},{1,9},{2,10},{3,11},{4,0},{5,1},{6,2},{7,3},{8,12},{9,13},{1... | collective-permute-start | bytes 442376 | tf_op jit(solution)/shard_map/ppermute | solution.py:403
  106.2 2.2 %down_delta.1 = (bf16[384,2048]{1,0:T(8,128)(2,1)}, f32[8,128]{1,0:T(8,128)S(1)}) custom-call(bf16[192,384]{1,0:T(8,128)(2,1)S(1)} %get-tuple-element.109.refs_1_.refs_0_, bf16[192,384]{1,0:T(8,128)(2,1)S(1)} %get-tuple-element.119.refs_3_.refs_1_, bf16[192,384]{1,0:T(8,128)(2,1)S(1)} %get-tuple-element.139.refs_4_.refs_2_, ...), custom_call_target="tpu_custom_call" | custom-call | flops 1000 | bytes 1000 | tf_op jit(solution)/shard_map/down_delta/pallas_call | solution.py:130
  108.7 3.1 %collective-permute-start.53 = (bf16[128,896]{1,0:T(8,128)(2,1)S(1)}, bf16[128,896]{1,0:T(8,128)(2,1)S(1)}, u32[]{:S(2)}, u32[]{:S(2)}) collective-permute-start(bf16[128,896]{1,0:T(8,128)(2,1)S(1)} %home.11.refs_5_), channel_id=1, source_target_pairs={{0,8},{1,9},{2,10},{3,11},{4,0},{5,1},{6,2},{7,3},{8,12},{9,13},{1... | collective-permute-start | bytes 688136 | tf_op jit(solution)/shard_map/ppermute | solution.py:403
  112.1 3.2 %collective-permute-start.54 = (bf16[128,640]{1,0:T(8,128)(2,1)S(1)}, bf16[128,640]{1,0:T(8,128)(2,1)S(1)}, u32[]{:S(2)}, u32[]{:S(2)}) collective-permute-start(bf16[128,640]{1,0:T(8,128)(2,1)S(1)} %home.12.refs_5_), channel_id=1, source_target_pairs={{0,8},{1,9},{2,10},{3,11},{4,0},{5,1},{6,2},{7,3},{8,12},{9,13},{1... | collective-permute-start | bytes 491528 | tf_op jit(solution)/shard_map/ppermute | solution.py:403
  115.5 2.9 %collective-permute-start.55 = (bf16[144,512]{1,0:T(8,128)(2,1)S(1)}, bf16[144,512]{1,0:T(8,128)(2,1)S(1)}, u32[]{:S(2)}, u32[]{:S(2)}) collective-permute-start(bf16[144,512]{1,0:T(8,128)(2,1)S(1)} %home.13.refs_16_), channel_id=1, source_target_pairs={{0,8},{1,9},{2,10},{3,11},{4,0},{5,1},{6,2},{7,3},{8,12},{9,13},{1... | collective-permute-start | bytes 442376 | tf_op jit(solution)/shard_map/ppermute | solution.py:403
  118.5 3.7 %gate_up_delta.1 = (bf16[2048,384]{1,0:T(8,128)(2,1)}, bf16[2048,384]{1,0:T(8,128)(2,1)}, f32[8,128]{1,0:T(8,128)S(1)}) custom-call(bf16[192,768]{1,0:T(8,128)(2,1)S(1)} %get-tuple-element.153.refs_0_, bf16[192,768]{1,0:T(8,128)(2,1)S(1)} %get-tuple-element.154.refs_1_, bf16[192,768]{1,0:T(8,128)(2,1)S(1)} %get-tuple-element.155.refs_2_, ...), custom_call_target="tpu_custom_call" | custom-call | flops 1000 | bytes 1000 | tf_op jit(solution)/shard_map/gate_up_delta/pallas_call | solution.py:130
  122.6 2.1 %collective-permute-done.55.refs_6_ = bf16[144,512]{1,0:T(8,128)(2,1)S(1)} collective-permute-done((bf16[144,512]{1,0:T(8,128)(2,1)S(1)}, bf16[144,512]{1,0:T(8,128)(2,1)S(1)}, u32[]{:S(2)}, u32[]{:S(2)}) %collective-permute-start.55) | collective-permute-done | bytes 147488 | tf_op jit(solution)/shard_map/ppermute | solution.py:403
  124.7 1.0 total.1
  (137 shorter events, 19.6 us)
Async XLA Ops:
  2.7 19.3 %collective-permute-start.7 = (bf16[2064,128]{1,0:T(8,128)(2,1)}, bf16[2064,128]{1,0:T(8,128)(2,1)S(1)}, u32[]{:S(2)}, u32[]{:S(2)}) collective-permute-start(bf16[2064,128]{1,0:T(8,128)(2,1)} %pack.1.refs_1_.refs_2_), channel_id=1, source_target_pairs={{0,8},{1,9},{2,10},{3,11},{4,0},{5,1},{6,2},{7,3},{8,12},{9,13},{1... | collective-permute-start | bytes 1585160 | tf_op jit(solution)/shard_map/ppermute | solution.py:403
  8.5 1.5 %collective-permute-start.1 = (bf16[32,2048]{1,0:T(8,128)(2,1)S(1)}, bf16[32,2048]{1,0:T(8,128)(2,1)S(1)}, u32[]{:S(2)}, u32[]{:S(2)}) collective-permute-start(bf16[32,2048]{1,0:T(8,128)(2,1)S(1)} %slice.42), channel_id=1, source_target_pairs={{0,1},{1,0},{2,3},{3,2},{4,5},{5,4},{6,7},{7,6},{8,9},{9,8},{10,11... | collective-permute-start | bytes 393224 | tf_op jit(solution)/shard_map/ppermute | solution.py:409
  9.0 3.5 %collective-permute-start = (bf16[48,2048]{1,0:T(8,128)(2,1)S(1)}, bf16[48,2048]{1,0:T(8,128)(2,1)S(1)}, u32[]{:S(2)}, u32[]{:S(2)}) collective-permute-start(bf16[48,2048]{1,0:T(8,128)(2,1)S(1)} %get-tuple-element.88), channel_id=1, source_target_pairs={{0,1},{1,0},{2,3},{3,2},{4,5},{5,4},{6,7},{7,6},{8,9},{9,8},{10,11... | collective-permute-start | bytes 589832 | tf_op jit(solution)/shard_map/ppermute | solution.py:409
  10.0 12.0 %collective-permute-start.3 = (bf16[96,2048]{1,0:T(8,128)(2,1)S(1)}, bf16[96,2048]{1,0:T(8,128)(2,1)S(1)}, u32[]{:S(2)}, u32[]{:S(2)}) collective-permute-start(bf16[96,2048]{1,0:T(8,128)(2,1)S(1)} %join.12.refs_2_), channel_id=1, source_target_pairs={{0,2},{1,3},{2,0},{3,1},{4,6},{5,7},{6,4},{7,5},{8,10},{9,11},{10,... | collective-permute-start | bytes 1179656 | tf_op jit(solution)/shard_map/ppermute | solution.py:406
  11.9 2.2 %collective-permute-start.4 = (bf16[48,2048]{1,0:T(8,128)(2,1)S(1)}, bf16[48,2048]{1,0:T(8,128)(2,1)S(1)}, u32[]{:S(2)}, u32[]{:S(2)}) collective-permute-start(bf16[48,2048]{1,0:T(8,128)(2,1)S(1)} %get-tuple-element.93), channel_id=1, source_target_pairs={{0,1},{1,0},{2,3},{3,2},{4,5},{5,4},{6,7},{7,6},{8,9},{9,8},{10,11... | collective-permute-start | bytes 589832 | tf_op jit(solution)/shard_map/ppermute | solution.py:409
  12.1 2.0 %collective-permute-start.5 = (bf16[48,2048]{1,0:T(8,128)(2,1)S(1)}, bf16[48,2048]{1,0:T(8,128)(2,1)S(1)}, u32[]{:S(2)}, u32[]{:S(2)}) collective-permute-start(bf16[48,2048]{1,0:T(8,128)(2,1)S(1)} %get-tuple-element.95), channel_id=1, source_target_pairs={{0,1},{1,0},{2,3},{3,2},{4,5},{5,4},{6,7},{7,6},{8,9},{9,8},{10,11... | collective-permute-start | bytes 589832 | tf_op jit(solution)/shard_map/ppermute | solution.py:409
  12.5 18.1 %collective-permute-start.8 = (bf16[128,2048]{1,0:T(8,128)(2,1)S(1)}, bf16[128,2048]{1,0:T(8,128)(2,1)S(1)}, u32[]{:S(2)}, u32[]{:S(2)}) collective-permute-start(bf16[128,2048]{1,0:T(8,128)(2,1)S(1)} %copy-done.4), channel_id=1, source_target_pairs={{0,8},{1,9},{2,10},{3,11},{4,0},{5,1},{6,2},{7,3},{8,12},{9,13},{1... | collective-permute-start | bytes 1572872 | tf_op jit(solution)/shard_map/ppermute | solution.py:403
  14.1 16.5 %collective-permute-start.6 = (bf16[96,2048]{1,0:T(8,128)(2,1)S(1)}, bf16[96,2048]{1,0:T(8,128)(2,1)S(1)}, u32[]{:S(2)}, u32[]{:S(2)}) collective-permute-start(bf16[96,2048]{1,0:T(8,128)(2,1)S(1)} %join.13.refs_1_), channel_id=1, source_target_pairs={{0,2},{1,3},{2,0},{3,1},{4,6},{5,7},{6,4},{7,5},{8,10},{9,11},{10,... | collective-permute-start | bytes 1179656 | tf_op jit(solution)/shard_map/ppermute | solution.py:406
  22.6 2.2 %collective-permute-start.9 = (bf16[48,2048]{1,0:T(8,128)(2,1)S(1)}, bf16[48,2048]{1,0:T(8,128)(2,1)S(1)}, u32[]{:S(2)}, u32[]{:S(2)}) collective-permute-start(bf16[48,2048]{1,0:T(8,128)(2,1)S(1)} %get-tuple-element.98), channel_id=1, source_target_pairs={{0,1},{1,0},{2,3},{3,2},{4,5},{5,4},{6,7},{7,6},{8,9},{9,8},{10,11... | collective-permute-start | bytes 589832 | tf_op jit(solution)/shard_map/ppermute | solution.py:409
  22.7 2.1 %collective-permute-start.10 = (bf16[48,2048]{1,0:T(8,128)(2,1)S(1)}, bf16[48,2048]{1,0:T(8,128)(2,1)S(1)}, u32[]{:S(2)}, u32[]{:S(2)}) collective-permute-start(bf16[48,2048]{1,0:T(8,128)(2,1)S(1)} %get-tuple-element.100), channel_id=1, source_target_pairs={{0,1},{1,0},{2,3},{3,2},{4,5},{5,4},{6,7},{7,6},{8,9},{9,8},{10,11... | collective-permute-start | bytes 589832 | tf_op jit(solution)/shard_map/ppermute | solution.py:409
  23.2 18.8 %collective-permute-start.13 = (bf16[2064,128]{1,0:T(8,128)(2,1)S(1)}, bf16[2064,128]{1,0:T(8,128)(2,1)S(1)}, u32[]{:S(2)}, u32[]{:S(2)}) collective-permute-start(bf16[2064,128]{1,0:T(8,128)(2,1)S(1)} %hold.9.refs_1_.refs_2_), channel_id=1, source_target_pairs={{0,8},{1,9},{2,10},{3,11},{4,0},{5,1},{6,2},{7,3},{8,12},{9,13},{1... | collective-permute-start | bytes 1585160 | tf_op jit(solution)/shard_map/ppermute | solution.py:403
  24.8 17.2 %collective-permute-start.14 = (bf16[96,2048]{1,0:T(8,128)(2,1)S(1)}, bf16[96,2048]{1,0:T(8,128)(2,1)S(1)}, u32[]{:S(2)}, u32[]{:S(2)}) collective-permute-start(bf16[96,2048]{1,0:T(8,128)(2,1)S(1)} %join.14.refs_1_), channel_id=1, source_target_pairs={{0,2},{1,3},{2,0},{3,1},{4,6},{5,7},{6,4},{7,5},{8,10},{9,11},{10,... | collective-permute-start | bytes 1179656 | tf_op jit(solution)/shard_map/ppermute | solution.py:406
  31.0 1.5 %collective-permute-start.11 = (bf16[48,2048]{1,0:T(8,128)(2,1)S(1)}, bf16[48,2048]{1,0:T(8,128)(2,1)S(1)}, u32[]{:S(2)}, u32[]{:S(2)}) collective-permute-start(bf16[48,2048]{1,0:T(8,128)(2,1)S(1)} %get-tuple-element.102), channel_id=1, source_target_pairs={{0,1},{1,0},{2,3},{3,2},{4,5},{5,4},{6,7},{7,6},{8,9},{9,8},{10,11... | collective-permute-start | bytes 589832 | tf_op jit(solution)/shard_map/ppermute | solution.py:409
  31.1 1.7 %collective-permute-start.12 = (bf16[48,2048]{1,0:T(8,128)(2,1)S(1)}, bf16[48,2048]{1,0:T(8,128)(2,1)S(1)}, u32[]{:S(2)}, u32[]{:S(2)}) collective-permute-start(bf16[48,2048]{1,0:T(8,128)(2,1)S(1)} %get-tuple-element.104), channel_id=1, source_target_pairs={{0,1},{1,0},{2,3},{3,2},{4,5},{5,4},{6,7},{7,6},{8,9},{9,8},{10,11... | collective-permute-start | bytes 589832 | tf_op jit(solution)/shard_map/ppermute | solution.py:409
  32.8 13.9 %collective-permute-start.19 = (bf16[96,2048]{1,0:T(8,128)(2,1)S(1)}, bf16[96,2048]{1,0:T(8,128)(2,1)S(1)}, u32[]{:S(2)}, u32[]{:S(2)}) collective-permute-start(bf16[96,2048]{1,0:T(8,128)(2,1)S(1)} %join.15.refs_10_), channel_id=1, source_target_pairs={{0,2},{1,3},{2,0},{3,1},{4,6},{5,7},{6,4},{7,5},{8,10},{9,11},{10,... | collective-permute-start | bytes 1179656 | tf_op jit(solution)/shard_map/ppermute | solution.py:406
  34.4 19.6 %collective-permute-start.18 = (bf16[128,2048]{1,0:T(8,128)(2,1)S(1)}, bf16[128,2048]{1,0:T(8,128)(2,1)S(1)}, u32[]{:S(2)}, u32[]{:S(2)}) collective-permute-start(bf16[128,2048]{1,0:T(8,128)(2,1)S(1)} %hold.10.refs_1_.refs_2_), channel_id=1, source_target_pairs={{0,8},{1,9},{2,10},{3,11},{4,0},{5,1},{6,2},{7,3},{8,12},{9,13},{1... | collective-permute-start | bytes 1572872 | tf_op jit(solution)/shard_map/ppermute | solution.py:403
  42.6 1.7 %collective-permute-start.16 = (bf16[48,2048]{1,0:T(8,128)(2,1)S(1)}, bf16[48,2048]{1,0:T(8,128)(2,1)S(1)}, u32[]{:S(2)}, u32[]{:S(2)}) collective-permute-start(bf16[48,2048]{1,0:T(8,128)(2,1)S(1)} %get-tuple-element.113), channel_id=1, source_target_pairs={{0,1},{1,0},{2,3},{3,2},{4,5},{5,4},{6,7},{7,6},{8,9},{9,8},{10,11... | collective-permute-start | bytes 589832 | tf_op jit(solution)/shard_map/ppermute | solution.py:409
  44.4 11.5 %collective-permute-start.17 = (bf16[96,2048]{1,0:T(8,128)(2,1)S(1)}, bf16[96,2048]{1,0:T(8,128)(2,1)S(1)}, u32[]{:S(2)}, u32[]{:S(2)}) collective-permute-start(bf16[96,2048]{1,0:T(8,128)(2,1)S(1)} %join.16.refs_10_), channel_id=1, source_target_pairs={{0,2},{1,3},{2,0},{3,1},{4,6},{5,7},{6,4},{7,5},{8,10},{9,11},{10,... | collective-permute-start | bytes 1179656 | tf_op jit(solution)/shard_map/ppermute | solution.py:406
  49.3 4.0 %collective-permute-start.20 = (bf16[32,2176]{1,0:T(8,128)(2,1)S(1)}, bf16[32,2176]{1,0:T(8,128)(2,1)S(1)}, u32[]{:S(2)}, u32[]{:S(2)}) collective-permute-start(bf16[32,2176]{1,0:T(8,128)(2,1)S(1)} %slice.44), channel_id=1, source_target_pairs={{0,1},{1,0},{2,3},{3,2},{4,5},{5,4},{6,7},{7,6},{8,9},{9,8},{10,11... | collective-permute-start | bytes 417800 | tf_op jit(solution)/shard_map/ppermute | solution.py:409
  49.4 15.0 %collective-permute-start.26 = (bf16[2064,128]{1,0:T(8,128)(2,1)S(1)}, bf16[2064,128]{1,0:T(8,128)(2,1)S(1)}, u32[]{:S(2)}, u32[]{:S(2)}) collective-permute-start(bf16[2064,128]{1,0:T(8,128)(2,1)S(1)} %hold.11.refs_1_.refs_2_), channel_id=1, source_target_pairs={{0,8},{1,9},{2,10},{3,11},{4,0},{5,1},{6,2},{7,3},{8,12},{9,13},{1... | collective-permute-start | bytes 1585160 | tf_op jit(solution)/shard_map/ppermute | solution.py:403
  53.5 12.1 %collective-permute-start.27 = (bf16[1552,128]{1,0:T(8,128)(2,1)S(1)}, bf16[1552,128]{1,0:T(8,128)(2,1)S(1)}, u32[]{:S(2)}, u32[]{:S(2)}) collective-permute-start(bf16[1552,128]{1,0:T(8,128)(2,1)S(1)} %join.17.refs_1_), channel_id=1, source_target_pairs={{0,2},{1,3},{2,0},{3,1},{4,6},{5,7},{6,4},{7,5},{8,10},{9,11},{10,... | collective-permute-start | bytes 1191944 | tf_op jit(solution)/shard_map/ppermute | solution.py:406
  54.4 1.5 %collective-permute-start.23 = (bf16[32,2048]{1,0:T(8,128)(2,1)S(1)}, bf16[32,2048]{1,0:T(8,128)(2,1)S(1)}, u32[]{:S(2)}, u32[]{:S(2)}) collective-permute-start(bf16[32,2048]{1,0:T(8,128)(2,1)S(1)} %slice.46), channel_id=1, source_target_pairs={{0,1},{1,0},{2,3},{3,2},{4,5},{5,4},{6,7},{7,6},{8,9},{9,8},{10,11... | collective-permute-start | bytes 393224 | tf_op jit(solution)/shard_map/ppermute | solution.py:409
  56.0 19.7 %collective-permute-start.28 = (bf16[128,2048]{1,0:T(8,128)(2,1)S(1)}, bf16[128,2048]{1,0:T(8,128)(2,1)S(1)}, u32[]{:S(2)}, u32[]{:S(2)}) collective-permute-start(bf16[128,2048]{1,0:T(8,128)(2,1)S(1)} %hold.13.refs_1_), channel_id=1, source_target_pairs={{0,8},{1,9},{2,10},{3,11},{4,0},{5,1},{6,2},{7,3},{8,12},{9,13},{1... | collective-permute-start | bytes 1572872 | tf_op jit(solution)/shard_map/ppermute | solution.py:403
  59.9 14.1 %collective-permute-start.25 = (bf16[96,2048]{1,0:T(8,128)(2,1)S(1)}, bf16[96,2048]{1,0:T(8,128)(2,1)S(1)}, u32[]{:S(2)}, u32[]{:S(2)}) collective-permute-start(bf16[96,2048]{1,0:T(8,128)(2,1)S(1)} %join.18.refs_1_), channel_id=1, source_target_pairs={{0,2},{1,3},{2,0},{3,1},{4,6},{5,7},{6,4},{7,5},{8,10},{9,11},{10,... | collective-permute-start | bytes 1179656 | tf_op jit(solution)/shard_map/ppermute | solution.py:406
  61.4 7.0 %collective-permute-start.29 = (bf16[48,2176]{1,0:T(8,128)(2,1)S(1)}, bf16[48,2176]{1,0:T(8,128)(2,1)S(1)}, u32[]{:S(2)}, u32[]{:S(2)}) collective-permute-start(bf16[48,2176]{1,0:T(8,128)(2,1)S(1)} %get-tuple-element.126), channel_id=1, source_target_pairs={{0,1},{1,0},{2,3},{3,2},{4,5},{5,4},{6,7},{7,6},{8,9},{9,8},{10,11... | collective-permute-start | bytes 626696 | tf_op jit(solution)/shard_map/ppermute | solution.py:409
  66.2 1.5 %collective-permute-start.30 = (bf16[32,2048]{1,0:T(8,128)(2,1)S(1)}, bf16[32,2048]{1,0:T(8,128)(2,1)S(1)}, u32[]{:S(2)}, u32[]{:S(2)}) collective-permute-start(bf16[32,2048]{1,0:T(8,128)(2,1)S(1)} %slice.48), channel_id=1, source_target_pairs={{0,1},{1,0},{2,3},{3,2},{4,5},{5,4},{6,7},{7,6},{8,9},{9,8},{10,11... | collective-permute-start | bytes 393224 | tf_op jit(solution)/shard_map/ppermute | solution.py:409
  67.5 5.3 %collective-permute-start.32 = (bf16[48,2048]{1,0:T(8,128)(2,1)S(1)}, bf16[48,2048]{1,0:T(8,128)(2,1)S(1)}, u32[]{:S(2)}, u32[]{:S(2)}) collective-permute-start(bf16[48,2048]{1,0:T(8,128)(2,1)S(1)} %get-tuple-element.130), channel_id=1, source_target_pairs={{0,1},{1,0},{2,3},{3,2},{4,5},{5,4},{6,7},{7,6},{8,9},{9,8},{10,11... | collective-permute-start | bytes 589832 | tf_op jit(solution)/shard_map/ppermute | solution.py:409
  67.8 14.6 %collective-permute-start.35 = (bf16[96,2048]{1,0:T(8,128)(2,1)S(1)}, bf16[96,2048]{1,0:T(8,128)(2,1)S(1)}, u32[]{:S(2)}, u32[]{:S(2)}) collective-permute-start(bf16[96,2048]{1,0:T(8,128)(2,1)S(1)} %join.19.refs_4_), channel_id=1, source_target_pairs={{0,2},{1,3},{2,0},{3,1},{4,6},{5,7},{6,4},{7,5},{8,10},{9,11},{10,... | collective-permute-start | bytes 1179656 | tf_op jit(solution)/shard_map/ppermute | solution.py:406
  68.8 19.1 %collective-permute-start.39 = (bf16[144,2048]{1,0:T(8,128)(2,1)S(1)}, bf16[144,2048]{1,0:T(8,128)(2,1)S(1)}, u32[]{:S(2)}, u32[]{:S(2)}) collective-permute-start(bf16[144,2048]{1,0:T(8,128)(2,1)S(1)} %home.7.refs_1_), channel_id=1, source_target_pairs={{0,8},{1,9},{2,10},{3,11},{4,0},{5,1},{6,2},{7,3},{8,12},{9,13},{1... | collective-permute-start | bytes 1769480 | tf_op jit(solution)/shard_map/ppermute | solution.py:403
  76.1 1.7 %collective-permute-start.34 = (bf16[48,2048]{1,0:T(8,128)(2,1)S(1)}, bf16[48,2048]{1,0:T(8,128)(2,1)S(1)}, u32[]{:S(2)}, u32[]{:S(2)}) collective-permute-start(bf16[48,2048]{1,0:T(8,128)(2,1)S(1)} %get-tuple-element.134), channel_id=1, source_target_pairs={{0,1},{1,0},{2,3},{3,2},{4,5},{5,4},{6,7},{7,6},{8,9},{9,8},{10,11... | collective-permute-start | bytes 589832 | tf_op jit(solution)/shard_map/ppermute | solution.py:409
  76.6 2.7 %collective-permute-start.22 = (bf16[48,2048]{1,0:T(8,128)(2,1)S(1)}, bf16[48,2048]{1,0:T(8,128)(2,1)S(1)}, u32[]{:S(2)}, u32[]{:S(2)}) collective-permute-start(bf16[48,2048]{1,0:T(8,128)(2,1)S(1)} %get-tuple-element.121), channel_id=1, source_target_pairs={{0,1},{1,0},{2,3},{3,2},{4,5},{5,4},{6,7},{7,6},{8,9},{9,8},{10,11... | collective-permute-start | bytes 589832 | tf_op jit(solution)/shard_map/ppermute | solution.py:409
  77.8 13.0 %collective-permute-start.43 = (bf16[96,2048]{1,0:T(8,128)(2,1)S(1)}, bf16[96,2048]{1,0:T(8,128)(2,1)S(1)}, u32[]{:S(2)}, u32[]{:S(2)}) collective-permute-start(bf16[96,2048]{1,0:T(8,128)(2,1)S(1)} %join.20.refs_10_), channel_id=1, source_target_pairs={{0,2},{1,3},{2,0},{3,1},{4,6},{5,7},{6,4},{7,5},{8,10},{9,11},{10,... | collective-permute-start | bytes 1179656 | tf_op jit(solution)/shard_map/ppermute | solution.py:406
  82.4 5.4 %collective-permute-start.38 = (bf16[48,2176]{1,0:T(8,128)(2,1)S(1)}, bf16[48,2176]{1,0:T(8,128)(2,1)S(1)}, u32[]{:S(2)}, u32[]{:S(2)}) collective-permute-start(bf16[48,2176]{1,0:T(8,128)(2,1)S(1)} %get-tuple-element.143), channel_id=1, source_target_pairs={{0,1},{1,0},{2,3},{3,2},{4,5},{5,4},{6,7},{7,6},{8,9},{9,8},{10,11... | collective-permute-start | bytes 626696 | tf_op jit(solution)/shard_map/ppermute | solution.py:409
  82.4 1.8 %collective-permute-start.36 = (bf16[32,2176]{1,0:T(8,128)(2,1)S(1)}, bf16[32,2176]{1,0:T(8,128)(2,1)S(1)}, u32[]{:S(2)}, u32[]{:S(2)}) collective-permute-start(bf16[32,2176]{1,0:T(8,128)(2,1)S(1)} %slice.50), channel_id=1, source_target_pairs={{0,1},{1,0},{2,3},{3,2},{4,5},{5,4},{6,7},{7,6},{8,9},{9,8},{10,11... | collective-permute-start | bytes 417800 | tf_op jit(solution)/shard_map/ppermute | solution.py:409
  84.4 14.6 %collective-permute-start.49 = (bf16[1552,128]{1,0:T(8,128)(2,1)S(1)}, bf16[1552,128]{1,0:T(8,128)(2,1)S(1)}, u32[]{:S(2)}, u32[]{:S(2)}) collective-permute-start(bf16[1552,128]{1,0:T(8,128)(2,1)S(1)} %join.21.refs_4_), channel_id=1, source_target_pairs={{0,2},{1,3},{2,0},{3,1},{4,6},{5,7},{6,4},{7,5},{8,10},{9,11},{10,... | collective-permute-start | bytes 1191944 | tf_op jit(solution)/shard_map/ppermute | solution.py:406
  87.9 6.4 %collective-permute-start.40 = (bf16[48,2176]{1,0:T(8,128)(2,1)S(1)}, bf16[48,2176]{1,0:T(8,128)(2,1)S(1)}, u32[]{:S(2)}, u32[]{:S(2)}) collective-permute-start(bf16[48,2176]{1,0:T(8,128)(2,1)S(1)} %get-tuple-element.145), channel_id=1, source_target_pairs={{0,1},{1,0},{2,3},{3,2},{4,5},{5,4},{6,7},{7,6},{8,9},{9,8},{10,11... | collective-permute-start | bytes 626696 | tf_op jit(solution)/shard_map/ppermute | solution.py:409
  87.9 6.2 %collective-permute-start.41 = (bf16[32,2176]{1,0:T(8,128)(2,1)S(1)}, bf16[32,2176]{1,0:T(8,128)(2,1)S(1)}, u32[]{:S(2)}, u32[]{:S(2)}) collective-permute-start(bf16[32,2176]{1,0:T(8,128)(2,1)S(1)} %slice.52), channel_id=1, source_target_pairs={{0,1},{1,0},{2,3},{3,2},{4,5},{5,4},{6,7},{7,6},{8,9},{9,8},{10,11... | collective-permute-start | bytes 417800 | tf_op jit(solution)/shard_map/ppermute | solution.py:409
  88.5 5.1 %collective-permute-start.42 = (bf16[16,2176]{1,0:T(8,128)(2,1)S(1)}, bf16[16,2176]{1,0:T(8,128)(2,1)S(1)}, u32[]{:S(2)}, u32[]{:S(2)}) collective-permute-start(bf16[16,2176]{1,0:T(8,128)(2,1)S(1)} %slice.53), channel_id=1, source_target_pairs={{0,1},{1,0},{2,3},{3,2},{4,5},{5,4},{6,7},{7,6},{8,9},{9,8},{10,11... | collective-permute-start | bytes 208904 | tf_op jit(solution)/shard_map/ppermute | solution.py:409
  93.5 1.6 %collective-permute-start.44 = (bf16[32,2176]{1,0:T(8,128)(2,1)S(1)}, bf16[32,2176]{1,0:T(8,128)(2,1)S(1)}, u32[]{:S(2)}, u32[]{:S(2)}) collective-permute-start(bf16[32,2176]{1,0:T(8,128)(2,1)S(1)} %slice.54), channel_id=1, source_target_pairs={{0,1},{1,0},{2,3},{3,2},{4,5},{5,4},{6,7},{7,6},{8,9},{9,8},{10,11... | collective-permute-start | bytes 417800 | tf_op jit(solution)/shard_map/ppermute | solution.py:409
  94.1 1.6 %collective-permute-start.46 = (bf16[48,2176]{1,0:T(8,128)(2,1)S(1)}, bf16[48,2176]{1,0:T(8,128)(2,1)S(1)}, u32[]{:S(2)}, u32[]{:S(2)}) collective-permute-start(bf16[48,2176]{1,0:T(8,128)(2,1)S(1)} %get-tuple-element.152), channel_id=1, source_target_pairs={{0,1},{1,0},{2,3},{3,2},{4,5},{5,4},{6,7},{7,6},{8,9},{9,8},{10,11... | collective-permute-start | bytes 626696 | tf_op jit(solution)/shard_map/ppermute | solution.py:409
  95.2 13.3 %collective-permute-start.48 = (bf16[1552,128]{1,0:T(8,128)(2,1)S(1)}, bf16[1552,128]{1,0:T(8,128)(2,1)S(1)}, u32[]{:S(2)}, u32[]{:S(2)}) collective-permute-start(bf16[1552,128]{1,0:T(8,128)(2,1)S(1)} %join.22.refs_3_), channel_id=1, source_target_pairs={{0,2},{1,3},{2,0},{3,1},{4,6},{5,7},{6,4},{7,5},{8,10},{9,11},{10,... | collective-permute-start | bytes 1191944 | tf_op jit(solution)/shard_map/ppermute | solution.py:406
  99.2 9.2 %collective-permute-start.52 = (bf16[128,896]{1,0:T(8,128)(2,1)S(1)}, bf16[128,896]{1,0:T(8,128)(2,1)S(1)}, u32[]{:S(2)}, u32[]{:S(2)}) collective-permute-start(bf16[128,896]{1,0:T(8,128)(2,1)S(1)} %home.8.refs_5_), channel_id=1, source_target_pairs={{0,8},{1,9},{2,10},{3,11},{4,0},{5,1},{6,2},{7,3},{8,12},{9,13},{1... | collective-permute-start | bytes 688136 | tf_op jit(solution)/shard_map/ppermute | solution.py:403
  102.1 20.2 %collective-permute-start.47 = (bf16[1552,128]{1,0:T(8,128)(2,1)S(1)}, bf16[1552,128]{1,0:T(8,128)(2,1)S(1)}, u32[]{:S(2)}, u32[]{:S(2)}) collective-permute-start(bf16[1552,128]{1,0:T(8,128)(2,1)S(1)} %join.23.refs_5_), channel_id=1, source_target_pairs={{0,2},{1,3},{2,0},{3,1},{4,6},{5,7},{6,4},{7,5},{8,10},{9,11},{10,... | collective-permute-start | bytes 1191944 | tf_op jit(solution)/shard_map/ppermute | solution.py:406
  103.9 7.9 %collective-permute-start.51 = (bf16[128,640]{1,0:T(8,128)(2,1)S(1)}, bf16[128,640]{1,0:T(8,128)(2,1)S(1)}, u32[]{:S(2)}, u32[]{:S(2)}) collective-permute-start(bf16[128,640]{1,0:T(8,128)(2,1)S(1)} %home.9.refs_5_), channel_id=1, source_target_pairs={{0,8},{1,9},{2,10},{3,11},{4,0},{5,1},{6,2},{7,3},{8,12},{9,13},{1... | collective-permute-start | bytes 491528 | tf_op jit(solution)/shard_map/ppermute | solution.py:403
  104.9 10.4 %collective-permute-start.50 = (bf16[144,512]{1,0:T(8,128)(2,1)S(1)}, bf16[144,512]{1,0:T(8,128)(2,1)S(1)}, u32[]{:S(2)}, u32[]{:S(2)}) collective-permute-start(bf16[144,512]{1,0:T(8,128)(2,1)S(1)} %home.10.refs_16_), channel_id=1, source_target_pairs={{0,8},{1,9},{2,10},{3,11},{4,0},{5,1},{6,2},{7,3},{8,12},{9,13},{1... | collective-permute-start | bytes 442376 | tf_op jit(solution)/shard_map/ppermute | solution.py:403
  108.7 16.0 %collective-permute-start.53 = (bf16[128,896]{1,0:T(8,128)(2,1)S(1)}, bf16[128,896]{1,0:T(8,128)(2,1)S(1)}, u32[]{:S(2)}, u32[]{:S(2)}) collective-permute-start(bf16[128,896]{1,0:T(8,128)(2,1)S(1)} %home.11.refs_5_), channel_id=1, source_target_pairs={{0,8},{1,9},{2,10},{3,11},{4,0},{5,1},{6,2},{7,3},{8,12},{9,13},{1... | collective-permute-start | bytes 688136 | tf_op jit(solution)/shard_map/ppermute | solution.py:403
  112.1 12.7 %collective-permute-start.54 = (bf16[128,640]{1,0:T(8,128)(2,1)S(1)}, bf16[128,640]{1,0:T(8,128)(2,1)S(1)}, u32[]{:S(2)}, u32[]{:S(2)}) collective-permute-start(bf16[128,640]{1,0:T(8,128)(2,1)S(1)} %home.12.refs_5_), channel_id=1, source_target_pairs={{0,8},{1,9},{2,10},{3,11},{4,0},{5,1},{6,2},{7,3},{8,12},{9,13},{1... | collective-permute-start | bytes 491528 | tf_op jit(solution)/shard_map/ppermute | solution.py:403
  115.5 9.2 %collective-permute-start.55 = (bf16[144,512]{1,0:T(8,128)(2,1)S(1)}, bf16[144,512]{1,0:T(8,128)(2,1)S(1)}, u32[]{:S(2)}, u32[]{:S(2)}) collective-permute-start(bf16[144,512]{1,0:T(8,128)(2,1)S(1)} %home.13.refs_16_), channel_id=1, source_target_pairs={{0,8},{1,9},{2,10},{3,11},{4,0},{5,1},{6,2},{7,3},{8,12},{9,13},{1... | collective-permute-start | bytes 442376 | tf_op jit(solution)/shard_map/ppermute | solution.py:403
  (15 other events, 63.1 us)
